TPU v7x, 256 devices: a whole 4x4x8 slice. The times are simulated.
256 devices in a mesh: gx: 8 (over z_lo, y), gy: 4 (over z_hi), gz: 8 (over x, core).
Axes of the slice: x: 4, y: 4, z: 8 (z_hi: 4, z_lo: 2; z = z_hi * 2 + z_lo), core: 2. Of those that a mesh axis runs over, the one named last changes fastest.
Arguments:
- tokens: bfloat16 [1024, 12288], P(('gy', 'gz'), 'gx'), may hold values from -6 to 6
- weight_in: bfloat16 [12288, 24576], P('gx', ('gy', 'gz')), may hold values from -0.0546875 to 0.0546875
- bias_hidden: float32 [24576], P(('gy', 'gz')), may hold values from -3 to 3
- weight_out: bfloat16 [24576, 12288], P(('gy', 'gz'), 'gx'), may hold values from -0.0390625 to 0.0390625
- grad_output: bfloat16 [1024, 12288], P(('gy', 'gz'), 'gx'), may hold values from -6 to 6
Outputs:
- grad_tokens: bfloat16 [1024, 12288], P(('gy', 'gz'), 'gx')
- grad_weight_in: bfloat16 [12288, 24576], P('gx', ('gy', 'gz'))
- grad_weight_out: bfloat16 [24576, 12288], P(('gy', 'gz'), 'gx')
All inputs are finite; a program needn't handle non-finite values.
Results may differ from a plain program's by a relative error of at most 0.005.
Values may be sent and summed in bfloat16 or wider, within the bound.
No kernel may reach another device: no remote copies, remote signals or barrier semaphores. Data moves between devices by JAX's collectives and lax.ppermute only.
A program may use at most 128 MiB of HBM per device.

v0:
```python
import math

import jax
import jax.numpy as jnp
from jax import lax
from jax.sharding import PartitionSpec as P

root_coef = math.sqrt(2.0 / math.pi)
cubic_coef = 0.044715


def gelu_pair(pre_act, upstream):
    tanh_part = jnp.tanh(root_coef * (pre_act + cubic_coef * pre_act * pre_act * pre_act))
    activation = 0.5 * pre_act * (1.0 + tanh_part)
    slope_value = 0.5 * (1.0 + tanh_part) + 0.5 * pre_act * (
        1.0 - tanh_part * tanh_part
    ) * root_coef * (1.0 + 3.0 * cubic_coef * pre_act * pre_act)
    return (activation.astype(jnp.bfloat16), (upstream * slope_value).astype(jnp.bfloat16))


def contract_last(left, right):
    return lax.dot_general(
        left, right, (((1,), (1,)), ((), ())), preferred_element_type=jnp.float32
    )


def contract_first(left, right):
    return lax.dot_general(
        left, right, (((0,), (0,)), ((), ())), preferred_element_type=jnp.float32
    )


def shards(tokens, weight_in, bias_hidden, weight_out, grad_output):
    tokens_all, grad_all = (
        lax.all_gather(tokens, ("gy", "gz"), axis=0, tiled=True),
        lax.all_gather(grad_output, ("gy", "gz"), axis=0, tiled=True),
    )
    total_rows = tokens_all.shape[0]
    norm_scale = 1.0 / math.sqrt(total_rows)
    pre_act = (
        lax.psum_scatter(
            jnp.dot(tokens_all, weight_in, preferred_element_type=jnp.float32),
            "gx",
            scatter_dimension=0,
            tiled=True,
        )
        + bias_hidden
    )
    upstream = lax.psum_scatter(
        contract_last(grad_all, weight_out), "gx", scatter_dimension=0, tiled=True
    )
    act_share, grad_share = gelu_pair(pre_act, upstream)
    activation, grad_hidden = (
        lax.all_gather(act_share, "gx", axis=0, tiled=True),
        lax.all_gather(grad_share, "gx", axis=0, tiled=True),
    )
    grad_weight_out = (contract_first(activation, grad_all) * norm_scale).astype(jnp.bfloat16)
    grad_weight_in = (contract_first(tokens_all, grad_hidden) * norm_scale).astype(jnp.bfloat16)
    grad_tokens = lax.psum_scatter(
        contract_last(grad_hidden, weight_in), ("gy", "gz"), scatter_dimension=0, tiled=True
    ).astype(jnp.bfloat16)
    return (grad_tokens, grad_weight_in, grad_weight_out)


def solution(mesh):
    return jax.shard_map(
        shards,
        mesh=mesh,
        in_specs=(
            P(("gy", "gz"), "gx"),
            P("gx", ("gy", "gz")),
            P(("gy", "gz")),
            P(("gy", "gz"), "gx"),
            P(("gy", "gz"), "gx"),
        ),
        out_specs=(P(("gy", "gz"), "gx"), P("gx", ("gy", "gz")), P(("gy", "gz"), "gx")),
        check_vma=False,
    )
```

profile of v0, /device:TPU:32, one launch (start us, length us, event | category | flops | bytes accessed | tf_op | source)
XLA Modules:
  0.0 436.5 jit_solution(4649984326041252300)
XLA Ops:
  7.2 0.0 copy-start
  7.2 0.0 all-gather.5.cloned.1.call-start
  7.2 0.7 all-gather.5.cloned.1.call-update
  7.9 0.0 all-gather.7.cloned.1.call-start
  8.0 0.7 all-gather.7.cloned.1.call-update
  8.7 0.0 reduce-scatter.4.cloned.1.call-start
  8.7 60.4 %all-gather.5.cloned.1.call-done = bf16[1024,1536]{1,0:T(8,128)(2,1)} async-done(((bf16[32,1536]{1,0:T(8,128)(2,1)}), bf16[1024,1536]{1,0:T(8,128)(2,1)}) %all-gather.5.cloned.1.call-update) | async-done | bytes 3145744 | tf_op jit(solution)/shard_map/all_gather | solution.py:36
  69.2 6.9 %fusion.8 = f32[1024,768]{1,0:T(8,128)} fusion(bf16[1024,1536]{1,0:T(8,128)(2,1)} %all-gather.5.cloned.1.call-done, bf16[768,1536]{1,0:T(8,128)(2,1)} %param.8), kind=kOutput, calls=%fused_computation.13 | convolution fusion | flops 2415919104 | bytes 8650752 | tf_op jit(solution)/shard_map/dot_general | solution.py:22
  76.1 0.0 reduce-scatter.4.cloned.1.call-update
  76.1 0.0 reduce-scatter.6.cloned.1.call-start
  76.1 50.4 %all-gather.7.cloned.1.call-done = bf16[1024,1536]{1,0:T(8,128)(2,1)} async-done(((bf16[32,1536]{1,0:T(8,128)(2,1)}), bf16[1024,1536]{1,0:T(8,128)(2,1)}) %all-gather.7.cloned.1.call-update) | async-done | bytes 3145744 | tf_op jit(solution)/shard_map/all_gather | solution.py:35
  126.6 0.0 copy-done
  126.6 6.2 %fusion.9 = f32[1024,768]{1,0:T(8,128)} fusion(bf16[1024,1536]{1,0:T(8,128)(2,1)} %all-gather.7.cloned.1.call-done, bf16[1536,768]{1,0:T(8,128)(2,1)S(1)} %copy-done), kind=kOutput, calls=%fused_computation.14 | convolution fusion | flops 2415919104 | bytes 8650752 | tf_op jit(solution)/shard_map/dot_general | solution.py:42
  132.7 0.0 copy-start.1
  132.7 0.0 reduce-scatter.6.cloned.1.call-update
  132.7 0.0 all-gather.9.cloned.1.call-start
  132.8 43.2 %reduce-scatter.4.cloned.1.call-done = f32[128,768]{1,0:T(8,128)} async-done(((f32[1024,768]{1,0:T(8,128)}), f32[128,768]{1,0:T(8,128)}) %reduce-scatter.4.cloned.1.call-update) | async-done | bytes 393232 | tf_op jit(solution)/shard_map/reduce_scatter | solution.py:49
  176.0 50.1 %reduce-scatter.6.cloned.1.call-done = f32[128,768]{1,0:T(8,128)} async-done(((f32[1024,768]{1,0:T(8,128)}), f32[128,768]{1,0:T(8,128)}) %reduce-scatter.6.cloned.1.call-update) | async-done | bytes 393232 | tf_op jit(solution)/shard_map/reduce_scatter | solution.py:41
  226.0 0.0 copy-done.1
  226.0 2.1 multiply_convert_fusion.2
  228.2 0.0 all-gather.9.cloned.1.call-update
  228.2 0.0 all-gather.11.cloned.1.call-start
  228.2 0.5 all-gather.11.cloned.1.call-update
  228.8 0.0 reduce-scatter.8.cloned.1.call-start
  228.8 42.5 %all-gather.9.cloned.1.call-done = bf16[1024,768]{1,0:T(8,128)(2,1)} async-done(((bf16[128,768]{1,0:T(8,128)(2,1)}), bf16[1024,768]{1,0:T(8,128)(2,1)}) %all-gather.9.cloned.1.call-update) | async-done | bytes 1572880 | tf_op jit(solution)/shard_map/all_gather | solution.py:55
  271.3 6.1 %fusion.10 = f32[1024,1536]{1,0:T(8,128)} fusion(bf16[1024,768]{1,0:T(8,128)(2,1)} %all-gather.9.cloned.1.call-done, bf16[1536,768]{1,0:T(8,128)(2,1)S(1)} %copy-done), kind=kOutput, calls=%fused_computation.15 | convolution fusion | flops 2415919104 | bytes 10223616 | tf_op jit(solution)/shard_map/dot_general | solution.py:22
  277.4 0.0 reduce-scatter.8.cloned.1.call-update
  277.4 6.4 %fusion = bf16[1536,768]{0,1:T(8,128)(2,1)} fusion(bf16[1024,768]{1,0:T(8,128)(2,1)} %all-gather.9.cloned.1.call-done, bf16[1024,1536]{1,0:T(8,128)(2,1)} %all-gather.7.cloned.1.call-done), kind=kOutput, calls=%fused_computation.2 | convolution fusion | flops 2418278400 | bytes 7077888 | tf_op jit(solution)/shard_map/dot_general | solution.py:28
  283.8 4.3 copy.8
  288.2 27.2 %all-gather.11.cloned.1.call-done = bf16[1024,768]{1,0:T(8,128)(2,1)} async-done(((bf16[128,768]{1,0:T(8,128)(2,1)}), bf16[1024,768]{1,0:T(8,128)(2,1)}) %all-gather.11.cloned.1.call-update) | async-done | bytes 1572880 | tf_op jit(solution)/shard_map/all_gather | solution.py:54
  315.4 6.4 %multiply_convert_fusion = bf16[768,1536]{1,0:T(8,128)(2,1)} fusion(bf16[1024,768]{1,0:T(8,128)(2,1)} %all-gather.11.cloned.1.call-done, bf16[1024,1536]{1,0:T(8,128)(2,1)} %all-gather.5.cloned.1.call-done), kind=kOutput, calls=%fused_computation | convolution fusion | flops 2418278400 | bytes 7077888 | tf_op jit(solution)/shard_map/dot_general | solution.py:28
  321.8 106.3 %reduce-scatter.8.cloned.1.call-done = f32[32,1536]{1,0:T(8,128)} async-done(((f32[1024,1536]{1,0:T(8,128)}), f32[32,1536]{1,0:T(8,128)}) %reduce-scatter.8.cloned.1.call-update) | async-done | bytes 196624 | tf_op jit(solution)/shard_map/reduce_scatter | solution.py:59
  428.1 1.6 convert_element_type.19
Async XLA Ops:
  7.2 119.4 %copy-start = (bf16[1536,768]{1,0:T(8,128)(2,1)S(1)}, bf16[1536,768]{1,0:T(8,128)(2,1)}, u32[]{:S(2)}) copy-start(bf16[1536,768]{1,0:T(8,128)(2,1)} %param.6) | copy-start | bytes 7077892
  7.2 62.0 %all-gather.5.cloned.1.call-start = ((), (), s32[]{:S(2)}) async-start(), calls=%async_computation.3 | async-start | bytes 3244032 | tf_op jit(solution)/shard_map/all_gather | solution.py:36
  7.9 118.6 %all-gather.7.cloned.1.call-start = ((), (), s32[]{:S(2)}) async-start(), calls=%async_computation.5 | async-start | bytes 3244032 | tf_op jit(solution)/shard_map/all_gather | solution.py:35
  8.7 167.3 %reduce-scatter.4.cloned.1.call-start = ((), (), s32[]{:S(2)}) async-start(), calls=%async_computation.4 | async-start | bytes 3538944 | tf_op jit(solution)/shard_map/reduce_scatter | solution.py:49
  76.1 149.9 %reduce-scatter.6.cloned.1.call-start = ((), (), s32[]{:S(2)}) async-start(), calls=%async_computation.6 | async-start | bytes 3538944 | tf_op jit(solution)/shard_map/reduce_scatter | solution.py:41
  132.7 93.3 %copy-start.1 = (f32[768]{0:T(1024)S(1)}, f32[768]{0:T(1024)}, u32[]{:S(2)}) copy-start(f32[768]{0:T(1024)} %param.7) | copy-start | bytes 9220
  132.7 138.6 %all-gather.9.cloned.1.call-start = ((), (), s32[]{:S(2)}) async-start(), calls=%async_computation.7 | async-start | bytes 1769472 | tf_op jit(solution)/shard_map/all_gather | solution.py:55
  228.2 87.2 %all-gather.11.cloned.1.call-start = ((), (), s32[]{:S(2)}) async-start(), calls=%async_computation.9 | async-start | bytes 1769472 | tf_op jit(solution)/shard_map/all_gather | solution.py:54
  228.8 199.3 %reduce-scatter.8.cloned.1.call-start = ((), (), s32[]{:S(2)}) async-start(), calls=%async_computation.8 | async-start | bytes 6488064 | tf_op jit(solution)/shard_map/reduce_scatter | solution.py:59
Sparse Core Ops, SparseCore 0:
  10.6 58.5 all-gather.4
  71.7 54.8 all-gather.6
  129.1 46.7 reduce-scatter.3
  178.4 47.6 reduce-scatter.5
  228.3 42.9 all-gather.8
  272.9 42.3 all-gather.10
  319.4 108.6 reduce-scatter.7
where the time goes:
time: 438 us; the launch traced here: 436 us
  waiting for transfers between devices  382 us (87%)
  matrix products  32 us (7%)
  between operations  14.1 us (3%)
    reduce_scatter x1, waiting for transfers between devices, shards(): lax.psum_scatter(contract_last(grad_hidden, weight_in), ('gy', 'gz'), sca...  106 us
    all_gather x1, waiting for transfers between devices, shards(): lax.all_gather(grad_output, ('gy', 'gz'), axis=0, tiled=True)  60.4 us
    all_gather x1, waiting for transfers between devices, shards(): lax.all_gather(tokens, ('gy', 'gz'), axis=0, tiled=True)  50.4 us
    reduce_scatter x1, waiting for transfers between devices, shards(): lax.psum_scatter(jnp.dot(tokens_all, weight_in, preferred_element_type=jn...  50.1 us
    reduce_scatter x1, waiting for transfers between devices, shards(): lax.psum_scatter(contract_last(grad_all, weight_out), 'gx', scatter_dimen...  43.2 us
    all_gather x1, waiting for transfers between devices, shards(): lax.all_gather(grad_share, 'gx', axis=0, tiled=True)  42.5 us
    all_gather x1, waiting for transfers between devices, shards(): lax.all_gather(act_share, 'gx', axis=0, tiled=True)  27.2 us
    dot_general x2, matrix products, contract_last(): lax.dot_general(left, right, (((1,), (1,)), ((), ())), preferred_element_...  13 us
  transfers between devices with their start and end apart: 7, of which 7 were waited for; matrix products, arithmetic and copies ran while one was open for 8% of the time, Pallas kernels for 0%

commit v1 on v0

v1 whole, which is shorter than its diff:
```python
import math

import jax
import jax.numpy as jnp
from jax import lax
from jax.sharding import PartitionSpec as P

root_coef = math.sqrt(2.0 / math.pi)
cubic_coef = 0.044715
bf16 = jnp.bfloat16
f32 = jnp.float32


def gelu_pair(pre_act, upstream):
    tanh_part = jnp.tanh(root_coef * (pre_act + cubic_coef * pre_act * pre_act * pre_act))
    activation = 0.5 * pre_act * (1.0 + tanh_part)
    slope_value = 0.5 * (1.0 + tanh_part) + 0.5 * pre_act * (
        1.0 - tanh_part * tanh_part
    ) * root_coef * (1.0 + 3.0 * cubic_coef * pre_act * pre_act)
    return (activation.astype(bf16), (upstream * slope_value).astype(bf16))


def contract_last(left, right):
    return lax.dot_general(left, right, (((1,), (1,)), ((), ())), preferred_element_type=f32)


def contract_first(left, right):
    return lax.dot_general(left, right, (((0,), (0,)), ((), ())), preferred_element_type=f32)


def solution(mesh):
    n_x, n_y, n_z = (mesh.shape[a] for a in ("gx", "gy", "gz"))

    def shift_y(a, k):
        return lax.ppermute(a, "gy", [(i, (i + k) % n_y) for i in range(n_y)])

    def shift_chip(a, k):
        return lax.ppermute(a, "gz", [(i, (i + 2 * k) % n_z) for i in range(n_z)])

    def swap_core(a):
        return lax.ppermute(a, "gz", [(i, i ^ 1) for i in range(n_z)])

    def gather_rows(a):
        a = jnp.concatenate([a] + [shift_y(a, k) for k in range(1, n_y)], axis=0)
        a = jnp.concatenate([a] + [shift_chip(a, k) for k in range(1, n_z // 2)], axis=0)
        return jnp.concatenate([a, swap_core(a)], axis=0)

    def scatter_rows(a):
        half = a.shape[0] // 2
        a = a[:half] + swap_core(a[half:].astype(bf16)).astype(f32)
        for shift, n in ((shift_chip, n_z // 2), (shift_y, n_y)):
            rows = a.shape[0] // n
            total = a[:rows]
            for k in range(1, n):
                part = a[k * rows : (k + 1) * rows].astype(bf16)
                total = total + shift(part, -k).astype(f32)
            a = total
        return a.astype(bf16)

    def sum_width(part):
        part = part.astype(bf16).reshape(n_x, part.shape[0] // n_x, part.shape[1])
        parts = lax.all_to_all(part, "gx", 0, 0, tiled=True)
        return jnp.sum(parts.astype(f32), axis=0)

    def gather_width(share):
        copies = jnp.broadcast_to(share[None], (n_x, *share.shape))
        parts = lax.all_to_all(copies, "gx", 0, 0, tiled=True)
        return parts.reshape(-1, share.shape[1])

    def shards(tokens, weight_in, bias_hidden, weight_out, grad_output):
        tokens_all = gather_rows(tokens)
        grad_all = gather_rows(grad_output)
        norm_scale = 1.0 / math.sqrt(tokens_all.shape[0])
        pre_act = sum_width(jnp.dot(tokens_all, weight_in, preferred_element_type=f32)) + bias_hidden
        upstream = sum_width(contract_last(grad_all, weight_out))
        act_share, grad_share = gelu_pair(pre_act, upstream)
        grad_hidden = gather_width(grad_share)
        grad_tokens = scatter_rows(contract_last(grad_hidden, weight_in))
        activation = gather_width(act_share)
        grad_weight_in = (contract_first(tokens_all, grad_hidden) * norm_scale).astype(bf16)
        grad_weight_out = (contract_first(activation, grad_all) * norm_scale).astype(bf16)
        return (grad_tokens, grad_weight_in, grad_weight_out)

    return jax.shard_map(
        shards,
        mesh=mesh,
        in_specs=(
            P(("gy", "gz"), "gx"),
            P("gx", ("gy", "gz")),
            P(("gy", "gz")),
            P(("gy", "gz"), "gx"),
            P(("gy", "gz"), "gx"),
        ),
        out_specs=(P(("gy", "gz"), "gx"), P("gx", ("gy", "gz")), P(("gy", "gz"), "gx")),
        check_vma=False,
    )
```

time: 438 us -> 204 us (0.47)
  waiting for transfers between devices: 382 us -> 78.9 us
  starting transfers between devices: 0.28 us -> 55.6 us
  blocking collectives: 0 us -> 24.2 us
  between operations: 14.1 us -> 0.93 us
  matrix products: 32 us -> 22.3 us
  local copies, waits for them, and re-layouts: 4.35 us -> 13 us
  other arithmetic: 3.71 us -> 8.46 us
    reduce_scatter x3 -> x0, waiting for transfers between devices: 199 us -> none  [the longest x1 106 us: shards(): lax.psum_scatter(contract_last(grad_hidden, weight_in), ('gy', 'gz'), sca...]
    all_gather x4 -> x0, waiting for transfers between devices: 181 us -> none  [the longest x1 60.4 us: shards(): lax.all_gather(grad_output, ('gy', 'gz'), axis=0, tiled=True)]
    ppermute x0 -> x21, waiting for transfers between devices: none -> 52.2 us  [the longest x9 43.4 us: shift_chip(): return lax.ppermute(a, 'gz', [(i, (i + 2 * k) % n_z) for i in range(n_z)])]
    ppermute x0 -> x21, starting transfers between devices: none -> 39.7 us  [the longest x9 24.4 us: shift_y(): return lax.ppermute(a, 'gy', [(i, (i + k) % n_y) for i in range(n_y)])]
    all_to_all x0 -> x3, waiting for transfers between devices: none -> 26.7 us  [the longest x2 26.7 us: sum_width(): parts = lax.all_to_all(part, 'gx', 0, 0, tiled=True)]
    all_to_all x0 -> x1, blocking collectives: none -> 24.2 us  [gather_width(): parts = lax.all_to_all(copies, 'gx', 0, 0, tiled=True)]
    all_to_all x0 -> x3, starting transfers between devices: none -> 16 us  [the longest x2 10.3 us: sum_width(): parts = lax.all_to_all(part, 'gx', 0, 0, tiled=True)]
    dot_general x2, matrix products: 13 us -> 8.3 us  [contract_last(): lax.dot_general(left, right, (((1,), (1,)), ((), ())), preferred_element_...]
  transfers between devices with their start and end apart: 7 -> 24, of which waited for: 7 -> 12; matrix products, arithmetic and copies ran while one was open for 8% -> 15% of each run, Pallas kernels for 0% -> 0%
where the time goes in v1:
time: 204 us; the launch traced here: 203 us
  waiting for transfers between devices  78.9 us (39%)
  starting transfers between devices  55.6 us (27%)
  blocking collectives  24.2 us (12%)
  matrix products  22.3 us (11%)
  local copies, waits for them, and re-layouts  13 us (6%)
  other arithmetic  8.46 us (4%)
    ppermute x9, waiting for transfers between devices, shift_chip(): return lax.ppermute(a, 'gz', [(i, (i + 2 * k) % n_z) for i in range(n_z)])  43.4 us
    all_to_all x2, waiting for transfers between devices, sum_width(): parts = lax.all_to_all(part, 'gx', 0, 0, tiled=True)  26.7 us
    ppermute x9, starting transfers between devices, shift_y(): return lax.ppermute(a, 'gy', [(i, (i + k) % n_y) for i in range(n_y)])  24.4 us
    all_to_all x1, blocking collectives, gather_width(): parts = lax.all_to_all(copies, 'gx', 0, 0, tiled=True)  24.2 us
    ppermute x9, starting transfers between devices, shift_chip(): return lax.ppermute(a, 'gz', [(i, (i + 2 * k) % n_z) for i in range(n_z)])  15.1 us
    dot_general x2, matrix products, contract_first(): lax.dot_general(left, right, (((0,), (0,)), ((), ())), preferred_element_...  10.4 us
    all_to_all x2, starting transfers between devices, sum_width(): parts = lax.all_to_all(part, 'gx', 0, 0, tiled=True)  10.3 us
    dot_general x2, matrix products, contract_last(): lax.dot_general(left, right, (((1,), (1,)), ((), ())), preferred_element_...  8.3 us
  transfers between devices with their start and end apart: 24, of which 12 were waited for; matrix products, arithmetic and copies ran while one was open for 15% of the time, Pallas kernels for 0%

profile of v1, /device:TPU:32, one launch (start us, length us, event | category | flops | bytes accessed | tf_op | source)
XLA Modules:
  0.0 203.4 jit_solution(7453007875366686126)
XLA Ops:
  0.6 6.4 %collective-permute-start.8 = (bf16[32,1536]{1,0:T(8,128)(2,1)}, bf16[32,1536]{1,0:T(8,128)(2,1)S(1)}, u32[]{:S(2)}, u32[]{:S(2)}) collective-permute-start(bf16[32,1536]{1,0:T(8,128)(2,1)} %param.5), channel_id=1, source_target_pairs={{0,16},{8,24},{16,0},{24,8},{1,17},{9,25},{17,1},{25,9},{2,18},{10... | collective-permute-start | bytes 294920 | tf_op jit(solution)/shard_map/ppermute | solution.py:35
  7.0 1.5 collective-permute-start.7
  8.5 2.7 %collective-permute-start.9 = (bf16[32,1536]{1,0:T(8,128)(2,1)}, bf16[32,1536]{1,0:T(8,128)(2,1)S(1)}, u32[]{:S(2)}, u32[]{:S(2)}) collective-permute-start(bf16[32,1536]{1,0:T(8,128)(2,1)} %param.5), channel_id=1, source_target_pairs={{0,24},{8,0},{16,8},{24,16},{1,25},{9,1},{17,9},{25,17},{2,26},{10... | collective-permute-start | bytes 294920 | tf_op jit(solution)/shard_map/ppermute | solution.py:35
  11.2 0.9 constant_dynamic-update-slice_fusion.29
  12.1 4.2 %collective-permute-done.7 = bf16[32,1536]{1,0:T(8,128)(2,1)S(1)} collective-permute-done((bf16[32,1536]{1,0:T(8,128)(2,1)}, bf16[32,1536]{1,0:T(8,128)(2,1)S(1)}, u32[]{:S(2)}, u32[]{:S(2)}) %collective-permute-start.7) | collective-permute-done | bytes 98336 | tf_op jit(solution)/shard_map/ppermute | solution.py:35
  16.4 1.6 collective-permute-start.10
  17.9 4.8 %collective-permute-start.1 = (bf16[32,1536]{1,0:T(8,128)(2,1)}, bf16[32,1536]{1,0:T(8,128)(2,1)S(1)}, u32[]{:S(2)}, u32[]{:S(2)}) collective-permute-start(bf16[32,1536]{1,0:T(8,128)(2,1)} %param.9), channel_id=1, source_target_pairs={{0,16},{8,24},{16,0},{24,8},{1,17},{9,25},{17,1},{25,9},{2,18},{10... | collective-permute-start | bytes 294920 | tf_op jit(solution)/shard_map/ppermute | solution.py:35
  22.7 1.5 collective-permute-start
  24.2 2.6 %collective-permute-start.2 = (bf16[32,1536]{1,0:T(8,128)(2,1)}, bf16[32,1536]{1,0:T(8,128)(2,1)S(1)}, u32[]{:S(2)}, u32[]{:S(2)}) collective-permute-start(bf16[32,1536]{1,0:T(8,128)(2,1)} %param.9), channel_id=1, source_target_pairs={{0,24},{8,0},{16,8},{24,16},{1,25},{9,1},{17,9},{25,17},{2,26},{10... | collective-permute-start | bytes 294920 | tf_op jit(solution)/shard_map/ppermute | solution.py:35
  26.9 2.7 %collective-permute-start.11 = (bf16[128,1536]{1,0:T(8,128)(2,1)S(1)}, bf16[128,1536]{1,0:T(8,128)(2,1)S(1)}, u32[]{:S(2)}, u32[]{:S(2)}) collective-permute-start(bf16[128,1536]{1,0:T(8,128)(2,1)S(1)} %get-tuple-element.29), channel_id=1, source_target_pairs={{0,4},{1,5},{2,6},{3,7},{4,0},{5,1},{6,2},{7,3},{8,12},{9,13},{10,... | collective-permute-start | bytes 1179656 | tf_op jit(solution)/shard_map/ppermute | solution.py:38
  29.6 0.9 constant_dynamic-update-slice_fusion.10
  30.5 1.5 collective-permute-start.12
  32.0 0.1 constant_dynamic-update-slice_fusion.25
  32.1 5.5 %collective-permute-done.11 = bf16[128,1536]{1,0:T(8,128)(2,1)S(1)} collective-permute-done((bf16[128,1536]{1,0:T(8,128)(2,1)S(1)}, bf16[128,1536]{1,0:T(8,128)(2,1)S(1)}, u32[]{:S(2)}, u32[]{:S(2)}) %collective-permute-start.11) | collective-permute-done | bytes 393248 | tf_op jit(solution)/shard_map/ppermute | solution.py:38
  37.6 0.1 constant_dynamic-update-slice_fusion.24
  37.7 7.8 %collective-permute-done.12 = bf16[128,1536]{1,0:T(8,128)(2,1)S(1)} collective-permute-done((bf16[128,1536]{1,0:T(8,128)(2,1)S(1)}, bf16[128,1536]{1,0:T(8,128)(2,1)S(1)}, u32[]{:S(2)}, u32[]{:S(2)}) %collective-permute-start.12) | collective-permute-done | bytes 393248 | tf_op jit(solution)/shard_map/ppermute | solution.py:38
  45.5 0.1 constant_dynamic-update-slice_fusion.23
  45.5 0.1 collective-permute-start.13
  45.8 2.1 %collective-permute-start.3 = (bf16[128,1536]{1,0:T(8,128)(2,1)S(1)}, bf16[128,1536]{1,0:T(8,128)(2,1)S(1)}, u32[]{:S(2)}, u32[]{:S(2)}) collective-permute-start(bf16[128,1536]{1,0:T(8,128)(2,1)S(1)} %get-tuple-element.41), channel_id=1, source_target_pairs={{0,2},{1,3},{2,4},{3,5},{4,6},{5,7},{6,0},{7,1},{8,10},{9,11},{10,... | collective-permute-start | bytes 1179656 | tf_op jit(solution)/shard_map/ppermute | solution.py:38
  47.9 2.1 %collective-permute-start.4 = (bf16[128,1536]{1,0:T(8,128)(2,1)S(1)}, bf16[128,1536]{1,0:T(8,128)(2,1)S(1)}, u32[]{:S(2)}, u32[]{:S(2)}) collective-permute-start(bf16[128,1536]{1,0:T(8,128)(2,1)S(1)} %get-tuple-element.41), channel_id=1, source_target_pairs={{0,4},{1,5},{2,6},{3,7},{4,0},{5,1},{6,2},{7,3},{8,12},{9,13},{10,... | collective-permute-start | bytes 1179656 | tf_op jit(solution)/shard_map/ppermute | solution.py:38
  49.9 1.2 collective-permute-start.5
  51.2 7.4 %collective-permute-done.3 = bf16[128,1536]{1,0:T(8,128)(2,1)S(1)} collective-permute-done((bf16[128,1536]{1,0:T(8,128)(2,1)S(1)}, bf16[128,1536]{1,0:T(8,128)(2,1)S(1)}, u32[]{:S(2)}, u32[]{:S(2)}) %collective-permute-start.3) | collective-permute-done | bytes 393248 | tf_op jit(solution)/shard_map/ppermute | solution.py:38
  58.6 0.1 constant_dynamic-update-slice_fusion.6
  58.6 9.2 %collective-permute-done.4 = bf16[128,1536]{1,0:T(8,128)(2,1)S(1)} collective-permute-done((bf16[128,1536]{1,0:T(8,128)(2,1)S(1)}, bf16[128,1536]{1,0:T(8,128)(2,1)S(1)}, u32[]{:S(2)}, u32[]{:S(2)}) %collective-permute-start.4) | collective-permute-done | bytes 393248 | tf_op jit(solution)/shard_map/ppermute | solution.py:38
  67.8 0.1 constant_dynamic-update-slice_fusion.5
  67.9 1.1 copy-done.4
  69.0 1.1 copy-done.6
  70.2 0.1 constant_dynamic-update-slice_fusion.30
  70.3 3.7 %convolution_convert_fusion = bf16[1024,768]{1,0:T(8,128)(2,1)} fusion(bf16[1024,1536]{1,0:T(8,128)(2,1)S(1)} %constant_dynamic-update-slice_fusion.30, bf16[1536,768]{1,0:T(8,128)(2,1)S(1)} %copy-done), kind=kOutput, calls=%fused_computation.6 | convolution fusion | flops 2416705536 | bytes 7077888 | tf_op jit(solution)/shard_map/dot_general | solution.py:74
  74.0 5.6 %all-to-all-start.1 = ((bf16[8,128,768]{2,1,0:T(8,128)(2,1)}), bf16[8,128,768]{2,1,0:T(8,128)(2,1)}, u32[]{:S(2)}, u32[]{:S(2)}) async-start(bf16[8,128,768]{2,1,0:T(8,128)(2,1)} %bitcast.16), calls=%async_computation.1 | async-start | bytes 3145728 | tf_op jit(solution)/shard_map/all_to_all | solution.py:62
  79.6 0.9 constant_dynamic-update-slice_fusion.4
  80.5 3.6 %collective-permute-done.6 = bf16[512,1536]{1,0:T(8,128)(2,1)S(1)} collective-permute-done((bf16[512,1536]{1,0:T(8,128)(2,1)}, bf16[512,1536]{1,0:T(8,128)(2,1)S(1)}, u32[]{:S(2)}, u32[]{:S(2)}) %collective-permute-start.6) | collective-permute-done | bytes 1572896 | tf_op jit(solution)/shard_map/ppermute | solution.py:41
  84.1 1.4 constant_dynamic-update-slice_fusion.11
  85.5 5.7 %convolution_convert_fusion.1 = bf16[1024,768]{1,0:T(8,128)(2,1)} fusion(bf16[1024,1536]{1,0:T(8,128)(2,1)} %constant_dynamic-update-slice_fusion.11, bf16[768,1536]{1,0:T(8,128)(2,1)S(1)} %copy-done.9), kind=kOutput, calls=%fused_computation.7 | convolution fusion | flops 2416705536 | bytes 7077888 | tf_op jit(solution)/shard_map/dot_general | solution.py:24
  91.1 8.2 %all-to-all-done.1 = bf16[8,128,768]{2,1,0:T(8,128)(2,1)} async-done(((bf16[8,128,768]{2,1,0:T(8,128)(2,1)}), bf16[8,128,768]{2,1,0:T(8,128)(2,1)}, u32[]{:S(2)}, u32[]{:S(2)}) %all-to-all-start.1) | async-done | bytes 1572896 | tf_op jit(solution)/shard_map/all_to_all | solution.py:62
  99.4 4.8 %all-to-all-start = ((bf16[8,128,768]{2,1,0:T(8,128)(2,1)}), bf16[8,128,768]{2,1,0:T(8,128)(2,1)}, u32[]{:S(2)}, u32[]{:S(2)}) async-start(bf16[8,128,768]{2,1,0:T(8,128)(2,1)} %bitcast.17), calls=%async_computation | async-start | bytes 3145728 | tf_op jit(solution)/shard_map/all_to_all | solution.py:62
  104.1 1.7 convert_reduce_fusion
  105.8 18.4 %all-to-all-done = bf16[8,128,768]{2,1,0:T(8,128)(2,1)} async-done(((bf16[8,128,768]{2,1,0:T(8,128)(2,1)}), bf16[8,128,768]{2,1,0:T(8,128)(2,1)}, u32[]{:S(2)}, u32[]{:S(2)}) %all-to-all-start) | async-done | bytes 1572896 | tf_op jit(solution)/shard_map/all_to_all | solution.py:62
  124.2 1.7 convert_reduce_fusion.1
  125.9 0.3 multiply_convert_fusion.2
  126.2 0.1 broadcast_in_dim.4
  126.3 24.2 %all_to_all.20 = bf16[8,128,768]{2,1,0:T(8,128)(2,1)S(1)} all-to-all(bf16[8,128,768]{2,1,0:T(8,128)(2,1)S(1)} %broadcast_in_dim.4), channel_id=1, replica_groups=mesh['gx'=8,'gy'=4,'gz'=8] {'gx'}, dimensions={0} | all-to-all | bytes 3145728 | tf_op jit(solution)/shard_map/all_to_all | solution.py:67
  150.5 2.6 %fusion.17 = f32[1024,1536]{1,0:T(8,128)S(1)} fusion(bf16[1024,768]{1,0:T(8,128)(2,1)S(1)} %bitcast.14, bf16[1536,768]{1,0:T(8,128)(2,1)S(1)} %copy-done), kind=kOutput, calls=%fused_computation.67 | convolution fusion | flops 2415919104 | bytes 10223616 | tf_op jit(solution)/shard_map/dot_general | solution.py:24
  153.2 2.7 %copy-done.1 = f32[1024,1536]{1,0:T(8,128)} copy-done((f32[1024,1536]{1,0:T(8,128)}, f32[1024,1536]{1,0:T(8,128)S(1)}, u32[]{:S(2)}) %copy-start.1) | copy-done | bytes 6291480
  155.8 1.3 slice.71
  157.2 1.3 broadcast_in_dim.5
  158.4 5.6 %all-to-all-start.3 = ((bf16[8,128,768]{2,1,0:T(8,128)(2,1)}), bf16[8,128,768]{2,1,0:T(8,128)(2,1)}, u32[]{:S(2)}, u32[]{:S(2)}) async-start(bf16[8,128,768]{2,1,0:T(8,128)(2,1)} %broadcast_in_dim.5), calls=%async_computation.3 | async-start | bytes 3145728 | tf_op jit(solution)/shard_map/all_to_all | solution.py:67
  164.1 3.1 %fusion.14 = (bf16[512,1536]{1,0:T(8,128)(2,1)S(1)}, f32[512,1536]{1,0:T(8,128)S(1)}) fusion(bf16[512,1536]{1,0:T(8,128)(2,1)} %collective-permute-done.14, f32[1024,1536]{1,0:T(8,128)} %copy-done.1), kind=kLoop, calls=%fused_computation.64 | loop fusion | flops 2359296 | bytes 9437184 | tf_op jit(solution)/shard_map/convert.5
  167.2 0.1 fusion.15
  167.2 0.1 collective-permute-start.15
  167.3 2.0 collective-permute-start.17
  169.3 1.8 collective-permute-start.16
  171.2 3.9 %multiply_convert_fusion.1 = bf16[1536,768]{1,0:T(8,128)(2,1)} fusion(bf16[1024,1536]{1,0:T(8,128)(2,1)S(1)} %copy-done.8, bf16[1024,768]{1,0:T(8,128)(2,1)S(1)} %bitcast.15), kind=kOutput, calls=%fused_computation.1 | convolution fusion | flops 2418278400 | bytes 7077888 | tf_op jit(solution)/shard_map/dot_general | solution.py:28
  175.1 4.2 %collective-permute-done.15 = bf16[128,1536]{1,0:T(8,128)(2,1)S(1)} collective-permute-done((bf16[128,1536]{1,0:T(8,128)(2,1)S(1)}, bf16[128,1536]{1,0:T(8,128)(2,1)S(1)}, u32[]{:S(2)}, u32[]{:S(2)}) %collective-permute-start.15) | collective-permute-done | bytes 393248 | tf_op jit(solution)/shard_map/ppermute | solution.py:38
  179.3 1.4 collective-permute-done.17
  180.7 7.9 %collective-permute-done.16 = bf16[128,1536]{1,0:T(8,128)(2,1)S(1)} collective-permute-done((bf16[128,1536]{1,0:T(8,128)(2,1)S(1)}, bf16[128,1536]{1,0:T(8,128)(2,1)S(1)}, u32[]{:S(2)}, u32[]{:S(2)}) %collective-permute-start.16) | collective-permute-done | bytes 393248 | tf_op jit(solution)/shard_map/ppermute | solution.py:38
  188.5 0.2 fusion.12
  188.7 0.7 fusion.16
  189.4 0.6 collective-permute-start.18
  190.0 2.4 %collective-permute-start.20 = (bf16[32,1536]{1,0:T(8,128)(2,1)S(1)}, bf16[32,1536]{1,0:T(8,128)(2,1)S(1)}, u32[]{:S(2)}, u32[]{:S(2)}) collective-permute-start(bf16[32,1536]{1,0:T(8,128)(2,1)S(1)} %get-tuple-element.13), channel_id=1, source_target_pairs={{0,8},{8,16},{16,24},{24,0},{1,9},{9,17},{17,25},{25,1},{2,10},{10... | collective-permute-start | bytes 294920 | tf_op jit(solution)/shard_map/ppermute | solution.py:35
  192.3 2.1 %collective-permute-start.19 = (bf16[32,1536]{1,0:T(8,128)(2,1)S(1)}, bf16[32,1536]{1,0:T(8,128)(2,1)}, u32[]{:S(2)}, u32[]{:S(2)}) collective-permute-start(bf16[32,1536]{1,0:T(8,128)(2,1)S(1)} %get-tuple-element.14), channel_id=1, source_target_pairs={{0,16},{8,24},{16,0},{24,8},{1,17},{9,25},{17,1},{25,9},{2,18},{10... | collective-permute-start | bytes 294920 | tf_op jit(solution)/shard_map/ppermute | solution.py:35
  194.4 6.4 %multiply_convert_fusion = bf16[768,1536]{1,0:T(8,128)(2,1)} fusion(bf16[1024,768]{1,0:T(8,128)(2,1)} %bitcast.3, bf16[1024,1536]{1,0:T(8,128)(2,1)} %constant_dynamic-update-slice_fusion.11), kind=kOutput, calls=%fused_computation | convolution fusion | flops 2418278400 | bytes 7077888 | tf_op jit(solution)/shard_map/dot_general | solution.py:28
  200.8 1.0 collective-permute-done.19
  201.8 1.6 fusion.11
  (37 shorter events, 0.2 us)
Async XLA Ops:
  0.6 69.6 %copy-start = (bf16[1536,768]{1,0:T(8,128)(2,1)S(1)}, bf16[1536,768]{1,0:T(8,128)(2,1)}, u32[]{:S(2)}) copy-start(bf16[1536,768]{1,0:T(8,128)(2,1)} %param.6) | copy-start | bytes 7077892
  0.6 15.6 %collective-permute-start.8 = (bf16[32,1536]{1,0:T(8,128)(2,1)}, bf16[32,1536]{1,0:T(8,128)(2,1)S(1)}, u32[]{:S(2)}, u32[]{:S(2)}) collective-permute-start(bf16[32,1536]{1,0:T(8,128)(2,1)} %param.5), channel_id=1, source_target_pairs={{0,16},{8,24},{16,0},{24,8},{1,17},{9,25},{17,1},{25,9},{2,18},{10... | collective-permute-start | bytes 294920 | tf_op jit(solution)/shard_map/ppermute | solution.py:35
  7.0 9.2 %collective-permute-start.7 = (bf16[32,1536]{1,0:T(8,128)(2,1)}, bf16[32,1536]{1,0:T(8,128)(2,1)S(1)}, u32[]{:S(2)}, u32[]{:S(2)}) collective-permute-start(bf16[32,1536]{1,0:T(8,128)(2,1)} %param.5), channel_id=1, source_target_pairs={{0,8},{8,16},{16,24},{24,0},{1,9},{9,17},{17,25},{25,1},{2,10},{10... | collective-permute-start | bytes 294920 | tf_op jit(solution)/shard_map/ppermute | solution.py:35
  8.5 7.8 %collective-permute-start.9 = (bf16[32,1536]{1,0:T(8,128)(2,1)}, bf16[32,1536]{1,0:T(8,128)(2,1)S(1)}, u32[]{:S(2)}, u32[]{:S(2)}) collective-permute-start(bf16[32,1536]{1,0:T(8,128)(2,1)} %param.5), channel_id=1, source_target_pairs={{0,24},{8,0},{16,8},{24,16},{1,25},{9,1},{17,9},{25,17},{2,26},{10... | collective-permute-start | bytes 294920 | tf_op jit(solution)/shard_map/ppermute | solution.py:35
  16.4 14.1 %collective-permute-start.10 = (bf16[128,1536]{1,0:T(8,128)(2,1)S(1)}, bf16[128,1536]{1,0:T(8,128)(2,1)S(1)}, u32[]{:S(2)}, u32[]{:S(2)}) collective-permute-start(bf16[128,1536]{1,0:T(8,128)(2,1)S(1)} %get-tuple-element.29), channel_id=1, source_target_pairs={{0,2},{1,3},{2,4},{3,5},{4,6},{5,7},{6,0},{7,1},{8,10},{9,11},{10,... | collective-permute-start | bytes 1179656 | tf_op jit(solution)/shard_map/ppermute | solution.py:38
  17.9 27.7 %collective-permute-start.1 = (bf16[32,1536]{1,0:T(8,128)(2,1)}, bf16[32,1536]{1,0:T(8,128)(2,1)S(1)}, u32[]{:S(2)}, u32[]{:S(2)}) collective-permute-start(bf16[32,1536]{1,0:T(8,128)(2,1)} %param.9), channel_id=1, source_target_pairs={{0,16},{8,24},{16,0},{24,8},{1,17},{9,25},{17,1},{25,9},{2,18},{10... | collective-permute-start | bytes 294920 | tf_op jit(solution)/shard_map/ppermute | solution.py:35
  22.7 22.9 %collective-permute-start = (bf16[32,1536]{1,0:T(8,128)(2,1)}, bf16[32,1536]{1,0:T(8,128)(2,1)S(1)}, u32[]{:S(2)}, u32[]{:S(2)}) collective-permute-start(bf16[32,1536]{1,0:T(8,128)(2,1)} %param.9), channel_id=1, source_target_pairs={{0,8},{8,16},{16,24},{24,0},{1,9},{9,17},{17,25},{25,1},{2,10},{10... | collective-permute-start | bytes 294920 | tf_op jit(solution)/shard_map/ppermute | solution.py:35
  24.2 21.5 %collective-permute-start.2 = (bf16[32,1536]{1,0:T(8,128)(2,1)}, bf16[32,1536]{1,0:T(8,128)(2,1)S(1)}, u32[]{:S(2)}, u32[]{:S(2)}) collective-permute-start(bf16[32,1536]{1,0:T(8,128)(2,1)} %param.9), channel_id=1, source_target_pairs={{0,24},{8,0},{16,8},{24,16},{1,25},{9,1},{17,9},{25,17},{2,26},{10... | collective-permute-start | bytes 294920 | tf_op jit(solution)/shard_map/ppermute | solution.py:35
  26.9 10.7 %collective-permute-start.11 = (bf16[128,1536]{1,0:T(8,128)(2,1)S(1)}, bf16[128,1536]{1,0:T(8,128)(2,1)S(1)}, u32[]{:S(2)}, u32[]{:S(2)}) collective-permute-start(bf16[128,1536]{1,0:T(8,128)(2,1)S(1)} %get-tuple-element.29), channel_id=1, source_target_pairs={{0,4},{1,5},{2,6},{3,7},{4,0},{5,1},{6,2},{7,3},{8,12},{9,13},{10,... | collective-permute-start | bytes 1179656 | tf_op jit(solution)/shard_map/ppermute | solution.py:38
  30.5 15.0 %collective-permute-start.12 = (bf16[128,1536]{1,0:T(8,128)(2,1)S(1)}, bf16[128,1536]{1,0:T(8,128)(2,1)S(1)}, u32[]{:S(2)}, u32[]{:S(2)}) collective-permute-start(bf16[128,1536]{1,0:T(8,128)(2,1)S(1)} %get-tuple-element.29), channel_id=1, source_target_pairs={{0,6},{1,7},{2,0},{3,1},{4,2},{5,3},{6,4},{7,5},{8,14},{9,15},{10,... | collective-permute-start | bytes 1179656 | tf_op jit(solution)/shard_map/ppermute | solution.py:38
  45.5 22.4 %collective-permute-start.13 = (bf16[512,1536]{1,0:T(8,128)(2,1)S(1)}, bf16[512,1536]{1,0:T(8,128)(2,1)S(1)}, u32[]{:S(2)}, u32[]{:S(2)}) collective-permute-start(bf16[512,1536]{1,0:T(8,128)(2,1)S(1)} %get-tuple-element.15), channel_id=1, source_target_pairs={{0,1},{1,0},{2,3},{3,2},{4,5},{5,4},{6,7},{7,6},{8,9},{9,8},{10,11... | collective-permute-start | bytes 4718600 | tf_op jit(solution)/shard_map/ppermute | solution.py:41
  45.8 12.8 %collective-permute-start.3 = (bf16[128,1536]{1,0:T(8,128)(2,1)S(1)}, bf16[128,1536]{1,0:T(8,128)(2,1)S(1)}, u32[]{:S(2)}, u32[]{:S(2)}) collective-permute-start(bf16[128,1536]{1,0:T(8,128)(2,1)S(1)} %get-tuple-element.41), channel_id=1, source_target_pairs={{0,2},{1,3},{2,4},{3,5},{4,6},{5,7},{6,0},{7,1},{8,10},{9,11},{10,... | collective-permute-start | bytes 1179656 | tf_op jit(solution)/shard_map/ppermute | solution.py:38
  47.9 20.0 %collective-permute-start.4 = (bf16[128,1536]{1,0:T(8,128)(2,1)S(1)}, bf16[128,1536]{1,0:T(8,128)(2,1)S(1)}, u32[]{:S(2)}, u32[]{:S(2)}) collective-permute-start(bf16[128,1536]{1,0:T(8,128)(2,1)S(1)} %get-tuple-element.41), channel_id=1, source_target_pairs={{0,4},{1,5},{2,6},{3,7},{4,0},{5,1},{6,2},{7,3},{8,12},{9,13},{10,... | collective-permute-start | bytes 1179656 | tf_op jit(solution)/shard_map/ppermute | solution.py:38
  49.9 29.6 %collective-permute-start.5 = (bf16[128,1536]{1,0:T(8,128)(2,1)S(1)}, bf16[128,1536]{1,0:T(8,128)(2,1)S(1)}, u32[]{:S(2)}, u32[]{:S(2)}) collective-permute-start(bf16[128,1536]{1,0:T(8,128)(2,1)S(1)} %get-tuple-element.41), channel_id=1, source_target_pairs={{0,6},{1,7},{2,0},{3,1},{4,2},{5,3},{6,4},{7,5},{8,14},{9,15},{10,... | collective-permute-start | bytes 1179656 | tf_op jit(solution)/shard_map/ppermute | solution.py:38
  67.9 1.1 copy-start.4
  67.9 2.3 %copy-start.6 = (bf16[1024,1536]{1,0:T(8,128)(2,1)}, bf16[1024,1536]{1,0:T(8,128)(2,1)S(1)}, u32[]{:S(2)}) copy-start(bf16[1024,1536]{1,0:T(8,128)(2,1)S(1)} %get-tuple-element.24) | copy-start | bytes 9437188
  70.3 3.7 %copy-start.7 = (bf16[1024,1536]{1,0:T(8,128)(2,1)}, bf16[1024,1536]{1,0:T(8,128)(2,1)S(1)}, u32[]{:S(2)}) copy-start(bf16[1024,1536]{1,0:T(8,128)(2,1)S(1)} %constant_dynamic-update-slice_fusion.30) | copy-start | bytes 9437188
  74.0 25.4 %all-to-all-start.1 = ((bf16[8,128,768]{2,1,0:T(8,128)(2,1)}), bf16[8,128,768]{2,1,0:T(8,128)(2,1)}, u32[]{:S(2)}, u32[]{:S(2)}) async-start(bf16[8,128,768]{2,1,0:T(8,128)(2,1)} %bitcast.16), calls=%async_computation.1 | async-start | bytes 3145728 | tf_op jit(solution)/shard_map/all_to_all | solution.py:62
  79.5 5.9 %copy-start.9 = (bf16[768,1536]{1,0:T(8,128)(2,1)S(1)}, bf16[768,1536]{1,0:T(8,128)(2,1)}, u32[]{:S(2)}) copy-start(bf16[768,1536]{1,0:T(8,128)(2,1)} %param.8) | copy-start | bytes 7077892
  80.5 3.6 %collective-permute-start.6 = (bf16[512,1536]{1,0:T(8,128)(2,1)}, bf16[512,1536]{1,0:T(8,128)(2,1)S(1)}, u32[]{:S(2)}, u32[]{:S(2)}) collective-permute-start(bf16[512,1536]{1,0:T(8,128)(2,1)} %get-tuple-element.21), channel_id=1, source_target_pairs={{0,1},{1,0},{2,3},{3,2},{4,5},{5,4},{6,7},{7,6},{8,9},{9,8},{10,11... | collective-permute-start | bytes 4718600 | tf_op jit(solution)/shard_map/ppermute | solution.py:41
  99.4 24.8 %all-to-all-start = ((bf16[8,128,768]{2,1,0:T(8,128)(2,1)}), bf16[8,128,768]{2,1,0:T(8,128)(2,1)}, u32[]{:S(2)}, u32[]{:S(2)}) async-start(bf16[8,128,768]{2,1,0:T(8,128)(2,1)} %bitcast.17), calls=%async_computation | async-start | bytes 3145728 | tf_op jit(solution)/shard_map/all_to_all | solution.py:62
  104.1 21.7 %copy-start.5 = (f32[768]{0:T(1024)S(1)}, f32[768]{0:T(1024)}, u32[]{:S(2)}) copy-start(f32[768]{0:T(1024)} %param.7) | copy-start | bytes 9220
  150.5 2.6 %copy-start.2 = (bf16[8,128,768]{2,1,0:T(8,128)(2,1)}, bf16[8,128,768]{2,1,0:T(8,128)(2,1)S(1)}, u32[]{:S(2)}) copy-start(bf16[8,128,768]{2,1,0:T(8,128)(2,1)S(1)} %all_to_all.20) | copy-start | bytes 4718596
  153.1 2.7 %copy-start.1 = (f32[1024,1536]{1,0:T(8,128)}, f32[1024,1536]{1,0:T(8,128)S(1)}, u32[]{:S(2)}) copy-start(f32[1024,1536]{1,0:T(8,128)S(1)} %fusion.17) | copy-start | bytes 18874372
  157.2 6.9 %collective-permute-start.14 = (bf16[512,1536]{1,0:T(8,128)(2,1)}, bf16[512,1536]{1,0:T(8,128)(2,1)}, u32[]{:S(2)}, u32[]{:S(2)}) collective-permute-start(bf16[512,1536]{1,0:T(8,128)(2,1)} %slice.71), channel_id=1, source_target_pairs={{0,1},{1,0},{2,3},{3,2},{4,5},{5,4},{6,7},{7,6},{8,9},{9,8},{10,11... | collective-permute-start | bytes 4718600 | tf_op jit(solution)/shard_map/ppermute | solution.py:41
  158.4 36.0 %all-to-all-start.3 = ((bf16[8,128,768]{2,1,0:T(8,128)(2,1)}), bf16[8,128,768]{2,1,0:T(8,128)(2,1)}, u32[]{:S(2)}, u32[]{:S(2)}) async-start(bf16[8,128,768]{2,1,0:T(8,128)(2,1)} %broadcast_in_dim.5), calls=%async_computation.3 | async-start | bytes 3145728 | tf_op jit(solution)/shard_map/all_to_all | solution.py:67
  164.1 7.1 %copy-start.8 = (bf16[1024,1536]{1,0:T(8,128)(2,1)S(1)}, bf16[1024,1536]{1,0:T(8,128)(2,1)}, u32[]{:S(2)}) copy-start(bf16[1024,1536]{1,0:T(8,128)(2,1)} %copy-done.7) | copy-start | bytes 9437188
  167.1 4.0 %copy-start.3 = (bf16[8,128,768]{2,1,0:T(8,128)(2,1)S(1)}, bf16[8,128,768]{2,1,0:T(8,128)(2,1)}, u32[]{:S(2)}) copy-start(bf16[8,128,768]{2,1,0:T(8,128)(2,1)} %copy-done.2) | copy-start | bytes 4718596
  167.2 12.0 %collective-permute-start.15 = (bf16[128,1536]{1,0:T(8,128)(2,1)S(1)}, bf16[128,1536]{1,0:T(8,128)(2,1)S(1)}, u32[]{:S(2)}, u32[]{:S(2)}) collective-permute-start(bf16[128,1536]{1,0:T(8,128)(2,1)S(1)} %get-tuple-element.7), channel_id=1, source_target_pairs={{0,6},{1,7},{2,0},{3,1},{4,2},{5,3},{6,4},{7,5},{8,14},{9,15},{10,... | collective-permute-start | bytes 1179656 | tf_op jit(solution)/shard_map/ppermute | solution.py:38
  167.3 13.3 %collective-permute-start.17 = (bf16[128,1536]{1,0:T(8,128)(2,1)S(1)}, bf16[128,1536]{1,0:T(8,128)(2,1)S(1)}, u32[]{:S(2)}, u32[]{:S(2)}) collective-permute-start(bf16[128,1536]{1,0:T(8,128)(2,1)S(1)} %get-tuple-element.8), channel_id=1, source_target_pairs={{0,2},{1,3},{2,4},{3,5},{4,6},{5,7},{6,0},{7,1},{8,10},{9,11},{10,... | collective-permute-start | bytes 1179656 | tf_op jit(solution)/shard_map/ppermute | solution.py:38
  169.3 19.2 %collective-permute-start.16 = (bf16[128,1536]{1,0:T(8,128)(2,1)S(1)}, bf16[128,1536]{1,0:T(8,128)(2,1)S(1)}, u32[]{:S(2)}, u32[]{:S(2)}) collective-permute-start(bf16[128,1536]{1,0:T(8,128)(2,1)S(1)} %get-tuple-element.9), channel_id=1, source_target_pairs={{0,4},{1,5},{2,6},{3,7},{4,0},{5,1},{6,2},{7,3},{8,12},{9,13},{10,... | collective-permute-start | bytes 1179656 | tf_op jit(solution)/shard_map/ppermute | solution.py:38
  189.4 11.4 %collective-permute-start.18 = (bf16[32,1536]{1,0:T(8,128)(2,1)}, bf16[32,1536]{1,0:T(8,128)(2,1)S(1)}, u32[]{:S(2)}, u32[]{:S(2)}) collective-permute-start(bf16[32,1536]{1,0:T(8,128)(2,1)} %get-tuple-element.12), channel_id=1, source_target_pairs={{0,24},{8,0},{16,8},{24,16},{1,25},{9,1},{17,9},{25,17},{2,26},{10... | collective-permute-start | bytes 294920 | tf_op jit(solution)/shard_map/ppermute | solution.py:35
  190.0 10.8 %collective-permute-start.20 = (bf16[32,1536]{1,0:T(8,128)(2,1)S(1)}, bf16[32,1536]{1,0:T(8,128)(2,1)S(1)}, u32[]{:S(2)}, u32[]{:S(2)}) collective-permute-start(bf16[32,1536]{1,0:T(8,128)(2,1)S(1)} %get-tuple-element.13), channel_id=1, source_target_pairs={{0,8},{8,16},{16,24},{24,0},{1,9},{9,17},{17,25},{25,1},{2,10},{10... | collective-permute-start | bytes 294920 | tf_op jit(solution)/shard_map/ppermute | solution.py:35
  192.3 9.5 %collective-permute-start.19 = (bf16[32,1536]{1,0:T(8,128)(2,1)S(1)}, bf16[32,1536]{1,0:T(8,128)(2,1)}, u32[]{:S(2)}, u32[]{:S(2)}) collective-permute-start(bf16[32,1536]{1,0:T(8,128)(2,1)S(1)} %get-tuple-element.14), channel_id=1, source_target_pairs={{0,16},{8,24},{16,0},{24,8},{1,17},{9,25},{17,1},{25,9},{2,18},{10... | collective-permute-start | bytes 294920 | tf_op jit(solution)/shard_map/ppermute | solution.py:35

commit v2 on v1

--- a/solution.py
+++ b/solution.py
@@ -40,14 +40,13 @@
     def swap_core(a):
         return lax.ppermute(a, "gz", [(i, i ^ 1) for i in range(n_z)])
 
-    def gather_rows(a):
-        a = jnp.concatenate([a] + [shift_y(a, k) for k in range(1, n_y)], axis=0)
-        a = jnp.concatenate([a] + [shift_chip(a, k) for k in range(1, n_z // 2)], axis=0)
-        return jnp.concatenate([a, swap_core(a)], axis=0)
+    def gather_far(a):
+        return jnp.concatenate([a] + [shift_y(a, k) for k in range(1, n_y)], axis=0)
+
+    def chips(a):
+        return [shift_chip(a, k) for k in range(1, n_z // 2)]
 
     def scatter_rows(a):
-        half = a.shape[0] // 2
-        a = a[:half] + swap_core(a[half:].astype(bf16)).astype(f32)
         for shift, n in ((shift_chip, n_z // 2), (shift_y, n_y)):
             rows = a.shape[0] // n
             total = a[:rows]
@@ -67,16 +66,30 @@
         parts = lax.all_to_all(copies, "gx", 0, 0, tiled=True)
         return parts.reshape(-1, share.shape[1])
 
+    def after(a, *others):
+        return lax.optimization_barrier((a, *others))[0]
+
     def shards(tokens, weight_in, bias_hidden, weight_out, grad_output):
-        tokens_all = gather_rows(tokens)
-        grad_all = gather_rows(grad_output)
-        norm_scale = 1.0 / math.sqrt(tokens_all.shape[0])
-        pre_act = sum_width(jnp.dot(tokens_all, weight_in, preferred_element_type=f32)) + bias_hidden
+        tokens_far = gather_far(tokens)
+        grad_far = gather_far(after(grad_output, tokens_far))
+        tokens_near = jnp.concatenate([tokens_far] + chips(tokens_far), axis=0)
+        grad_chips = chips(after(grad_far, tokens_near))
+        tokens_all = jnp.concatenate([tokens_near, swap_core(tokens_near)], axis=0)
+        total_rows = tokens_all.shape[0]
+        half = total_rows // 2
+        norm_scale = 1.0 / math.sqrt(total_rows)
+        pre_part = jnp.dot(tokens_all, weight_in, preferred_element_type=f32).astype(bf16)
+        pre_act = sum_width(pre_part) + bias_hidden
+        grad_chips = [after(a, pre_part) for a in grad_chips]
+        grad_near = jnp.concatenate([grad_far] + grad_chips, axis=0)
+        grad_all = jnp.concatenate([grad_near, swap_core(grad_near)], axis=0)
         upstream = sum_width(contract_last(grad_all, weight_out))
         act_share, grad_share = gelu_pair(pre_act, upstream)
         grad_hidden = gather_width(grad_share)
-        grad_tokens = scatter_rows(contract_last(grad_hidden, weight_in))
-        activation = gather_width(act_share)
+        other = contract_last(grad_hidden[half:], weight_in).astype(bf16)
+        own = contract_last(grad_hidden[:half], weight_in)
+        activation = gather_width(after(act_share, other, own))
+        grad_tokens = scatter_rows(own + swap_core(other).astype(f32))
         grad_weight_in = (contract_first(tokens_all, grad_hidden) * norm_scale).astype(bf16)
         grad_weight_out = (contract_first(activation, grad_all) * norm_scale).astype(bf16)
         return (grad_tokens, grad_weight_in, grad_weight_out)

time: 204 us -> 218 us (1.069)
  waiting for transfers between devices: 78.9 us -> 97.3 us
  other arithmetic: 8.46 us -> 5.63 us
  starting transfers between devices: 55.6 us -> 52.9 us
  matrix products: 22.3 us -> 24.7 us
    ppermute x9, waiting for transfers between devices: 5.2 us -> 17.7 us  [shift_y(): return lax.ppermute(a, 'gy', [(i, (i + k) % n_y) for i in range(n_y)])]
    ppermute x9, waiting for transfers between devices: 43.4 us -> 47.4 us  [shift_chip(): return lax.ppermute(a, 'gz', [(i, (i + 2 * k) % n_z) for i in range(n_z)])]
    ppermute x3, waiting for transfers between devices: 3.62 us -> 7.02 us  [swap_core(): return lax.ppermute(a, 'gz', [(i, i ^ 1) for i in range(n_z)])]
    dot_general x2 -> x3, matrix products: 8.3 us -> 10.7 us  [contract_last(): lax.dot_general(left, right, (((1,), (1,)), ((), ())), preferred_element_...]
    unnamed x32 -> x29, local copies, waits for them, and re-layouts: 7.14 us -> 6.92 us
  transfers between devices with their start and end apart: 24 -> 24, of which waited for: 12 -> 13; matrix products, arithmetic and copies ran while one was open for 15% -> 12% of each run, Pallas kernels for 0% -> 0%
where the time goes in v2:
time: 218 us
  waiting for transfers between devices  97.3 us (45%)
  starting transfers between devices  52.9 us (24%)
  matrix products  24.7 us (11%)
  blocking collectives  24.2 us (11%)
  local copies, waits for them, and re-layouts  12.3 us (6%)
  other arithmetic  5.63 us (3%)
    ppermute x9, waiting for transfers between devices, shift_chip(): return lax.ppermute(a, 'gz', [(i, (i + 2 * k) % n_z) for i in range(n_z)])  47.4 us
    all_to_all x2, waiting for transfers between devices, sum_width(): parts = lax.all_to_all(part, 'gx', 0, 0, tiled=True)  25.2 us
    all_to_all x1, blocking collectives, gather_width(): parts = lax.all_to_all(copies, 'gx', 0, 0, tiled=True)  24.2 us
    ppermute x9, starting transfers between devices, shift_y(): return lax.ppermute(a, 'gy', [(i, (i + k) % n_y) for i in range(n_y)])  23.3 us
    ppermute x9, waiting for transfers between devices, shift_y(): return lax.ppermute(a, 'gy', [(i, (i + k) % n_y) for i in range(n_y)])  17.7 us
    ppermute x9, starting transfers between devices, shift_chip(): return lax.ppermute(a, 'gz', [(i, (i + 2 * k) % n_z) for i in range(n_z)])  13.1 us
    all_to_all x2, starting transfers between devices, sum_width(): parts = lax.all_to_all(part, 'gx', 0, 0, tiled=True)  10.7 us
    dot_general x3, matrix products, contract_last(): lax.dot_general(left, right, (((1,), (1,)), ((), ())), preferred_element_...  10.7 us
  transfers between devices with their start and end apart: 24, of which 13 were waited for; matrix products, arithmetic and copies ran while one was open for 12% of the time, Pallas kernels for 0%

profile of v2, /device:TPU:32, one launch (start us, length us, event | category | flops | bytes accessed | tf_op | source)
XLA Modules:
  0.0 217.9 jit_solution(15876017020354370985)
XLA Ops:
  0.6 6.4 %collective-permute-start.1 = (bf16[32,1536]{1,0:T(8,128)(2,1)}, bf16[32,1536]{1,0:T(8,128)(2,1)S(1)}, u32[]{:S(2)}, u32[]{:S(2)}) collective-permute-start(bf16[32,1536]{1,0:T(8,128)(2,1)} %param.5), channel_id=1, source_target_pairs={{0,16},{8,24},{16,0},{24,8},{1,17},{9,25},{17,1},{25,9},{2,18},{10... | collective-permute-start | bytes 294920 | tf_op jit(solution)/shard_map/ppermute | solution.py:35
  7.0 1.5 collective-permute-start
  8.5 2.7 %collective-permute-start.2 = (bf16[32,1536]{1,0:T(8,128)(2,1)}, bf16[32,1536]{1,0:T(8,128)(2,1)S(1)}, u32[]{:S(2)}, u32[]{:S(2)}) collective-permute-start(bf16[32,1536]{1,0:T(8,128)(2,1)} %param.5), channel_id=1, source_target_pairs={{0,24},{8,0},{16,8},{24,16},{1,25},{9,1},{17,9},{25,17},{2,26},{10... | collective-permute-start | bytes 294920 | tf_op jit(solution)/shard_map/ppermute | solution.py:35
  11.2 0.9 constant_dynamic-update-slice_fusion.18
  12.1 4.2 %collective-permute-done = bf16[32,1536]{1,0:T(8,128)(2,1)S(1)} collective-permute-done((bf16[32,1536]{1,0:T(8,128)(2,1)}, bf16[32,1536]{1,0:T(8,128)(2,1)S(1)}, u32[]{:S(2)}, u32[]{:S(2)}) %collective-permute-start) | collective-permute-done | bytes 98336 | tf_op jit(solution)/shard_map/ppermute | solution.py:35
  16.4 1.6 collective-permute-start.6
  17.9 2.7 %collective-permute-start.7 = (bf16[128,1536]{1,0:T(8,128)(2,1)S(1)}, bf16[128,1536]{1,0:T(8,128)(2,1)S(1)}, u32[]{:S(2)}, u32[]{:S(2)}) collective-permute-start(bf16[128,1536]{1,0:T(8,128)(2,1)S(1)} %get-tuple-element.51), channel_id=1, source_target_pairs={{0,4},{1,5},{2,6},{3,7},{4,0},{5,1},{6,2},{7,3},{8,12},{9,13},{10,... | collective-permute-start | bytes 1179656 | tf_op jit(solution)/shard_map/ppermute | solution.py:38
  20.7 1.4 collective-permute-start.8
  22.1 6.8 %collective-permute-done.6 = bf16[128,1536]{1,0:T(8,128)(2,1)S(1)} collective-permute-done((bf16[128,1536]{1,0:T(8,128)(2,1)S(1)}, bf16[128,1536]{1,0:T(8,128)(2,1)S(1)}, u32[]{:S(2)}, u32[]{:S(2)}) %collective-permute-start.6) | collective-permute-done | bytes 393248 | tf_op jit(solution)/shard_map/ppermute | solution.py:38
  28.9 8.7 %collective-permute-done.7 = bf16[128,1536]{1,0:T(8,128)(2,1)S(1)} collective-permute-done((bf16[128,1536]{1,0:T(8,128)(2,1)S(1)}, bf16[128,1536]{1,0:T(8,128)(2,1)S(1)}, u32[]{:S(2)}, u32[]{:S(2)}) %collective-permute-start.7) | collective-permute-done | bytes 393248 | tf_op jit(solution)/shard_map/ppermute | solution.py:38
  37.7 0.1 constant_dynamic-update-slice_fusion.12
  37.7 0.1 collective-permute-start.10
  37.9 2.4 %collective-permute-start.5 = (bf16[32,1536]{1,0:T(8,128)(2,1)S(1)}, bf16[32,1536]{1,0:T(8,128)(2,1)S(1)}, u32[]{:S(2)}, u32[]{:S(2)}) collective-permute-start(bf16[32,1536]{1,0:T(8,128)(2,1)S(1)} %copy-done.3), channel_id=1, source_target_pairs={{0,24},{8,0},{16,8},{24,16},{1,25},{9,1},{17,9},{25,17},{2,26},{10... | collective-permute-start | bytes 294920 | tf_op jit(solution)/shard_map/ppermute | solution.py:35
  40.2 4.1 %collective-permute-start.4 = (bf16[32,1536]{1,0:T(8,128)(2,1)S(1)}, bf16[32,1536]{1,0:T(8,128)(2,1)S(1)}, u32[]{:S(2)}, u32[]{:S(2)}) collective-permute-start(bf16[32,1536]{1,0:T(8,128)(2,1)S(1)} %copy-done.3), channel_id=1, source_target_pairs={{0,16},{8,24},{16,0},{24,8},{1,17},{9,25},{17,1},{25,9},{2,18},{10... | collective-permute-start | bytes 294920 | tf_op jit(solution)/shard_map/ppermute | solution.py:35
  44.3 1.1 collective-permute-start.3
  45.5 0.7 constant_dynamic-update-slice_fusion.25
  46.1 10.2 %collective-permute-done.3 = bf16[32,1536]{1,0:T(8,128)(2,1)S(1)} collective-permute-done((bf16[32,1536]{1,0:T(8,128)(2,1)S(1)}, bf16[32,1536]{1,0:T(8,128)(2,1)S(1)}, u32[]{:S(2)}, u32[]{:S(2)}) %collective-permute-start.3) | collective-permute-done | bytes 98336 | tf_op jit(solution)/shard_map/ppermute | solution.py:35
  56.4 0.7 constant_dynamic-update-slice_fusion.24
  57.0 0.7 constant_dynamic-update-slice_fusion.23
  57.7 0.7 constant_dynamic-update-slice_fusion.22
  58.5 2.3 %collective-permute-start.12 = (bf16[128,1536]{1,0:T(8,128)(2,1)S(1)}, bf16[128,1536]{1,0:T(8,128)(2,1)S(1)}, u32[]{:S(2)}, u32[]{:S(2)}) collective-permute-start(bf16[128,1536]{1,0:T(8,128)(2,1)S(1)} %pad_maximum_fusion), channel_id=1, source_target_pairs={{0,6},{1,7},{2,0},{3,1},{4,2},{5,3},{6,4},{7,5},{8,14},{9,15},{10,... | collective-permute-start | bytes 1179656 | tf_op jit(solution)/shard_map/ppermute | solution.py:38
  60.7 1.1 collective-permute-start.11
  61.9 0.7 collective-permute-start.9
  62.5 0.1 constant_dynamic-update-slice_fusion.11
  62.7 3.7 %convolution_convert_fusion.2 = bf16[1024,768]{1,0:T(8,128)(2,1)} fusion(bf16[1024,1536]{1,0:T(8,128)(2,1)S(1)} %constant_dynamic-update-slice_fusion.11, bf16[1536,768]{1,0:T(8,128)(2,1)S(1)} %copy-done), kind=kOutput, calls=%fused_computation.7 | convolution fusion | flops 2416705536 | bytes 7077888 | tf_op jit(solution)/shard_map/dot_general | solution.py:81
  66.3 10.8 %collective-permute-done.12 = bf16[128,1536]{1,0:T(8,128)(2,1)S(1)} collective-permute-done((bf16[128,1536]{1,0:T(8,128)(2,1)S(1)}, bf16[128,1536]{1,0:T(8,128)(2,1)S(1)}, u32[]{:S(2)}, u32[]{:S(2)}) %collective-permute-start.12) | collective-permute-done | bytes 393248 | tf_op jit(solution)/shard_map/ppermute | solution.py:38
  77.2 3.7 %collective-permute-done.9 = bf16[128,1536]{1,0:T(8,128)(2,1)S(1)} collective-permute-done((bf16[128,1536]{1,0:T(8,128)(2,1)S(1)}, bf16[128,1536]{1,0:T(8,128)(2,1)S(1)}, u32[]{:S(2)}, u32[]{:S(2)}) %collective-permute-start.9) | collective-permute-done | bytes 393248 | tf_op jit(solution)/shard_map/ppermute | solution.py:38
  80.8 5.9 %all-to-all-start.1 = ((bf16[8,128,768]{2,1,0:T(8,128)(2,1)}), bf16[8,128,768]{2,1,0:T(8,128)(2,1)}, u32[]{:S(2)}, u32[]{:S(2)}) async-start(bf16[8,128,768]{2,1,0:T(8,128)(2,1)} %bitcast.20), calls=%async_computation.1 | async-start | bytes 3145728 | tf_op jit(solution)/shard_map/all_to_all | solution.py:61
  86.8 0.9 constant_dynamic-update-slice_fusion.21
  87.7 0.9 constant_dynamic-update-slice_fusion.20
  88.6 1.0 constant_dynamic-update-slice_fusion.19
  89.6 3.6 %collective-permute-done.13 = bf16[512,1536]{1,0:T(8,128)(2,1)S(1)} collective-permute-done((bf16[512,1536]{1,0:T(8,128)(2,1)}, bf16[512,1536]{1,0:T(8,128)(2,1)S(1)}, u32[]{:S(2)}, u32[]{:S(2)}) %collective-permute-start.13) | collective-permute-done | bytes 1572896 | tf_op jit(solution)/shard_map/ppermute | solution.py:41
  93.2 1.3 constant_dynamic-update-slice_fusion.26
  94.5 5.7 %convolution_convert_fusion.1 = bf16[1024,768]{1,0:T(8,128)(2,1)} fusion(bf16[1024,1536]{1,0:T(8,128)(2,1)} %constant_dynamic-update-slice_fusion.26, bf16[768,1536]{1,0:T(8,128)(2,1)S(1)} %copy-done.7), kind=kOutput, calls=%fused_computation.6 | convolution fusion | flops 2416705536 | bytes 7077888 | tf_op jit(solution)/shard_map/dot_general | solution.py:24
  100.2 6.7 %all-to-all-done.1 = bf16[8,128,768]{2,1,0:T(8,128)(2,1)} async-done(((bf16[8,128,768]{2,1,0:T(8,128)(2,1)}), bf16[8,128,768]{2,1,0:T(8,128)(2,1)}, u32[]{:S(2)}, u32[]{:S(2)}) %all-to-all-start.1) | async-done | bytes 1572896 | tf_op jit(solution)/shard_map/all_to_all | solution.py:61
  106.9 4.8 %all-to-all-start = ((bf16[8,128,768]{2,1,0:T(8,128)(2,1)}), bf16[8,128,768]{2,1,0:T(8,128)(2,1)}, u32[]{:S(2)}, u32[]{:S(2)}) async-start(bf16[8,128,768]{2,1,0:T(8,128)(2,1)} %bitcast.21), calls=%async_computation | async-start | bytes 3145728 | tf_op jit(solution)/shard_map/all_to_all | solution.py:61
  111.7 1.7 convert_reduce_fusion
  113.3 18.5 %all-to-all-done = bf16[8,128,768]{2,1,0:T(8,128)(2,1)} async-done(((bf16[8,128,768]{2,1,0:T(8,128)(2,1)}), bf16[8,128,768]{2,1,0:T(8,128)(2,1)}, u32[]{:S(2)}, u32[]{:S(2)}) %all-to-all-start) | async-done | bytes 1572896 | tf_op jit(solution)/shard_map/all_to_all | solution.py:61
  131.8 1.7 convert_reduce_fusion.1
  133.5 0.3 multiply_convert_fusion.2
  133.8 0.1 broadcast_in_dim.4
  133.9 24.2 %all_to_all.20 = bf16[8,128,768]{2,1,0:T(8,128)(2,1)S(1)} all-to-all(bf16[8,128,768]{2,1,0:T(8,128)(2,1)S(1)} %broadcast_in_dim.4), channel_id=1, replica_groups=mesh['gx'=8,'gy'=4,'gz'=8] {'gx'}, dimensions={0} | all-to-all | bytes 3145728 | tf_op jit(solution)/shard_map/all_to_all | solution.py:66
  158.1 1.1 copy-done.1
  159.2 0.1 fusion.16
  159.3 1.4 convolution_convert_fusion
  160.7 0.1 collective-permute-start.14
  160.8 3.4 %collective-permute-done.14 = bf16[512,1536]{1,0:T(8,128)(2,1)S(1)} collective-permute-done((bf16[512,1536]{1,0:T(8,128)(2,1)S(1)}, bf16[512,1536]{1,0:T(8,128)(2,1)S(1)}, u32[]{:S(2)}, u32[]{:S(2)}) %collective-permute-start.14) | collective-permute-done | bytes 1572896 | tf_op jit(solution)/shard_map/ppermute | solution.py:41
  164.2 3.6 %fusion.14 = (bf16[512,1536]{1,0:T(8,128)(2,1)}, f32[512,1536]{1,0:T(8,128)}) fusion(bf16[512,1536]{1,0:T(8,128)(2,1)S(1)} %collective-permute-done.14, bf16[512,768]{1,0:T(8,128)(2,1)S(1)} %bitcast.19, bf16[1536,768]{1,0:T(8,128)(2,1)S(1)} %copy-done), kind=kOutput, calls=%fused_computation.61 | convolution fusion | flops 1210318848 | bytes 9437184 | tf_op jit(solution)/shard_map/dot_general | solution.py:24
  167.8 1.3 broadcast_in_dim.5
  169.2 5.6 %all-to-all-start.3 = ((bf16[8,128,768]{2,1,0:T(8,128)(2,1)}), bf16[8,128,768]{2,1,0:T(8,128)(2,1)}, u32[]{:S(2)}, u32[]{:S(2)}) async-start(bf16[8,128,768]{2,1,0:T(8,128)(2,1)} %broadcast_in_dim.5), calls=%async_computation.3 | async-start | bytes 3145728 | tf_op jit(solution)/shard_map/all_to_all | solution.py:66
  174.8 1.5 fusion.15
  176.3 0.1 collective-permute-start.15
  176.4 2.0 collective-permute-start.17
  178.4 1.1 collective-permute-start.16
  179.5 8.8 %collective-permute-done.15 = bf16[128,1536]{1,0:T(8,128)(2,1)S(1)} collective-permute-done((bf16[128,1536]{1,0:T(8,128)(2,1)S(1)}, bf16[128,1536]{1,0:T(8,128)(2,1)S(1)}, u32[]{:S(2)}, u32[]{:S(2)}) %collective-permute-start.15) | collective-permute-done | bytes 393248 | tf_op jit(solution)/shard_map/ppermute | solution.py:38
  188.4 8.6 %collective-permute-done.17 = bf16[128,1536]{1,0:T(8,128)(2,1)S(1)} collective-permute-done((bf16[128,1536]{1,0:T(8,128)(2,1)S(1)}, bf16[128,1536]{1,0:T(8,128)(2,1)S(1)}, u32[]{:S(2)}, u32[]{:S(2)}) %collective-permute-start.17) | collective-permute-done | bytes 393248 | tf_op jit(solution)/shard_map/ppermute | solution.py:38
  197.0 1.3 fusion.12
  198.3 1.0 collective-permute-start.18
  199.3 2.0 collective-permute-start.20
  201.3 2.2 %collective-permute-start.19 = (bf16[32,1536]{1,0:T(8,128)(2,1)S(1)}, bf16[32,1536]{1,0:T(8,128)(2,1)S(1)}, u32[]{:S(2)}, u32[]{:S(2)}) collective-permute-start(bf16[32,1536]{1,0:T(8,128)(2,1)S(1)} %get-tuple-element.28), channel_id=1, source_target_pairs={{0,16},{8,24},{16,0},{24,8},{1,17},{9,25},{17,1},{25,9},{2,18},{10... | collective-permute-start | bytes 294920 | tf_op jit(solution)/shard_map/ppermute | solution.py:35
  203.6 3.9 %multiply_convert_fusion.1 = bf16[1536,768]{1,0:T(8,128)(2,1)} fusion(bf16[1024,1536]{1,0:T(8,128)(2,1)S(1)} %copy-done.6, bf16[1024,768]{1,0:T(8,128)(2,1)S(1)} %bitcast.18), kind=kOutput, calls=%fused_computation.1 | convolution fusion | flops 2418278400 | bytes 7077888 | tf_op jit(solution)/shard_map/dot_general | solution.py:28
  207.5 3.3 %collective-permute-done.19 = bf16[32,1536]{1,0:T(8,128)(2,1)S(1)} collective-permute-done((bf16[32,1536]{1,0:T(8,128)(2,1)S(1)}, bf16[32,1536]{1,0:T(8,128)(2,1)S(1)}, u32[]{:S(2)}, u32[]{:S(2)}) %collective-permute-start.19) | collective-permute-done | bytes 98336 | tf_op jit(solution)/shard_map/ppermute | solution.py:35
  210.8 0.7 fusion.11
  211.5 6.4 %multiply_convert_fusion = bf16[768,1536]{1,0:T(8,128)(2,1)} fusion(bf16[1024,768]{1,0:T(8,128)(2,1)} %bitcast.5, bf16[1024,1536]{1,0:T(8,128)(2,1)} %constant_dynamic-update-slice_fusion.26), kind=kOutput, calls=%fused_computation | convolution fusion | flops 2418278400 | bytes 7077888 | tf_op jit(solution)/shard_map/dot_general | solution.py:28
  (34 shorter events, 0.3 us)
Async XLA Ops:
  0.6 62.0 %copy-start = (bf16[1536,768]{1,0:T(8,128)(2,1)S(1)}, bf16[1536,768]{1,0:T(8,128)(2,1)}, u32[]{:S(2)}) copy-start(bf16[1536,768]{1,0:T(8,128)(2,1)} %param.6) | copy-start | bytes 7077892
  0.6 15.6 %collective-permute-start.1 = (bf16[32,1536]{1,0:T(8,128)(2,1)}, bf16[32,1536]{1,0:T(8,128)(2,1)S(1)}, u32[]{:S(2)}, u32[]{:S(2)}) collective-permute-start(bf16[32,1536]{1,0:T(8,128)(2,1)} %param.5), channel_id=1, source_target_pairs={{0,16},{8,24},{16,0},{24,8},{1,17},{9,25},{17,1},{25,9},{2,18},{10... | collective-permute-start | bytes 294920 | tf_op jit(solution)/shard_map/ppermute | solution.py:35
  7.0 9.2 %collective-permute-start = (bf16[32,1536]{1,0:T(8,128)(2,1)}, bf16[32,1536]{1,0:T(8,128)(2,1)S(1)}, u32[]{:S(2)}, u32[]{:S(2)}) collective-permute-start(bf16[32,1536]{1,0:T(8,128)(2,1)} %param.5), channel_id=1, source_target_pairs={{0,8},{8,16},{16,24},{24,0},{1,9},{9,17},{17,25},{25,1},{2,10},{10... | collective-permute-start | bytes 294920 | tf_op jit(solution)/shard_map/ppermute | solution.py:35
  8.5 7.8 %collective-permute-start.2 = (bf16[32,1536]{1,0:T(8,128)(2,1)}, bf16[32,1536]{1,0:T(8,128)(2,1)S(1)}, u32[]{:S(2)}, u32[]{:S(2)}) collective-permute-start(bf16[32,1536]{1,0:T(8,128)(2,1)} %param.5), channel_id=1, source_target_pairs={{0,24},{8,0},{16,8},{24,16},{1,25},{9,1},{17,9},{25,17},{2,26},{10... | collective-permute-start | bytes 294920 | tf_op jit(solution)/shard_map/ppermute | solution.py:35
  16.3 21.6 %copy-start.3 = (bf16[32,1536]{1,0:T(8,128)(2,1)S(1)}, bf16[32,1536]{1,0:T(8,128)(2,1)}, u32[]{:S(2)}) copy-start(bf16[32,1536]{1,0:T(8,128)(2,1)} %param.9) | copy-start | bytes 294916
  16.4 12.5 %collective-permute-start.6 = (bf16[128,1536]{1,0:T(8,128)(2,1)S(1)}, bf16[128,1536]{1,0:T(8,128)(2,1)S(1)}, u32[]{:S(2)}, u32[]{:S(2)}) collective-permute-start(bf16[128,1536]{1,0:T(8,128)(2,1)S(1)} %get-tuple-element.51), channel_id=1, source_target_pairs={{0,2},{1,3},{2,4},{3,5},{4,6},{5,7},{6,0},{7,1},{8,10},{9,11},{10,... | collective-permute-start | bytes 1179656 | tf_op jit(solution)/shard_map/ppermute | solution.py:38
  17.9 19.7 %collective-permute-start.7 = (bf16[128,1536]{1,0:T(8,128)(2,1)S(1)}, bf16[128,1536]{1,0:T(8,128)(2,1)S(1)}, u32[]{:S(2)}, u32[]{:S(2)}) collective-permute-start(bf16[128,1536]{1,0:T(8,128)(2,1)S(1)} %get-tuple-element.51), channel_id=1, source_target_pairs={{0,4},{1,5},{2,6},{3,7},{4,0},{5,1},{6,2},{7,3},{8,12},{9,13},{10,... | collective-permute-start | bytes 1179656 | tf_op jit(solution)/shard_map/ppermute | solution.py:38
  20.7 17.0 %collective-permute-start.8 = (bf16[128,1536]{1,0:T(8,128)(2,1)S(1)}, bf16[128,1536]{1,0:T(8,128)(2,1)S(1)}, u32[]{:S(2)}, u32[]{:S(2)}) collective-permute-start(bf16[128,1536]{1,0:T(8,128)(2,1)S(1)} %get-tuple-element.51), channel_id=1, source_target_pairs={{0,6},{1,7},{2,0},{3,1},{4,2},{5,3},{6,4},{7,5},{8,14},{9,15},{10,... | collective-permute-start | bytes 1179656 | tf_op jit(solution)/shard_map/ppermute | solution.py:38
  37.7 24.8 %collective-permute-start.10 = (bf16[512,1536]{1,0:T(8,128)(2,1)S(1)}, bf16[512,1536]{1,0:T(8,128)(2,1)S(1)}, u32[]{:S(2)}, u32[]{:S(2)}) collective-permute-start(bf16[512,1536]{1,0:T(8,128)(2,1)S(1)} %get-tuple-element.36), channel_id=1, source_target_pairs={{0,1},{1,0},{2,3},{3,2},{4,5},{5,4},{6,7},{7,6},{8,9},{9,8},{10,11... | collective-permute-start | bytes 4718600 | tf_op jit(solution)/shard_map/ppermute | solution.py:41
  37.9 19.9 %collective-permute-start.5 = (bf16[32,1536]{1,0:T(8,128)(2,1)S(1)}, bf16[32,1536]{1,0:T(8,128)(2,1)S(1)}, u32[]{:S(2)}, u32[]{:S(2)}) collective-permute-start(bf16[32,1536]{1,0:T(8,128)(2,1)S(1)} %copy-done.3), channel_id=1, source_target_pairs={{0,24},{8,0},{16,8},{24,16},{1,25},{9,1},{17,9},{25,17},{2,26},{10... | collective-permute-start | bytes 294920 | tf_op jit(solution)/shard_map/ppermute | solution.py:35
  40.2 16.8 %collective-permute-start.4 = (bf16[32,1536]{1,0:T(8,128)(2,1)S(1)}, bf16[32,1536]{1,0:T(8,128)(2,1)S(1)}, u32[]{:S(2)}, u32[]{:S(2)}) collective-permute-start(bf16[32,1536]{1,0:T(8,128)(2,1)S(1)} %copy-done.3), channel_id=1, source_target_pairs={{0,16},{8,24},{16,0},{24,8},{1,17},{9,25},{17,1},{25,9},{2,18},{10... | collective-permute-start | bytes 294920 | tf_op jit(solution)/shard_map/ppermute | solution.py:35
  44.3 12.0 %collective-permute-start.3 = (bf16[32,1536]{1,0:T(8,128)(2,1)S(1)}, bf16[32,1536]{1,0:T(8,128)(2,1)S(1)}, u32[]{:S(2)}, u32[]{:S(2)}) collective-permute-start(bf16[32,1536]{1,0:T(8,128)(2,1)S(1)} %copy-done.3), channel_id=1, source_target_pairs={{0,8},{8,16},{16,24},{24,0},{1,9},{9,17},{17,25},{25,1},{2,10},{10... | collective-permute-start | bytes 294920 | tf_op jit(solution)/shard_map/ppermute | solution.py:35
  58.5 18.7 %collective-permute-start.12 = (bf16[128,1536]{1,0:T(8,128)(2,1)S(1)}, bf16[128,1536]{1,0:T(8,128)(2,1)S(1)}, u32[]{:S(2)}, u32[]{:S(2)}) collective-permute-start(bf16[128,1536]{1,0:T(8,128)(2,1)S(1)} %pad_maximum_fusion), channel_id=1, source_target_pairs={{0,6},{1,7},{2,0},{3,1},{4,2},{5,3},{6,4},{7,5},{8,14},{9,15},{10,... | collective-permute-start | bytes 1179656 | tf_op jit(solution)/shard_map/ppermute | solution.py:38
  60.7 16.4 %collective-permute-start.11 = (bf16[128,1536]{1,0:T(8,128)(2,1)S(1)}, bf16[128,1536]{1,0:T(8,128)(2,1)S(1)}, u32[]{:S(2)}, u32[]{:S(2)}) collective-permute-start(bf16[128,1536]{1,0:T(8,128)(2,1)S(1)} %pad_maximum_fusion), channel_id=1, source_target_pairs={{0,4},{1,5},{2,6},{3,7},{4,0},{5,1},{6,2},{7,3},{8,12},{9,13},{10,... | collective-permute-start | bytes 1179656 | tf_op jit(solution)/shard_map/ppermute | solution.py:38
  61.9 19.0 %collective-permute-start.9 = (bf16[128,1536]{1,0:T(8,128)(2,1)S(1)}, bf16[128,1536]{1,0:T(8,128)(2,1)S(1)}, u32[]{:S(2)}, u32[]{:S(2)}) collective-permute-start(bf16[128,1536]{1,0:T(8,128)(2,1)S(1)} %pad_maximum_fusion), channel_id=1, source_target_pairs={{0,2},{1,3},{2,4},{3,5},{4,6},{5,7},{6,0},{7,1},{8,10},{9,11},{10,... | collective-permute-start | bytes 1179656 | tf_op jit(solution)/shard_map/ppermute | solution.py:38
  62.7 3.7 %copy-start.5 = (bf16[1024,1536]{1,0:T(8,128)(2,1)}, bf16[1024,1536]{1,0:T(8,128)(2,1)S(1)}, u32[]{:S(2)}) copy-start(bf16[1024,1536]{1,0:T(8,128)(2,1)S(1)} %constant_dynamic-update-slice_fusion.11) | copy-start | bytes 9437188
  80.8 26.1 %all-to-all-start.1 = ((bf16[8,128,768]{2,1,0:T(8,128)(2,1)}), bf16[8,128,768]{2,1,0:T(8,128)(2,1)}, u32[]{:S(2)}, u32[]{:S(2)}) async-start(bf16[8,128,768]{2,1,0:T(8,128)(2,1)} %bitcast.20), calls=%async_computation.1 | async-start | bytes 3145728 | tf_op jit(solution)/shard_map/all_to_all | solution.py:61
  88.6 5.9 %copy-start.7 = (bf16[768,1536]{1,0:T(8,128)(2,1)S(1)}, bf16[768,1536]{1,0:T(8,128)(2,1)}, u32[]{:S(2)}) copy-start(bf16[768,1536]{1,0:T(8,128)(2,1)} %param.8) | copy-start | bytes 7077892
  89.6 3.6 %collective-permute-start.13 = (bf16[512,1536]{1,0:T(8,128)(2,1)}, bf16[512,1536]{1,0:T(8,128)(2,1)S(1)}, u32[]{:S(2)}, u32[]{:S(2)}) collective-permute-start(bf16[512,1536]{1,0:T(8,128)(2,1)} %get-tuple-element.29), channel_id=1, source_target_pairs={{0,1},{1,0},{2,3},{3,2},{4,5},{5,4},{6,7},{7,6},{8,9},{9,8},{10,11... | collective-permute-start | bytes 4718600 | tf_op jit(solution)/shard_map/ppermute | solution.py:41
  106.9 24.9 %all-to-all-start = ((bf16[8,128,768]{2,1,0:T(8,128)(2,1)}), bf16[8,128,768]{2,1,0:T(8,128)(2,1)}, u32[]{:S(2)}, u32[]{:S(2)}) async-start(bf16[8,128,768]{2,1,0:T(8,128)(2,1)} %bitcast.21), calls=%async_computation | async-start | bytes 3145728 | tf_op jit(solution)/shard_map/all_to_all | solution.py:61
  111.7 21.8 %copy-start.4 = (f32[768]{0:T(1024)S(1)}, f32[768]{0:T(1024)}, u32[]{:S(2)}) copy-start(f32[768]{0:T(1024)} %param.7) | copy-start | bytes 9220
  158.1 1.1 copy-start.1
  160.7 3.5 %collective-permute-start.14 = (bf16[512,1536]{1,0:T(8,128)(2,1)S(1)}, bf16[512,1536]{1,0:T(8,128)(2,1)S(1)}, u32[]{:S(2)}, u32[]{:S(2)}) collective-permute-start(bf16[512,1536]{1,0:T(8,128)(2,1)S(1)} %convolution_convert_fusion), channel_id=1, source_target_pairs={{0,1},{1,0},{2,3},{3,2},{4,5},{5,4},{6,7},{7,6},{8,9},{9,8},{10,11... | collective-permute-start | bytes 4718600 | tf_op jit(solution)/shard_map/ppermute | solution.py:41
  169.2 42.3 %all-to-all-start.3 = ((bf16[8,128,768]{2,1,0:T(8,128)(2,1)}), bf16[8,128,768]{2,1,0:T(8,128)(2,1)}, u32[]{:S(2)}, u32[]{:S(2)}) async-start(bf16[8,128,768]{2,1,0:T(8,128)(2,1)} %broadcast_in_dim.5), calls=%async_computation.3 | async-start | bytes 3145728 | tf_op jit(solution)/shard_map/all_to_all | solution.py:66
  174.8 28.7 %copy-start.6 = (bf16[1024,1536]{1,0:T(8,128)(2,1)S(1)}, bf16[1024,1536]{1,0:T(8,128)(2,1)}, u32[]{:S(2)}) copy-start(bf16[1024,1536]{1,0:T(8,128)(2,1)} %copy-done.5) | copy-start | bytes 9437188
  176.3 27.3 %copy-start.2 = (bf16[8,128,768]{2,1,0:T(8,128)(2,1)S(1)}, bf16[8,128,768]{2,1,0:T(8,128)(2,1)}, u32[]{:S(2)}) copy-start(bf16[8,128,768]{2,1,0:T(8,128)(2,1)} %copy-done.1) | copy-start | bytes 4718596
  176.3 12.1 %collective-permute-start.15 = (bf16[128,1536]{1,0:T(8,128)(2,1)S(1)}, bf16[128,1536]{1,0:T(8,128)(2,1)S(1)}, u32[]{:S(2)}, u32[]{:S(2)}) collective-permute-start(bf16[128,1536]{1,0:T(8,128)(2,1)S(1)} %get-tuple-element.19), channel_id=1, source_target_pairs={{0,6},{1,7},{2,0},{3,1},{4,2},{5,3},{6,4},{7,5},{8,14},{9,15},{10,... | collective-permute-start | bytes 1179656 | tf_op jit(solution)/shard_map/ppermute | solution.py:38
  176.4 20.6 %collective-permute-start.17 = (bf16[128,1536]{1,0:T(8,128)(2,1)S(1)}, bf16[128,1536]{1,0:T(8,128)(2,1)S(1)}, u32[]{:S(2)}, u32[]{:S(2)}) collective-permute-start(bf16[128,1536]{1,0:T(8,128)(2,1)S(1)} %get-tuple-element.20), channel_id=1, source_target_pairs={{0,2},{1,3},{2,4},{3,5},{4,6},{5,7},{6,0},{7,1},{8,10},{9,11},{10,... | collective-permute-start | bytes 1179656 | tf_op jit(solution)/shard_map/ppermute | solution.py:38
  178.4 18.6 %collective-permute-start.16 = (bf16[128,1536]{1,0:T(8,128)(2,1)S(1)}, bf16[128,1536]{1,0:T(8,128)(2,1)S(1)}, u32[]{:S(2)}, u32[]{:S(2)}) collective-permute-start(bf16[128,1536]{1,0:T(8,128)(2,1)S(1)} %get-tuple-element.21), channel_id=1, source_target_pairs={{0,4},{1,5},{2,6},{3,7},{4,0},{5,1},{6,2},{7,3},{8,12},{9,13},{10,... | collective-permute-start | bytes 1179656 | tf_op jit(solution)/shard_map/ppermute | solution.py:38
  198.3 9.2 %collective-permute-start.18 = (bf16[32,1536]{1,0:T(8,128)(2,1)S(1)}, bf16[32,1536]{1,0:T(8,128)(2,1)S(1)}, u32[]{:S(2)}, u32[]{:S(2)}) collective-permute-start(bf16[32,1536]{1,0:T(8,128)(2,1)S(1)} %get-tuple-element.26), channel_id=1, source_target_pairs={{0,24},{8,0},{16,8},{24,16},{1,25},{9,1},{17,9},{25,17},{2,26},{10... | collective-permute-start | bytes 294920 | tf_op jit(solution)/shard_map/ppermute | solution.py:35
  199.3 8.2 %collective-permute-start.20 = (bf16[32,1536]{1,0:T(8,128)(2,1)S(1)}, bf16[32,1536]{1,0:T(8,128)(2,1)S(1)}, u32[]{:S(2)}, u32[]{:S(2)}) collective-permute-start(bf16[32,1536]{1,0:T(8,128)(2,1)S(1)} %get-tuple-element.27), channel_id=1, source_target_pairs={{0,8},{8,16},{16,24},{24,0},{1,9},{9,17},{17,25},{25,1},{2,10},{10... | collective-permute-start | bytes 294920 | tf_op jit(solution)/shard_map/ppermute | solution.py:35
  201.3 9.5 %collective-permute-start.19 = (bf16[32,1536]{1,0:T(8,128)(2,1)S(1)}, bf16[32,1536]{1,0:T(8,128)(2,1)S(1)}, u32[]{:S(2)}, u32[]{:S(2)}) collective-permute-start(bf16[32,1536]{1,0:T(8,128)(2,1)S(1)} %get-tuple-element.28), channel_id=1, source_target_pairs={{0,16},{8,24},{16,0},{24,8},{1,17},{9,25},{17,1},{25,9},{2,18},{10... | collective-permute-start | bytes 294920 | tf_op jit(solution)/shard_map/ppermute | solution.py:35

commit v3 on v2

--- a/solution.py
+++ b/solution.py
@@ -40,21 +40,20 @@
     def swap_core(a):
         return lax.ppermute(a, "gz", [(i, i ^ 1) for i in range(n_z)])
 
-    def gather_far(a):
-        return jnp.concatenate([a] + [shift_y(a, k) for k in range(1, n_y)], axis=0)
+    def groups(a):
+        return [shift_y(a, k) for k in range(1, n_y)]
 
     def chips(a):
         return [shift_chip(a, k) for k in range(1, n_z // 2)]
 
-    def scatter_rows(a):
-        for shift, n in ((shift_chip, n_z // 2), (shift_y, n_y)):
-            rows = a.shape[0] // n
-            total = a[:rows]
-            for k in range(1, n):
-                part = a[k * rows : (k + 1) * rows].astype(bf16)
-                total = total + shift(part, -k).astype(f32)
-            a = total
-        return a.astype(bf16)
+    def scatter_stage(a, shift, n, beside):
+        rows = a.shape[0] // n
+        sent = [shift(a[k * rows : (k + 1) * rows].astype(bf16), -k) for k in range(1, n)]
+        sent, beside = lax.optimization_barrier((sent, beside))
+        total = a[:rows]
+        for part in sent:
+            total = total + part.astype(f32)
+        return total, beside
 
     def sum_width(part):
         part = part.astype(bf16).reshape(n_x, part.shape[0] // n_x, part.shape[1])
@@ -70,17 +69,22 @@
         return lax.optimization_barrier((a, *others))[0]
 
     def shards(tokens, weight_in, bias_hidden, weight_out, grad_output):
-        tokens_far = gather_far(tokens)
-        grad_far = gather_far(after(grad_output, tokens_far))
-        tokens_near = jnp.concatenate([tokens_far] + chips(tokens_far), axis=0)
-        grad_chips = chips(after(grad_far, tokens_near))
+        tokens_far = jnp.concatenate([tokens] + groups(tokens), axis=0)
+        grad_groups = groups(after(grad_output, tokens_far))
+        tokens_chips, grad_groups = lax.optimization_barrier((chips(tokens_far), grad_groups))
+        grad_far = jnp.concatenate([grad_output] + grad_groups, axis=0)
+        tokens_near = jnp.concatenate([tokens_far] + tokens_chips, axis=0)
         tokens_all = jnp.concatenate([tokens_near, swap_core(tokens_near)], axis=0)
         total_rows = tokens_all.shape[0]
         half = total_rows // 2
         norm_scale = 1.0 / math.sqrt(total_rows)
         pre_part = jnp.dot(tokens_all, weight_in, preferred_element_type=f32).astype(bf16)
         pre_act = sum_width(pre_part) + bias_hidden
-        grad_chips = [after(a, pre_part) for a in grad_chips]
+        last = n_z // 4
+        grad_chips = [
+            shift_chip(after(grad_far, pre_part) if k == last else grad_far, k)
+            for k in range(1, n_z // 2)
+        ]
         grad_near = jnp.concatenate([grad_far] + grad_chips, axis=0)
         grad_all = jnp.concatenate([grad_near, swap_core(grad_near)], axis=0)
         upstream = sum_width(contract_last(grad_all, weight_out))
@@ -89,10 +93,12 @@
         other = contract_last(grad_hidden[half:], weight_in).astype(bf16)
         own = contract_last(grad_hidden[:half], weight_in)
         activation = gather_width(after(act_share, other, own))
-        grad_tokens = scatter_rows(own + swap_core(other).astype(f32))
         grad_weight_in = (contract_first(tokens_all, grad_hidden) * norm_scale).astype(bf16)
         grad_weight_out = (contract_first(activation, grad_all) * norm_scale).astype(bf16)
-        return (grad_tokens, grad_weight_in, grad_weight_out)
+        own = own + swap_core(other).astype(f32)
+        own, grad_weight_in = scatter_stage(own, shift_chip, n_z // 2, grad_weight_in)
+        own, grad_weight_out = scatter_stage(own, shift_y, n_y, grad_weight_out)
+        return (own.astype(bf16), grad_weight_in, grad_weight_out)
 
     return jax.shard_map(
         shards,

time: 218 us -> 202 us (0.927)
  waiting for transfers between devices: 97.3 us -> 70.8 us
  starting transfers between devices: 52.9 us -> 57.5 us
    ppermute x9, waiting for transfers between devices: 47.4 us -> 26.7 us  [shift_chip(): return lax.ppermute(a, 'gz', [(i, (i + 2 * k) % n_z) for i in range(n_z)])]
    ppermute x9, waiting for transfers between devices: 17.7 us -> 11 us  [shift_y(): return lax.ppermute(a, 'gy', [(i, (i + k) % n_y) for i in range(n_y)])]
    ppermute x9, starting transfers between devices: 23.3 us -> 29.5 us  [shift_y(): return lax.ppermute(a, 'gy', [(i, (i + k) % n_y) for i in range(n_y)])]
    unnamed x29 -> x28, local copies, waits for them, and re-layouts: 6.92 us -> 7.77 us
  transfers between devices with their start and end apart: 24 -> 24, of which waited for: 13 -> 13; matrix products, arithmetic and copies ran while one was open for 12% -> 17% of each run, Pallas kernels for 0% -> 0%
where the time goes in v3:
time: 202 us; the launch traced here: 200 us
  waiting for transfers between devices  70.8 us (35%)
  starting transfers between devices  57.5 us (28%)
  matrix products  26.8 us (13%)
  blocking collectives  24.2 us (12%)
  local copies, waits for them, and re-layouts  13.9 us (7%)
  other arithmetic  6.51 us (3%)
    ppermute x9, starting transfers between devices, shift_y(): return lax.ppermute(a, 'gy', [(i, (i + k) % n_y) for i in range(n_y)])  29.5 us
    ppermute x9, waiting for transfers between devices, shift_chip(): return lax.ppermute(a, 'gz', [(i, (i + 2 * k) % n_z) for i in range(n_z)])  26.7 us
    all_to_all x2, waiting for transfers between devices, sum_width(): parts = lax.all_to_all(part, 'gx', 0, 0, tiled=True)  25.7 us
    all_to_all x1, blocking collectives, gather_width(): parts = lax.all_to_all(copies, 'gx', 0, 0, tiled=True)  24.2 us
    dot_general x2, matrix products, contract_first(): lax.dot_general(left, right, (((0,), (0,)), ((), ())), preferred_element_...  12.4 us
    ppermute x9, starting transfers between devices, shift_chip(): return lax.ppermute(a, 'gz', [(i, (i + 2 * k) % n_z) for i in range(n_z)])  11.4 us
    ppermute x9, waiting for transfers between devices, shift_y(): return lax.ppermute(a, 'gy', [(i, (i + k) % n_y) for i in range(n_y)])  11 us
    all_to_all x2, starting transfers between devices, sum_width(): parts = lax.all_to_all(part, 'gx', 0, 0, tiled=True)  10.7 us
  transfers between devices with their start and end apart: 24, of which 13 were waited for; matrix products, arithmetic and copies ran while one was open for 17% of the time, Pallas kernels for 0%

profile of v3, /device:TPU:32, one launch (start us, length us, event | category | flops | bytes accessed | tf_op | source)
XLA Modules:
  0.0 200.4 jit_solution(17623904593384175223)
XLA Ops:
  0.6 6.4 %collective-permute-start.1 = (bf16[32,1536]{1,0:T(8,128)(2,1)}, bf16[32,1536]{1,0:T(8,128)(2,1)S(1)}, u32[]{:S(2)}, u32[]{:S(2)}) collective-permute-start(bf16[32,1536]{1,0:T(8,128)(2,1)} %param.5), channel_id=1, source_target_pairs={{0,16},{8,24},{16,0},{24,8},{1,17},{9,25},{17,1},{25,9},{2,18},{10... | collective-permute-start | bytes 294920 | tf_op jit(solution)/shard_map/ppermute | solution.py:35
  7.0 1.5 collective-permute-start
  8.5 2.7 %collective-permute-start.2 = (bf16[32,1536]{1,0:T(8,128)(2,1)}, bf16[32,1536]{1,0:T(8,128)(2,1)S(1)}, u32[]{:S(2)}, u32[]{:S(2)}) collective-permute-start(bf16[32,1536]{1,0:T(8,128)(2,1)} %param.5), channel_id=1, source_target_pairs={{0,24},{8,0},{16,8},{24,16},{1,25},{9,1},{17,9},{25,17},{2,26},{10... | collective-permute-start | bytes 294920 | tf_op jit(solution)/shard_map/ppermute | solution.py:35
  11.2 0.9 constant_dynamic-update-slice_fusion.14
  12.1 4.2 %collective-permute-done = bf16[32,1536]{1,0:T(8,128)(2,1)S(1)} collective-permute-done((bf16[32,1536]{1,0:T(8,128)(2,1)}, bf16[32,1536]{1,0:T(8,128)(2,1)S(1)}, u32[]{:S(2)}, u32[]{:S(2)}) %collective-permute-start) | collective-permute-done | bytes 98336 | tf_op jit(solution)/shard_map/ppermute | solution.py:35
  16.4 2.8 %collective-permute-start.5 = (bf16[128,1536]{1,0:T(8,128)(2,1)S(1)}, bf16[128,1536]{1,0:T(8,128)(2,1)S(1)}, u32[]{:S(2)}, u32[]{:S(2)}) collective-permute-start(bf16[128,1536]{1,0:T(8,128)(2,1)S(1)} %get-tuple-element.77), channel_id=1, source_target_pairs={{0,6},{1,7},{2,0},{3,1},{4,2},{5,3},{6,4},{7,5},{8,14},{9,15},{10,... | collective-permute-start | bytes 1179656 | tf_op jit(solution)/shard_map/ppermute | solution.py:38
  19.2 0.8 collective-permute-start.4
  20.0 0.9 collective-permute-start.3
  20.9 3.9 %collective-permute-start.8 = (bf16[32,1536]{1,0:T(8,128)(2,1)}, bf16[32,1536]{1,0:T(8,128)(2,1)S(1)}, u32[]{:S(2)}, u32[]{:S(2)}) collective-permute-start(bf16[32,1536]{1,0:T(8,128)(2,1)} %param.9), channel_id=1, source_target_pairs={{0,24},{8,0},{16,8},{24,16},{1,25},{9,1},{17,9},{25,17},{2,26},{10... | collective-permute-start | bytes 294920 | tf_op jit(solution)/shard_map/ppermute | solution.py:35
  24.8 2.0 collective-permute-start.7
  26.8 3.3 %collective-permute-done.8 = bf16[32,1536]{1,0:T(8,128)(2,1)S(1)} collective-permute-done((bf16[32,1536]{1,0:T(8,128)(2,1)}, bf16[32,1536]{1,0:T(8,128)(2,1)S(1)}, u32[]{:S(2)}, u32[]{:S(2)}) %collective-permute-start.8) | collective-permute-done | bytes 98336 | tf_op jit(solution)/shard_map/ppermute | solution.py:35
  30.1 4.4 %collective-permute-start.6 = (bf16[32,1536]{1,0:T(8,128)(2,1)}, bf16[32,1536]{1,0:T(8,128)(2,1)S(1)}, u32[]{:S(2)}, u32[]{:S(2)}) collective-permute-start(bf16[32,1536]{1,0:T(8,128)(2,1)} %param.9), channel_id=1, source_target_pairs={{0,8},{8,16},{16,24},{24,0},{1,9},{9,17},{17,25},{25,1},{2,10},{10... | collective-permute-start | bytes 294920 | tf_op jit(solution)/shard_map/ppermute | solution.py:35
  34.5 0.5 collective-permute-done.7
  35.0 3.1 %collective-permute-done.6 = bf16[32,1536]{1,0:T(8,128)(2,1)S(1)} collective-permute-done((bf16[32,1536]{1,0:T(8,128)(2,1)}, bf16[32,1536]{1,0:T(8,128)(2,1)S(1)}, u32[]{:S(2)}, u32[]{:S(2)}) %collective-permute-start.6) | collective-permute-done | bytes 98336 | tf_op jit(solution)/shard_map/ppermute | solution.py:35
  38.1 1.3 collective-permute-done.3
  39.6 0.1 collective-permute-start.10
  39.7 0.7 constant_dynamic-update-slice_fusion.29
  40.3 0.7 constant_dynamic-update-slice_fusion.28
  41.0 0.7 constant_dynamic-update-slice_fusion.27
  41.7 0.7 constant_dynamic-update-slice_fusion.26
  42.3 0.5 collective-permute-start.9
  42.8 0.3 collective-permute-done.10
  43.1 0.1 constant_dynamic-update-slice_fusion.15
  43.2 3.7 %convolution_convert_fusion.2 = bf16[1024,768]{1,0:T(8,128)(2,1)} fusion(bf16[1024,1536]{1,0:T(8,128)(2,1)S(1)} %constant_dynamic-update-slice_fusion.15, bf16[1536,768]{1,0:T(8,128)(2,1)S(1)} %copy-done), kind=kOutput, calls=%fused_computation.7 | convolution fusion | flops 2416705536 | bytes 7077888 | tf_op jit(solution)/shard_map/dot_general | solution.py:81
  46.9 1.5 collective-permute-start.11
  48.4 1.6 collective-permute-start.12
  50.0 13.4 %collective-permute-done.9 = bf16[128,1536]{1,0:T(8,128)(2,1)S(1)} collective-permute-done((bf16[128,1536]{1,0:T(8,128)(2,1)S(1)}, bf16[128,1536]{1,0:T(8,128)(2,1)S(1)}, u32[]{:S(2)}, u32[]{:S(2)}) %collective-permute-start.9) | collective-permute-done | bytes 393248 | tf_op jit(solution)/shard_map/ppermute | solution.py:38
  63.5 0.8 constant_dynamic-update-slice_fusion.25
  64.3 1.1 copy-done.4
  65.4 5.9 %all-to-all-start.1 = ((bf16[8,128,768]{2,1,0:T(8,128)(2,1)}), bf16[8,128,768]{2,1,0:T(8,128)(2,1)}, u32[]{:S(2)}, u32[]{:S(2)}) async-start(bf16[8,128,768]{2,1,0:T(8,128)(2,1)} %bitcast.20), calls=%async_computation.1 | async-start | bytes 3145728 | tf_op jit(solution)/shard_map/all_to_all | solution.py:60
  71.3 0.9 constant_dynamic-update-slice_fusion.24
  72.3 1.0 constant_dynamic-update-slice_fusion.23
  73.2 3.6 %collective-permute-done.13 = bf16[512,1536]{1,0:T(8,128)(2,1)S(1)} collective-permute-done((bf16[512,1536]{1,0:T(8,128)(2,1)}, bf16[512,1536]{1,0:T(8,128)(2,1)S(1)}, u32[]{:S(2)}, u32[]{:S(2)}) %collective-permute-start.13) | collective-permute-done | bytes 1572896 | tf_op jit(solution)/shard_map/ppermute | solution.py:41
  76.9 1.3 constant_dynamic-update-slice_fusion.30
  78.2 5.7 %convolution_convert_fusion.1 = bf16[1024,768]{1,0:T(8,128)(2,1)} fusion(bf16[1024,1536]{1,0:T(8,128)(2,1)} %constant_dynamic-update-slice_fusion.30, bf16[768,1536]{1,0:T(8,128)(2,1)S(1)} %copy-done.7), kind=kOutput, calls=%fused_computation.6 | convolution fusion | flops 2416705536 | bytes 7077888 | tf_op jit(solution)/shard_map/dot_general | solution.py:24
  83.9 7.3 %all-to-all-done.1 = bf16[8,128,768]{2,1,0:T(8,128)(2,1)} async-done(((bf16[8,128,768]{2,1,0:T(8,128)(2,1)}), bf16[8,128,768]{2,1,0:T(8,128)(2,1)}, u32[]{:S(2)}, u32[]{:S(2)}) %all-to-all-start.1) | async-done | bytes 1572896 | tf_op jit(solution)/shard_map/all_to_all | solution.py:60
  91.2 4.8 %all-to-all-start = ((bf16[8,128,768]{2,1,0:T(8,128)(2,1)}), bf16[8,128,768]{2,1,0:T(8,128)(2,1)}, u32[]{:S(2)}, u32[]{:S(2)}) async-start(bf16[8,128,768]{2,1,0:T(8,128)(2,1)} %bitcast.21), calls=%async_computation | async-start | bytes 3145728 | tf_op jit(solution)/shard_map/all_to_all | solution.py:60
  95.9 1.7 convert_reduce_fusion
  97.6 18.4 %all-to-all-done = bf16[8,128,768]{2,1,0:T(8,128)(2,1)} async-done(((bf16[8,128,768]{2,1,0:T(8,128)(2,1)}), bf16[8,128,768]{2,1,0:T(8,128)(2,1)}, u32[]{:S(2)}, u32[]{:S(2)}) %all-to-all-start) | async-done | bytes 1572896 | tf_op jit(solution)/shard_map/all_to_all | solution.py:60
  116.0 1.7 convert_reduce_fusion.1
  117.7 0.3 multiply_convert_fusion.2
  118.0 0.1 broadcast_in_dim.4
  118.1 24.2 %all_to_all.20 = bf16[8,128,768]{2,1,0:T(8,128)(2,1)S(1)} all-to-all(bf16[8,128,768]{2,1,0:T(8,128)(2,1)S(1)} %broadcast_in_dim.4), channel_id=1, replica_groups=mesh['gx'=8,'gy'=4,'gz'=8] {'gx'}, dimensions={0} | all-to-all | bytes 3145728 | tf_op jit(solution)/shard_map/all_to_all | solution.py:65
  142.3 1.1 copy-done.1
  143.4 0.1 fusion.16
  143.6 1.4 convolution_convert_fusion
  145.0 0.1 collective-permute-start.14
  145.1 3.4 %collective-permute-done.14 = bf16[512,1536]{1,0:T(8,128)(2,1)S(1)} collective-permute-done((bf16[512,1536]{1,0:T(8,128)(2,1)S(1)}, bf16[512,1536]{1,0:T(8,128)(2,1)S(1)}, u32[]{:S(2)}, u32[]{:S(2)}) %collective-permute-start.14) | collective-permute-done | bytes 1572896 | tf_op jit(solution)/shard_map/ppermute | solution.py:41
  148.5 3.6 %fusion.14 = (bf16[512,1536]{1,0:T(8,128)(2,1)}, f32[512,1536]{1,0:T(8,128)}) fusion(bf16[512,1536]{1,0:T(8,128)(2,1)S(1)} %collective-permute-done.14, bf16[512,768]{1,0:T(8,128)(2,1)S(1)} %bitcast.19, bf16[1536,768]{1,0:T(8,128)(2,1)S(1)} %copy-done), kind=kOutput, calls=%fused_computation.64 | convolution fusion | flops 1210318848 | bytes 9437184 | tf_op jit(solution)/shard_map/dot_general | solution.py:24
  152.1 1.3 broadcast_in_dim.5
  153.4 5.6 %all-to-all-start.3 = ((bf16[8,128,768]{2,1,0:T(8,128)(2,1)}), bf16[8,128,768]{2,1,0:T(8,128)(2,1)}, u32[]{:S(2)}, u32[]{:S(2)}) async-start(bf16[8,128,768]{2,1,0:T(8,128)(2,1)} %broadcast_in_dim.5), calls=%async_computation.3 | async-start | bytes 3145728 | tf_op jit(solution)/shard_map/all_to_all | solution.py:65
  159.0 1.4 fusion.15
  160.6 0.9 collective-permute-start.16
  161.4 2.4 %collective-permute-start.15 = (bf16[128,1536]{1,0:T(8,128)(2,1)S(1)}, bf16[128,1536]{1,0:T(8,128)(2,1)S(1)}, u32[]{:S(2)}, u32[]{:S(2)}) collective-permute-start(bf16[128,1536]{1,0:T(8,128)(2,1)S(1)} %get-tuple-element.43), channel_id=1, source_target_pairs={{0,6},{1,7},{2,0},{3,1},{4,2},{5,3},{6,4},{7,5},{8,14},{9,15},{10,... | collective-permute-start | bytes 1179656 | tf_op jit(solution)/shard_map/ppermute | solution.py:38
  163.8 6.0 %multiply_convert_fusion.1 = bf16[1536,768]{1,0:T(8,128)(2,1)} fusion(bf16[1024,1536]{1,0:T(8,128)(2,1)} %copy-done.6, bf16[1024,768]{1,0:T(8,128)(2,1)S(1)} %bitcast.18), kind=kOutput, calls=%fused_computation.1 | convolution fusion | flops 2418278400 | bytes 7077888 | tf_op jit(solution)/shard_map/dot_general | solution.py:28
  169.8 11.3 %collective-permute-done.17 = bf16[128,1536]{1,0:T(8,128)(2,1)S(1)} collective-permute-done((bf16[128,1536]{1,0:T(8,128)(2,1)S(1)}, bf16[128,1536]{1,0:T(8,128)(2,1)S(1)}, u32[]{:S(2)}, u32[]{:S(2)}) %collective-permute-start.17) | collective-permute-done | bytes 393248 | tf_op jit(solution)/shard_map/ppermute | solution.py:38
  181.1 0.6 collective-permute-done.15
  181.7 1.3 fusion.12
  183.0 0.7 fusion.17
  183.7 2.8 %collective-permute-start.20 = (bf16[32,1536]{1,0:T(8,128)(2,1)}, bf16[32,1536]{1,0:T(8,128)(2,1)S(1)}, u32[]{:S(2)}, u32[]{:S(2)}) collective-permute-start(bf16[32,1536]{1,0:T(8,128)(2,1)} %get-tuple-element.48), channel_id=1, source_target_pairs={{0,8},{8,16},{16,24},{24,0},{1,9},{9,17},{17,25},{25,1},{2,10},{10... | collective-permute-start | bytes 294920 | tf_op jit(solution)/shard_map/ppermute | solution.py:35
  186.5 1.8 collective-permute-start.19
  188.3 4.1 %collective-permute-start.18 = (bf16[32,1536]{1,0:T(8,128)(2,1)S(1)}, bf16[32,1536]{1,0:T(8,128)(2,1)}, u32[]{:S(2)}, u32[]{:S(2)}) collective-permute-start(bf16[32,1536]{1,0:T(8,128)(2,1)S(1)} %get-tuple-element.50), channel_id=1, source_target_pairs={{0,24},{8,0},{16,8},{24,16},{1,25},{9,1},{17,9},{25,17},{2,26},{10... | collective-permute-start | bytes 294920 | tf_op jit(solution)/shard_map/ppermute | solution.py:35
  192.4 6.4 %multiply_convert_fusion = bf16[768,1536]{1,0:T(8,128)(2,1)} fusion(bf16[1024,768]{1,0:T(8,128)(2,1)} %bitcast.5, bf16[1024,1536]{1,0:T(8,128)(2,1)} %constant_dynamic-update-slice_fusion.30), kind=kOutput, calls=%fused_computation | convolution fusion | flops 2418278400 | bytes 7077888 | tf_op jit(solution)/shard_map/dot_general | solution.py:28
  198.8 1.6 fusion.11
  (33 shorter events, 0.4 us)
Async XLA Ops:
  0.6 42.6 %copy-start = (bf16[1536,768]{1,0:T(8,128)(2,1)S(1)}, bf16[1536,768]{1,0:T(8,128)(2,1)}, u32[]{:S(2)}) copy-start(bf16[1536,768]{1,0:T(8,128)(2,1)} %param.6) | copy-start | bytes 7077892
  0.6 15.6 %collective-permute-start.1 = (bf16[32,1536]{1,0:T(8,128)(2,1)}, bf16[32,1536]{1,0:T(8,128)(2,1)S(1)}, u32[]{:S(2)}, u32[]{:S(2)}) collective-permute-start(bf16[32,1536]{1,0:T(8,128)(2,1)} %param.5), channel_id=1, source_target_pairs={{0,16},{8,24},{16,0},{24,8},{1,17},{9,25},{17,1},{25,9},{2,18},{10... | collective-permute-start | bytes 294920 | tf_op jit(solution)/shard_map/ppermute | solution.py:35
  7.0 9.2 %collective-permute-start = (bf16[32,1536]{1,0:T(8,128)(2,1)}, bf16[32,1536]{1,0:T(8,128)(2,1)S(1)}, u32[]{:S(2)}, u32[]{:S(2)}) collective-permute-start(bf16[32,1536]{1,0:T(8,128)(2,1)} %param.5), channel_id=1, source_target_pairs={{0,8},{8,16},{16,24},{24,0},{1,9},{9,17},{17,25},{25,1},{2,10},{10... | collective-permute-start | bytes 294920 | tf_op jit(solution)/shard_map/ppermute | solution.py:35
  8.5 7.8 %collective-permute-start.2 = (bf16[32,1536]{1,0:T(8,128)(2,1)}, bf16[32,1536]{1,0:T(8,128)(2,1)S(1)}, u32[]{:S(2)}, u32[]{:S(2)}) collective-permute-start(bf16[32,1536]{1,0:T(8,128)(2,1)} %param.5), channel_id=1, source_target_pairs={{0,24},{8,0},{16,8},{24,16},{1,25},{9,1},{17,9},{25,17},{2,26},{10... | collective-permute-start | bytes 294920 | tf_op jit(solution)/shard_map/ppermute | solution.py:35
  16.3 23.4 %copy-start.3 = (bf16[32,1536]{1,0:T(8,128)(2,1)S(1)}, bf16[32,1536]{1,0:T(8,128)(2,1)}, u32[]{:S(2)}) copy-start(bf16[32,1536]{1,0:T(8,128)(2,1)} %param.9) | copy-start | bytes 294916
  16.4 21.7 %collective-permute-start.5 = (bf16[128,1536]{1,0:T(8,128)(2,1)S(1)}, bf16[128,1536]{1,0:T(8,128)(2,1)S(1)}, u32[]{:S(2)}, u32[]{:S(2)}) collective-permute-start(bf16[128,1536]{1,0:T(8,128)(2,1)S(1)} %get-tuple-element.77), channel_id=1, source_target_pairs={{0,6},{1,7},{2,0},{3,1},{4,2},{5,3},{6,4},{7,5},{8,14},{9,15},{10,... | collective-permute-start | bytes 1179656 | tf_op jit(solution)/shard_map/ppermute | solution.py:38
  19.2 18.9 %collective-permute-start.4 = (bf16[128,1536]{1,0:T(8,128)(2,1)S(1)}, bf16[128,1536]{1,0:T(8,128)(2,1)S(1)}, u32[]{:S(2)}, u32[]{:S(2)}) collective-permute-start(bf16[128,1536]{1,0:T(8,128)(2,1)S(1)} %get-tuple-element.77), channel_id=1, source_target_pairs={{0,4},{1,5},{2,6},{3,7},{4,0},{5,1},{6,2},{7,3},{8,12},{9,13},{10,... | collective-permute-start | bytes 1179656 | tf_op jit(solution)/shard_map/ppermute | solution.py:38
  20.0 19.4 %collective-permute-start.3 = (bf16[128,1536]{1,0:T(8,128)(2,1)S(1)}, bf16[128,1536]{1,0:T(8,128)(2,1)S(1)}, u32[]{:S(2)}, u32[]{:S(2)}) collective-permute-start(bf16[128,1536]{1,0:T(8,128)(2,1)S(1)} %get-tuple-element.77), channel_id=1, source_target_pairs={{0,2},{1,3},{2,4},{3,5},{4,6},{5,7},{6,0},{7,1},{8,10},{9,11},{10,... | collective-permute-start | bytes 1179656 | tf_op jit(solution)/shard_map/ppermute | solution.py:38
  20.9 9.2 %collective-permute-start.8 = (bf16[32,1536]{1,0:T(8,128)(2,1)}, bf16[32,1536]{1,0:T(8,128)(2,1)S(1)}, u32[]{:S(2)}, u32[]{:S(2)}) collective-permute-start(bf16[32,1536]{1,0:T(8,128)(2,1)} %param.9), channel_id=1, source_target_pairs={{0,24},{8,0},{16,8},{24,16},{1,25},{9,1},{17,9},{25,17},{2,26},{10... | collective-permute-start | bytes 294920 | tf_op jit(solution)/shard_map/ppermute | solution.py:35
  24.8 10.2 %collective-permute-start.7 = (bf16[32,1536]{1,0:T(8,128)(2,1)}, bf16[32,1536]{1,0:T(8,128)(2,1)S(1)}, u32[]{:S(2)}, u32[]{:S(2)}) collective-permute-start(bf16[32,1536]{1,0:T(8,128)(2,1)} %param.9), channel_id=1, source_target_pairs={{0,16},{8,24},{16,0},{24,8},{1,17},{9,25},{17,1},{25,9},{2,18},{10... | collective-permute-start | bytes 294920 | tf_op jit(solution)/shard_map/ppermute | solution.py:35
  30.1 8.0 %collective-permute-start.6 = (bf16[32,1536]{1,0:T(8,128)(2,1)}, bf16[32,1536]{1,0:T(8,128)(2,1)S(1)}, u32[]{:S(2)}, u32[]{:S(2)}) collective-permute-start(bf16[32,1536]{1,0:T(8,128)(2,1)} %param.9), channel_id=1, source_target_pairs={{0,8},{8,16},{16,24},{24,0},{1,9},{9,17},{17,25},{25,1},{2,10},{10... | collective-permute-start | bytes 294920 | tf_op jit(solution)/shard_map/ppermute | solution.py:35
  39.6 3.5 %collective-permute-start.10 = (bf16[512,1536]{1,0:T(8,128)(2,1)S(1)}, bf16[512,1536]{1,0:T(8,128)(2,1)S(1)}, u32[]{:S(2)}, u32[]{:S(2)}) collective-permute-start(bf16[512,1536]{1,0:T(8,128)(2,1)S(1)} %get-tuple-element.57), channel_id=1, source_target_pairs={{0,1},{1,0},{2,3},{3,2},{4,5},{5,4},{6,7},{7,6},{8,9},{9,8},{10,11... | collective-permute-start | bytes 4718600 | tf_op jit(solution)/shard_map/ppermute | solution.py:41
  42.3 21.1 %collective-permute-start.9 = (bf16[128,1536]{1,0:T(8,128)(2,1)S(1)}, bf16[128,1536]{1,0:T(8,128)(2,1)S(1)}, u32[]{:S(2)}, u32[]{:S(2)}) collective-permute-start(bf16[128,1536]{1,0:T(8,128)(2,1)S(1)} %get-tuple-element.27), channel_id=1, source_target_pairs={{0,2},{1,3},{2,4},{3,5},{4,6},{5,7},{6,0},{7,1},{8,10},{9,11},{10,... | collective-permute-start | bytes 1179656 | tf_op jit(solution)/shard_map/ppermute | solution.py:38
  43.2 3.7 %copy-start.6 = (bf16[1024,1536]{1,0:T(8,128)(2,1)}, bf16[1024,1536]{1,0:T(8,128)(2,1)S(1)}, u32[]{:S(2)}) copy-start(bf16[1024,1536]{1,0:T(8,128)(2,1)S(1)} %constant_dynamic-update-slice_fusion.15) | copy-start | bytes 9437188
  46.9 24.4 %collective-permute-start.11 = (bf16[128,1536]{1,0:T(8,128)(2,1)S(1)}, bf16[128,1536]{1,0:T(8,128)(2,1)S(1)}, u32[]{:S(2)}, u32[]{:S(2)}) collective-permute-start(bf16[128,1536]{1,0:T(8,128)(2,1)S(1)} %get-tuple-element.27), channel_id=1, source_target_pairs={{0,4},{1,5},{2,6},{3,7},{4,0},{5,1},{6,2},{7,3},{8,12},{9,13},{10,... | collective-permute-start | bytes 1179656 | tf_op jit(solution)/shard_map/ppermute | solution.py:38
  48.4 23.9 %collective-permute-start.12 = (bf16[128,1536]{1,0:T(8,128)(2,1)S(1)}, bf16[128,1536]{1,0:T(8,128)(2,1)S(1)}, u32[]{:S(2)}, u32[]{:S(2)}) collective-permute-start(bf16[128,1536]{1,0:T(8,128)(2,1)S(1)} %get-tuple-element.27), channel_id=1, source_target_pairs={{0,6},{1,7},{2,0},{3,1},{4,2},{5,3},{6,4},{7,5},{8,14},{9,15},{10,... | collective-permute-start | bytes 1179656 | tf_op jit(solution)/shard_map/ppermute | solution.py:38
  64.3 1.1 copy-start.4
  65.4 25.8 %all-to-all-start.1 = ((bf16[8,128,768]{2,1,0:T(8,128)(2,1)}), bf16[8,128,768]{2,1,0:T(8,128)(2,1)}, u32[]{:S(2)}, u32[]{:S(2)}) async-start(bf16[8,128,768]{2,1,0:T(8,128)(2,1)} %bitcast.20), calls=%async_computation.1 | async-start | bytes 3145728 | tf_op jit(solution)/shard_map/all_to_all | solution.py:60
  72.3 5.9 %copy-start.7 = (bf16[768,1536]{1,0:T(8,128)(2,1)S(1)}, bf16[768,1536]{1,0:T(8,128)(2,1)}, u32[]{:S(2)}) copy-start(bf16[768,1536]{1,0:T(8,128)(2,1)} %param.8) | copy-start | bytes 7077892
  73.2 3.6 %collective-permute-start.13 = (bf16[512,1536]{1,0:T(8,128)(2,1)}, bf16[512,1536]{1,0:T(8,128)(2,1)S(1)}, u32[]{:S(2)}, u32[]{:S(2)}) collective-permute-start(bf16[512,1536]{1,0:T(8,128)(2,1)} %get-tuple-element.51), channel_id=1, source_target_pairs={{0,1},{1,0},{2,3},{3,2},{4,5},{5,4},{6,7},{7,6},{8,9},{9,8},{10,11... | collective-permute-start | bytes 4718600 | tf_op jit(solution)/shard_map/ppermute | solution.py:41
  91.2 24.9 %all-to-all-start = ((bf16[8,128,768]{2,1,0:T(8,128)(2,1)}), bf16[8,128,768]{2,1,0:T(8,128)(2,1)}, u32[]{:S(2)}, u32[]{:S(2)}) async-start(bf16[8,128,768]{2,1,0:T(8,128)(2,1)} %bitcast.21), calls=%async_computation | async-start | bytes 3145728 | tf_op jit(solution)/shard_map/all_to_all | solution.py:60
  95.9 21.7 %copy-start.5 = (f32[768]{0:T(1024)S(1)}, f32[768]{0:T(1024)}, u32[]{:S(2)}) copy-start(f32[768]{0:T(1024)} %param.7) | copy-start | bytes 9220
  142.3 1.1 copy-start.1
  145.0 3.5 %collective-permute-start.14 = (bf16[512,1536]{1,0:T(8,128)(2,1)S(1)}, bf16[512,1536]{1,0:T(8,128)(2,1)S(1)}, u32[]{:S(2)}, u32[]{:S(2)}) collective-permute-start(bf16[512,1536]{1,0:T(8,128)(2,1)S(1)} %convolution_convert_fusion), channel_id=1, source_target_pairs={{0,1},{1,0},{2,3},{3,2},{4,5},{5,4},{6,7},{7,6},{8,9},{9,8},{10,11... | collective-permute-start | bytes 4718600 | tf_op jit(solution)/shard_map/ppermute | solution.py:41
  153.4 39.0 %all-to-all-start.3 = ((bf16[8,128,768]{2,1,0:T(8,128)(2,1)}), bf16[8,128,768]{2,1,0:T(8,128)(2,1)}, u32[]{:S(2)}, u32[]{:S(2)}) async-start(bf16[8,128,768]{2,1,0:T(8,128)(2,1)} %broadcast_in_dim.5), calls=%async_computation.3 | async-start | bytes 3145728 | tf_op jit(solution)/shard_map/all_to_all | solution.py:65
  159.0 4.8 %copy-start.2 = (bf16[8,128,768]{2,1,0:T(8,128)(2,1)S(1)}, bf16[8,128,768]{2,1,0:T(8,128)(2,1)}, u32[]{:S(2)}) copy-start(bf16[8,128,768]{2,1,0:T(8,128)(2,1)} %copy-done.1) | copy-start | bytes 4718596
  160.5 20.6 %collective-permute-start.17 = (bf16[128,1536]{1,0:T(8,128)(2,1)S(1)}, bf16[128,1536]{1,0:T(8,128)(2,1)S(1)}, u32[]{:S(2)}, u32[]{:S(2)}) collective-permute-start(bf16[128,1536]{1,0:T(8,128)(2,1)S(1)} %get-tuple-element.41), channel_id=1, source_target_pairs={{0,2},{1,3},{2,4},{3,5},{4,6},{5,7},{6,0},{7,1},{8,10},{9,11},{10,... | collective-permute-start | bytes 1179656 | tf_op jit(solution)/shard_map/ppermute | solution.py:38
  160.6 20.5 %collective-permute-start.16 = (bf16[128,1536]{1,0:T(8,128)(2,1)S(1)}, bf16[128,1536]{1,0:T(8,128)(2,1)S(1)}, u32[]{:S(2)}, u32[]{:S(2)}) collective-permute-start(bf16[128,1536]{1,0:T(8,128)(2,1)S(1)} %get-tuple-element.42), channel_id=1, source_target_pairs={{0,4},{1,5},{2,6},{3,7},{4,0},{5,1},{6,2},{7,3},{8,12},{9,13},{10,... | collective-permute-start | bytes 1179656 | tf_op jit(solution)/shard_map/ppermute | solution.py:38
  161.4 20.3 %collective-permute-start.15 = (bf16[128,1536]{1,0:T(8,128)(2,1)S(1)}, bf16[128,1536]{1,0:T(8,128)(2,1)S(1)}, u32[]{:S(2)}, u32[]{:S(2)}) collective-permute-start(bf16[128,1536]{1,0:T(8,128)(2,1)S(1)} %get-tuple-element.43), channel_id=1, source_target_pairs={{0,6},{1,7},{2,0},{3,1},{4,2},{5,3},{6,4},{7,5},{8,14},{9,15},{10,... | collective-permute-start | bytes 1179656 | tf_op jit(solution)/shard_map/ppermute | solution.py:38
  183.7 15.1 %collective-permute-start.20 = (bf16[32,1536]{1,0:T(8,128)(2,1)}, bf16[32,1536]{1,0:T(8,128)(2,1)S(1)}, u32[]{:S(2)}, u32[]{:S(2)}) collective-permute-start(bf16[32,1536]{1,0:T(8,128)(2,1)} %get-tuple-element.48), channel_id=1, source_target_pairs={{0,8},{8,16},{16,24},{24,0},{1,9},{9,17},{17,25},{25,1},{2,10},{10... | collective-permute-start | bytes 294920 | tf_op jit(solution)/shard_map/ppermute | solution.py:35
  186.5 12.3 %collective-permute-start.19 = (bf16[32,1536]{1,0:T(8,128)(2,1)S(1)}, bf16[32,1536]{1,0:T(8,128)(2,1)S(1)}, u32[]{:S(2)}, u32[]{:S(2)}) collective-permute-start(bf16[32,1536]{1,0:T(8,128)(2,1)S(1)} %get-tuple-element.49), channel_id=1, source_target_pairs={{0,16},{8,24},{16,0},{24,8},{1,17},{9,25},{17,1},{25,9},{2,18},{10... | collective-permute-start | bytes 294920 | tf_op jit(solution)/shard_map/ppermute | solution.py:35
  188.3 10.6 %collective-permute-start.18 = (bf16[32,1536]{1,0:T(8,128)(2,1)S(1)}, bf16[32,1536]{1,0:T(8,128)(2,1)}, u32[]{:S(2)}, u32[]{:S(2)}) collective-permute-start(bf16[32,1536]{1,0:T(8,128)(2,1)S(1)} %get-tuple-element.50), channel_id=1, source_target_pairs={{0,24},{8,0},{16,8},{24,16},{1,25},{9,1},{17,9},{25,17},{2,26},{10... | collective-permute-start | bytes 294920 | tf_op jit(solution)/shard_map/ppermute | solution.py:35

commit v4 on v3

v4 whole, which is shorter than its diff:
```python
import math

import jax
import jax.numpy as jnp
from jax import lax
from jax.sharding import PartitionSpec as P

root_coef = math.sqrt(2.0 / math.pi)
cubic_coef = 0.044715
bf16 = jnp.bfloat16
f32 = jnp.float32


def gelu_pair(pre_act, upstream):
    tanh_part = jnp.tanh(root_coef * (pre_act + cubic_coef * pre_act * pre_act * pre_act))
    activation = 0.5 * pre_act * (1.0 + tanh_part)
    slope_value = 0.5 * (1.0 + tanh_part) + 0.5 * pre_act * (
        1.0 - tanh_part * tanh_part
    ) * root_coef * (1.0 + 3.0 * cubic_coef * pre_act * pre_act)
    return (activation.astype(bf16), (upstream * slope_value).astype(bf16))


def contract_last(left, right):
    return lax.dot_general(left, right, (((1,), (1,)), ((), ())), preferred_element_type=f32)


def contract_first(left, right):
    return lax.dot_general(left, right, (((0,), (0,)), ((), ())), preferred_element_type=f32)


def solution(mesh):
    n_x, n_y, n_z = (mesh.shape[a] for a in ("gx", "gy", "gz"))

    def shift_y(a, k):
        return lax.ppermute(a, "gy", [(i, (i + k) % n_y) for i in range(n_y)])

    def shift_chip(a, k):
        return lax.ppermute(a, "gz", [(i, (i + 2 * k) % n_z) for i in range(n_z)])

    def swap_core(a):
        return lax.ppermute(a, "gz", [(i, i ^ 1) for i in range(n_z)])

    def groups(a):
        return [shift_y(a, k) for k in range(1, n_y)]

    def chips(a):
        return [shift_chip(a, k) for k in range(1, n_z // 2)]

    def sum_blocks(parts, n):
        rows = parts[0].shape[0] // n
        sums = []
        for k in range(n):
            cut = [part[k * rows : (k + 1) * rows].astype(f32) for part in parts]
            sums.append(sum(cut[1:], cut[0]))
        return sums[:1] + [a.astype(bf16) for a in sums[1:]]

    def exchange(parts, shift):
        return parts[:1] + [shift(part, -k) for k, part in enumerate(parts) if k]

    def sum_width(part):
        part = part.astype(bf16).reshape(n_x, part.shape[0] // n_x, part.shape[1])
        parts = lax.all_to_all(part, "gx", 0, 0, tiled=True)
        return jnp.sum(parts.astype(f32), axis=0)

    def copies(share):
        return jnp.broadcast_to(share[None], (n_x, *share.shape))

    def gather_width(share_copies):
        parts = lax.all_to_all(share_copies, "gx", 0, 0, tiled=True)
        return parts.reshape(-1, parts.shape[-1])

    def after(a, *others):
        return lax.optimization_barrier((a, *others))[0]

    def shards(tokens, weight_in, bias_hidden, weight_out, grad_output):
        n_chip = n_z // 2
        rows = tokens.shape[0]
        tokens_groups, grad_chips = lax.optimization_barrier((groups(tokens), chips(grad_output)))
        tokens_far = jnp.concatenate([tokens] + tokens_groups, axis=0)
        grad_far = jnp.concatenate([grad_output] + grad_chips, axis=0)
        tokens_chips = chips(tokens_far)
        middle = n_y // 2
        grad_groups = {k: shift_y(grad_far, k) for k in range(1, n_y) if k != middle}
        tokens_chips, grad_groups = lax.optimization_barrier((tokens_chips, grad_groups))
        tokens_near = jnp.concatenate([tokens_far] + tokens_chips, axis=0)
        tokens_all = jnp.concatenate([tokens_near, swap_core(tokens_near)], axis=0)
        total_rows = tokens_all.shape[0]
        half = total_rows // 2
        norm_scale = 1.0 / math.sqrt(total_rows)
        pre_part = jnp.dot(tokens_all, weight_in, preferred_element_type=f32).astype(bf16)
        pre_act = sum_width(pre_part) + bias_hidden
        first = (n_chip - 1) * rows
        grad_groups[middle] = jnp.concatenate(
            [shift_y(grad_far[:first], middle), shift_y(after(grad_far[first:], pre_part), middle)],
            axis=0,
        )
        grad_near = jnp.stack(
            [
                a.reshape(n_chip, rows, a.shape[1])
                for a in [grad_far] + [grad_groups[k] for k in range(1, n_y)]
            ],
            axis=1,
        ).reshape(-1, grad_far.shape[1])
        grad_all = jnp.concatenate([grad_near, swap_core(grad_near)], axis=0)
        upstream = sum_width(contract_last(grad_all, weight_out))
        act_share, grad_share = gelu_pair(pre_act, upstream)
        grad_hidden = gather_width(copies(grad_share))
        other = contract_last(grad_hidden[half:], weight_in).astype(bf16)
        other, act_copies = lax.optimization_barrier((other, copies(act_share)))
        activation = gather_width(act_copies)
        own = contract_last(grad_hidden[:half], weight_in)
        own, other = lax.optimization_barrier((own, swap_core(other)))
        parts, beside = lax.optimization_barrier((sum_blocks([own, other], n_chip), grad_hidden))
        parts = exchange(parts, shift_chip)
        grad_weight_in = (contract_first(tokens_all, beside) * norm_scale).astype(bf16)
        parts, grad_weight_in = lax.optimization_barrier((parts, grad_weight_in))
        parts = exchange(sum_blocks(parts, n_y), shift_y)
        grad_weight_out = (contract_first(activation, grad_all) * norm_scale).astype(bf16)
        parts, grad_weight_out = lax.optimization_barrier((parts, grad_weight_out))
        (grad_tokens,) = sum_blocks(parts, 1)
        return (grad_tokens.astype(bf16), grad_weight_in, grad_weight_out)

    return jax.shard_map(
        shards,
        mesh=mesh,
        in_specs=(
            P(("gy", "gz"), "gx"),
            P("gx", ("gy", "gz")),
            P(("gy", "gz")),
            P(("gy", "gz"), "gx"),
            P(("gy", "gz"), "gx"),
        ),
        out_specs=(P(("gy", "gz"), "gx"), P("gx", ("gy", "gz")), P(("gy", "gz"), "gx")),
        check_vma=False,
    )
```

time: 202 us -> 192 us (0.950)
  local copies, waits for them, and re-layouts: 13.9 us -> 6.91 us
  matrix products: 26.8 us -> 22.7 us
  starting transfers between devices: 57.5 us -> 55.1 us
    ppermute x9, waiting for transfers between devices: 26.7 us -> 19.8 us  [shift_chip(): return lax.ppermute(a, 'gz', [(i, (i + 2 * k) % n_z) for i in range(n_z)])]
    all_to_all x2, waiting for transfers between devices: 25.7 us -> 31.9 us  [sum_width(): parts = lax.all_to_all(part, 'gx', 0, 0, tiled=True)]
    ppermute x9 -> x10, waiting for transfers between devices: 11 us -> 16.3 us  [shift_y(): return lax.ppermute(a, 'gy', [(i, (i + k) % n_y) for i in range(n_y)])]
    ppermute x3, waiting for transfers between devices: 7.3 us -> 3.4 us  [swap_core(): return lax.ppermute(a, 'gz', [(i, i ^ 1) for i in range(n_z)])]
    unnamed x28 -> x29, local copies, waits for them, and re-layouts: 7.77 us -> 4.36 us
    ppermute x9 -> x10, starting transfers between devices: 29.5 us -> 26.6 us  [shift_y(): return lax.ppermute(a, 'gy', [(i, (i + k) % n_y) for i in range(n_y)])]
    all_to_all x2, starting transfers between devices: 10.7 us -> 12.8 us  [sum_width(): parts = lax.all_to_all(part, 'gx', 0, 0, tiled=True)]
    slice x2 -> x0, local copies, waits for them, and re-layouts: 2.09 us -> none  [scatter_stage(): a[k * rows:(k + 1) * rows].astype(bf16)]
  transfers between devices with their start and end apart: 24 -> 25, of which waited for: 13 -> 14; matrix products, arithmetic and copies ran while one was open for 17% -> 15% of each run, Pallas kernels for 0% -> 0%
where the time goes in v4:
time: 192 us; the launch traced here: 190 us
  waiting for transfers between devices  71.5 us (37%)
  starting transfers between devices  55.1 us (29%)
  blocking collectives  24.2 us (13%)
  matrix products  22.7 us (12%)
  other arithmetic  8.49 us (4%)
  local copies, waits for them, and re-layouts  6.91 us (4%)
    all_to_all x2, waiting for transfers between devices, sum_width(): parts = lax.all_to_all(part, 'gx', 0, 0, tiled=True)  31.9 us
    ppermute x10, starting transfers between devices, shift_y(): return lax.ppermute(a, 'gy', [(i, (i + k) % n_y) for i in range(n_y)])  26.6 us
    all_to_all x1, blocking collectives, gather_width(): parts = lax.all_to_all(share_copies, 'gx', 0, 0, tiled=True)  24.2 us
    ppermute x9, waiting for transfers between devices, shift_chip(): return lax.ppermute(a, 'gz', [(i, (i + 2 * k) % n_z) for i in range(n_z)])  19.8 us
    ppermute x10, waiting for transfers between devices, shift_y(): return lax.ppermute(a, 'gy', [(i, (i + k) % n_y) for i in range(n_y)])  16.3 us
    all_to_all x2, starting transfers between devices, sum_width(): parts = lax.all_to_all(part, 'gx', 0, 0, tiled=True)  12.8 us
    dot_general x2, matrix products, contract_first(): lax.dot_general(left, right, (((0,), (0,)), ((), ())), preferred_element_...  10.4 us
    ppermute x9, starting transfers between devices, shift_chip(): return lax.ppermute(a, 'gz', [(i, (i + 2 * k) % n_z) for i in range(n_z)])  9.64 us
  transfers between devices with their start and end apart: 25, of which 14 were waited for; matrix products, arithmetic and copies ran while one was open for 15% of the time, Pallas kernels for 0%

profile of v4, /device:TPU:32, one launch (start us, length us, event | category | flops | bytes accessed | tf_op | source)
XLA Modules:
  0.0 189.7 jit_solution(16966290602535782335)
XLA Ops:
  0.6 6.4 %collective-permute-start.1 = (bf16[32,1536]{1,0:T(8,128)(2,1)}, bf16[32,1536]{1,0:T(8,128)(2,1)S(1)}, u32[]{:S(2)}, u32[]{:S(2)}) collective-permute-start(bf16[32,1536]{1,0:T(8,128)(2,1)} %param.5), channel_id=1, source_target_pairs={{0,16},{8,24},{16,0},{24,8},{1,17},{9,25},{17,1},{25,9},{2,18},{10... | collective-permute-start | bytes 294920 | tf_op jit(solution)/shard_map/ppermute | solution.py:35
  7.0 1.5 collective-permute-start
  8.5 2.7 %collective-permute-start.2 = (bf16[32,1536]{1,0:T(8,128)(2,1)}, bf16[32,1536]{1,0:T(8,128)(2,1)S(1)}, u32[]{:S(2)}, u32[]{:S(2)}) collective-permute-start(bf16[32,1536]{1,0:T(8,128)(2,1)} %param.5), channel_id=1, source_target_pairs={{0,24},{8,0},{16,8},{24,16},{1,25},{9,1},{17,9},{25,17},{2,26},{10... | collective-permute-start | bytes 294920 | tf_op jit(solution)/shard_map/ppermute | solution.py:35
  11.2 2.8 %collective-permute-start.5 = (bf16[32,1536]{1,0:T(8,128)(2,1)}, bf16[32,1536]{1,0:T(8,128)(2,1)}, u32[]{:S(2)}, u32[]{:S(2)}) collective-permute-start(bf16[32,1536]{1,0:T(8,128)(2,1)} %param.9), channel_id=1, source_target_pairs={{0,6},{1,7},{2,0},{3,1},{4,2},{5,3},{6,4},{7,5},{8,14},{9,15},{10,... | collective-permute-start | bytes 294920 | tf_op jit(solution)/shard_map/ppermute | solution.py:38
  13.9 0.8 collective-permute-start.4
  14.7 0.9 constant_dynamic-update-slice_fusion.14
  15.6 1.0 collective-permute-start.3
  16.6 0.9 constant_dynamic-update-slice_fusion.3
  17.6 0.4 collective-permute-done.5
  17.9 2.3 %collective-permute-done.4 = bf16[32,1536]{1,0:T(8,128)(2,1)S(1)} collective-permute-done((bf16[32,1536]{1,0:T(8,128)(2,1)}, bf16[32,1536]{1,0:T(8,128)(2,1)S(1)}, u32[]{:S(2)}, u32[]{:S(2)}) %collective-permute-start.4) | collective-permute-done | bytes 98336 | tf_op jit(solution)/shard_map/ppermute | solution.py:38
  20.3 1.5 collective-permute-done.3
  21.8 0.9 constant_dynamic-update-slice_fusion
  22.7 0.6 collective-permute-start.10
  23.3 2.3 %collective-permute-start.9 = (bf16[128,1536]{1,0:T(8,128)(2,1)S(1)}, bf16[128,1536]{1,0:T(8,128)(2,1)S(1)}, u32[]{:S(2)}, u32[]{:S(2)}) collective-permute-start(bf16[128,1536]{1,0:T(8,128)(2,1)S(1)} %constant_dynamic-update-slice_fusion), channel_id=1, source_target_pairs={{0,8},{8,16},{16,24},{24,0},{1,9},{9,17},{17,25},{25,1},{2,10},{10... | collective-permute-start | bytes 1179656 | tf_op jit(solution)/shard_map/ppermute | solution.py:35
  25.7 0.2 collective-permute-start.8
  25.9 1.6 collective-permute-start.7
  27.5 1.2 collective-permute-start.6
  28.7 9.4 %collective-permute-done.10 = bf16[128,1536]{1,0:T(8,128)(2,1)S(1)} collective-permute-done((bf16[128,1536]{1,0:T(8,128)(2,1)S(1)}, bf16[128,1536]{1,0:T(8,128)(2,1)S(1)}, u32[]{:S(2)}, u32[]{:S(2)}) %collective-permute-start.10) | collective-permute-done | bytes 393248 | tf_op jit(solution)/shard_map/ppermute | solution.py:35
  38.1 5.5 %collective-permute-done.9 = bf16[128,1536]{1,0:T(8,128)(2,1)S(1)} collective-permute-done((bf16[128,1536]{1,0:T(8,128)(2,1)S(1)}, bf16[128,1536]{1,0:T(8,128)(2,1)S(1)}, u32[]{:S(2)}, u32[]{:S(2)}) %collective-permute-start.9) | collective-permute-done | bytes 393248 | tf_op jit(solution)/shard_map/ppermute | solution.py:35
  43.6 0.3 collective-permute-done.6
  44.0 0.1 constant_dynamic-update-slice_fusion.9
  44.1 0.1 collective-permute-start.12
  44.2 0.7 pad_maximum_fusion.7
  45.0 3.3 %collective-permute-start.11 = (bf16[96,1536]{1,0:T(8,128)(2,1)}, bf16[96,1536]{1,0:T(8,128)(2,1)}, u32[]{:S(2)}, u32[]{:S(2)}) collective-permute-start(bf16[96,1536]{1,0:T(8,128)(2,1)} %pad_maximum_fusion.7), channel_id=1, source_target_pairs={{0,16},{8,24},{16,0},{24,8},{1,17},{9,25},{17,1},{25,9},{2,18},{10... | collective-permute-start | bytes 884744 | tf_op jit(solution)/shard_map/ppermute | solution.py:35
  48.3 0.1 constant_dynamic-update-slice_fusion.15
  48.5 3.7 %convolution_convert_fusion.1 = bf16[1024,768]{1,0:T(8,128)(2,1)} fusion(bf16[1024,1536]{1,0:T(8,128)(2,1)S(1)} %constant_dynamic-update-slice_fusion.15, bf16[1536,768]{1,0:T(8,128)(2,1)S(1)} %copy-done), kind=kOutput, calls=%fused_computation.8 | convolution fusion | flops 2416705536 | bytes 7077888 | tf_op jit(solution)/shard_map/dot_general | solution.py:90
  52.1 2.6 %collective-permute-start.13 = (bf16[32,1536]{1,0:T(8,128)(2,1)}, bf16[32,1536]{1,0:T(8,128)(2,1)}, u32[]{:S(2)}, u32[]{:S(2)}) collective-permute-start(bf16[32,1536]{1,0:T(8,128)(2,1)} %collective-permute-done.5), channel_id=1, source_target_pairs={{0,16},{8,24},{16,0},{24,8},{1,17},{9,25},{17,1},{25,9},{2,18},{10... | collective-permute-start | bytes 294920 | tf_op jit(solution)/shard_map/ppermute | solution.py:35
  54.8 6.2 %all-to-all-start.1 = ((bf16[8,128,768]{2,1,0:T(8,128)(2,1)}), bf16[8,128,768]{2,1,0:T(8,128)(2,1)}, u32[]{:S(2)}, u32[]{:S(2)}) async-start(bf16[8,128,768]{2,1,0:T(8,128)(2,1)} %bitcast.25), calls=%async_computation.1 | async-start | bytes 3145728 | tf_op jit(solution)/shard_map/all_to_all | solution.py:62
  61.0 1.1 collective-permute-done.13
  62.1 1.0 pad_maximum_fusion.6
  63.1 0.2 pad_maximum_fusion.5
  63.3 0.3 collective-permute-start.14
  63.6 3.4 %collective-permute-done.14 = bf16[512,1536]{1,0:T(8,128)(2,1)S(1)} collective-permute-done((bf16[512,1536]{1,0:T(8,128)(2,1)S(1)}, bf16[512,1536]{1,0:T(8,128)(2,1)S(1)}, u32[]{:S(2)}, u32[]{:S(2)}) %collective-permute-start.14) | collective-permute-done | bytes 1572896 | tf_op jit(solution)/shard_map/ppermute | solution.py:41
  67.0 1.1 copy-done.9
  68.1 4.7 %fusion.1 = bf16[1024,768]{1,0:T(8,128)(2,1)} fusion(bf16[768,1536]{1,0:T(8,128)(2,1)S(1)} %copy-done.8, bf16[512,1536]{1,0:T(8,128)(2,1)S(1)} %collective-permute-done.14, bf16[512,1536]{1,0:T(8,128)(2,1)S(1)} %bitcast.23), kind=kOutput, calls=%fused_computation.7 | convolution fusion | flops 2422996992 | bytes 7077888 | tf_op jit(solution)/shard_map/dot_general | solution.py:24
  72.8 13.2 %all-to-all-done.1 = bf16[8,128,768]{2,1,0:T(8,128)(2,1)} async-done(((bf16[8,128,768]{2,1,0:T(8,128)(2,1)}), bf16[8,128,768]{2,1,0:T(8,128)(2,1)}, u32[]{:S(2)}, u32[]{:S(2)}) %all-to-all-start.1) | async-done | bytes 1572896 | tf_op jit(solution)/shard_map/all_to_all | solution.py:62
  86.0 6.7 %all-to-all-start = ((bf16[8,128,768]{2,1,0:T(8,128)(2,1)}), bf16[8,128,768]{2,1,0:T(8,128)(2,1)}, u32[]{:S(2)}, u32[]{:S(2)}) async-start(bf16[8,128,768]{2,1,0:T(8,128)(2,1)} %bitcast.26), calls=%async_computation | async-start | bytes 3145728 | tf_op jit(solution)/shard_map/all_to_all | solution.py:62
  92.7 1.7 convert_reduce_fusion
  94.4 18.8 %all-to-all-done = bf16[8,128,768]{2,1,0:T(8,128)(2,1)} async-done(((bf16[8,128,768]{2,1,0:T(8,128)(2,1)}), bf16[8,128,768]{2,1,0:T(8,128)(2,1)}, u32[]{:S(2)}, u32[]{:S(2)}) %all-to-all-start) | async-done | bytes 1572896 | tf_op jit(solution)/shard_map/all_to_all | solution.py:62
  113.1 1.7 convert_reduce_fusion.1
  114.8 0.3 multiply_convert_fusion.2
  115.1 0.1 broadcast_in_dim.4
  115.2 24.2 %all_to_all.20 = bf16[8,128,768]{2,1,0:T(8,128)(2,1)S(1)} all-to-all(bf16[8,128,768]{2,1,0:T(8,128)(2,1)S(1)} %broadcast_in_dim.4), channel_id=1, replica_groups=mesh['gx'=8,'gy'=4,'gz'=8] {'gx'}, dimensions={0} | all-to-all | bytes 3145728 | tf_op jit(solution)/shard_map/all_to_all | solution.py:69
  139.4 1.1 copy-done.1
  140.6 0.1 fusion.11
  140.7 2.6 %convolution_convert_fusion = bf16[512,1536]{1,0:T(8,128)(2,1)} fusion(bf16[512,768]{1,0:T(8,128)(2,1)S(1)} %bitcast.29, bf16[1536,768]{1,0:T(8,128)(2,1)S(1)} %copy-done), kind=kOutput, calls=%fused_computation.5 | convolution fusion | flops 1208745984 | bytes 4718592 | tf_op jit(solution)/shard_map/dot_general | solution.py:24
  143.2 1.3 broadcast_in_dim.5
  144.5 5.6 %all-to-all-start.3 = ((bf16[8,128,768]{2,1,0:T(8,128)(2,1)}), bf16[8,128,768]{2,1,0:T(8,128)(2,1)}, u32[]{:S(2)}, u32[]{:S(2)}) async-start(bf16[8,128,768]{2,1,0:T(8,128)(2,1)} %broadcast_in_dim.5), calls=%async_computation.3 | async-start | bytes 3145728 | tf_op jit(solution)/shard_map/all_to_all | solution.py:69
  150.1 1.4 fusion.12
  151.6 2.1 %add_convert_fusion = (bf16[128,1536]{1,0:T(8,128)(2,1)S(1)}, bf16[128,1536]{1,0:T(8,128)(2,1)S(1)}, bf16[128,1536]{1,0:T(8,128)(2,1)S(1)}, f32[128,1536]{1,0:T(8,128)S(1)}) fusion(f32[512,1536]{1,0:T(8,128)S(1)} %fusion.12, bf16[512,1536]{1,0:T(8,128)(2,1)} %collective-permute-done.15), kind=kLoop, calls=%fused_computation.10 | loop fusion | flops 2162688 | bytes 6684672 | tf_op jit(solution)/shard_map/convert_element_type | solution.py:55
  153.6 0.1 collective-permute-start.16
  153.7 1.1 collective-permute-start.17
  154.8 0.9 collective-permute-start.18
  155.8 4.0 %multiply_convert_fusion.1 = bf16[1536,768]{1,0:T(8,128)(2,1)} fusion(bf16[1024,1536]{1,0:T(8,128)(2,1)S(1)} %copy-done.7, bf16[1024,768]{1,0:T(8,128)(2,1)S(1)} %bitcast.21), kind=kOutput, calls=%fused_computation.1 | convolution fusion | flops 2418278400 | bytes 7077888 | tf_op jit(solution)/shard_map/dot_general | solution.py:28
  159.7 6.0 %collective-permute-done.16 = bf16[128,1536]{1,0:T(8,128)(2,1)S(1)} collective-permute-done((bf16[128,1536]{1,0:T(8,128)(2,1)S(1)}, bf16[128,1536]{1,0:T(8,128)(2,1)S(1)}, u32[]{:S(2)}, u32[]{:S(2)}) %collective-permute-start.16) | collective-permute-done | bytes 393248 | tf_op jit(solution)/shard_map/ppermute | solution.py:38
  165.7 1.6 collective-permute-done.17
  167.3 7.7 %collective-permute-done.18 = bf16[128,1536]{1,0:T(8,128)(2,1)S(1)} collective-permute-done((bf16[128,1536]{1,0:T(8,128)(2,1)S(1)}, bf16[128,1536]{1,0:T(8,128)(2,1)S(1)}, u32[]{:S(2)}, u32[]{:S(2)}) %collective-permute-start.18) | collective-permute-done | bytes 393248 | tf_op jit(solution)/shard_map/ppermute | solution.py:38
  175.0 0.2 add_convert_fusion.4
  175.2 0.4 collective-permute-start.21
  175.6 2.8 %collective-permute-start.20 = (bf16[32,1536]{1,0:T(8,128)(2,1)S(1)}, bf16[32,1536]{1,0:T(8,128)(2,1)S(1)}, u32[]{:S(2)}, u32[]{:S(2)}) collective-permute-start(bf16[32,1536]{1,0:T(8,128)(2,1)S(1)} %get-tuple-element.70), channel_id=1, source_target_pairs={{0,16},{8,24},{16,0},{24,8},{1,17},{9,25},{17,1},{25,9},{2,18},{10... | collective-permute-start | bytes 294920 | tf_op jit(solution)/shard_map/ppermute | solution.py:35
  178.3 4.0 %collective-permute-start.19 = (bf16[32,1536]{1,0:T(8,128)(2,1)S(1)}, bf16[32,1536]{1,0:T(8,128)(2,1)S(1)}, u32[]{:S(2)}, u32[]{:S(2)}) collective-permute-start(bf16[32,1536]{1,0:T(8,128)(2,1)S(1)} %get-tuple-element.71), channel_id=1, source_target_pairs={{0,24},{8,0},{16,8},{24,16},{1,25},{9,1},{17,9},{25,17},{2,26},{10... | collective-permute-start | bytes 294920 | tf_op jit(solution)/shard_map/ppermute | solution.py:35
  182.4 6.4 %multiply_convert_fusion = bf16[768,1536]{1,0:T(8,128)(2,1)} fusion(bf16[1024,768]{1,0:T(8,128)(2,1)} %bitcast.10, bf16[512,1536]{1,0:T(8,128)(2,1)} %copy-done.9, bf16[512,1536]{1,0:T(8,128)(2,1)} %bitcast.24), kind=kOutput, calls=%fused_computation | convolution fusion | flops 2424569856 | bytes 7077888 | tf_op jit(solution)/shard_map/dot_general | solution.py:28
  188.8 0.3 collective-permute-done.19
  189.1 0.7 add_convert_fusion.3
  (37 shorter events, 0.3 us)
Async XLA Ops:
  0.6 47.8 %copy-start = (bf16[1536,768]{1,0:T(8,128)(2,1)S(1)}, bf16[1536,768]{1,0:T(8,128)(2,1)}, u32[]{:S(2)}) copy-start(bf16[1536,768]{1,0:T(8,128)(2,1)} %param.6) | copy-start | bytes 7077892
  0.6 15.0 %collective-permute-start.1 = (bf16[32,1536]{1,0:T(8,128)(2,1)}, bf16[32,1536]{1,0:T(8,128)(2,1)S(1)}, u32[]{:S(2)}, u32[]{:S(2)}) collective-permute-start(bf16[32,1536]{1,0:T(8,128)(2,1)} %param.5), channel_id=1, source_target_pairs={{0,16},{8,24},{16,0},{24,8},{1,17},{9,25},{17,1},{25,9},{2,18},{10... | collective-permute-start | bytes 294920 | tf_op jit(solution)/shard_map/ppermute | solution.py:35
  7.0 10.5 %collective-permute-start = (bf16[32,1536]{1,0:T(8,128)(2,1)}, bf16[32,1536]{1,0:T(8,128)(2,1)S(1)}, u32[]{:S(2)}, u32[]{:S(2)}) collective-permute-start(bf16[32,1536]{1,0:T(8,128)(2,1)} %param.5), channel_id=1, source_target_pairs={{0,8},{8,16},{16,24},{24,0},{1,9},{9,17},{17,25},{25,1},{2,10},{10... | collective-permute-start | bytes 294920 | tf_op jit(solution)/shard_map/ppermute | solution.py:35
  8.5 9.1 %collective-permute-start.2 = (bf16[32,1536]{1,0:T(8,128)(2,1)}, bf16[32,1536]{1,0:T(8,128)(2,1)S(1)}, u32[]{:S(2)}, u32[]{:S(2)}) collective-permute-start(bf16[32,1536]{1,0:T(8,128)(2,1)} %param.5), channel_id=1, source_target_pairs={{0,24},{8,0},{16,8},{24,16},{1,25},{9,1},{17,9},{25,17},{2,26},{10... | collective-permute-start | bytes 294920 | tf_op jit(solution)/shard_map/ppermute | solution.py:35
  11.2 6.8 %collective-permute-start.5 = (bf16[32,1536]{1,0:T(8,128)(2,1)}, bf16[32,1536]{1,0:T(8,128)(2,1)}, u32[]{:S(2)}, u32[]{:S(2)}) collective-permute-start(bf16[32,1536]{1,0:T(8,128)(2,1)} %param.9), channel_id=1, source_target_pairs={{0,6},{1,7},{2,0},{3,1},{4,2},{5,3},{6,4},{7,5},{8,14},{9,15},{10,... | collective-permute-start | bytes 294920 | tf_op jit(solution)/shard_map/ppermute | solution.py:38
  13.9 6.4 %collective-permute-start.4 = (bf16[32,1536]{1,0:T(8,128)(2,1)}, bf16[32,1536]{1,0:T(8,128)(2,1)S(1)}, u32[]{:S(2)}, u32[]{:S(2)}) collective-permute-start(bf16[32,1536]{1,0:T(8,128)(2,1)} %param.9), channel_id=1, source_target_pairs={{0,4},{1,5},{2,6},{3,7},{4,0},{5,1},{6,2},{7,3},{8,12},{9,13},{10,... | collective-permute-start | bytes 294920 | tf_op jit(solution)/shard_map/ppermute | solution.py:38
  15.6 6.1 %collective-permute-start.3 = (bf16[32,1536]{1,0:T(8,128)(2,1)}, bf16[32,1536]{1,0:T(8,128)(2,1)S(1)}, u32[]{:S(2)}, u32[]{:S(2)}) collective-permute-start(bf16[32,1536]{1,0:T(8,128)(2,1)} %param.9), channel_id=1, source_target_pairs={{0,2},{1,3},{2,4},{3,5},{4,6},{5,7},{6,0},{7,1},{8,10},{9,11},{10,... | collective-permute-start | bytes 294920 | tf_op jit(solution)/shard_map/ppermute | solution.py:38
  22.7 15.4 %collective-permute-start.10 = (bf16[128,1536]{1,0:T(8,128)(2,1)S(1)}, bf16[128,1536]{1,0:T(8,128)(2,1)S(1)}, u32[]{:S(2)}, u32[]{:S(2)}) collective-permute-start(bf16[128,1536]{1,0:T(8,128)(2,1)S(1)} %constant_dynamic-update-slice_fusion), channel_id=1, source_target_pairs={{0,24},{8,0},{16,8},{24,16},{1,25},{9,1},{17,9},{25,17},{2,26},{10... | collective-permute-start | bytes 1179656 | tf_op jit(solution)/shard_map/ppermute | solution.py:35
  23.3 20.3 %collective-permute-start.9 = (bf16[128,1536]{1,0:T(8,128)(2,1)S(1)}, bf16[128,1536]{1,0:T(8,128)(2,1)S(1)}, u32[]{:S(2)}, u32[]{:S(2)}) collective-permute-start(bf16[128,1536]{1,0:T(8,128)(2,1)S(1)} %constant_dynamic-update-slice_fusion), channel_id=1, source_target_pairs={{0,8},{8,16},{16,24},{24,0},{1,9},{9,17},{17,25},{25,1},{2,10},{10... | collective-permute-start | bytes 1179656 | tf_op jit(solution)/shard_map/ppermute | solution.py:35
  25.6 18.6 %copy-start.4 = (bf16[32,1536]{1,0:T(8,128)(2,1)S(1)}, bf16[32,1536]{1,0:T(8,128)(2,1)}, u32[]{:S(2)}) copy-start(bf16[32,1536]{1,0:T(8,128)(2,1)} %param.9) | copy-start | bytes 294916
  25.7 17.9 %collective-permute-start.8 = (bf16[128,1536]{1,0:T(8,128)(2,1)S(1)}, bf16[128,1536]{1,0:T(8,128)(2,1)S(1)}, u32[]{:S(2)}, u32[]{:S(2)}) collective-permute-start(bf16[128,1536]{1,0:T(8,128)(2,1)S(1)} %get-tuple-element.85), channel_id=1, source_target_pairs={{0,6},{1,7},{2,0},{3,1},{4,2},{5,3},{6,4},{7,5},{8,14},{9,15},{10,... | collective-permute-start | bytes 1179656 | tf_op jit(solution)/shard_map/ppermute | solution.py:38
  25.9 17.7 %collective-permute-start.7 = (bf16[128,1536]{1,0:T(8,128)(2,1)S(1)}, bf16[128,1536]{1,0:T(8,128)(2,1)S(1)}, u32[]{:S(2)}, u32[]{:S(2)}) collective-permute-start(bf16[128,1536]{1,0:T(8,128)(2,1)S(1)} %get-tuple-element.85), channel_id=1, source_target_pairs={{0,4},{1,5},{2,6},{3,7},{4,0},{5,1},{6,2},{7,3},{8,12},{9,13},{10,... | collective-permute-start | bytes 1179656 | tf_op jit(solution)/shard_map/ppermute | solution.py:38
  27.5 16.4 %collective-permute-start.6 = (bf16[128,1536]{1,0:T(8,128)(2,1)S(1)}, bf16[128,1536]{1,0:T(8,128)(2,1)S(1)}, u32[]{:S(2)}, u32[]{:S(2)}) collective-permute-start(bf16[128,1536]{1,0:T(8,128)(2,1)S(1)} %get-tuple-element.85), channel_id=1, source_target_pairs={{0,2},{1,3},{2,4},{3,5},{4,6},{5,7},{6,0},{7,1},{8,10},{9,11},{10,... | collective-permute-start | bytes 1179656 | tf_op jit(solution)/shard_map/ppermute | solution.py:38
  44.1 4.2 %collective-permute-start.12 = (bf16[512,1536]{1,0:T(8,128)(2,1)S(1)}, bf16[512,1536]{1,0:T(8,128)(2,1)S(1)}, u32[]{:S(2)}, u32[]{:S(2)}) collective-permute-start(bf16[512,1536]{1,0:T(8,128)(2,1)S(1)} %get-tuple-element.77), channel_id=1, source_target_pairs={{0,1},{1,0},{2,3},{3,2},{4,5},{5,4},{6,7},{7,6},{8,9},{9,8},{10,11... | collective-permute-start | bytes 4718600 | tf_op jit(solution)/shard_map/ppermute | solution.py:41
  45.0 16.0 %collective-permute-start.11 = (bf16[96,1536]{1,0:T(8,128)(2,1)}, bf16[96,1536]{1,0:T(8,128)(2,1)}, u32[]{:S(2)}, u32[]{:S(2)}) collective-permute-start(bf16[96,1536]{1,0:T(8,128)(2,1)} %pad_maximum_fusion.7), channel_id=1, source_target_pairs={{0,16},{8,24},{16,0},{24,8},{1,17},{9,25},{17,1},{25,9},{2,18},{10... | collective-permute-start | bytes 884744 | tf_op jit(solution)/shard_map/ppermute | solution.py:35
  48.4 3.7 %copy-start.6 = (bf16[1024,1536]{1,0:T(8,128)(2,1)}, bf16[1024,1536]{1,0:T(8,128)(2,1)S(1)}, u32[]{:S(2)}) copy-start(bf16[1024,1536]{1,0:T(8,128)(2,1)S(1)} %constant_dynamic-update-slice_fusion.15) | copy-start | bytes 9437188
  52.1 9.9 %collective-permute-start.13 = (bf16[32,1536]{1,0:T(8,128)(2,1)}, bf16[32,1536]{1,0:T(8,128)(2,1)}, u32[]{:S(2)}, u32[]{:S(2)}) collective-permute-start(bf16[32,1536]{1,0:T(8,128)(2,1)} %collective-permute-done.5), channel_id=1, source_target_pairs={{0,16},{8,24},{16,0},{24,8},{1,17},{9,25},{17,1},{25,9},{2,18},{10... | collective-permute-start | bytes 294920 | tf_op jit(solution)/shard_map/ppermute | solution.py:35
  54.8 31.2 %all-to-all-start.1 = ((bf16[8,128,768]{2,1,0:T(8,128)(2,1)}), bf16[8,128,768]{2,1,0:T(8,128)(2,1)}, u32[]{:S(2)}, u32[]{:S(2)}) async-start(bf16[8,128,768]{2,1,0:T(8,128)(2,1)} %bitcast.25), calls=%async_computation.1 | async-start | bytes 3145728 | tf_op jit(solution)/shard_map/all_to_all | solution.py:62
  60.9 7.2 %copy-start.8 = (bf16[768,1536]{1,0:T(8,128)(2,1)S(1)}, bf16[768,1536]{1,0:T(8,128)(2,1)}, u32[]{:S(2)}) copy-start(bf16[768,1536]{1,0:T(8,128)(2,1)} %param.8) | copy-start | bytes 7077892
  63.3 3.7 %copy-start.3 = (bf16[4,4,32,1536]{3,2,1,0:T(8,128)(2,1)}, bf16[4,4,32,1536]{3,2,1,0:T(8,128)(2,1)S(1)}, u32[]{:S(2)}) copy-start(bf16[4,4,32,1536]{3,2,1,0:T(8,128)(2,1)S(1)} %pad_maximum_fusion.5) | copy-start | bytes 4718596
  63.3 3.7 %collective-permute-start.14 = (bf16[512,1536]{1,0:T(8,128)(2,1)S(1)}, bf16[512,1536]{1,0:T(8,128)(2,1)S(1)}, u32[]{:S(2)}, u32[]{:S(2)}) collective-permute-start(bf16[512,1536]{1,0:T(8,128)(2,1)S(1)} %bitcast.22), channel_id=1, source_target_pairs={{0,1},{1,0},{2,3},{3,2},{4,5},{5,4},{6,7},{7,6},{8,9},{9,8},{10,11... | collective-permute-start | bytes 4718600 | tf_op jit(solution)/shard_map/ppermute | solution.py:41
  67.0 1.1 copy-start.9
  86.0 27.1 %all-to-all-start = ((bf16[8,128,768]{2,1,0:T(8,128)(2,1)}), bf16[8,128,768]{2,1,0:T(8,128)(2,1)}, u32[]{:S(2)}, u32[]{:S(2)}) async-start(bf16[8,128,768]{2,1,0:T(8,128)(2,1)} %bitcast.26), calls=%async_computation | async-start | bytes 3145728 | tf_op jit(solution)/shard_map/all_to_all | solution.py:62
  92.7 22.1 %copy-start.5 = (f32[768]{0:T(1024)S(1)}, f32[768]{0:T(1024)}, u32[]{:S(2)}) copy-start(f32[768]{0:T(1024)} %param.7) | copy-start | bytes 9220
  139.4 1.1 copy-start.1
  144.5 7.0 %collective-permute-start.15 = (bf16[512,1536]{1,0:T(8,128)(2,1)}, bf16[512,1536]{1,0:T(8,128)(2,1)}, u32[]{:S(2)}, u32[]{:S(2)}) collective-permute-start(bf16[512,1536]{1,0:T(8,128)(2,1)} %convolution_convert_fusion), channel_id=1, source_target_pairs={{0,1},{1,0},{2,3},{3,2},{4,5},{5,4},{6,7},{7,6},{8,9},{9,8},{10,11... | collective-permute-start | bytes 4718600 | tf_op jit(solution)/shard_map/ppermute | solution.py:41
  144.5 37.9 %all-to-all-start.3 = ((bf16[8,128,768]{2,1,0:T(8,128)(2,1)}), bf16[8,128,768]{2,1,0:T(8,128)(2,1)}, u32[]{:S(2)}, u32[]{:S(2)}) async-start(bf16[8,128,768]{2,1,0:T(8,128)(2,1)} %broadcast_in_dim.5), calls=%async_computation.3 | async-start | bytes 3145728 | tf_op jit(solution)/shard_map/all_to_all | solution.py:69
  151.6 4.2 %copy-start.2 = (bf16[8,128,768]{2,1,0:T(8,128)(2,1)S(1)}, bf16[8,128,768]{2,1,0:T(8,128)(2,1)}, u32[]{:S(2)}) copy-start(bf16[8,128,768]{2,1,0:T(8,128)(2,1)} %copy-done.1) | copy-start | bytes 4718596
  151.6 4.2 %copy-start.7 = (bf16[1024,1536]{1,0:T(8,128)(2,1)S(1)}, bf16[1024,1536]{1,0:T(8,128)(2,1)}, u32[]{:S(2)}) copy-start(bf16[1024,1536]{1,0:T(8,128)(2,1)} %copy-done.6) | copy-start | bytes 9437188
  153.6 12.0 %collective-permute-start.16 = (bf16[128,1536]{1,0:T(8,128)(2,1)S(1)}, bf16[128,1536]{1,0:T(8,128)(2,1)S(1)}, u32[]{:S(2)}, u32[]{:S(2)}) collective-permute-start(bf16[128,1536]{1,0:T(8,128)(2,1)S(1)} %get-tuple-element.50), channel_id=1, source_target_pairs={{0,6},{1,7},{2,0},{3,1},{4,2},{5,3},{6,4},{7,5},{8,14},{9,15},{10,... | collective-permute-start | bytes 1179656 | tf_op jit(solution)/shard_map/ppermute | solution.py:38
  153.7 13.6 %collective-permute-start.17 = (bf16[128,1536]{1,0:T(8,128)(2,1)S(1)}, bf16[128,1536]{1,0:T(8,128)(2,1)S(1)}, u32[]{:S(2)}, u32[]{:S(2)}) collective-permute-start(bf16[128,1536]{1,0:T(8,128)(2,1)S(1)} %get-tuple-element.51), channel_id=1, source_target_pairs={{0,4},{1,5},{2,6},{3,7},{4,0},{5,1},{6,2},{7,3},{8,12},{9,13},{10,... | collective-permute-start | bytes 1179656 | tf_op jit(solution)/shard_map/ppermute | solution.py:38
  154.8 20.2 %collective-permute-start.18 = (bf16[128,1536]{1,0:T(8,128)(2,1)S(1)}, bf16[128,1536]{1,0:T(8,128)(2,1)S(1)}, u32[]{:S(2)}, u32[]{:S(2)}) collective-permute-start(bf16[128,1536]{1,0:T(8,128)(2,1)S(1)} %get-tuple-element.52), channel_id=1, source_target_pairs={{0,2},{1,3},{2,4},{3,5},{4,6},{5,7},{6,0},{7,1},{8,10},{9,11},{10,... | collective-permute-start | bytes 1179656 | tf_op jit(solution)/shard_map/ppermute | solution.py:38
  175.2 13.6 %collective-permute-start.21 = (bf16[32,1536]{1,0:T(8,128)(2,1)S(1)}, bf16[32,1536]{1,0:T(8,128)(2,1)S(1)}, u32[]{:S(2)}, u32[]{:S(2)}) collective-permute-start(bf16[32,1536]{1,0:T(8,128)(2,1)S(1)} %get-tuple-element.69), channel_id=1, source_target_pairs={{0,8},{8,16},{16,24},{24,0},{1,9},{9,17},{17,25},{25,1},{2,10},{10... | collective-permute-start | bytes 294920 | tf_op jit(solution)/shard_map/ppermute | solution.py:35
  175.6 13.2 %collective-permute-start.20 = (bf16[32,1536]{1,0:T(8,128)(2,1)S(1)}, bf16[32,1536]{1,0:T(8,128)(2,1)S(1)}, u32[]{:S(2)}, u32[]{:S(2)}) collective-permute-start(bf16[32,1536]{1,0:T(8,128)(2,1)S(1)} %get-tuple-element.70), channel_id=1, source_target_pairs={{0,16},{8,24},{16,0},{24,8},{1,17},{9,25},{17,1},{25,9},{2,18},{10... | collective-permute-start | bytes 294920 | tf_op jit(solution)/shard_map/ppermute | solution.py:35
  178.3 10.7 %collective-permute-start.19 = (bf16[32,1536]{1,0:T(8,128)(2,1)S(1)}, bf16[32,1536]{1,0:T(8,128)(2,1)S(1)}, u32[]{:S(2)}, u32[]{:S(2)}) collective-permute-start(bf16[32,1536]{1,0:T(8,128)(2,1)S(1)} %get-tuple-element.71), channel_id=1, source_target_pairs={{0,24},{8,0},{16,8},{24,16},{1,25},{9,1},{17,9},{25,17},{2,26},{10... | collective-permute-start | bytes 294920 | tf_op jit(solution)/shard_map/ppermute | solution.py:35

commit v5 on v1

v5 whole, which is shorter than its diff:
```python
import math

import jax
import jax.numpy as jnp
from jax import lax
from jax.sharding import PartitionSpec as P

root_coef = math.sqrt(2.0 / math.pi)
cubic_coef = 0.044715
bf16 = jnp.bfloat16
f32 = jnp.float32


def gelu_pair(pre_act, upstream):
    tanh_part = jnp.tanh(root_coef * (pre_act + cubic_coef * pre_act * pre_act * pre_act))
    activation = 0.5 * pre_act * (1.0 + tanh_part)
    slope_value = 0.5 * (1.0 + tanh_part) + 0.5 * pre_act * (
        1.0 - tanh_part * tanh_part
    ) * root_coef * (1.0 + 3.0 * cubic_coef * pre_act * pre_act)
    return (activation.astype(bf16), (upstream * slope_value).astype(bf16))


def contract_last(left, right):
    return lax.dot_general(left, right, (((1,), (1,)), ((), ())), preferred_element_type=f32)


def contract_first(left, right):
    return lax.dot_general(left, right, (((0,), (0,)), ((), ())), preferred_element_type=f32)


def solution(mesh):
    n_x, n_y, n_z = (mesh.shape[a] for a in ("gx", "gy", "gz"))

    def shift_y(a, k):
        return lax.ppermute(a, "gy", [(i, (i + k) % n_y) for i in range(n_y)])

    def shift_chip(a, k):
        return lax.ppermute(a, "gz", [(i, (i + 2 * k) % n_z) for i in range(n_z)])

    def swap_core(a):
        return lax.ppermute(a, "gz", [(i, i ^ 1) for i in range(n_z)])

    n_chip = n_z // 2

    def groups(a):
        return [a] + [shift_y(a, k) for k in range(1, n_y)]

    def sum_blocks(parts, n):
        rows = parts[0].shape[0] // n
        sums = []
        for k in range(n):
            cut = [part[k * rows : (k + 1) * rows].astype(f32) for part in parts]
            sums.append(sum(cut[1:], cut[0]))
        return sums[:1] + [a.astype(bf16) for a in sums[1:]]

    def exchange(parts, shift):
        return parts[:1] + [shift(part, -k) for k, part in enumerate(parts) if k]

    def copies(share):
        return jnp.broadcast_to(share[None], (n_x, *share.shape))

    def trade_width(parts):
        return lax.all_to_all(parts, "gx", 0, 0, tiled=True)

    def after(a, *others):
        return lax.optimization_barrier((a, *others))[0]

    def join(parts):
        return jnp.concatenate(parts, axis=1)

    def barrier(*values):
        return lax.optimization_barrier(values)

    def shards(tokens, weight_in, bias_hidden, weight_out, grad_output):
        norm_scale = 1.0 / math.sqrt(tokens.shape[0] * n_y * n_z)
        rows = tokens.shape[0] // 2
        chunks = [
            jnp.stack([a[c * rows : (c + 1) * rows] for a in (tokens, grad_output)]) for c in range(2)
        ]

        def partial_sums(near):
            both = [jnp.concatenate([a, swap_core(a)], axis=0) for a in near]
            pre_part = jnp.dot(both[0], weight_in, preferred_element_type=f32).astype(bf16)
            up_part = contract_last(both[1], weight_out).astype(bf16)
            parts = [a.reshape(n_x, 1, -1, a.shape[1]) for a in (pre_part, up_part)]
            return both, jnp.concatenate(parts, axis=1)

        def hidden(parts):
            sums = jnp.sum(parts.astype(f32), axis=0)
            return gelu_pair(sums[0] + bias_hidden, sums[1])

        far0 = join(groups(chunks[0]))
        groups1 = groups(after(chunks[1], far0))
        chips0, groups1 = barrier([far0] + [shift_chip(far0, k) for k in range(1, n_chip)], groups1)
        far1 = join(groups1)
        both0, part0 = partial_sums(join(chips0))
        last = n_chip // 2
        chips1 = [far1] + [
            shift_chip(after(far1, part0) if k == last else far1, k) for k in range(1, n_chip)
        ]
        both1, part1 = partial_sums(join(chips1))
        sums0 = trade_width(part0)
        sums1 = trade_width(part1)
        act0, grad0 = hidden(sums0)
        copies0, sums1 = barrier(copies(grad0), sums1)
        act1, grad1 = hidden(sums1)
        act_copies = copies(jnp.stack([act0, act1]))

        def two_halves(grad_hidden):
            half = grad_hidden.shape[0] // 2
            other = contract_last(grad_hidden[half:], weight_in).astype(bf16)
            return other, contract_last(grad_hidden[:half], weight_in)

        hidden0 = trade_width(copies0).reshape(-1, act0.shape[1])
        hidden1 = trade_width(after(copies(grad1), hidden0)).reshape(-1, act0.shape[1])
        other0, own0 = two_halves(hidden0)
        own0, other0 = barrier(own0, swap_core(other0))
        parts0 = exchange(sum_blocks([own0, other0], n_chip), shift_chip)
        other1, own1 = two_halves(hidden1)
        parts0, other1, act_copies = barrier(parts0, other1, act_copies)
        activation = trade_width(act_copies)
        own1, other1 = barrier(own1, swap_core(other1))
        parts1, beside = barrier(
            sum_blocks([own1, other1], n_chip), jnp.concatenate([hidden0, hidden1], axis=0)
        )
        parts1 = exchange(parts1, shift_chip)
        parts0 = exchange(sum_blocks(parts0, n_y), shift_y)
        tokens_all = jnp.concatenate([both0[0], both1[0]], axis=0)
        grad_weight_in = (contract_first(tokens_all, beside) * norm_scale).astype(bf16)
        parts0, parts1, grad_weight_in = barrier(parts0, parts1, grad_weight_in)
        parts1 = exchange(sum_blocks(parts1, n_y), shift_y)
        (tokens0,) = sum_blocks(parts0, 1)
        activation = activation.transpose(1, 0, 2, 3).reshape(-1, act0.shape[1])
        grad_all = jnp.concatenate([both0[1], both1[1]], axis=0)
        grad_weight_out = (contract_first(activation, grad_all) * norm_scale).astype(bf16)
        parts1, grad_weight_out = barrier(parts1, grad_weight_out)
        (tokens1,) = sum_blocks(parts1, 1)
        grad_tokens = jnp.concatenate([tokens0, tokens1], axis=0).astype(bf16)
        return (grad_tokens, grad_weight_in, grad_weight_out)

    return jax.shard_map(
        shards,
        mesh=mesh,
        in_specs=(
            P(("gy", "gz"), "gx"),
            P("gx", ("gy", "gz")),
            P(("gy", "gz")),
            P(("gy", "gz"), "gx"),
            P(("gy", "gz"), "gx"),
        ),
        out_specs=(P(("gy", "gz"), "gx"), P("gx", ("gy", "gz")), P(("gy", "gz"), "gx")),
        check_vma=False,
    )
```

time: 204 us -> 200 us (0.980)
  blocking collectives: 24.2 us -> 0 us
  starting transfers between devices: 55.6 us -> 74.8 us
  other arithmetic: 8.46 us -> 13.5 us
  matrix products: 22.3 us -> 17.6 us
  local copies, waits for them, and re-layouts: 13 us -> 15.4 us
    ppermute x9 -> x12, waiting for transfers between devices: 43.4 us -> 17.4 us  [shift_chip(): return lax.ppermute(a, 'gz', [(i, (i + 2 * k) % n_z) for i in range(n_z)])]
    all_to_all x1 -> x0, blocking collectives: 24.2 us -> none  [gather_width(): parts = lax.all_to_all(copies, 'gx', 0, 0, tiled=True)]
    ppermute x9 -> x12, waiting for transfers between devices: 5.2 us -> 25.1 us  [shift_y(): return lax.ppermute(a, 'gy', [(i, (i + k) % n_y) for i in range(n_y)])]
    all_to_all x3 -> x5, starting transfers between devices: 16 us -> 26.6 us  [trade_width(): return lax.all_to_all(parts, 'gx', 0, 0, tiled=True)]
    ppermute x9 -> x12, starting transfers between devices: 24.4 us -> 33 us  [shift_y(): return lax.ppermute(a, 'gy', [(i, (i + k) % n_y) for i in range(n_y)])]
    all_to_all x3 -> x5, waiting for transfers between devices: 26.7 us -> 32.1 us  [trade_width(): return lax.all_to_all(parts, 'gx', 0, 0, tiled=True)]
    concatenate x0 -> x5, other arithmetic: none -> 4.54 us  [the longest x2 2.58 us: partial_sums(): return (both, jnp.concatenate(parts, axis=1))]
    unnamed x32 -> x52, local copies, waits for them, and re-layouts: 7.14 us -> 4.34 us
  transfers between devices with their start and end apart: 24 -> 35, of which waited for: 12 -> 17; matrix products, arithmetic and copies ran while one was open for 15% -> 20% of each run, Pallas kernels for 0% -> 0%
where the time goes in v5:
time: 200 us
  waiting for transfers between devices  77.2 us (39%)
  starting transfers between devices  74.8 us (37%)
  matrix products  17.6 us (9%)
  local copies, waits for them, and re-layouts  15.4 us (8%)
  other arithmetic  13.5 us (7%)
    ppermute x12, starting transfers between devices, shift_y(): return lax.ppermute(a, 'gy', [(i, (i + k) % n_y) for i in range(n_y)])  33 us
    all_to_all x5, waiting for transfers between devices, trade_width(): return lax.all_to_all(parts, 'gx', 0, 0, tiled=True)  32.1 us
    all_to_all x5, starting transfers between devices, trade_width(): return lax.all_to_all(parts, 'gx', 0, 0, tiled=True)  26.6 us
    ppermute x12, waiting for transfers between devices, shift_y(): return lax.ppermute(a, 'gy', [(i, (i + k) % n_y) for i in range(n_y)])  25.1 us
    ppermute x12, waiting for transfers between devices, shift_chip(): return lax.ppermute(a, 'gz', [(i, (i + 2 * k) % n_z) for i in range(n_z)])  17.4 us
    ppermute x12, starting transfers between devices, shift_chip(): return lax.ppermute(a, 'gz', [(i, (i + 2 * k) % n_z) for i in range(n_z)])  13.9 us
    dot_general x2, matrix products, contract_first(): lax.dot_general(left, right, (((0,), (0,)), ((), ())), preferred_element_...  7.9 us
    dot_general x6, matrix products, contract_last(): lax.dot_general(left, right, (((1,), (1,)), ((), ())), preferred_element_...  6.94 us
  transfers between devices with their start and end apart: 35, of which 17 were waited for; matrix products, arithmetic and copies ran while one was open for 20% of the time, Pallas kernels for 0%

profile of v5, /device:TPU:32, one launch (start us, length us, event | category | flops | bytes accessed | tf_op | source)
XLA Modules:
  0.0 199.7 jit_solution(16387966797651163730)
XLA Ops:
  0.6 1.0 slice_bitcast_fusion.4
  1.7 5.5 %collective-permute-start.2 = (bf16[2,16,1536]{2,1,0:T(8,128)(2,1)S(1)}, bf16[2,16,1536]{2,1,0:T(8,128)(2,1)S(1)}, u32[]{:S(2)}, u32[]{:S(2)}) collective-permute-start(bf16[2,16,1536]{2,1,0:T(8,128)(2,1)S(1)} %pad_maximum_fusion.5), channel_id=1, source_target_pairs={{0,24},{8,0},{16,8},{24,16},{1,25},{9,1},{17,9},{25,17},{2,26},{10... | collective-permute-start | bytes 294920 | tf_op jit(solution)/shard_map/ppermute | solution.py:35
  7.2 1.4 collective-permute-start.1
  8.6 2.4 %collective-permute-start = (bf16[2,16,1536]{2,1,0:T(8,128)(2,1)S(1)}, bf16[2,16,1536]{2,1,0:T(8,128)(2,1)S(1)}, u32[]{:S(2)}, u32[]{:S(2)}) collective-permute-start(bf16[2,16,1536]{2,1,0:T(8,128)(2,1)S(1)} %pad_maximum_fusion.5), channel_id=1, source_target_pairs={{0,8},{8,16},{16,24},{24,0},{1,9},{9,17},{17,25},{25,1},{2,10},{10... | collective-permute-start | bytes 294920 | tf_op jit(solution)/shard_map/ppermute | solution.py:35
  11.0 7.1 %collective-permute-done.1 = bf16[2,16,1536]{2,1,0:T(8,128)(2,1)S(1)} collective-permute-done((bf16[2,16,1536]{2,1,0:T(8,128)(2,1)S(1)}, bf16[2,16,1536]{2,1,0:T(8,128)(2,1)S(1)}, u32[]{:S(2)}, u32[]{:S(2)}) %collective-permute-start.1) | collective-permute-done | bytes 98336 | tf_op jit(solution)/shard_map/ppermute | solution.py:35
  18.7 1.6 collective-permute-start.3
  20.3 2.7 %collective-permute-start.4 = (bf16[2,64,1536]{2,1,0:T(8,128)(2,1)S(1)}, bf16[2,64,1536]{2,1,0:T(8,128)(2,1)S(1)}, u32[]{:S(2)}, u32[]{:S(2)}) collective-permute-start(bf16[2,64,1536]{2,1,0:T(8,128)(2,1)S(1)} %pad_maximum_fusion.3), channel_id=1, source_target_pairs={{0,4},{1,5},{2,6},{3,7},{4,0},{5,1},{6,2},{7,3},{8,12},{9,13},{10,... | collective-permute-start | bytes 1179656 | tf_op jit(solution)/shard_map/ppermute | solution.py:38
  23.0 1.4 collective-permute-start.5
  24.5 1.8 collective-permute-start.6
  26.3 4.2 %collective-permute-start.7 = (bf16[2,16,1536]{2,1,0:T(8,128)(2,1)S(1)}, bf16[2,16,1536]{2,1,0:T(8,128)(2,1)S(1)}, u32[]{:S(2)}, u32[]{:S(2)}) collective-permute-start(bf16[2,16,1536]{2,1,0:T(8,128)(2,1)S(1)} %pad_maximum_fusion.6), channel_id=1, source_target_pairs={{0,16},{8,24},{16,0},{24,8},{1,17},{9,25},{17,1},{25,9},{2,18},{10... | collective-permute-start | bytes 294920 | tf_op jit(solution)/shard_map/ppermute | solution.py:35
  30.5 3.2 %collective-permute-done.6 = bf16[2,16,1536]{2,1,0:T(8,128)(2,1)S(1)} collective-permute-done((bf16[2,16,1536]{2,1,0:T(8,128)(2,1)S(1)}, bf16[2,16,1536]{2,1,0:T(8,128)(2,1)S(1)}, u32[]{:S(2)}, u32[]{:S(2)}) %collective-permute-start.6) | collective-permute-done | bytes 98336 | tf_op jit(solution)/shard_map/ppermute | solution.py:35
  33.7 2.7 %collective-permute-start.8 = (bf16[2,16,1536]{2,1,0:T(8,128)(2,1)S(1)}, bf16[2,16,1536]{2,1,0:T(8,128)(2,1)S(1)}, u32[]{:S(2)}, u32[]{:S(2)}) collective-permute-start(bf16[2,16,1536]{2,1,0:T(8,128)(2,1)S(1)} %pad_maximum_fusion.6), channel_id=1, source_target_pairs={{0,24},{8,0},{16,8},{24,16},{1,25},{9,1},{17,9},{25,17},{2,26},{10... | collective-permute-start | bytes 294920 | tf_op jit(solution)/shard_map/ppermute | solution.py:35
  36.5 4.4 %collective-permute-done.8 = bf16[2,16,1536]{2,1,0:T(8,128)(2,1)S(1)} collective-permute-done((bf16[2,16,1536]{2,1,0:T(8,128)(2,1)S(1)}, bf16[2,16,1536]{2,1,0:T(8,128)(2,1)S(1)}, u32[]{:S(2)}, u32[]{:S(2)}) %collective-permute-start.8) | collective-permute-done | bytes 98336 | tf_op jit(solution)/shard_map/ppermute | solution.py:35
  45.1 1.4 fusion.36
  46.6 1.4 fusion.39
  48.0 1.3 pad_maximum_fusion
  49.3 1.8 collective-permute-start.12
  51.1 1.3 collective-permute-start.13
  52.4 5.9 %all-to-all-start = ((bf16[8,2,64,768]{3,2,1,0:T(8,128)(2,1)}), bf16[8,2,64,768]{3,2,1,0:T(8,128)(2,1)}, u32[]{:S(2)}, u32[]{:S(2)}) async-start(bf16[8,2,64,768]{3,2,1,0:T(8,128)(2,1)} %pad_maximum_fusion), calls=%async_computation | async-start | bytes 3145728 | tf_op jit(solution)/shard_map/all_to_all | solution.py:63
  58.3 7.2 %collective-permute-done.11 = bf16[2,64,1536]{2,1,0:T(8,128)(2,1)S(1)} collective-permute-done((bf16[2,64,1536]{2,1,0:T(8,128)(2,1)}, bf16[2,64,1536]{2,1,0:T(8,128)(2,1)S(1)}, u32[]{:S(2)}, u32[]{:S(2)}) %collective-permute-start.11) | collective-permute-done | bytes 393248 | tf_op jit(solution)/shard_map/ppermute | solution.py:38
  65.5 0.8 constant_dynamic-update-slice_fusion.10
  66.3 0.8 constant_dynamic-update-slice_fusion.9
  67.1 3.2 %collective-permute-done.13 = bf16[2,64,1536]{2,1,0:T(8,128)(2,1)S(1)} collective-permute-done((bf16[2,64,1536]{2,1,0:T(8,128)(2,1)}, bf16[2,64,1536]{2,1,0:T(8,128)(2,1)S(1)}, u32[]{:S(2)}, u32[]{:S(2)}) %collective-permute-start.13) | collective-permute-done | bytes 393248 | tf_op jit(solution)/shard_map/ppermute | solution.py:38
  71.1 1.6 slice_bitcast_fusion.1
  73.3 1.8 collective-permute-done.15
  75.1 1.4 fusion.30
  76.6 1.4 fusion.33
  78.0 1.3 pad_maximum_fusion.1
  79.3 6.1 %all-to-all-start.1 = ((bf16[8,2,64,768]{3,2,1,0:T(8,128)(2,1)}), bf16[8,2,64,768]{3,2,1,0:T(8,128)(2,1)}, u32[]{:S(2)}, u32[]{:S(2)}) async-start(bf16[8,2,64,768]{3,2,1,0:T(8,128)(2,1)} %pad_maximum_fusion.1), calls=%async_computation.1 | async-start | bytes 3145728 | tf_op jit(solution)/shard_map/all_to_all | solution.py:63
  85.4 1.7 convert_reduce_fusion.1
  87.2 18.5 %all-to-all-done.1 = bf16[8,2,64,768]{3,2,1,0:T(8,128)(2,1)} async-done(((bf16[8,2,64,768]{3,2,1,0:T(8,128)(2,1)}), bf16[8,2,64,768]{3,2,1,0:T(8,128)(2,1)}, u32[]{:S(2)}, u32[]{:S(2)}) %all-to-all-start.1) | async-done | bytes 1572896 | tf_op jit(solution)/shard_map/all_to_all | solution.py:63
  105.7 0.9 broadcast_in_dim.11
  106.6 4.2 %all-to-all-start.2 = ((bf16[8,64,768]{2,1,0:T(8,128)(2,1)}), bf16[8,64,768]{2,1,0:T(8,128)(2,1)S(1)}, u32[]{:S(2)}, u32[]{:S(2)}) async-start(bf16[8,64,768]{2,1,0:T(8,128)(2,1)} %broadcast_in_dim.11), calls=%async_computation.2 | async-start | bytes 1572864 | tf_op jit(solution)/shard_map/all_to_all | solution.py:63
  110.8 1.7 convert_reduce_fusion
  112.6 9.8 %all-to-all-done.2 = bf16[8,64,768]{2,1,0:T(8,128)(2,1)S(1)} async-done(((bf16[8,64,768]{2,1,0:T(8,128)(2,1)}), bf16[8,64,768]{2,1,0:T(8,128)(2,1)S(1)}, u32[]{:S(2)}, u32[]{:S(2)}) %all-to-all-start.2) | async-done | bytes 786464 | tf_op jit(solution)/shard_map/all_to_all | solution.py:63
  122.5 0.9 broadcast_in_dim.13
  123.4 4.6 %all-to-all-start.3 = ((bf16[8,64,768]{2,1,0:T(8,128)(2,1)}), bf16[8,64,768]{2,1,0:T(8,128)(2,1)}, u32[]{:S(2)}, u32[]{:S(2)}) async-start(bf16[8,64,768]{2,1,0:T(8,128)(2,1)} %broadcast_in_dim.13), calls=%async_computation.3 | async-start | bytes 1572864 | tf_op jit(solution)/shard_map/all_to_all | solution.py:63
  128.1 0.8 convolution_convert_fusion.1
  129.7 0.8 fusion.66
  130.5 0.8 collective-permute-done.16
  131.3 0.9 add_convert_fusion.3
  132.2 2.4 %collective-permute-start.17 = (bf16[64,1536]{1,0:T(8,128)(2,1)}, bf16[64,1536]{1,0:T(8,128)(2,1)}, u32[]{:S(2)}, u32[]{:S(2)}) collective-permute-start(bf16[64,1536]{1,0:T(8,128)(2,1)} %get-tuple-element.93), channel_id=1, source_target_pairs={{0,6},{1,7},{2,0},{3,1},{4,2},{5,3},{6,4},{7,5},{8,14},{9,15},{10,... | collective-permute-start | bytes 589832 | tf_op jit(solution)/shard_map/ppermute | solution.py:38
  134.6 0.9 collective-permute-start.19
  135.4 3.8 %all-to-all-done.3 = bf16[8,64,768]{2,1,0:T(8,128)(2,1)} async-done(((bf16[8,64,768]{2,1,0:T(8,128)(2,1)}), bf16[8,64,768]{2,1,0:T(8,128)(2,1)}, u32[]{:S(2)}, u32[]{:S(2)}) %all-to-all-start.3) | async-done | bytes 786464 | tf_op jit(solution)/shard_map/all_to_all | solution.py:63
  139.3 1.9 fusion.64
  141.2 1.7 convolution_convert_fusion
  144.2 2.8 %collective-permute-done.19 = bf16[64,1536]{1,0:T(8,128)(2,1)} collective-permute-done((bf16[64,1536]{1,0:T(8,128)(2,1)}, bf16[64,1536]{1,0:T(8,128)(2,1)}, u32[]{:S(2)}, u32[]{:S(2)}) %collective-permute-start.19) | collective-permute-done | bytes 196640 | tf_op jit(solution)/shard_map/ppermute | solution.py:38
  147.0 1.3 broadcast_in_dim.28
  148.3 5.7 %all-to-all-start.4 = ((bf16[8,2,64,768]{3,2,1,0:T(8,128)(2,1)}), bf16[8,2,64,768]{3,2,1,0:T(8,128)(2,1)}, u32[]{:S(2)}, u32[]{:S(2)}) async-start(bf16[8,2,64,768]{3,2,1,0:T(8,128)(2,1)} %broadcast_in_dim.28), calls=%async_computation.4 | async-start | bytes 3145728 | tf_op jit(solution)/shard_map/all_to_all | solution.py:63
  154.0 1.1 add_convert_fusion.11
  155.2 3.4 %collective-permute-start.20 = (bf16[16,1536]{1,0:T(8,128)(2,1)S(1)}, bf16[16,1536]{1,0:T(8,128)(2,1)S(1)}, u32[]{:S(2)}, u32[]{:S(2)}) collective-permute-start(bf16[16,1536]{1,0:T(8,128)(2,1)S(1)} %get-tuple-element.105), channel_id=1, source_target_pairs={{0,24},{8,0},{16,8},{24,16},{1,25},{9,1},{17,9},{25,17},{2,26},{10... | collective-permute-start | bytes 147464 | tf_op jit(solution)/shard_map/ppermute | solution.py:35
  158.6 4.2 %collective-permute-start.21 = (bf16[16,1536]{1,0:T(8,128)(2,1)S(1)}, bf16[16,1536]{1,0:T(8,128)(2,1)S(1)}, u32[]{:S(2)}, u32[]{:S(2)}) collective-permute-start(bf16[16,1536]{1,0:T(8,128)(2,1)S(1)} %get-tuple-element.104), channel_id=1, source_target_pairs={{0,16},{8,24},{16,0},{24,8},{1,17},{9,25},{17,1},{25,9},{2,18},{10... | collective-permute-start | bytes 147464 | tf_op jit(solution)/shard_map/ppermute | solution.py:35
  162.8 1.0 collective-permute-start.22
  163.8 1.3 pad_maximum_fusion.2
  165.1 0.8 fusion.67
  165.9 1.6 add_convert_fusion
  167.5 1.0 collective-permute-start.24
  168.8 9.8 %collective-permute-done.20 = bf16[16,1536]{1,0:T(8,128)(2,1)S(1)} collective-permute-done((bf16[16,1536]{1,0:T(8,128)(2,1)S(1)}, bf16[16,1536]{1,0:T(8,128)(2,1)S(1)}, u32[]{:S(2)}, u32[]{:S(2)}) %collective-permute-start.20) | collective-permute-done | bytes 49184 | tf_op jit(solution)/shard_map/ppermute | solution.py:35
  178.6 4.0 %multiply_convert_fusion.1 = bf16[1536,768]{1,0:T(8,128)(2,1)} fusion(bf16[1024,768]{1,0:T(8,128)(2,1)S(1)} %pad_maximum_fusion.2, bf16[256,1536]{1,0:T(8,128)(2,1)S(1)} %copy-done.21, bf16[256,1536]{1,0:T(8,128)(2,1)S(1)} %copy-done.10, bf16[256,1536]{1,0:T(8,128)(2,1)S(1)} %copy-done.17, bf16[256,1536]{1,0:T(8,128)(2,1)S(1)} %copy-done.6), kind=kOutput, calls=%fused_computation.1 | convolution fusion | flops 2430861312 | bytes 7077888 | tf_op jit(solution)/shard_map/dot_general | solution.py:28
  182.6 2.9 %collective-permute-done.26 = bf16[64,1536]{1,0:T(8,128)(2,1)S(1)} collective-permute-done((bf16[64,1536]{1,0:T(8,128)(2,1)S(1)}, bf16[64,1536]{1,0:T(8,128)(2,1)S(1)}, u32[]{:S(2)}, u32[]{:S(2)}) %collective-permute-start.26) | collective-permute-done | bytes 196640 | tf_op jit(solution)/shard_map/ppermute | solution.py:38
  185.8 6.1 %collective-permute-start.28 = (bf16[16,1536]{1,0:T(8,128)(2,1)S(1)}, bf16[16,1536]{1,0:T(8,128)(2,1)S(1)}, u32[]{:S(2)}, u32[]{:S(2)}) collective-permute-start(bf16[16,1536]{1,0:T(8,128)(2,1)S(1)} %get-tuple-element.100), channel_id=1, source_target_pairs={{0,16},{8,24},{16,0},{24,8},{1,17},{9,25},{17,1},{25,9},{2,18},{10... | collective-permute-start | bytes 147464 | tf_op jit(solution)/shard_map/ppermute | solution.py:35
  192.0 1.7 copy.12
  194.3 3.9 %multiply_convert_fusion = bf16[768,1536]{1,0:T(8,128)(2,1)} fusion(bf16[1024,768]{1,0:T(8,128)(2,1)S(1)} %bitcast.56, bf16[256,1536]{1,0:T(8,128)(2,1)S(1)} %copy-done.19, bf16[256,1536]{1,0:T(8,128)(2,1)S(1)} %copy-done.8, bf16[256,1536]{1,0:T(8,128)(2,1)S(1)} %copy-done.15, bf16[256,1536]{1,0:T(8,128)(2,1)S(1)} %copy-done.4), kind=kOutput, calls=%fused_computation | convolution fusion | flops 2430861312 | bytes 7077888 | tf_op jit(solution)/shard_map/dot_general | solution.py:28
  198.2 0.8 add_convert_fusion.6
  (98 shorter events, 10.7 us)
Async XLA Ops:
  0.6 46.0 %copy-start = (bf16[1536,768]{1,0:T(8,128)(2,1)S(1)}, bf16[1536,768]{1,0:T(8,128)(2,1)}, u32[]{:S(2)}) copy-start(bf16[1536,768]{1,0:T(8,128)(2,1)} %param.6) | copy-start | bytes 7077892
  1.7 9.3 %collective-permute-start.2 = (bf16[2,16,1536]{2,1,0:T(8,128)(2,1)S(1)}, bf16[2,16,1536]{2,1,0:T(8,128)(2,1)S(1)}, u32[]{:S(2)}, u32[]{:S(2)}) collective-permute-start(bf16[2,16,1536]{2,1,0:T(8,128)(2,1)S(1)} %pad_maximum_fusion.5), channel_id=1, source_target_pairs={{0,24},{8,0},{16,8},{24,16},{1,25},{9,1},{17,9},{25,17},{2,26},{10... | collective-permute-start | bytes 294920 | tf_op jit(solution)/shard_map/ppermute | solution.py:35
  7.2 10.9 %collective-permute-start.1 = (bf16[2,16,1536]{2,1,0:T(8,128)(2,1)S(1)}, bf16[2,16,1536]{2,1,0:T(8,128)(2,1)S(1)}, u32[]{:S(2)}, u32[]{:S(2)}) collective-permute-start(bf16[2,16,1536]{2,1,0:T(8,128)(2,1)S(1)} %pad_maximum_fusion.5), channel_id=1, source_target_pairs={{0,16},{8,24},{16,0},{24,8},{1,17},{9,25},{17,1},{25,9},{2,18},{10... | collective-permute-start | bytes 294920 | tf_op jit(solution)/shard_map/ppermute | solution.py:35
  8.6 10.0 %collective-permute-start = (bf16[2,16,1536]{2,1,0:T(8,128)(2,1)S(1)}, bf16[2,16,1536]{2,1,0:T(8,128)(2,1)S(1)}, u32[]{:S(2)}, u32[]{:S(2)}) collective-permute-start(bf16[2,16,1536]{2,1,0:T(8,128)(2,1)S(1)} %pad_maximum_fusion.5), channel_id=1, source_target_pairs={{0,8},{8,16},{16,24},{24,0},{1,9},{9,17},{17,25},{25,1},{2,10},{10... | collective-permute-start | bytes 294920 | tf_op jit(solution)/shard_map/ppermute | solution.py:35
  18.7 22.2 %collective-permute-start.3 = (bf16[2,64,1536]{2,1,0:T(8,128)(2,1)S(1)}, bf16[2,64,1536]{2,1,0:T(8,128)(2,1)S(1)}, u32[]{:S(2)}, u32[]{:S(2)}) collective-permute-start(bf16[2,64,1536]{2,1,0:T(8,128)(2,1)S(1)} %pad_maximum_fusion.3), channel_id=1, source_target_pairs={{0,2},{1,3},{2,4},{3,5},{4,6},{5,7},{6,0},{7,1},{8,10},{9,11},{10,... | collective-permute-start | bytes 1179656 | tf_op jit(solution)/shard_map/ppermute | solution.py:38
  20.3 20.6 %collective-permute-start.4 = (bf16[2,64,1536]{2,1,0:T(8,128)(2,1)S(1)}, bf16[2,64,1536]{2,1,0:T(8,128)(2,1)S(1)}, u32[]{:S(2)}, u32[]{:S(2)}) collective-permute-start(bf16[2,64,1536]{2,1,0:T(8,128)(2,1)S(1)} %pad_maximum_fusion.3), channel_id=1, source_target_pairs={{0,4},{1,5},{2,6},{3,7},{4,0},{5,1},{6,2},{7,3},{8,12},{9,13},{10,... | collective-permute-start | bytes 1179656 | tf_op jit(solution)/shard_map/ppermute | solution.py:38
  23.0 17.9 %collective-permute-start.5 = (bf16[2,64,1536]{2,1,0:T(8,128)(2,1)S(1)}, bf16[2,64,1536]{2,1,0:T(8,128)(2,1)S(1)}, u32[]{:S(2)}, u32[]{:S(2)}) collective-permute-start(bf16[2,64,1536]{2,1,0:T(8,128)(2,1)S(1)} %pad_maximum_fusion.3), channel_id=1, source_target_pairs={{0,6},{1,7},{2,0},{3,1},{4,2},{5,3},{6,4},{7,5},{8,14},{9,15},{10,... | collective-permute-start | bytes 1179656 | tf_op jit(solution)/shard_map/ppermute | solution.py:38
  24.5 9.2 %collective-permute-start.6 = (bf16[2,16,1536]{2,1,0:T(8,128)(2,1)S(1)}, bf16[2,16,1536]{2,1,0:T(8,128)(2,1)S(1)}, u32[]{:S(2)}, u32[]{:S(2)}) collective-permute-start(bf16[2,16,1536]{2,1,0:T(8,128)(2,1)S(1)} %pad_maximum_fusion.6), channel_id=1, source_target_pairs={{0,8},{8,16},{16,24},{24,0},{1,9},{9,17},{17,25},{25,1},{2,10},{10... | collective-permute-start | bytes 294920 | tf_op jit(solution)/shard_map/ppermute | solution.py:35
  26.3 10.3 %collective-permute-start.7 = (bf16[2,16,1536]{2,1,0:T(8,128)(2,1)S(1)}, bf16[2,16,1536]{2,1,0:T(8,128)(2,1)S(1)}, u32[]{:S(2)}, u32[]{:S(2)}) collective-permute-start(bf16[2,16,1536]{2,1,0:T(8,128)(2,1)S(1)} %pad_maximum_fusion.6), channel_id=1, source_target_pairs={{0,16},{8,24},{16,0},{24,8},{1,17},{9,25},{17,1},{25,9},{2,18},{10... | collective-permute-start | bytes 294920 | tf_op jit(solution)/shard_map/ppermute | solution.py:35
  33.7 7.2 %collective-permute-start.8 = (bf16[2,16,1536]{2,1,0:T(8,128)(2,1)S(1)}, bf16[2,16,1536]{2,1,0:T(8,128)(2,1)S(1)}, u32[]{:S(2)}, u32[]{:S(2)}) collective-permute-start(bf16[2,16,1536]{2,1,0:T(8,128)(2,1)S(1)} %pad_maximum_fusion.6), channel_id=1, source_target_pairs={{0,24},{8,0},{16,8},{24,16},{1,25},{9,1},{17,9},{25,17},{2,26},{10... | collective-permute-start | bytes 294920 | tf_op jit(solution)/shard_map/ppermute | solution.py:35
  41.1 4.1 %copy-start.12 = (bf16[768,1536]{1,0:T(8,128)(2,1)S(1)}, bf16[768,1536]{1,0:T(8,128)(2,1)}, u32[]{:S(2)}) copy-start(bf16[768,1536]{1,0:T(8,128)(2,1)} %param.8) | copy-start | bytes 7077892
  41.2 5.4 %copy-start.3 = (bf16[256,1536]{1,0:T(8,128)(2,1)}, bf16[256,1536]{1,0:T(8,128)(2,1)S(1)}, u32[]{:S(2)}) copy-start(bf16[256,1536]{1,0:T(8,128)(2,1)S(1)} %get-tuple-element.98) | copy-start | bytes 2359300
  41.2 5.4 %copy-start.5 = (bf16[256,1536]{1,0:T(8,128)(2,1)}, bf16[256,1536]{1,0:T(8,128)(2,1)S(1)}, u32[]{:S(2)}) copy-start(bf16[256,1536]{1,0:T(8,128)(2,1)S(1)} %get-tuple-element.97) | copy-start | bytes 2359300
  41.2 3.9 %collective-permute-start.10 = (bf16[256,1536]{1,0:T(8,128)(2,1)S(1)}, bf16[256,1536]{1,0:T(8,128)(2,1)S(1)}, u32[]{:S(2)}, u32[]{:S(2)}) collective-permute-start(bf16[256,1536]{1,0:T(8,128)(2,1)S(1)} %get-tuple-element.98), channel_id=1, source_target_pairs={{0,1},{1,0},{2,3},{3,2},{4,5},{5,4},{6,7},{7,6},{8,9},{9,8},{10,11... | collective-permute-start | bytes 2359304 | tf_op jit(solution)/shard_map/ppermute | solution.py:41
  41.3 5.3 %collective-permute-start.9 = (bf16[256,1536]{1,0:T(8,128)(2,1)S(1)}, bf16[256,1536]{1,0:T(8,128)(2,1)S(1)}, u32[]{:S(2)}, u32[]{:S(2)}) collective-permute-start(bf16[256,1536]{1,0:T(8,128)(2,1)S(1)} %get-tuple-element.97), channel_id=1, source_target_pairs={{0,1},{1,0},{2,3},{3,2},{4,5},{5,4},{6,7},{7,6},{8,9},{9,8},{10,11... | collective-permute-start | bytes 2359304 | tf_op jit(solution)/shard_map/ppermute | solution.py:41
  44.5 21.0 %collective-permute-start.11 = (bf16[2,64,1536]{2,1,0:T(8,128)(2,1)}, bf16[2,64,1536]{2,1,0:T(8,128)(2,1)S(1)}, u32[]{:S(2)}, u32[]{:S(2)}) collective-permute-start(bf16[2,64,1536]{2,1,0:T(8,128)(2,1)} %get-tuple-element.54), channel_id=1, source_target_pairs={{0,2},{1,3},{2,4},{3,5},{4,6},{5,7},{6,0},{7,1},{8,10},{9,11},{10,... | collective-permute-start | bytes 1179656 | tf_op jit(solution)/shard_map/ppermute | solution.py:38
  45.1 1.4 copy-start.14
  46.6 1.4 copy-start.16
  49.3 17.0 %collective-permute-start.12 = (bf16[2,64,1536]{2,1,0:T(8,128)(2,1)}, bf16[2,64,1536]{2,1,0:T(8,128)(2,1)S(1)}, u32[]{:S(2)}, u32[]{:S(2)}) collective-permute-start(bf16[2,64,1536]{2,1,0:T(8,128)(2,1)} %get-tuple-element.54), channel_id=1, source_target_pairs={{0,4},{1,5},{2,6},{3,7},{4,0},{5,1},{6,2},{7,3},{8,12},{9,13},{10,... | collective-permute-start | bytes 1179656 | tf_op jit(solution)/shard_map/ppermute | solution.py:38
  51.1 19.2 %collective-permute-start.13 = (bf16[2,64,1536]{2,1,0:T(8,128)(2,1)}, bf16[2,64,1536]{2,1,0:T(8,128)(2,1)S(1)}, u32[]{:S(2)}, u32[]{:S(2)}) collective-permute-start(bf16[2,64,1536]{2,1,0:T(8,128)(2,1)} %get-tuple-element.54), channel_id=1, source_target_pairs={{0,6},{1,7},{2,0},{3,1},{4,2},{5,3},{6,4},{7,5},{8,14},{9,15},{10,... | collective-permute-start | bytes 1179656 | tf_op jit(solution)/shard_map/ppermute | solution.py:38
  52.4 26.9 %all-to-all-start = ((bf16[8,2,64,768]{3,2,1,0:T(8,128)(2,1)}), bf16[8,2,64,768]{3,2,1,0:T(8,128)(2,1)}, u32[]{:S(2)}, u32[]{:S(2)}) async-start(bf16[8,2,64,768]{3,2,1,0:T(8,128)(2,1)} %pad_maximum_fusion), calls=%async_computation | async-start | bytes 3145728 | tf_op jit(solution)/shard_map/all_to_all | solution.py:63
  71.1 4.0 %copy-start.13 = (bf16[768,1536]{1,0:T(8,128)(2,1)S(1)}, bf16[768,1536]{1,0:T(8,128)(2,1)}, u32[]{:S(2)}) copy-start(bf16[768,1536]{1,0:T(8,128)(2,1)} %param.8) | copy-start | bytes 7077892
  72.7 3.8 %copy-start.7 = (bf16[256,1536]{1,0:T(8,128)(2,1)}, bf16[256,1536]{1,0:T(8,128)(2,1)S(1)}, u32[]{:S(2)}) copy-start(bf16[256,1536]{1,0:T(8,128)(2,1)S(1)} %get-tuple-element.96) | copy-start | bytes 2359300
  72.7 3.8 %copy-start.9 = (bf16[256,1536]{1,0:T(8,128)(2,1)}, bf16[256,1536]{1,0:T(8,128)(2,1)S(1)}, u32[]{:S(2)}) copy-start(bf16[256,1536]{1,0:T(8,128)(2,1)S(1)} %get-tuple-element.95) | copy-start | bytes 2359300
  72.7 2.4 %collective-permute-start.15 = (bf16[256,1536]{1,0:T(8,128)(2,1)S(1)}, bf16[256,1536]{1,0:T(8,128)(2,1)S(1)}, u32[]{:S(2)}, u32[]{:S(2)}) collective-permute-start(bf16[256,1536]{1,0:T(8,128)(2,1)S(1)} %get-tuple-element.96), channel_id=1, source_target_pairs={{0,1},{1,0},{2,3},{3,2},{4,5},{5,4},{6,7},{7,6},{8,9},{9,8},{10,11... | collective-permute-start | bytes 2359304 | tf_op jit(solution)/shard_map/ppermute | solution.py:41
  72.8 3.7 %collective-permute-start.14 = (bf16[256,1536]{1,0:T(8,128)(2,1)S(1)}, bf16[256,1536]{1,0:T(8,128)(2,1)S(1)}, u32[]{:S(2)}, u32[]{:S(2)}) collective-permute-start(bf16[256,1536]{1,0:T(8,128)(2,1)S(1)} %get-tuple-element.95), channel_id=1, source_target_pairs={{0,1},{1,0},{2,3},{3,2},{4,5},{5,4},{6,7},{7,6},{8,9},{9,8},{10,11... | collective-permute-start | bytes 2359304 | tf_op jit(solution)/shard_map/ppermute | solution.py:41
  75.1 1.4 copy-start.18
  76.6 1.4 copy-start.20
  79.3 26.4 %all-to-all-start.1 = ((bf16[8,2,64,768]{3,2,1,0:T(8,128)(2,1)}), bf16[8,2,64,768]{3,2,1,0:T(8,128)(2,1)}, u32[]{:S(2)}, u32[]{:S(2)}) async-start(bf16[8,2,64,768]{3,2,1,0:T(8,128)(2,1)} %pad_maximum_fusion.1), calls=%async_computation.1 | async-start | bytes 3145728 | tf_op jit(solution)/shard_map/all_to_all | solution.py:63
  85.4 1.7 copy-start.11
  106.6 15.8 %all-to-all-start.2 = ((bf16[8,64,768]{2,1,0:T(8,128)(2,1)}), bf16[8,64,768]{2,1,0:T(8,128)(2,1)S(1)}, u32[]{:S(2)}, u32[]{:S(2)}) async-start(bf16[8,64,768]{2,1,0:T(8,128)(2,1)} %broadcast_in_dim.11), calls=%async_computation.2 | async-start | bytes 1572864 | tf_op jit(solution)/shard_map/all_to_all | solution.py:63
  123.4 15.9 %all-to-all-start.3 = ((bf16[8,64,768]{2,1,0:T(8,128)(2,1)}), bf16[8,64,768]{2,1,0:T(8,128)(2,1)}, u32[]{:S(2)}, u32[]{:S(2)}) async-start(bf16[8,64,768]{2,1,0:T(8,128)(2,1)} %broadcast_in_dim.13), calls=%async_computation.3 | async-start | bytes 1572864 | tf_op jit(solution)/shard_map/all_to_all | solution.py:63
  128.9 2.4 %collective-permute-start.16 = (bf16[256,1536]{1,0:T(8,128)(2,1)S(1)}, bf16[256,1536]{1,0:T(8,128)(2,1)S(1)}, u32[]{:S(2)}, u32[]{:S(2)}) collective-permute-start(bf16[256,1536]{1,0:T(8,128)(2,1)S(1)} %convolution_convert_fusion.1), channel_id=1, source_target_pairs={{0,1},{1,0},{2,3},{3,2},{4,5},{5,4},{6,7},{7,6},{8,9},{9,8},{10,11... | collective-permute-start | bytes 2359304 | tf_op jit(solution)/shard_map/ppermute | solution.py:41
  132.2 11.4 %collective-permute-start.17 = (bf16[64,1536]{1,0:T(8,128)(2,1)}, bf16[64,1536]{1,0:T(8,128)(2,1)}, u32[]{:S(2)}, u32[]{:S(2)}) collective-permute-start(bf16[64,1536]{1,0:T(8,128)(2,1)} %get-tuple-element.93), channel_id=1, source_target_pairs={{0,6},{1,7},{2,0},{3,1},{4,2},{5,3},{6,4},{7,5},{8,14},{9,15},{10,... | collective-permute-start | bytes 589832 | tf_op jit(solution)/shard_map/ppermute | solution.py:38
  134.6 9.6 %collective-permute-start.18 = (bf16[64,1536]{1,0:T(8,128)(2,1)}, bf16[64,1536]{1,0:T(8,128)(2,1)}, u32[]{:S(2)}, u32[]{:S(2)}) collective-permute-start(bf16[64,1536]{1,0:T(8,128)(2,1)} %get-tuple-element.92), channel_id=1, source_target_pairs={{0,4},{1,5},{2,6},{3,7},{4,0},{5,1},{6,2},{7,3},{8,12},{9,13},{10,... | collective-permute-start | bytes 589832 | tf_op jit(solution)/shard_map/ppermute | solution.py:38
  134.6 12.4 %collective-permute-start.19 = (bf16[64,1536]{1,0:T(8,128)(2,1)}, bf16[64,1536]{1,0:T(8,128)(2,1)}, u32[]{:S(2)}, u32[]{:S(2)}) collective-permute-start(bf16[64,1536]{1,0:T(8,128)(2,1)} %get-tuple-element.91), channel_id=1, source_target_pairs={{0,2},{1,3},{2,4},{3,5},{4,6},{5,7},{6,0},{7,1},{8,10},{9,11},{10,... | collective-permute-start | bytes 589832 | tf_op jit(solution)/shard_map/ppermute | solution.py:38
  141.2 5.8 %copy-start.2 = (bf16[2,64,768]{2,1,0:T(8,128)(2,1)S(1)}, bf16[2,64,768]{2,1,0:T(8,128)(2,1)}, u32[]{:S(2)}) copy-start(bf16[2,64,768]{2,1,0:T(8,128)(2,1)} %pad_maximum_fusion.4) | copy-start | bytes 589828
  148.3 17.6 %collective-permute-start.23 = (bf16[256,1536]{1,0:T(8,128)(2,1)}, bf16[256,1536]{1,0:T(8,128)(2,1)}, u32[]{:S(2)}, u32[]{:S(2)}) collective-permute-start(bf16[256,1536]{1,0:T(8,128)(2,1)} %convolution_convert_fusion), channel_id=1, source_target_pairs={{0,1},{1,0},{2,3},{3,2},{4,5},{5,4},{6,7},{7,6},{8,9},{9,8},{10,11... | collective-permute-start | bytes 2359304 | tf_op jit(solution)/shard_map/ppermute | solution.py:41
  148.3 43.7 %all-to-all-start.4 = ((bf16[8,2,64,768]{3,2,1,0:T(8,128)(2,1)}), bf16[8,2,64,768]{3,2,1,0:T(8,128)(2,1)}, u32[]{:S(2)}, u32[]{:S(2)}) async-start(bf16[8,2,64,768]{3,2,1,0:T(8,128)(2,1)} %broadcast_in_dim.28), calls=%async_computation.4 | async-start | bytes 3145728 | tf_op jit(solution)/shard_map/all_to_all | solution.py:63
  155.2 23.4 %collective-permute-start.20 = (bf16[16,1536]{1,0:T(8,128)(2,1)S(1)}, bf16[16,1536]{1,0:T(8,128)(2,1)S(1)}, u32[]{:S(2)}, u32[]{:S(2)}) collective-permute-start(bf16[16,1536]{1,0:T(8,128)(2,1)S(1)} %get-tuple-element.105), channel_id=1, source_target_pairs={{0,24},{8,0},{16,8},{24,16},{1,25},{9,1},{17,9},{25,17},{2,26},{10... | collective-permute-start | bytes 147464 | tf_op jit(solution)/shard_map/ppermute | solution.py:35
  158.6 23.9 %collective-permute-start.21 = (bf16[16,1536]{1,0:T(8,128)(2,1)S(1)}, bf16[16,1536]{1,0:T(8,128)(2,1)S(1)}, u32[]{:S(2)}, u32[]{:S(2)}) collective-permute-start(bf16[16,1536]{1,0:T(8,128)(2,1)S(1)} %get-tuple-element.104), channel_id=1, source_target_pairs={{0,16},{8,24},{16,0},{24,8},{1,17},{9,25},{17,1},{25,9},{2,18},{10... | collective-permute-start | bytes 147464 | tf_op jit(solution)/shard_map/ppermute | solution.py:35
  162.8 19.8 %collective-permute-start.22 = (bf16[16,1536]{1,0:T(8,128)(2,1)S(1)}, bf16[16,1536]{1,0:T(8,128)(2,1)S(1)}, u32[]{:S(2)}, u32[]{:S(2)}) collective-permute-start(bf16[16,1536]{1,0:T(8,128)(2,1)S(1)} %get-tuple-element.103), channel_id=1, source_target_pairs={{0,8},{8,16},{16,24},{24,0},{1,9},{9,17},{17,25},{25,1},{2,10},{10... | collective-permute-start | bytes 147464 | tf_op jit(solution)/shard_map/ppermute | solution.py:35
  163.8 1.3 copy-start.1
  165.9 12.7 %copy-start.6 = (bf16[256,1536]{1,0:T(8,128)(2,1)S(1)}, bf16[256,1536]{1,0:T(8,128)(2,1)}, u32[]{:S(2)}) copy-start(bf16[256,1536]{1,0:T(8,128)(2,1)} %copy-done.5) | copy-start | bytes 2359300
  165.9 12.7 %copy-start.10 = (bf16[256,1536]{1,0:T(8,128)(2,1)S(1)}, bf16[256,1536]{1,0:T(8,128)(2,1)}, u32[]{:S(2)}) copy-start(bf16[256,1536]{1,0:T(8,128)(2,1)} %copy-done.9) | copy-start | bytes 2359300
  165.9 12.6 %copy-start.17 = (bf16[256,1536]{1,0:T(8,128)(2,1)S(1)}, bf16[256,1536]{1,0:T(8,128)(2,1)}, u32[]{:S(2)}) copy-start(bf16[256,1536]{1,0:T(8,128)(2,1)} %copy-done.16) | copy-start | bytes 2359300
  165.9 12.6 %copy-start.21 = (bf16[256,1536]{1,0:T(8,128)(2,1)S(1)}, bf16[256,1536]{1,0:T(8,128)(2,1)}, u32[]{:S(2)}) copy-start(bf16[256,1536]{1,0:T(8,128)(2,1)} %copy-done.20) | copy-start | bytes 2359300
  167.5 15.0 %collective-permute-start.24 = (bf16[64,1536]{1,0:T(8,128)(2,1)S(1)}, bf16[64,1536]{1,0:T(8,128)(2,1)S(1)}, u32[]{:S(2)}, u32[]{:S(2)}) collective-permute-start(bf16[64,1536]{1,0:T(8,128)(2,1)S(1)} %get-tuple-element.68), channel_id=1, source_target_pairs={{0,6},{1,7},{2,0},{3,1},{4,2},{5,3},{6,4},{7,5},{8,14},{9,15},{10,... | collective-permute-start | bytes 589832 | tf_op jit(solution)/shard_map/ppermute | solution.py:38
  168.5 14.1 %collective-permute-start.25 = (bf16[64,1536]{1,0:T(8,128)(2,1)S(1)}, bf16[64,1536]{1,0:T(8,128)(2,1)S(1)}, u32[]{:S(2)}, u32[]{:S(2)}) collective-permute-start(bf16[64,1536]{1,0:T(8,128)(2,1)S(1)} %get-tuple-element.69), channel_id=1, source_target_pairs={{0,4},{1,5},{2,6},{3,7},{4,0},{5,1},{6,2},{7,3},{8,12},{9,13},{10,... | collective-permute-start | bytes 589832 | tf_op jit(solution)/shard_map/ppermute | solution.py:38
  178.5 6.9 %collective-permute-start.26 = (bf16[64,1536]{1,0:T(8,128)(2,1)S(1)}, bf16[64,1536]{1,0:T(8,128)(2,1)S(1)}, u32[]{:S(2)}, u32[]{:S(2)}) collective-permute-start(bf16[64,1536]{1,0:T(8,128)(2,1)S(1)} %get-tuple-element.70), channel_id=1, source_target_pairs={{0,2},{1,3},{2,4},{3,5},{4,6},{5,7},{6,0},{7,1},{8,10},{9,11},{10,... | collective-permute-start | bytes 589832 | tf_op jit(solution)/shard_map/ppermute | solution.py:38
  185.5 12.7 %collective-permute-start.27 = (bf16[16,1536]{1,0:T(8,128)(2,1)S(1)}, bf16[16,1536]{1,0:T(8,128)(2,1)S(1)}, u32[]{:S(2)}, u32[]{:S(2)}) collective-permute-start(bf16[16,1536]{1,0:T(8,128)(2,1)S(1)} %get-tuple-element.101), channel_id=1, source_target_pairs={{0,24},{8,0},{16,8},{24,16},{1,25},{9,1},{17,9},{25,17},{2,26},{10... | collective-permute-start | bytes 147464 | tf_op jit(solution)/shard_map/ppermute | solution.py:35
  185.8 12.4 %collective-permute-start.28 = (bf16[16,1536]{1,0:T(8,128)(2,1)S(1)}, bf16[16,1536]{1,0:T(8,128)(2,1)S(1)}, u32[]{:S(2)}, u32[]{:S(2)}) collective-permute-start(bf16[16,1536]{1,0:T(8,128)(2,1)S(1)} %get-tuple-element.100), channel_id=1, source_target_pairs={{0,16},{8,24},{16,0},{24,8},{1,17},{9,25},{17,1},{25,9},{2,18},{10... | collective-permute-start | bytes 147464 | tf_op jit(solution)/shard_map/ppermute | solution.py:35
  191.9 6.3 %collective-permute-start.29 = (bf16[16,1536]{1,0:T(8,128)(2,1)S(1)}, bf16[16,1536]{1,0:T(8,128)(2,1)}, u32[]{:S(2)}, u32[]{:S(2)}) collective-permute-start(bf16[16,1536]{1,0:T(8,128)(2,1)S(1)} %get-tuple-element.99), channel_id=1, source_target_pairs={{0,8},{8,16},{16,24},{24,0},{1,9},{9,17},{17,25},{25,1},{2,10},{10... | collective-permute-start | bytes 147464 | tf_op jit(solution)/shard_map/ppermute | solution.py:35
  191.9 1.8 copy-start.4
  192.0 1.8 copy-start.8
  192.0 2.1 %copy-start.15 = (bf16[256,1536]{1,0:T(8,128)(2,1)S(1)}, bf16[256,1536]{1,0:T(8,128)(2,1)}, u32[]{:S(2)}) copy-start(bf16[256,1536]{1,0:T(8,128)(2,1)} %copy-done.14) | copy-start | bytes 2359300
  192.0 2.3 %copy-start.19 = (bf16[256,1536]{1,0:T(8,128)(2,1)S(1)}, bf16[256,1536]{1,0:T(8,128)(2,1)}, u32[]{:S(2)}) copy-start(bf16[256,1536]{1,0:T(8,128)(2,1)} %copy-done.18) | copy-start | bytes 2359300

commit v6 on v5

--- a/solution.py
+++ b/solution.py
@@ -94,9 +94,8 @@
         chips0, groups1 = barrier([far0] + [shift_chip(far0, k) for k in range(1, n_chip)], groups1)
         far1 = join(groups1)
         both0, part0 = partial_sums(join(chips0))
-        last = n_chip // 2
         chips1 = [far1] + [
-            shift_chip(after(far1, part0) if k == last else far1, k) for k in range(1, n_chip)
+            shift_chip(far1, k) for k in range(1, n_chip)
         ]
         both1, part1 = partial_sums(join(chips1))
         sums0 = trade_width(part0)
@@ -115,28 +114,29 @@
         hidden1 = trade_width(after(copies(grad1), hidden0)).reshape(-1, act0.shape[1])
         other0, own0 = two_halves(hidden0)
         own0, other0 = barrier(own0, swap_core(other0))
-        parts0 = exchange(sum_blocks([own0, other0], n_chip), shift_chip)
+        parts0, act_copies = barrier(sum_blocks([own0, other0], n_chip), act_copies)
+        parts0 = exchange(parts0, shift_chip)
         other1, own1 = two_halves(hidden1)
         parts0, other1, act_copies = barrier(parts0, other1, act_copies)
         activation = trade_width(act_copies)
         own1, other1 = barrier(own1, swap_core(other1))
-        parts1, beside = barrier(
-            sum_blocks([own1, other1], n_chip), jnp.concatenate([hidden0, hidden1], axis=0)
-        )
+        parts1, hidden0, hidden1 = barrier(sum_blocks([own1, other1], n_chip), hidden0, hidden1)
         parts1 = exchange(parts1, shift_chip)
-        parts0 = exchange(sum_blocks(parts0, n_y), shift_y)
+        hidden_all = jnp.concatenate([hidden0, hidden1], axis=0)
         tokens_all = jnp.concatenate([both0[0], both1[0]], axis=0)
-        grad_weight_in = (contract_first(tokens_all, beside) * norm_scale).astype(bf16)
+        grad_weight_in = (contract_first(tokens_all, hidden_all) * norm_scale).astype(bf16)
         parts0, parts1, grad_weight_in = barrier(parts0, parts1, grad_weight_in)
-        parts1 = exchange(sum_blocks(parts1, n_y), shift_y)
-        (tokens0,) = sum_blocks(parts0, 1)
+        parts = [
+            jnp.concatenate(pair, axis=0)
+            for pair in zip(sum_blocks(parts0, n_y), sum_blocks(parts1, n_y))
+        ]
+        parts = exchange(parts, shift_y)
         activation = activation.transpose(1, 0, 2, 3).reshape(-1, act0.shape[1])
         grad_all = jnp.concatenate([both0[1], both1[1]], axis=0)
         grad_weight_out = (contract_first(activation, grad_all) * norm_scale).astype(bf16)
-        parts1, grad_weight_out = barrier(parts1, grad_weight_out)
-        (tokens1,) = sum_blocks(parts1, 1)
-        grad_tokens = jnp.concatenate([tokens0, tokens1], axis=0).astype(bf16)
-        return (grad_tokens, grad_weight_in, grad_weight_out)
+        parts, grad_weight_out = barrier(parts, grad_weight_out)
+        (grad_tokens,) = sum_blocks(parts, 1)
+        return (grad_tokens.astype(bf16), grad_weight_in, grad_weight_out)
 
     return jax.shard_map(
         shards,

time: 200 us -> 188 us (0.940)
  waiting for transfers between devices: 77.2 us -> 68.2 us
  starting transfers between devices: 74.8 us -> 69.3 us
  other arithmetic: 13.5 us -> 10.7 us
  matrix products: 17.6 us -> 19.7 us
    ppermute x12 -> x9, waiting for transfers between devices: 25.1 us -> 17 us  [shift_y(): return lax.ppermute(a, 'gy', [(i, (i + k) % n_y) for i in range(n_y)])]
    ppermute x12 -> x9, starting transfers between devices: 33 us -> 26.7 us  [shift_y(): return lax.ppermute(a, 'gy', [(i, (i + k) % n_y) for i in range(n_y)])]
    unnamed x52 -> x48, local copies, waits for them, and re-layouts: 4.34 us -> 6.33 us
  transfers between devices with their start and end apart: 35 -> 32, of which waited for: 17 -> 18; matrix products, arithmetic and copies ran while one was open for 20% -> 23% of each run, Pallas kernels for 0% -> 0%
where the time goes in v6:
time: 188 us; the launch traced here: 187 us
  starting transfers between devices  69.3 us (37%)
  waiting for transfers between devices  68.2 us (36%)
  matrix products  19.7 us (10%)
  local copies, waits for them, and re-layouts  17.4 us (9%)
  other arithmetic  10.7 us (6%)
    all_to_all x5, waiting for transfers between devices, trade_width(): return lax.all_to_all(parts, 'gx', 0, 0, tiled=True)  31.5 us
    ppermute x9, starting transfers between devices, shift_y(): return lax.ppermute(a, 'gy', [(i, (i + k) % n_y) for i in range(n_y)])  26.7 us
    all_to_all x5, starting transfers between devices, trade_width(): return lax.all_to_all(parts, 'gx', 0, 0, tiled=True)  26.6 us
    ppermute x9, waiting for transfers between devices, shift_y(): return lax.ppermute(a, 'gy', [(i, (i + k) % n_y) for i in range(n_y)])  17 us
    ppermute x12, waiting for transfers between devices, shift_chip(): return lax.ppermute(a, 'gz', [(i, (i + 2 * k) % n_z) for i in range(n_z)])  16.5 us
    ppermute x12, starting transfers between devices, shift_chip(): return lax.ppermute(a, 'gz', [(i, (i + 2 * k) % n_z) for i in range(n_z)])  14.8 us
    dot_general x2, matrix products, contract_first(): lax.dot_general(left, right, (((0,), (0,)), ((), ())), preferred_element_...  9.02 us
    dot_general x6, matrix products, contract_last(): lax.dot_general(left, right, (((1,), (1,)), ((), ())), preferred_element_...  7.95 us
  transfers between devices with their start and end apart: 32, of which 18 were waited for; matrix products, arithmetic and copies ran while one was open for 23% of the time, Pallas kernels for 0%

profile of v6, /device:TPU:32, one launch (start us, length us, event | category | flops | bytes accessed | tf_op | source)
XLA Modules:
  0.0 186.5 jit_solution(302734864191521143)
XLA Ops:
  0.6 1.0 slice_bitcast_fusion.4
  1.7 5.5 %collective-permute-start.2 = (bf16[2,16,1536]{2,1,0:T(8,128)(2,1)S(1)}, bf16[2,16,1536]{2,1,0:T(8,128)(2,1)S(1)}, u32[]{:S(2)}, u32[]{:S(2)}) collective-permute-start(bf16[2,16,1536]{2,1,0:T(8,128)(2,1)S(1)} %pad_maximum_fusion.5), channel_id=1, source_target_pairs={{0,24},{8,0},{16,8},{24,16},{1,25},{9,1},{17,9},{25,17},{2,26},{10... | collective-permute-start | bytes 294920 | tf_op jit(solution)/shard_map/ppermute | solution.py:35
  7.2 1.4 collective-permute-start.1
  8.6 2.4 %collective-permute-start = (bf16[2,16,1536]{2,1,0:T(8,128)(2,1)S(1)}, bf16[2,16,1536]{2,1,0:T(8,128)(2,1)S(1)}, u32[]{:S(2)}, u32[]{:S(2)}) collective-permute-start(bf16[2,16,1536]{2,1,0:T(8,128)(2,1)S(1)} %pad_maximum_fusion.5), channel_id=1, source_target_pairs={{0,8},{8,16},{16,24},{24,0},{1,9},{9,17},{17,25},{25,1},{2,10},{10... | collective-permute-start | bytes 294920 | tf_op jit(solution)/shard_map/ppermute | solution.py:35
  11.0 7.1 %collective-permute-done.1 = bf16[2,16,1536]{2,1,0:T(8,128)(2,1)S(1)} collective-permute-done((bf16[2,16,1536]{2,1,0:T(8,128)(2,1)S(1)}, bf16[2,16,1536]{2,1,0:T(8,128)(2,1)S(1)}, u32[]{:S(2)}, u32[]{:S(2)}) %collective-permute-start.1) | collective-permute-done | bytes 98336 | tf_op jit(solution)/shard_map/ppermute | solution.py:35
  18.7 1.6 collective-permute-start.3
  20.3 2.7 %collective-permute-start.4 = (bf16[2,64,1536]{2,1,0:T(8,128)(2,1)S(1)}, bf16[2,64,1536]{2,1,0:T(8,128)(2,1)S(1)}, u32[]{:S(2)}, u32[]{:S(2)}) collective-permute-start(bf16[2,64,1536]{2,1,0:T(8,128)(2,1)S(1)} %pad_maximum_fusion.2), channel_id=1, source_target_pairs={{0,4},{1,5},{2,6},{3,7},{4,0},{5,1},{6,2},{7,3},{8,12},{9,13},{10,... | collective-permute-start | bytes 1179656 | tf_op jit(solution)/shard_map/ppermute | solution.py:38
  23.0 1.4 collective-permute-start.5
  24.5 1.8 collective-permute-start.6
  26.3 4.2 %collective-permute-start.7 = (bf16[2,16,1536]{2,1,0:T(8,128)(2,1)S(1)}, bf16[2,16,1536]{2,1,0:T(8,128)(2,1)S(1)}, u32[]{:S(2)}, u32[]{:S(2)}) collective-permute-start(bf16[2,16,1536]{2,1,0:T(8,128)(2,1)S(1)} %pad_maximum_fusion.6), channel_id=1, source_target_pairs={{0,16},{8,24},{16,0},{24,8},{1,17},{9,25},{17,1},{25,9},{2,18},{10... | collective-permute-start | bytes 294920 | tf_op jit(solution)/shard_map/ppermute | solution.py:35
  30.5 3.2 %collective-permute-done.6 = bf16[2,16,1536]{2,1,0:T(8,128)(2,1)S(1)} collective-permute-done((bf16[2,16,1536]{2,1,0:T(8,128)(2,1)S(1)}, bf16[2,16,1536]{2,1,0:T(8,128)(2,1)S(1)}, u32[]{:S(2)}, u32[]{:S(2)}) %collective-permute-start.6) | collective-permute-done | bytes 98336 | tf_op jit(solution)/shard_map/ppermute | solution.py:35
  33.7 2.7 %collective-permute-start.8 = (bf16[2,16,1536]{2,1,0:T(8,128)(2,1)S(1)}, bf16[2,16,1536]{2,1,0:T(8,128)(2,1)S(1)}, u32[]{:S(2)}, u32[]{:S(2)}) collective-permute-start(bf16[2,16,1536]{2,1,0:T(8,128)(2,1)S(1)} %pad_maximum_fusion.6), channel_id=1, source_target_pairs={{0,24},{8,0},{16,8},{24,16},{1,25},{9,1},{17,9},{25,17},{2,26},{10... | collective-permute-start | bytes 294920 | tf_op jit(solution)/shard_map/ppermute | solution.py:35
  36.5 4.4 %collective-permute-done.8 = bf16[2,16,1536]{2,1,0:T(8,128)(2,1)S(1)} collective-permute-done((bf16[2,16,1536]{2,1,0:T(8,128)(2,1)S(1)}, bf16[2,16,1536]{2,1,0:T(8,128)(2,1)S(1)}, u32[]{:S(2)}, u32[]{:S(2)}) %collective-permute-start.8) | collective-permute-done | bytes 98336 | tf_op jit(solution)/shard_map/ppermute | solution.py:35
  45.1 1.8 collective-permute-start.12
  47.0 1.3 collective-permute-start.13
  48.2 1.4 fusion.39
  49.7 1.4 fusion.42
  51.1 1.3 pad_maximum_fusion
  52.4 5.9 %all-to-all-start = ((bf16[8,2,64,768]{3,2,1,0:T(8,128)(2,1)}), bf16[8,2,64,768]{3,2,1,0:T(8,128)(2,1)}, u32[]{:S(2)}, u32[]{:S(2)}) async-start(bf16[8,2,64,768]{3,2,1,0:T(8,128)(2,1)} %pad_maximum_fusion), calls=%async_computation | async-start | bytes 3145728 | tf_op jit(solution)/shard_map/all_to_all | solution.py:63
  58.3 7.3 %collective-permute-done.11 = bf16[2,64,1536]{2,1,0:T(8,128)(2,1)} collective-permute-done((bf16[2,64,1536]{2,1,0:T(8,128)(2,1)}, bf16[2,64,1536]{2,1,0:T(8,128)(2,1)}, u32[]{:S(2)}, u32[]{:S(2)}) %collective-permute-start.11) | collective-permute-done | bytes 393248 | tf_op jit(solution)/shard_map/ppermute | solution.py:38
  65.6 1.8 constant_dynamic-update-slice_fusion.10
  67.4 1.8 constant_dynamic-update-slice_fusion.9
  69.2 0.8 constant_dynamic-update-slice_fusion.8
  69.9 1.6 slice_bitcast_fusion.1
  72.2 1.8 collective-permute-done.15
  74.0 1.4 fusion.33
  75.4 1.4 fusion.36
  76.8 1.3 pad_maximum_fusion.1
  78.1 6.1 %all-to-all-start.1 = ((bf16[8,2,64,768]{3,2,1,0:T(8,128)(2,1)}), bf16[8,2,64,768]{3,2,1,0:T(8,128)(2,1)}, u32[]{:S(2)}, u32[]{:S(2)}) async-start(bf16[8,2,64,768]{3,2,1,0:T(8,128)(2,1)} %pad_maximum_fusion.1), calls=%async_computation.1 | async-start | bytes 3145728 | tf_op jit(solution)/shard_map/all_to_all | solution.py:63
  84.3 1.7 convert_reduce_fusion.1
  86.1 18.5 %all-to-all-done.1 = bf16[8,2,64,768]{3,2,1,0:T(8,128)(2,1)} async-done(((bf16[8,2,64,768]{3,2,1,0:T(8,128)(2,1)}), bf16[8,2,64,768]{3,2,1,0:T(8,128)(2,1)}, u32[]{:S(2)}, u32[]{:S(2)}) %all-to-all-start.1) | async-done | bytes 1572896 | tf_op jit(solution)/shard_map/all_to_all | solution.py:63
  104.6 0.9 broadcast_in_dim.11
  105.5 4.2 %all-to-all-start.2 = ((bf16[8,64,768]{2,1,0:T(8,128)(2,1)}), bf16[8,64,768]{2,1,0:T(8,128)(2,1)S(1)}, u32[]{:S(2)}, u32[]{:S(2)}) async-start(bf16[8,64,768]{2,1,0:T(8,128)(2,1)} %broadcast_in_dim.11), calls=%async_computation.2 | async-start | bytes 1572864 | tf_op jit(solution)/shard_map/all_to_all | solution.py:63
  109.7 1.7 convert_reduce_fusion
  111.5 9.8 %all-to-all-done.2 = bf16[8,64,768]{2,1,0:T(8,128)(2,1)S(1)} async-done(((bf16[8,64,768]{2,1,0:T(8,128)(2,1)}), bf16[8,64,768]{2,1,0:T(8,128)(2,1)S(1)}, u32[]{:S(2)}, u32[]{:S(2)}) %all-to-all-start.2) | async-done | bytes 786464 | tf_op jit(solution)/shard_map/all_to_all | solution.py:63
  121.3 0.9 broadcast_in_dim.28
  122.2 4.7 %all-to-all-start.3 = ((bf16[8,64,768]{2,1,0:T(8,128)(2,1)}), bf16[8,64,768]{2,1,0:T(8,128)(2,1)}, u32[]{:S(2)}, u32[]{:S(2)}) async-start(bf16[8,64,768]{2,1,0:T(8,128)(2,1)} %broadcast_in_dim.28), calls=%async_computation.3 | async-start | bytes 1572864 | tf_op jit(solution)/shard_map/all_to_all | solution.py:63
  126.9 0.8 convolution_convert_fusion.1
  127.9 0.8 fusion.69
  128.7 1.4 collective-permute-done.16
  130.1 0.9 add_convert_fusion.3
  131.1 1.3 broadcast_in_dim.12
  132.4 1.5 collective-permute-start.18
  133.8 1.1 collective-permute-start.19
  135.0 3.2 %all-to-all-done.3 = bf16[8,64,768]{2,1,0:T(8,128)(2,1)} async-done(((bf16[8,64,768]{2,1,0:T(8,128)(2,1)}), bf16[8,64,768]{2,1,0:T(8,128)(2,1)}, u32[]{:S(2)}, u32[]{:S(2)}) %all-to-all-start.3) | async-done | bytes 786464 | tf_op jit(solution)/shard_map/all_to_all | solution.py:63
  138.1 1.9 %fusion.67 = (bf16[4,64,768]{2,1,0:T(8,128)(2,1)}, bf16[4,64,768]{2,1,0:T(8,128)(2,1)S(1)}) fusion(bf16[8,64,768]{2,1,0:T(8,128)(2,1)} %all-to-all-done.3), kind=kLoop, calls=%fused_computation.123 | loop fusion | bytes 1572864 | tf_op jit(solution)/shard_map/slice | solution.py:111
  140.1 1.7 convolution_convert_fusion
  142.0 3.4 %collective-permute-done.19 = bf16[64,1536]{1,0:T(8,128)(2,1)} collective-permute-done((bf16[64,1536]{1,0:T(8,128)(2,1)}, bf16[64,1536]{1,0:T(8,128)(2,1)}, u32[]{:S(2)}, u32[]{:S(2)}) %collective-permute-start.19) | collective-permute-done | bytes 196640 | tf_op jit(solution)/shard_map/ppermute | solution.py:38
  145.3 5.7 %all-to-all-start.4 = ((bf16[8,2,64,768]{3,2,1,0:T(8,128)(2,1)}), bf16[8,2,64,768]{3,2,1,0:T(8,128)(2,1)}, u32[]{:S(2)}, u32[]{:S(2)}) async-start(bf16[8,2,64,768]{3,2,1,0:T(8,128)(2,1)} %broadcast_in_dim.12), calls=%async_computation.4 | async-start | bytes 3145728 | tf_op jit(solution)/shard_map/all_to_all | solution.py:63
  151.1 1.8 fusion.70
  152.9 1.6 add_convert_fusion
  154.5 1.2 collective-permute-start.21
  156.4 0.8 collective-permute-start.23
  157.2 5.1 %multiply_convert_fusion.1 = bf16[1536,768]{1,0:T(8,128)(2,1)} fusion(bf16[256,1536]{1,0:T(8,128)(2,1)S(1)} %copy-done.19, bf16[256,1536]{1,0:T(8,128)(2,1)S(1)} %copy-done.8, bf16[256,1536]{1,0:T(8,128)(2,1)S(1)} %copy-done.15, bf16[256,1536]{1,0:T(8,128)(2,1)S(1)} %copy-done.4, bf16[512,768]{1,0:T(8,128)(2,1)} %bitcast.23, bf16[512,768]{1,0:T(8,128)(2,1)S(1)} %bitcast.54), kind=kOutput, calls=%fused_computation.1 | convolution fusion | flops 2434007040 | bytes 7077888 | tf_op jit(solution)/shard_map/dot_general | solution.py:28
  162.4 2.7 %collective-permute-done.22 = bf16[64,1536]{1,0:T(8,128)(2,1)S(1)} collective-permute-done((bf16[64,1536]{1,0:T(8,128)(2,1)S(1)}, bf16[64,1536]{1,0:T(8,128)(2,1)S(1)}, u32[]{:S(2)}, u32[]{:S(2)}) %collective-permute-start.22) | collective-permute-done | bytes 196640 | tf_op jit(solution)/shard_map/ppermute | solution.py:38
  165.1 2.8 %collective-permute-done.23 = bf16[64,1536]{1,0:T(8,128)(2,1)S(1)} collective-permute-done((bf16[64,1536]{1,0:T(8,128)(2,1)S(1)}, bf16[64,1536]{1,0:T(8,128)(2,1)S(1)}, u32[]{:S(2)}, u32[]{:S(2)}) %collective-permute-start.23) | collective-permute-done | bytes 196640 | tf_op jit(solution)/shard_map/ppermute | solution.py:38
  168.0 1.2 add_convert_fusion.8
  169.2 2.3 %collective-permute-start.24 = (bf16[32,1536]{1,0:T(8,128)(2,1)S(1)}, bf16[32,1536]{1,0:T(8,128)(2,1)S(1)}, u32[]{:S(2)}, u32[]{:S(2)}) collective-permute-start(bf16[32,1536]{1,0:T(8,128)(2,1)S(1)} %pad_maximum_fusion.7), channel_id=1, source_target_pairs={{0,24},{8,0},{16,8},{24,16},{1,25},{9,1},{17,9},{25,17},{2,26},{10... | collective-permute-start | bytes 294920 | tf_op jit(solution)/shard_map/ppermute | solution.py:35
  171.5 5.4 %collective-permute-start.25 = (bf16[32,1536]{1,0:T(8,128)(2,1)S(1)}, bf16[32,1536]{1,0:T(8,128)(2,1)S(1)}, u32[]{:S(2)}, u32[]{:S(2)}) collective-permute-start(bf16[32,1536]{1,0:T(8,128)(2,1)S(1)} %pad_maximum_fusion.8), channel_id=1, source_target_pairs={{0,16},{8,24},{16,0},{24,8},{1,17},{9,25},{17,1},{25,9},{2,18},{10... | collective-permute-start | bytes 294920 | tf_op jit(solution)/shard_map/ppermute | solution.py:35
  176.9 1.0 collective-permute-start.26
  178.0 1.7 copy.12
  180.3 3.9 %multiply_convert_fusion = bf16[768,1536]{1,0:T(8,128)(2,1)} fusion(bf16[1024,768]{1,0:T(8,128)(2,1)S(1)} %bitcast.55, bf16[256,1536]{1,0:T(8,128)(2,1)S(1)} %copy-done.17, bf16[256,1536]{1,0:T(8,128)(2,1)S(1)} %copy-done.6, bf16[256,1536]{1,0:T(8,128)(2,1)S(1)} %copy-done.13, bf16[256,1536]{1,0:T(8,128)(2,1)S(1)} %copy-done.2), kind=kOutput, calls=%fused_computation | convolution fusion | flops 2430861312 | bytes 7077888 | tf_op jit(solution)/shard_map/dot_general | solution.py:28
  184.2 0.9 collective-permute-done.25
  185.1 0.7 collective-permute-done.26
  (89 shorter events, 8.4 us)
Async XLA Ops:
  0.6 49.1 %copy-start = (bf16[1536,768]{1,0:T(8,128)(2,1)S(1)}, bf16[1536,768]{1,0:T(8,128)(2,1)}, u32[]{:S(2)}) copy-start(bf16[1536,768]{1,0:T(8,128)(2,1)} %param.6) | copy-start | bytes 7077892
  1.7 9.3 %collective-permute-start.2 = (bf16[2,16,1536]{2,1,0:T(8,128)(2,1)S(1)}, bf16[2,16,1536]{2,1,0:T(8,128)(2,1)S(1)}, u32[]{:S(2)}, u32[]{:S(2)}) collective-permute-start(bf16[2,16,1536]{2,1,0:T(8,128)(2,1)S(1)} %pad_maximum_fusion.5), channel_id=1, source_target_pairs={{0,24},{8,0},{16,8},{24,16},{1,25},{9,1},{17,9},{25,17},{2,26},{10... | collective-permute-start | bytes 294920 | tf_op jit(solution)/shard_map/ppermute | solution.py:35
  7.2 10.9 %collective-permute-start.1 = (bf16[2,16,1536]{2,1,0:T(8,128)(2,1)S(1)}, bf16[2,16,1536]{2,1,0:T(8,128)(2,1)S(1)}, u32[]{:S(2)}, u32[]{:S(2)}) collective-permute-start(bf16[2,16,1536]{2,1,0:T(8,128)(2,1)S(1)} %pad_maximum_fusion.5), channel_id=1, source_target_pairs={{0,16},{8,24},{16,0},{24,8},{1,17},{9,25},{17,1},{25,9},{2,18},{10... | collective-permute-start | bytes 294920 | tf_op jit(solution)/shard_map/ppermute | solution.py:35
  8.6 10.0 %collective-permute-start = (bf16[2,16,1536]{2,1,0:T(8,128)(2,1)S(1)}, bf16[2,16,1536]{2,1,0:T(8,128)(2,1)S(1)}, u32[]{:S(2)}, u32[]{:S(2)}) collective-permute-start(bf16[2,16,1536]{2,1,0:T(8,128)(2,1)S(1)} %pad_maximum_fusion.5), channel_id=1, source_target_pairs={{0,8},{8,16},{16,24},{24,0},{1,9},{9,17},{17,25},{25,1},{2,10},{10... | collective-permute-start | bytes 294920 | tf_op jit(solution)/shard_map/ppermute | solution.py:35
  18.7 22.2 %collective-permute-start.3 = (bf16[2,64,1536]{2,1,0:T(8,128)(2,1)S(1)}, bf16[2,64,1536]{2,1,0:T(8,128)(2,1)S(1)}, u32[]{:S(2)}, u32[]{:S(2)}) collective-permute-start(bf16[2,64,1536]{2,1,0:T(8,128)(2,1)S(1)} %pad_maximum_fusion.2), channel_id=1, source_target_pairs={{0,2},{1,3},{2,4},{3,5},{4,6},{5,7},{6,0},{7,1},{8,10},{9,11},{10,... | collective-permute-start | bytes 1179656 | tf_op jit(solution)/shard_map/ppermute | solution.py:38
  20.3 20.6 %collective-permute-start.4 = (bf16[2,64,1536]{2,1,0:T(8,128)(2,1)S(1)}, bf16[2,64,1536]{2,1,0:T(8,128)(2,1)S(1)}, u32[]{:S(2)}, u32[]{:S(2)}) collective-permute-start(bf16[2,64,1536]{2,1,0:T(8,128)(2,1)S(1)} %pad_maximum_fusion.2), channel_id=1, source_target_pairs={{0,4},{1,5},{2,6},{3,7},{4,0},{5,1},{6,2},{7,3},{8,12},{9,13},{10,... | collective-permute-start | bytes 1179656 | tf_op jit(solution)/shard_map/ppermute | solution.py:38
  23.0 17.9 %collective-permute-start.5 = (bf16[2,64,1536]{2,1,0:T(8,128)(2,1)S(1)}, bf16[2,64,1536]{2,1,0:T(8,128)(2,1)S(1)}, u32[]{:S(2)}, u32[]{:S(2)}) collective-permute-start(bf16[2,64,1536]{2,1,0:T(8,128)(2,1)S(1)} %pad_maximum_fusion.2), channel_id=1, source_target_pairs={{0,6},{1,7},{2,0},{3,1},{4,2},{5,3},{6,4},{7,5},{8,14},{9,15},{10,... | collective-permute-start | bytes 1179656 | tf_op jit(solution)/shard_map/ppermute | solution.py:38
  24.5 9.2 %collective-permute-start.6 = (bf16[2,16,1536]{2,1,0:T(8,128)(2,1)S(1)}, bf16[2,16,1536]{2,1,0:T(8,128)(2,1)S(1)}, u32[]{:S(2)}, u32[]{:S(2)}) collective-permute-start(bf16[2,16,1536]{2,1,0:T(8,128)(2,1)S(1)} %pad_maximum_fusion.6), channel_id=1, source_target_pairs={{0,8},{8,16},{16,24},{24,0},{1,9},{9,17},{17,25},{25,1},{2,10},{10... | collective-permute-start | bytes 294920 | tf_op jit(solution)/shard_map/ppermute | solution.py:35
  26.3 10.3 %collective-permute-start.7 = (bf16[2,16,1536]{2,1,0:T(8,128)(2,1)S(1)}, bf16[2,16,1536]{2,1,0:T(8,128)(2,1)S(1)}, u32[]{:S(2)}, u32[]{:S(2)}) collective-permute-start(bf16[2,16,1536]{2,1,0:T(8,128)(2,1)S(1)} %pad_maximum_fusion.6), channel_id=1, source_target_pairs={{0,16},{8,24},{16,0},{24,8},{1,17},{9,25},{17,1},{25,9},{2,18},{10... | collective-permute-start | bytes 294920 | tf_op jit(solution)/shard_map/ppermute | solution.py:35
  33.7 7.2 %collective-permute-start.8 = (bf16[2,16,1536]{2,1,0:T(8,128)(2,1)S(1)}, bf16[2,16,1536]{2,1,0:T(8,128)(2,1)S(1)}, u32[]{:S(2)}, u32[]{:S(2)}) collective-permute-start(bf16[2,16,1536]{2,1,0:T(8,128)(2,1)S(1)} %pad_maximum_fusion.6), channel_id=1, source_target_pairs={{0,24},{8,0},{16,8},{24,16},{1,25},{9,1},{17,9},{25,17},{2,26},{10... | collective-permute-start | bytes 294920 | tf_op jit(solution)/shard_map/ppermute | solution.py:35
  41.1 7.2 %copy-start.10 = (bf16[768,1536]{1,0:T(8,128)(2,1)S(1)}, bf16[768,1536]{1,0:T(8,128)(2,1)}, u32[]{:S(2)}) copy-start(bf16[768,1536]{1,0:T(8,128)(2,1)} %param.8) | copy-start | bytes 7077892
  41.2 8.5 %copy-start.1 = (bf16[256,1536]{1,0:T(8,128)(2,1)}, bf16[256,1536]{1,0:T(8,128)(2,1)S(1)}, u32[]{:S(2)}) copy-start(bf16[256,1536]{1,0:T(8,128)(2,1)S(1)} %get-tuple-element.108) | copy-start | bytes 2359300
  41.2 8.5 %copy-start.3 = (bf16[256,1536]{1,0:T(8,128)(2,1)}, bf16[256,1536]{1,0:T(8,128)(2,1)S(1)}, u32[]{:S(2)}) copy-start(bf16[256,1536]{1,0:T(8,128)(2,1)S(1)} %get-tuple-element.107) | copy-start | bytes 2359300
  41.2 7.0 %collective-permute-start.10 = (bf16[256,1536]{1,0:T(8,128)(2,1)S(1)}, bf16[256,1536]{1,0:T(8,128)(2,1)S(1)}, u32[]{:S(2)}, u32[]{:S(2)}) collective-permute-start(bf16[256,1536]{1,0:T(8,128)(2,1)S(1)} %get-tuple-element.108), channel_id=1, source_target_pairs={{0,1},{1,0},{2,3},{3,2},{4,5},{5,4},{6,7},{7,6},{8,9},{9,8},{10,11... | collective-permute-start | bytes 2359304 | tf_op jit(solution)/shard_map/ppermute | solution.py:41
  41.3 8.4 %collective-permute-start.9 = (bf16[256,1536]{1,0:T(8,128)(2,1)S(1)}, bf16[256,1536]{1,0:T(8,128)(2,1)S(1)}, u32[]{:S(2)}, u32[]{:S(2)}) collective-permute-start(bf16[256,1536]{1,0:T(8,128)(2,1)S(1)} %get-tuple-element.107), channel_id=1, source_target_pairs={{0,1},{1,0},{2,3},{3,2},{4,5},{5,4},{6,7},{7,6},{8,9},{9,8},{10,11... | collective-permute-start | bytes 2359304 | tf_op jit(solution)/shard_map/ppermute | solution.py:41
  44.5 21.1 %collective-permute-start.11 = (bf16[2,64,1536]{2,1,0:T(8,128)(2,1)}, bf16[2,64,1536]{2,1,0:T(8,128)(2,1)}, u32[]{:S(2)}, u32[]{:S(2)}) collective-permute-start(bf16[2,64,1536]{2,1,0:T(8,128)(2,1)} %get-tuple-element.125), channel_id=1, source_target_pairs={{0,2},{1,3},{2,4},{3,5},{4,6},{5,7},{6,0},{7,1},{8,10},{9,11},{10,... | collective-permute-start | bytes 1179656 | tf_op jit(solution)/shard_map/ppermute | solution.py:38
  45.1 22.2 %collective-permute-start.12 = (bf16[2,64,1536]{2,1,0:T(8,128)(2,1)}, bf16[2,64,1536]{2,1,0:T(8,128)(2,1)}, u32[]{:S(2)}, u32[]{:S(2)}) collective-permute-start(bf16[2,64,1536]{2,1,0:T(8,128)(2,1)} %get-tuple-element.125), channel_id=1, source_target_pairs={{0,4},{1,5},{2,6},{3,7},{4,0},{5,1},{6,2},{7,3},{8,12},{9,13},{10,... | collective-permute-start | bytes 1179656 | tf_op jit(solution)/shard_map/ppermute | solution.py:38
  47.0 22.2 %collective-permute-start.13 = (bf16[2,64,1536]{2,1,0:T(8,128)(2,1)}, bf16[2,64,1536]{2,1,0:T(8,128)(2,1)S(1)}, u32[]{:S(2)}, u32[]{:S(2)}) collective-permute-start(bf16[2,64,1536]{2,1,0:T(8,128)(2,1)} %get-tuple-element.125), channel_id=1, source_target_pairs={{0,6},{1,7},{2,0},{3,1},{4,2},{5,3},{6,4},{7,5},{8,14},{9,15},{10,... | collective-permute-start | bytes 1179656 | tf_op jit(solution)/shard_map/ppermute | solution.py:38
  48.2 1.4 copy-start.12
  49.7 1.4 copy-start.14
  52.4 25.7 %all-to-all-start = ((bf16[8,2,64,768]{3,2,1,0:T(8,128)(2,1)}), bf16[8,2,64,768]{3,2,1,0:T(8,128)(2,1)}, u32[]{:S(2)}, u32[]{:S(2)}) async-start(bf16[8,2,64,768]{3,2,1,0:T(8,128)(2,1)} %pad_maximum_fusion), calls=%async_computation | async-start | bytes 3145728 | tf_op jit(solution)/shard_map/all_to_all | solution.py:63
  69.9 4.0 %copy-start.11 = (bf16[768,1536]{1,0:T(8,128)(2,1)S(1)}, bf16[768,1536]{1,0:T(8,128)(2,1)}, u32[]{:S(2)}) copy-start(bf16[768,1536]{1,0:T(8,128)(2,1)} %param.8) | copy-start | bytes 7077892
  71.6 3.8 %copy-start.5 = (bf16[256,1536]{1,0:T(8,128)(2,1)}, bf16[256,1536]{1,0:T(8,128)(2,1)S(1)}, u32[]{:S(2)}) copy-start(bf16[256,1536]{1,0:T(8,128)(2,1)S(1)} %get-tuple-element.106) | copy-start | bytes 2359300
  71.6 3.8 %copy-start.7 = (bf16[256,1536]{1,0:T(8,128)(2,1)}, bf16[256,1536]{1,0:T(8,128)(2,1)S(1)}, u32[]{:S(2)}) copy-start(bf16[256,1536]{1,0:T(8,128)(2,1)S(1)} %get-tuple-element.105) | copy-start | bytes 2359300
  71.6 2.4 %collective-permute-start.15 = (bf16[256,1536]{1,0:T(8,128)(2,1)S(1)}, bf16[256,1536]{1,0:T(8,128)(2,1)S(1)}, u32[]{:S(2)}, u32[]{:S(2)}) collective-permute-start(bf16[256,1536]{1,0:T(8,128)(2,1)S(1)} %get-tuple-element.106), channel_id=1, source_target_pairs={{0,1},{1,0},{2,3},{3,2},{4,5},{5,4},{6,7},{7,6},{8,9},{9,8},{10,11... | collective-permute-start | bytes 2359304 | tf_op jit(solution)/shard_map/ppermute | solution.py:41
  71.7 3.7 %collective-permute-start.14 = (bf16[256,1536]{1,0:T(8,128)(2,1)S(1)}, bf16[256,1536]{1,0:T(8,128)(2,1)S(1)}, u32[]{:S(2)}, u32[]{:S(2)}) collective-permute-start(bf16[256,1536]{1,0:T(8,128)(2,1)S(1)} %get-tuple-element.105), channel_id=1, source_target_pairs={{0,1},{1,0},{2,3},{3,2},{4,5},{5,4},{6,7},{7,6},{8,9},{9,8},{10,11... | collective-permute-start | bytes 2359304 | tf_op jit(solution)/shard_map/ppermute | solution.py:41
  74.0 1.4 copy-start.16
  75.4 1.4 copy-start.18
  78.1 26.4 %all-to-all-start.1 = ((bf16[8,2,64,768]{3,2,1,0:T(8,128)(2,1)}), bf16[8,2,64,768]{3,2,1,0:T(8,128)(2,1)}, u32[]{:S(2)}, u32[]{:S(2)}) async-start(bf16[8,2,64,768]{3,2,1,0:T(8,128)(2,1)} %pad_maximum_fusion.1), calls=%async_computation.1 | async-start | bytes 3145728 | tf_op jit(solution)/shard_map/all_to_all | solution.py:63
  84.3 1.7 copy-start.9
  105.5 15.8 %all-to-all-start.2 = ((bf16[8,64,768]{2,1,0:T(8,128)(2,1)}), bf16[8,64,768]{2,1,0:T(8,128)(2,1)S(1)}, u32[]{:S(2)}, u32[]{:S(2)}) async-start(bf16[8,64,768]{2,1,0:T(8,128)(2,1)} %broadcast_in_dim.11), calls=%async_computation.2 | async-start | bytes 1572864 | tf_op jit(solution)/shard_map/all_to_all | solution.py:63
  122.2 15.9 %all-to-all-start.3 = ((bf16[8,64,768]{2,1,0:T(8,128)(2,1)}), bf16[8,64,768]{2,1,0:T(8,128)(2,1)}, u32[]{:S(2)}, u32[]{:S(2)}) async-start(bf16[8,64,768]{2,1,0:T(8,128)(2,1)} %broadcast_in_dim.28), calls=%async_computation.3 | async-start | bytes 1572864 | tf_op jit(solution)/shard_map/all_to_all | solution.py:63
  127.8 2.4 %collective-permute-start.16 = (bf16[256,1536]{1,0:T(8,128)(2,1)S(1)}, bf16[256,1536]{1,0:T(8,128)(2,1)S(1)}, u32[]{:S(2)}, u32[]{:S(2)}) collective-permute-start(bf16[256,1536]{1,0:T(8,128)(2,1)S(1)} %convolution_convert_fusion.1), channel_id=1, source_target_pairs={{0,1},{1,0},{2,3},{3,2},{4,5},{5,4},{6,7},{7,6},{8,9},{9,8},{10,11... | collective-permute-start | bytes 2359304 | tf_op jit(solution)/shard_map/ppermute | solution.py:41
  132.4 9.4 %collective-permute-start.17 = (bf16[64,1536]{1,0:T(8,128)(2,1)}, bf16[64,1536]{1,0:T(8,128)(2,1)}, u32[]{:S(2)}, u32[]{:S(2)}) collective-permute-start(bf16[64,1536]{1,0:T(8,128)(2,1)} %get-tuple-element.64), channel_id=1, source_target_pairs={{0,6},{1,7},{2,0},{3,1},{4,2},{5,3},{6,4},{7,5},{8,14},{9,15},{10,... | collective-permute-start | bytes 589832 | tf_op jit(solution)/shard_map/ppermute | solution.py:38
  132.4 9.6 %collective-permute-start.18 = (bf16[64,1536]{1,0:T(8,128)(2,1)}, bf16[64,1536]{1,0:T(8,128)(2,1)}, u32[]{:S(2)}, u32[]{:S(2)}) collective-permute-start(bf16[64,1536]{1,0:T(8,128)(2,1)} %get-tuple-element.65), channel_id=1, source_target_pairs={{0,4},{1,5},{2,6},{3,7},{4,0},{5,1},{6,2},{7,3},{8,12},{9,13},{10,... | collective-permute-start | bytes 589832 | tf_op jit(solution)/shard_map/ppermute | solution.py:38
  133.8 11.5 %collective-permute-start.19 = (bf16[64,1536]{1,0:T(8,128)(2,1)}, bf16[64,1536]{1,0:T(8,128)(2,1)}, u32[]{:S(2)}, u32[]{:S(2)}) collective-permute-start(bf16[64,1536]{1,0:T(8,128)(2,1)} %get-tuple-element.66), channel_id=1, source_target_pairs={{0,2},{1,3},{2,4},{3,5},{4,6},{5,7},{6,0},{7,1},{8,10},{9,11},{10,... | collective-permute-start | bytes 589832 | tf_op jit(solution)/shard_map/ppermute | solution.py:38
  145.3 7.6 %collective-permute-start.20 = (bf16[256,1536]{1,0:T(8,128)(2,1)}, bf16[256,1536]{1,0:T(8,128)(2,1)}, u32[]{:S(2)}, u32[]{:S(2)}) collective-permute-start(bf16[256,1536]{1,0:T(8,128)(2,1)} %convolution_convert_fusion), channel_id=1, source_target_pairs={{0,1},{1,0},{2,3},{3,2},{4,5},{5,4},{6,7},{7,6},{8,9},{9,8},{10,11... | collective-permute-start | bytes 2359304 | tf_op jit(solution)/shard_map/ppermute | solution.py:41
  145.3 32.6 %all-to-all-start.4 = ((bf16[8,2,64,768]{3,2,1,0:T(8,128)(2,1)}), bf16[8,2,64,768]{3,2,1,0:T(8,128)(2,1)}, u32[]{:S(2)}, u32[]{:S(2)}) async-start(bf16[8,2,64,768]{3,2,1,0:T(8,128)(2,1)} %broadcast_in_dim.12), calls=%async_computation.4 | async-start | bytes 3145728 | tf_op jit(solution)/shard_map/all_to_all | solution.py:63
  152.9 4.3 %copy-start.4 = (bf16[256,1536]{1,0:T(8,128)(2,1)S(1)}, bf16[256,1536]{1,0:T(8,128)(2,1)}, u32[]{:S(2)}) copy-start(bf16[256,1536]{1,0:T(8,128)(2,1)} %copy-done.3) | copy-start | bytes 2359300
  152.9 4.3 %copy-start.8 = (bf16[256,1536]{1,0:T(8,128)(2,1)S(1)}, bf16[256,1536]{1,0:T(8,128)(2,1)}, u32[]{:S(2)}) copy-start(bf16[256,1536]{1,0:T(8,128)(2,1)} %copy-done.7) | copy-start | bytes 2359300
  152.9 4.3 %copy-start.15 = (bf16[256,1536]{1,0:T(8,128)(2,1)S(1)}, bf16[256,1536]{1,0:T(8,128)(2,1)}, u32[]{:S(2)}) copy-start(bf16[256,1536]{1,0:T(8,128)(2,1)} %copy-done.14) | copy-start | bytes 2359300
  152.9 4.3 %copy-start.19 = (bf16[256,1536]{1,0:T(8,128)(2,1)S(1)}, bf16[256,1536]{1,0:T(8,128)(2,1)}, u32[]{:S(2)}) copy-start(bf16[256,1536]{1,0:T(8,128)(2,1)} %copy-done.18) | copy-start | bytes 2359300
  154.5 7.9 %collective-permute-start.21 = (bf16[64,1536]{1,0:T(8,128)(2,1)S(1)}, bf16[64,1536]{1,0:T(8,128)(2,1)S(1)}, u32[]{:S(2)}, u32[]{:S(2)}) collective-permute-start(bf16[64,1536]{1,0:T(8,128)(2,1)S(1)} %get-tuple-element.77), channel_id=1, source_target_pairs={{0,6},{1,7},{2,0},{3,1},{4,2},{5,3},{6,4},{7,5},{8,14},{9,15},{10,... | collective-permute-start | bytes 589832 | tf_op jit(solution)/shard_map/ppermute | solution.py:38
  155.7 9.4 %collective-permute-start.22 = (bf16[64,1536]{1,0:T(8,128)(2,1)S(1)}, bf16[64,1536]{1,0:T(8,128)(2,1)S(1)}, u32[]{:S(2)}, u32[]{:S(2)}) collective-permute-start(bf16[64,1536]{1,0:T(8,128)(2,1)S(1)} %get-tuple-element.78), channel_id=1, source_target_pairs={{0,4},{1,5},{2,6},{3,7},{4,0},{5,1},{6,2},{7,3},{8,12},{9,13},{10,... | collective-permute-start | bytes 589832 | tf_op jit(solution)/shard_map/ppermute | solution.py:38
  156.4 11.6 %collective-permute-start.23 = (bf16[64,1536]{1,0:T(8,128)(2,1)S(1)}, bf16[64,1536]{1,0:T(8,128)(2,1)S(1)}, u32[]{:S(2)}, u32[]{:S(2)}) collective-permute-start(bf16[64,1536]{1,0:T(8,128)(2,1)S(1)} %get-tuple-element.79), channel_id=1, source_target_pairs={{0,2},{1,3},{2,4},{3,5},{4,6},{5,7},{6,0},{7,1},{8,10},{9,11},{10,... | collective-permute-start | bytes 589832 | tf_op jit(solution)/shard_map/ppermute | solution.py:38
  169.2 15.0 %collective-permute-start.24 = (bf16[32,1536]{1,0:T(8,128)(2,1)S(1)}, bf16[32,1536]{1,0:T(8,128)(2,1)S(1)}, u32[]{:S(2)}, u32[]{:S(2)}) collective-permute-start(bf16[32,1536]{1,0:T(8,128)(2,1)S(1)} %pad_maximum_fusion.7), channel_id=1, source_target_pairs={{0,24},{8,0},{16,8},{24,16},{1,25},{9,1},{17,9},{25,17},{2,26},{10... | collective-permute-start | bytes 294920 | tf_op jit(solution)/shard_map/ppermute | solution.py:35
  171.5 13.6 %collective-permute-start.25 = (bf16[32,1536]{1,0:T(8,128)(2,1)S(1)}, bf16[32,1536]{1,0:T(8,128)(2,1)S(1)}, u32[]{:S(2)}, u32[]{:S(2)}) collective-permute-start(bf16[32,1536]{1,0:T(8,128)(2,1)S(1)} %pad_maximum_fusion.8), channel_id=1, source_target_pairs={{0,16},{8,24},{16,0},{24,8},{1,17},{9,25},{17,1},{25,9},{2,18},{10... | collective-permute-start | bytes 294920 | tf_op jit(solution)/shard_map/ppermute | solution.py:35
  176.9 9.0 %collective-permute-start.26 = (bf16[32,1536]{1,0:T(8,128)(2,1)S(1)}, bf16[32,1536]{1,0:T(8,128)(2,1)S(1)}, u32[]{:S(2)}, u32[]{:S(2)}) collective-permute-start(bf16[32,1536]{1,0:T(8,128)(2,1)S(1)} %pad_maximum_fusion.9), channel_id=1, source_target_pairs={{0,8},{8,16},{16,24},{24,0},{1,9},{9,17},{17,25},{25,1},{2,10},{10... | collective-permute-start | bytes 294920 | tf_op jit(solution)/shard_map/ppermute | solution.py:35
  177.9 1.7 copy-start.2
  177.9 1.8 copy-start.6
  177.9 2.1 %copy-start.13 = (bf16[256,1536]{1,0:T(8,128)(2,1)S(1)}, bf16[256,1536]{1,0:T(8,128)(2,1)}, u32[]{:S(2)}) copy-start(bf16[256,1536]{1,0:T(8,128)(2,1)} %copy-done.12) | copy-start | bytes 2359300
  178.0 2.3 %copy-start.17 = (bf16[256,1536]{1,0:T(8,128)(2,1)S(1)}, bf16[256,1536]{1,0:T(8,128)(2,1)}, u32[]{:S(2)}) copy-start(bf16[256,1536]{1,0:T(8,128)(2,1)} %copy-done.16) | copy-start | bytes 2359300

commit v7 on v6

--- a/solution.py
+++ b/solution.py
@@ -3,6 +3,8 @@
 import jax
 import jax.numpy as jnp
 from jax import lax
+from jax.experimental import pallas as pl
+from jax.experimental.pallas import tpu as pltpu
 from jax.sharding import PartitionSpec as P
 
 root_coef = math.sqrt(2.0 / math.pi)
@@ -28,6 +30,91 @@
     return lax.dot_general(left, right, (((0,), (0,)), ((), ())), preferred_element_type=f32)
 
 
+def vmem(mib):
+    return pltpu.CompilerParams(vmem_limit_bytes=mib << 20)
+
+
+def hidden_kernel(parts, bias, *refs):
+    before, (grad_copies, act_out) = refs[:-2], refs[-2:]
+    sums = jnp.sum(parts[...].astype(f32), axis=0)
+    act, grad = gelu_pair(sums[0] + bias[...], sums[1])
+    grad_copies[...] = jnp.broadcast_to(grad[None], grad_copies.shape)
+    if before:
+        act_out[:, 0] = jnp.broadcast_to(before[0][...][None], grad_copies.shape)
+        act_out[:, 1] = jnp.broadcast_to(act[None], grad_copies.shape)
+    else:
+        act_out[...] = act
+
+
+def hidden(parts, bias, *before):
+    n, pair, rows, columns = parts.shape
+    tile = columns // 3
+    act_shape = (n, 2, rows) if before else (rows,)
+    return pl.pallas_call(
+        hidden_kernel,
+        grid=(columns // tile,),
+        in_specs=[
+            pl.BlockSpec((n, pair, rows, tile), lambda i: (0, 0, 0, i)),
+            pl.BlockSpec((1, tile), lambda i: (0, i)),
+        ]
+        + [pl.BlockSpec((rows, tile), lambda i: (0, i))] * len(before),
+        out_specs=[
+            pl.BlockSpec((n, rows, tile), lambda i: (0, 0, i)),
+            pl.BlockSpec((*act_shape, tile), lambda i: (*([0] * len(act_shape)), i)),
+        ],
+        out_shape=[
+            jax.ShapeDtypeStruct((n, rows, columns), bf16),
+            jax.ShapeDtypeStruct((*act_shape, columns), bf16),
+        ],
+        compiler_params=vmem(32),
+        cost_estimate=pl.CostEstimate(
+            flops=40 * rows * columns,
+            bytes_accessed=2 * (parts.size + n * rows * columns),
+            transcendentals=rows * columns,
+        ),
+    )(parts, bias, *before)
+
+
+def times_weight(hidden_ref, weight_ref):
+    return lax.dot_general(
+        hidden_ref[...], weight_ref[...], (((1,), (1,)), ((), ())), preferred_element_type=f32
+    )
+
+
+def other_kernel(hidden_ref, weight_ref, out_ref):
+    out_ref[...] = times_weight(hidden_ref, weight_ref).astype(bf16)
+
+
+def own_kernel(hidden_ref, weight_ref, received_ref, *out_refs):
+    total = times_weight(hidden_ref, weight_ref) + received_ref[...].astype(f32)
+    rows = out_refs[0].shape[0]
+    for k, out_ref in enumerate(out_refs):
+        out_ref[...] = total[k * rows : (k + 1) * rows].astype(out_ref.dtype)
+
+
+def half_times_weight(kernel, place, grad_hidden, weight_in, received, out_shape):
+    half, depth = grad_hidden.shape[0] // 2, grad_hidden.shape[1]
+    width = weight_in.shape[0]
+    tile = width // 3
+    return pl.pallas_call(
+        kernel,
+        grid=(width // tile,),
+        in_specs=[
+            pl.BlockSpec((half, depth), lambda i: (place, 0)),
+            pl.BlockSpec((tile, depth), lambda i: (i, 0)),
+        ]
+        + [pl.BlockSpec((half, tile), lambda i: (0, i))] * len(received),
+        out_specs=[pl.BlockSpec((a.shape[0], tile), lambda i: (0, i)) for a in out_shape],
+        out_shape=out_shape,
+        compiler_params=vmem(32),
+        cost_estimate=pl.CostEstimate(
+            flops=2 * half * depth * width,
+            bytes_accessed=2 * (half * depth + depth * width + 2 * half * width),
+            transcendentals=0,
+        ),
+    )(grad_hidden, weight_in, *received)
+
+
 def solution(mesh):
     n_x, n_y, n_z = (mesh.shape[a] for a in ("gx", "gy", "gz"))
 
@@ -54,10 +141,7 @@
         return sums[:1] + [a.astype(bf16) for a in sums[1:]]
 
     def exchange(parts, shift):
-        return parts[:1] + [shift(part, -k) for k, part in enumerate(parts) if k]
-
-    def copies(share):
-        return jnp.broadcast_to(share[None], (n_x, *share.shape))
+        return [shift(part, -k) if k else part for k, part in enumerate(parts)]
 
     def trade_width(parts):
         return lax.all_to_all(parts, "gx", 0, 0, tiled=True)
@@ -77,50 +161,46 @@
         chunks = [
             jnp.stack([a[c * rows : (c + 1) * rows] for a in (tokens, grad_output)]) for c in range(2)
         ]
-
-        def partial_sums(near):
-            both = [jnp.concatenate([a, swap_core(a)], axis=0) for a in near]
+        bias = bias_hidden.reshape(1, -1)
+
+        def partial_sums(pieces):
+            both = [jnp.concatenate([a, swap_core(a)], axis=0) for a in join(pieces)]
             pre_part = jnp.dot(both[0], weight_in, preferred_element_type=f32).astype(bf16)
             up_part = contract_last(both[1], weight_out).astype(bf16)
             parts = [a.reshape(n_x, 1, -1, a.shape[1]) for a in (pre_part, up_part)]
             return both, jnp.concatenate(parts, axis=1)
 
-        def hidden(parts):
-            sums = jnp.sum(parts.astype(f32), axis=0)
-            return gelu_pair(sums[0] + bias_hidden, sums[1])
+        def other_rows(grad_hidden):
+            shape = jax.ShapeDtypeStruct((grad_hidden.shape[0] // 2, weight_in.shape[0]), bf16)
+            return half_times_weight(other_kernel, 1, grad_hidden, weight_in, [], [shape])[0]
+
+        def own_rows(grad_hidden, received):
+            shape = (received.shape[0] // n_chip, received.shape[1])
+            shapes = [jax.ShapeDtypeStruct(shape, bf16 if k else f32) for k in range(n_chip)]
+            return half_times_weight(own_kernel, 0, grad_hidden, weight_in, [received], shapes)
 
         far0 = join(groups(chunks[0]))
-        groups1 = groups(after(chunks[1], far0))
-        chips0, groups1 = barrier([far0] + [shift_chip(far0, k) for k in range(1, n_chip)], groups1)
-        far1 = join(groups1)
-        both0, part0 = partial_sums(join(chips0))
-        chips1 = [far1] + [
-            shift_chip(far1, k) for k in range(1, n_chip)
-        ]
-        both1, part1 = partial_sums(join(chips1))
+        far1 = join(groups(after(chunks[1], far0)))
+        chips0, far1 = barrier([far0] + [shift_chip(far0, k) for k in range(1, n_chip)], far1)
+        both0, part0 = partial_sums(chips0)
+        both1, part1 = partial_sums([far1] + [shift_chip(far1, k) for k in range(1, n_chip)])
         sums0 = trade_width(part0)
         sums1 = trade_width(part1)
-        act0, grad0 = hidden(sums0)
-        copies0, sums1 = barrier(copies(grad0), sums1)
-        act1, grad1 = hidden(sums1)
-        act_copies = copies(jnp.stack([act0, act1]))
-
-        def two_halves(grad_hidden):
-            half = grad_hidden.shape[0] // 2
-            other = contract_last(grad_hidden[half:], weight_in).astype(bf16)
-            return other, contract_last(grad_hidden[:half], weight_in)
-
-        hidden0 = trade_width(copies0).reshape(-1, act0.shape[1])
-        hidden1 = trade_width(after(copies(grad1), hidden0)).reshape(-1, act0.shape[1])
-        other0, own0 = two_halves(hidden0)
-        own0, other0 = barrier(own0, swap_core(other0))
-        parts0, act_copies = barrier(sum_blocks([own0, other0], n_chip), act_copies)
+        grad_copies0, act0 = hidden(sums0, bias)
+        grad_copies0, sums1 = barrier(grad_copies0, sums1)
+        grad_copies1, act_copies = hidden(sums1, bias, act0)
+        columns = act0.shape[1]
+        hidden0 = trade_width(grad_copies0)
+        hidden0, grad_copies1 = barrier(hidden0, grad_copies1)
+        hidden1 = trade_width(grad_copies1).reshape(-1, columns)
+        hidden0 = hidden0.reshape(-1, columns)
+        parts0 = own_rows(hidden0, swap_core(other_rows(hidden0)))
         parts0 = exchange(parts0, shift_chip)
-        other1, own1 = two_halves(hidden1)
-        parts0, other1, act_copies = barrier(parts0, other1, act_copies)
+        other1 = other_rows(hidden1)
+        parts0[: n_chip - 1], other1, act_copies = barrier(parts0[: n_chip - 1], other1, act_copies)
         activation = trade_width(act_copies)
-        own1, other1 = barrier(own1, swap_core(other1))
-        parts1, hidden0, hidden1 = barrier(sum_blocks([own1, other1], n_chip), hidden0, hidden1)
+        parts1 = own_rows(hidden1, swap_core(other1))
+        parts0, parts1, hidden0, hidden1 = barrier(parts0, parts1, hidden0, hidden1)
         parts1 = exchange(parts1, shift_chip)
         hidden_all = jnp.concatenate([hidden0, hidden1], axis=0)
         tokens_all = jnp.concatenate([both0[0], both1[0]], axis=0)
@@ -131,7 +211,7 @@
             for pair in zip(sum_blocks(parts0, n_y), sum_blocks(parts1, n_y))
         ]
         parts = exchange(parts, shift_y)
-        activation = activation.transpose(1, 0, 2, 3).reshape(-1, act0.shape[1])
+        activation = activation.transpose(1, 0, 2, 3).reshape(-1, columns)
         grad_all = jnp.concatenate([both0[1], both1[1]], axis=0)
         grad_weight_out = (contract_first(activation, grad_all) * norm_scale).astype(bf16)
         parts, grad_weight_out = barrier(parts, grad_weight_out)

time: 188 us -> 190 us (1.011)
  Pallas kernels: 0 us -> 14.6 us
  other arithmetic: 10.7 us -> 4.53 us
  matrix products: 19.7 us -> 14.6 us
  starting transfers between devices: 69.3 us -> 64.8 us
  waiting for transfers between devices: 68.2 us -> 71.9 us
    pallas_call x0 -> x6, Pallas kernels: none -> 14.6 us  [the longest x4 9.71 us: half_times_weight(): pl.pallas_call(kernel, grid=(width // tile,), in_specs=[pl.BlockSpec((hal...]
    ppermute x12, waiting for transfers between devices: 16.5 us -> 24.8 us  [shift_chip(): return lax.ppermute(a, 'gz', [(i, (i + 2 * k) % n_z) for i in range(n_z)])]
    unnamed x48 -> x60, local copies, waits for them, and re-layouts: 6.33 us -> 12.7 us
    all_to_all x5, waiting for transfers between devices: 31.5 us -> 25.2 us  [trade_width(): return lax.all_to_all(parts, 'gx', 0, 0, tiled=True)]
    dot_general x6 -> x2, matrix products: 7.95 us -> 2.85 us  [contract_last(): lax.dot_general(left, right, (((1,), (1,)), ((), ())), preferred_element_...]
    ppermute x9, starting transfers between devices: 26.7 us -> 22.2 us  [shift_y(): return lax.ppermute(a, 'gy', [(i, (i + k) % n_y) for i in range(n_y)])]
    reduce_sum x2 -> x0, other arithmetic: 3.32 us -> none  [hidden(): sums = jnp.sum(parts.astype(f32), axis=0)]
    broadcast_in_dim x3 -> x0, local copies, waits for them, and re-layouts: 3.17 us -> none  [copies(): return jnp.broadcast_to(share[None], (n_x, *share.shape))]
  transfers between devices with their start and end apart: 32 -> 32, of which waited for: 18 -> 20; matrix products, arithmetic and copies ran while one was open for 23% -> 14% of each run, Pallas kernels for 0% -> 8%
where the time goes in v7:
time: 190 us; the launch traced here: 189 us
  waiting for transfers between devices  71.9 us (38%)
  starting transfers between devices  64.8 us (34%)
  local copies, waits for them, and re-layouts  17.9 us (9%)
  matrix products  14.6 us (8%)
  Pallas kernels  14.6 us (8%)
  other arithmetic  4.53 us (2%)
    all_to_all x5, starting transfers between devices, trade_width(): return lax.all_to_all(parts, 'gx', 0, 0, tiled=True)  26.6 us
    all_to_all x5, waiting for transfers between devices, trade_width(): return lax.all_to_all(parts, 'gx', 0, 0, tiled=True)  25.2 us
    ppermute x12, waiting for transfers between devices, shift_chip(): return lax.ppermute(a, 'gz', [(i, (i + 2 * k) % n_z) for i in range(n_z)])  24.8 us
    ppermute x9, starting transfers between devices, shift_y(): return lax.ppermute(a, 'gy', [(i, (i + k) % n_y) for i in range(n_y)])  22.2 us
    ppermute x9, waiting for transfers between devices, shift_y(): return lax.ppermute(a, 'gy', [(i, (i + k) % n_y) for i in range(n_y)])  17.9 us
    ppermute x12, starting transfers between devices, shift_chip(): return lax.ppermute(a, 'gz', [(i, (i + 2 * k) % n_z) for i in range(n_z)])  14.7 us
    unnamed x60, local copies, waits for them, and re-layouts  12.7 us
    pallas_call x4, Pallas kernels, half_times_weight(): pl.pallas_call(kernel, grid=(width // tile,), in_specs=[pl.BlockSpec((hal...  9.71 us
  transfers between devices with their start and end apart: 32, of which 20 were waited for; matrix products, arithmetic and copies ran while one was open for 14% of the time, Pallas kernels for 8%

profile of v7, /device:TPU:32, one launch (start us, length us, event | category | flops | bytes accessed | tf_op | source)
XLA Modules:
  0.0 189.5 jit_solution(13000179260134815428)
XLA Ops:
  0.6 1.0 slice_bitcast_fusion.4
  1.7 5.5 %collective-permute-start.2 = (bf16[2,16,1536]{2,1,0:T(8,128)(2,1)S(1)}, bf16[2,16,1536]{2,1,0:T(8,128)(2,1)S(1)}, u32[]{:S(2)}, u32[]{:S(2)}) collective-permute-start(bf16[2,16,1536]{2,1,0:T(8,128)(2,1)S(1)} %pad_maximum_fusion.5), channel_id=1, source_target_pairs={{0,24},{8,0},{16,8},{24,16},{1,25},{9,1},{17,9},{25,17},{2,26},{10... | collective-permute-start | bytes 294920 | tf_op jit(solution)/shard_map/ppermute | solution.py:122
  7.2 1.4 collective-permute-start.1
  8.6 2.4 %collective-permute-start = (bf16[2,16,1536]{2,1,0:T(8,128)(2,1)S(1)}, bf16[2,16,1536]{2,1,0:T(8,128)(2,1)S(1)}, u32[]{:S(2)}, u32[]{:S(2)}) collective-permute-start(bf16[2,16,1536]{2,1,0:T(8,128)(2,1)S(1)} %pad_maximum_fusion.5), channel_id=1, source_target_pairs={{0,8},{8,16},{16,24},{24,0},{1,9},{9,17},{17,25},{25,1},{2,10},{10... | collective-permute-start | bytes 294920 | tf_op jit(solution)/shard_map/ppermute | solution.py:122
  11.0 7.0 %collective-permute-done.1 = bf16[2,16,1536]{2,1,0:T(8,128)(2,1)S(1)} collective-permute-done((bf16[2,16,1536]{2,1,0:T(8,128)(2,1)S(1)}, bf16[2,16,1536]{2,1,0:T(8,128)(2,1)S(1)}, u32[]{:S(2)}, u32[]{:S(2)}) %collective-permute-start.1) | collective-permute-done | bytes 98336 | tf_op jit(solution)/shard_map/ppermute | solution.py:122
  18.7 3.7 %collective-permute-start.8 = (bf16[2,16,1536]{2,1,0:T(8,128)(2,1)S(1)}, bf16[2,16,1536]{2,1,0:T(8,128)(2,1)S(1)}, u32[]{:S(2)}, u32[]{:S(2)}) collective-permute-start(bf16[2,16,1536]{2,1,0:T(8,128)(2,1)S(1)} %pad_maximum_fusion.6), channel_id=1, source_target_pairs={{0,24},{8,0},{16,8},{24,16},{1,25},{9,1},{17,9},{25,17},{2,26},{10... | collective-permute-start | bytes 294920 | tf_op jit(solution)/shard_map/ppermute | solution.py:122
  22.4 2.8 %collective-permute-start.5 = (bf16[2,64,1536]{2,1,0:T(8,128)(2,1)S(1)}, bf16[2,64,1536]{2,1,0:T(8,128)(2,1)S(1)}, u32[]{:S(2)}, u32[]{:S(2)}) collective-permute-start(bf16[2,64,1536]{2,1,0:T(8,128)(2,1)S(1)} %pad_maximum_fusion.2), channel_id=1, source_target_pairs={{0,6},{1,7},{2,0},{3,1},{4,2},{5,3},{6,4},{7,5},{8,14},{9,15},{10,... | collective-permute-start | bytes 1179656 | tf_op jit(solution)/shard_map/ppermute | solution.py:125
  25.1 0.8 collective-permute-start.4
  25.9 0.9 collective-permute-start.3
  26.8 1.7 collective-permute-start.7
  28.5 2.4 %collective-permute-start.6 = (bf16[2,16,1536]{2,1,0:T(8,128)(2,1)S(1)}, bf16[2,16,1536]{2,1,0:T(8,128)(2,1)S(1)}, u32[]{:S(2)}, u32[]{:S(2)}) collective-permute-start(bf16[2,16,1536]{2,1,0:T(8,128)(2,1)S(1)} %pad_maximum_fusion.6), channel_id=1, source_target_pairs={{0,8},{8,16},{16,24},{24,0},{1,9},{9,17},{17,25},{25,1},{2,10},{10... | collective-permute-start | bytes 294920 | tf_op jit(solution)/shard_map/ppermute | solution.py:122
  30.9 5.3 %collective-permute-done.7 = bf16[2,16,1536]{2,1,0:T(8,128)(2,1)S(1)} collective-permute-done((bf16[2,16,1536]{2,1,0:T(8,128)(2,1)S(1)}, bf16[2,16,1536]{2,1,0:T(8,128)(2,1)S(1)}, u32[]{:S(2)}, u32[]{:S(2)}) %collective-permute-start.7) | collective-permute-done | bytes 98336 | tf_op jit(solution)/shard_map/ppermute | solution.py:122
  36.2 1.0 collective-permute-done.6
  37.3 4.1 %collective-permute-done.5 = bf16[2,64,1536]{2,1,0:T(8,128)(2,1)S(1)} collective-permute-done((bf16[2,64,1536]{2,1,0:T(8,128)(2,1)S(1)}, bf16[2,64,1536]{2,1,0:T(8,128)(2,1)S(1)}, u32[]{:S(2)}, u32[]{:S(2)}) %collective-permute-start.5) | collective-permute-done | bytes 393248 | tf_op jit(solution)/shard_map/ppermute | solution.py:125
  41.4 3.7 %collective-permute-done.3 = bf16[2,64,1536]{2,1,0:T(8,128)(2,1)S(1)} collective-permute-done((bf16[2,64,1536]{2,1,0:T(8,128)(2,1)S(1)}, bf16[2,64,1536]{2,1,0:T(8,128)(2,1)S(1)}, u32[]{:S(2)}, u32[]{:S(2)}) %collective-permute-start.3) | collective-permute-done | bytes 393248 | tf_op jit(solution)/shard_map/ppermute | solution.py:125
  46.5 0.8 collective-permute-start.12
  47.3 0.8 collective-permute-start.11
  48.9 1.4 fusion.42
  50.4 1.4 fusion.39
  51.8 1.3 pad_maximum_fusion
  53.1 5.9 %all-to-all-start = ((bf16[8,2,64,768]{3,2,1,0:T(8,128)(2,1)}), bf16[8,2,64,768]{3,2,1,0:T(8,128)(2,1)}, u32[]{:S(2)}, u32[]{:S(2)}) async-start(bf16[8,2,64,768]{3,2,1,0:T(8,128)(2,1)} %pad_maximum_fusion), calls=%async_computation | async-start | bytes 3145728 | tf_op jit(solution)/shard_map/all_to_all | solution.py:147
  59.0 8.4 %collective-permute-done.11 = bf16[2,64,1536]{2,1,0:T(8,128)(2,1)} collective-permute-done((bf16[2,64,1536]{2,1,0:T(8,128)(2,1)S(1)}, bf16[2,64,1536]{2,1,0:T(8,128)(2,1)}, u32[]{:S(2)}, u32[]{:S(2)}) %collective-permute-start.11) | collective-permute-done | bytes 393248 | tf_op jit(solution)/shard_map/ppermute | solution.py:125
  67.4 1.8 constant_dynamic-update-slice_fusion.6
  69.2 0.8 constant_dynamic-update-slice_fusion.5
  70.7 1.6 slice_bitcast_fusion.1
  73.0 1.8 collective-permute-done.14
  74.8 1.4 fusion.36
  76.2 1.4 fusion.33
  77.6 1.3 pad_maximum_fusion.1
  78.9 6.1 %all-to-all-start.1 = ((bf16[8,2,64,768]{3,2,1,0:T(8,128)(2,1)}), bf16[8,2,64,768]{3,2,1,0:T(8,128)(2,1)}, u32[]{:S(2)}, u32[]{:S(2)}) async-start(bf16[8,2,64,768]{3,2,1,0:T(8,128)(2,1)} %pad_maximum_fusion.1), calls=%async_computation.1 | async-start | bytes 3145728 | tf_op jit(solution)/shard_map/all_to_all | solution.py:147
  85.0 2.4 %shard_map.76 = (bf16[8,64,768]{2,1,0:T(8,128)(2,1)S(1)}, bf16[64,768]{1,0:T(8,128)(2,1)S(1)}) custom-call(bf16[8,2,64,768]{3,2,1,0:T(8,128)(2,1)} %all-to-all-done.parts, f32[1,768]{1,0:T(1,128)S(1)} %reshape.32.bias), custom_call_target="tpu_custom_call" | custom-call | flops 1966080 | bytes 2359296 | tf_op jit(solution)/shard_map/pallas_call | solution.py:53
  87.4 0.9 copy-done.8
  88.3 16.9 %all-to-all-done.1.parts = bf16[8,2,64,768]{3,2,1,0:T(8,128)(2,1)} async-done(((bf16[8,2,64,768]{3,2,1,0:T(8,128)(2,1)}), bf16[8,2,64,768]{3,2,1,0:T(8,128)(2,1)}, u32[]{:S(2)}, u32[]{:S(2)}) %all-to-all-start.1) | async-done | bytes 1572896 | tf_op jit(solution)/shard_map/all_to_all | solution.py:147
  105.3 4.2 %all-to-all-start.2 = ((bf16[8,64,768]{2,1,0:T(8,128)(2,1)}), bf16[8,64,768]{2,1,0:T(8,128)(2,1)S(1)}, u32[]{:S(2)}, u32[]{:S(2)}) async-start(bf16[8,64,768]{2,1,0:T(8,128)(2,1)} %copy-done.8), calls=%async_computation.2 | async-start | bytes 1572864 | tf_op jit(solution)/shard_map/all_to_all | solution.py:147
  109.5 2.5 %shard_map.77 = (bf16[8,64,768]{2,1,0:T(8,128)(2,1)S(1)}, bf16[8,2,64,768]{3,2,1,0:T(8,128)(2,1)S(1)}) custom-call(bf16[8,2,64,768]{3,2,1,0:T(8,128)(2,1)} %all-to-all-done.1.parts, f32[1,768]{1,0:T(1,128)S(1)} %reshape.32.bias, bf16[64,768]{1,0:T(8,128)(2,1)S(1)} %get-tuple-element.63.refs_0_), custom_call_target="tpu_custom_call" | custom-call | flops 1966080 | bytes 2359296 | tf_op jit(solution)/shard_map/pallas_call | solution.py:53
  112.0 1.1 copy-done.6
  113.1 0.9 copy-done.7
  114.0 7.1 %all-to-all-done.2 = bf16[8,64,768]{2,1,0:T(8,128)(2,1)S(1)} async-done(((bf16[8,64,768]{2,1,0:T(8,128)(2,1)}), bf16[8,64,768]{2,1,0:T(8,128)(2,1)S(1)}, u32[]{:S(2)}, u32[]{:S(2)}) %all-to-all-start.2) | async-done | bytes 786464 | tf_op jit(solution)/shard_map/all_to_all | solution.py:147
  121.1 4.7 %all-to-all-start.3 = ((bf16[8,64,768]{2,1,0:T(8,128)(2,1)}), bf16[8,64,768]{2,1,0:T(8,128)(2,1)}, u32[]{:S(2)}, u32[]{:S(2)}) async-start(bf16[8,64,768]{2,1,0:T(8,128)(2,1)} %copy-done.7), calls=%async_computation.3 | async-start | bytes 1572864 | tf_op jit(solution)/shard_map/all_to_all | solution.py:147
  125.8 1.7 copy-done.3
  127.4 1.2 shard_map.78
  128.8 2.3 %collective-permute-done.16.received_ref = bf16[256,1536]{1,0:T(8,128)(2,1)S(1)} collective-permute-done((bf16[256,1536]{1,0:T(8,128)(2,1)S(1)}, bf16[256,1536]{1,0:T(8,128)(2,1)S(1)}, u32[]{:S(2)}, u32[]{:S(2)}) %collective-permute-start.16) | collective-permute-done | bytes 786464 | tf_op jit(solution)/shard_map/ppermute | solution.py:128
  131.0 2.2 %shard_map.79 = (f32[64,1536]{1,0:T(8,128)S(1)}, bf16[64,1536]{1,0:T(8,128)(2,1)}, bf16[64,1536]{1,0:T(8,128)(2,1)}, bf16[64,1536]{1,0:T(8,128)(2,1)S(1)}) custom-call(bf16[512,768]{1,0:T(8,128)(2,1)S(1)} %bitcast.30, bf16[1536,768]{1,0:T(8,128)(2,1)S(1)} %copy-done.3, bf16[256,1536]{1,0:T(8,128)(2,1)S(1)} %collective-permute-done.16.received_ref), custom_call_target="tpu_custom_call" | custom-call | flops 603979776 | bytes 4325376 | tf_op jit(solution)/shard_map/pallas_call | solution.py:99
  134.7 1.2 collective-permute-start.18
  135.8 1.1 all-to-all-done.3
  137.0 1.7 copy-done.4
  138.7 3.2 %shard_map.80 = bf16[256,1536]{1,0:T(8,128)(2,1)} custom-call(bf16[512,768]{1,0:T(8,128)(2,1)} %bitcast.13.hidden_ref, bf16[1536,768]{1,0:T(8,128)(2,1)S(1)} %copy-done.4), custom_call_target="tpu_custom_call" | custom-call | flops 603979776 | bytes 4325376 | tf_op jit(solution)/shard_map/pallas_call | solution.py:99
  142.0 1.2 collective-permute-done.18
  143.1 5.7 %all-to-all-start.4 = ((bf16[8,2,64,768]{3,2,1,0:T(8,128)(2,1)}), bf16[8,2,64,768]{3,2,1,0:T(8,128)(2,1)}, u32[]{:S(2)}, u32[]{:S(2)}) async-start(bf16[8,2,64,768]{3,2,1,0:T(8,128)(2,1)} %copy-done.6), calls=%async_computation.4 | async-start | bytes 3145728 | tf_op jit(solution)/shard_map/all_to_all | solution.py:147
  148.9 3.6 %collective-permute-start.19 = (bf16[64,1536]{1,0:T(8,128)(2,1)}, bf16[64,1536]{1,0:T(8,128)(2,1)S(1)}, u32[]{:S(2)}, u32[]{:S(2)}) collective-permute-start(bf16[64,1536]{1,0:T(8,128)(2,1)} %copy-done.9), channel_id=1, source_target_pairs={{0,2},{1,3},{2,4},{3,5},{4,6},{5,7},{6,0},{7,1},{8,10},{9,11},{10,... | collective-permute-start | bytes 589832 | tf_op jit(solution)/shard_map/ppermute | solution.py:125
  152.4 1.7 copy-done.5
  154.1 3.1 %shard_map.81 = (f32[64,1536]{1,0:T(8,128)S(1)}, bf16[64,1536]{1,0:T(8,128)(2,1)S(1)}, bf16[64,1536]{1,0:T(8,128)(2,1)S(1)}, bf16[64,1536]{1,0:T(8,128)(2,1)S(1)}) custom-call(bf16[512,768]{1,0:T(8,128)(2,1)} %bitcast.13.hidden_ref, bf16[1536,768]{1,0:T(8,128)(2,1)S(1)} %copy-done.5, bf16[256,1536]{1,0:T(8,128)(2,1)} %collective-permute-done.20.received_ref), custom_call_target="tpu_custom_call" | custom-call | flops 603979776 | bytes 4325376 | tf_op jit(solution)/shard_map/pallas_call | solution.py:99
  157.2 1.8 collective-permute-done.19
  159.0 1.7 collective-permute-start.21
  161.6 5.1 %multiply_convert_fusion.1 = bf16[1536,768]{1,0:T(8,128)(2,1)} fusion(bf16[256,1536]{1,0:T(8,128)(2,1)S(1)} %copy-done.26, bf16[256,1536]{1,0:T(8,128)(2,1)S(1)} %copy-done.17, bf16[256,1536]{1,0:T(8,128)(2,1)S(1)} %copy-done.24, bf16[256,1536]{1,0:T(8,128)(2,1)S(1)} %copy-done.15, bf16[512,768]{1,0:T(8,128)(2,1)} %bitcast.13.hidden_ref, ...), kind=kOutput, calls=%fused_computation.1 | convolution fusion | flops 2434007040 | bytes 7077888 | tf_op jit(solution)/shard_map/dot_general | solution.py:30
  166.9 3.3 %collective-permute-done.22 = bf16[64,1536]{1,0:T(8,128)(2,1)S(1)} collective-permute-done((bf16[64,1536]{1,0:T(8,128)(2,1)S(1)}, bf16[64,1536]{1,0:T(8,128)(2,1)S(1)}, u32[]{:S(2)}, u32[]{:S(2)}) %collective-permute-start.22) | collective-permute-done | bytes 196640 | tf_op jit(solution)/shard_map/ppermute | solution.py:125
  170.1 2.1 %collective-permute-done.23 = bf16[64,1536]{1,0:T(8,128)(2,1)S(1)} collective-permute-done((bf16[64,1536]{1,0:T(8,128)(2,1)S(1)}, bf16[64,1536]{1,0:T(8,128)(2,1)S(1)}, u32[]{:S(2)}, u32[]{:S(2)}) %collective-permute-start.23) | collective-permute-done | bytes 196640 | tf_op jit(solution)/shard_map/ppermute | solution.py:125
  172.2 1.1 add_convert_fusion.2
  173.4 2.1 %collective-permute-start.24 = (bf16[32,1536]{1,0:T(8,128)(2,1)S(1)}, bf16[32,1536]{1,0:T(8,128)(2,1)S(1)}, u32[]{:S(2)}, u32[]{:S(2)}) collective-permute-start(bf16[32,1536]{1,0:T(8,128)(2,1)S(1)} %pad_maximum_fusion.7), channel_id=1, source_target_pairs={{0,24},{8,0},{16,8},{24,16},{1,25},{9,1},{17,9},{25,17},{2,26},{10... | collective-permute-start | bytes 294920 | tf_op jit(solution)/shard_map/ppermute | solution.py:122
  175.8 2.6 %collective-permute-start.26 = (bf16[32,1536]{1,0:T(8,128)(2,1)S(1)}, bf16[32,1536]{1,0:T(8,128)(2,1)S(1)}, u32[]{:S(2)}, u32[]{:S(2)}) collective-permute-start(bf16[32,1536]{1,0:T(8,128)(2,1)S(1)} %pad_maximum_fusion.9), channel_id=1, source_target_pairs={{0,8},{8,16},{16,24},{24,0},{1,9},{9,17},{17,25},{25,1},{2,10},{10... | collective-permute-start | bytes 294920 | tf_op jit(solution)/shard_map/ppermute | solution.py:122
  178.5 1.7 copy.8
  180.8 3.9 %multiply_convert_fusion = bf16[768,1536]{1,0:T(8,128)(2,1)} fusion(bf16[1024,768]{1,0:T(8,128)(2,1)S(1)} %bitcast.32, bf16[256,1536]{1,0:T(8,128)(2,1)S(1)} %copy-done.22, bf16[256,1536]{1,0:T(8,128)(2,1)S(1)} %copy-done.13, bf16[256,1536]{1,0:T(8,128)(2,1)S(1)} %copy-done.20, bf16[256,1536]{1,0:T(8,128)(2,1)S(1)} %copy-done.11), kind=kOutput, calls=%fused_computation | convolution fusion | flops 2430861312 | bytes 7077888 | tf_op jit(solution)/shard_map/dot_general | solution.py:30
  184.8 1.2 collective-permute-done.25
  185.9 2.8 %collective-permute-done.26 = bf16[32,1536]{1,0:T(8,128)(2,1)S(1)} collective-permute-done((bf16[32,1536]{1,0:T(8,128)(2,1)S(1)}, bf16[32,1536]{1,0:T(8,128)(2,1)S(1)}, u32[]{:S(2)}, u32[]{:S(2)}) %collective-permute-start.26) | collective-permute-done | bytes 98336 | tf_op jit(solution)/shard_map/ppermute | solution.py:122
  (92 shorter events, 8.7 us)
Async XLA Ops:
  0.6 49.7 %copy-start = (bf16[768,1536]{1,0:T(8,128)(2,1)S(1)}, bf16[768,1536]{1,0:T(8,128)(2,1)}, u32[]{:S(2)}) copy-start(bf16[768,1536]{1,0:T(8,128)(2,1)} %param.8) | copy-start | bytes 7077892
  1.7 9.3 %collective-permute-start.2 = (bf16[2,16,1536]{2,1,0:T(8,128)(2,1)S(1)}, bf16[2,16,1536]{2,1,0:T(8,128)(2,1)S(1)}, u32[]{:S(2)}, u32[]{:S(2)}) collective-permute-start(bf16[2,16,1536]{2,1,0:T(8,128)(2,1)S(1)} %pad_maximum_fusion.5), channel_id=1, source_target_pairs={{0,24},{8,0},{16,8},{24,16},{1,25},{9,1},{17,9},{25,17},{2,26},{10... | collective-permute-start | bytes 294920 | tf_op jit(solution)/shard_map/ppermute | solution.py:122
  7.2 10.9 %collective-permute-start.1 = (bf16[2,16,1536]{2,1,0:T(8,128)(2,1)S(1)}, bf16[2,16,1536]{2,1,0:T(8,128)(2,1)S(1)}, u32[]{:S(2)}, u32[]{:S(2)}) collective-permute-start(bf16[2,16,1536]{2,1,0:T(8,128)(2,1)S(1)} %pad_maximum_fusion.5), channel_id=1, source_target_pairs={{0,16},{8,24},{16,0},{24,8},{1,17},{9,25},{17,1},{25,9},{2,18},{10... | collective-permute-start | bytes 294920 | tf_op jit(solution)/shard_map/ppermute | solution.py:122
  8.6 10.0 %collective-permute-start = (bf16[2,16,1536]{2,1,0:T(8,128)(2,1)S(1)}, bf16[2,16,1536]{2,1,0:T(8,128)(2,1)S(1)}, u32[]{:S(2)}, u32[]{:S(2)}) collective-permute-start(bf16[2,16,1536]{2,1,0:T(8,128)(2,1)S(1)} %pad_maximum_fusion.5), channel_id=1, source_target_pairs={{0,8},{8,16},{16,24},{24,0},{1,9},{9,17},{17,25},{25,1},{2,10},{10... | collective-permute-start | bytes 294920 | tf_op jit(solution)/shard_map/ppermute | solution.py:122
  18.7 9.9 %collective-permute-start.8 = (bf16[2,16,1536]{2,1,0:T(8,128)(2,1)S(1)}, bf16[2,16,1536]{2,1,0:T(8,128)(2,1)S(1)}, u32[]{:S(2)}, u32[]{:S(2)}) collective-permute-start(bf16[2,16,1536]{2,1,0:T(8,128)(2,1)S(1)} %pad_maximum_fusion.6), channel_id=1, source_target_pairs={{0,24},{8,0},{16,8},{24,16},{1,25},{9,1},{17,9},{25,17},{2,26},{10... | collective-permute-start | bytes 294920 | tf_op jit(solution)/shard_map/ppermute | solution.py:122
  22.4 19.0 %collective-permute-start.5 = (bf16[2,64,1536]{2,1,0:T(8,128)(2,1)S(1)}, bf16[2,64,1536]{2,1,0:T(8,128)(2,1)S(1)}, u32[]{:S(2)}, u32[]{:S(2)}) collective-permute-start(bf16[2,64,1536]{2,1,0:T(8,128)(2,1)S(1)} %pad_maximum_fusion.2), channel_id=1, source_target_pairs={{0,6},{1,7},{2,0},{3,1},{4,2},{5,3},{6,4},{7,5},{8,14},{9,15},{10,... | collective-permute-start | bytes 1179656 | tf_op jit(solution)/shard_map/ppermute | solution.py:125
  25.1 16.2 %collective-permute-start.4 = (bf16[2,64,1536]{2,1,0:T(8,128)(2,1)S(1)}, bf16[2,64,1536]{2,1,0:T(8,128)(2,1)S(1)}, u32[]{:S(2)}, u32[]{:S(2)}) collective-permute-start(bf16[2,64,1536]{2,1,0:T(8,128)(2,1)S(1)} %pad_maximum_fusion.2), channel_id=1, source_target_pairs={{0,4},{1,5},{2,6},{3,7},{4,0},{5,1},{6,2},{7,3},{8,12},{9,13},{10,... | collective-permute-start | bytes 1179656 | tf_op jit(solution)/shard_map/ppermute | solution.py:125
  25.9 19.1 %collective-permute-start.3 = (bf16[2,64,1536]{2,1,0:T(8,128)(2,1)S(1)}, bf16[2,64,1536]{2,1,0:T(8,128)(2,1)S(1)}, u32[]{:S(2)}, u32[]{:S(2)}) collective-permute-start(bf16[2,64,1536]{2,1,0:T(8,128)(2,1)S(1)} %pad_maximum_fusion.2), channel_id=1, source_target_pairs={{0,2},{1,3},{2,4},{3,5},{4,6},{5,7},{6,0},{7,1},{8,10},{9,11},{10,... | collective-permute-start | bytes 1179656 | tf_op jit(solution)/shard_map/ppermute | solution.py:125
  26.8 9.4 %collective-permute-start.7 = (bf16[2,16,1536]{2,1,0:T(8,128)(2,1)S(1)}, bf16[2,16,1536]{2,1,0:T(8,128)(2,1)S(1)}, u32[]{:S(2)}, u32[]{:S(2)}) collective-permute-start(bf16[2,16,1536]{2,1,0:T(8,128)(2,1)S(1)} %pad_maximum_fusion.6), channel_id=1, source_target_pairs={{0,16},{8,24},{16,0},{24,8},{1,17},{9,25},{17,1},{25,9},{2,18},{10... | collective-permute-start | bytes 294920 | tf_op jit(solution)/shard_map/ppermute | solution.py:122
  28.5 8.7 %collective-permute-start.6 = (bf16[2,16,1536]{2,1,0:T(8,128)(2,1)S(1)}, bf16[2,16,1536]{2,1,0:T(8,128)(2,1)S(1)}, u32[]{:S(2)}, u32[]{:S(2)}) collective-permute-start(bf16[2,16,1536]{2,1,0:T(8,128)(2,1)S(1)} %pad_maximum_fusion.6), channel_id=1, source_target_pairs={{0,8},{8,16},{16,24},{24,0},{1,9},{9,17},{17,25},{25,1},{2,10},{10... | collective-permute-start | bytes 294920 | tf_op jit(solution)/shard_map/ppermute | solution.py:122
  45.2 3.7 %copy-start.1 = (bf16[1536,768]{1,0:T(8,128)(2,1)S(1)}, bf16[1536,768]{1,0:T(8,128)(2,1)}, u32[]{:S(2)}) copy-start(bf16[1536,768]{1,0:T(8,128)(2,1)} %weight_ref.7) | copy-start | bytes 7077892
  45.3 5.0 %copy-start.14 = (bf16[256,1536]{1,0:T(8,128)(2,1)}, bf16[256,1536]{1,0:T(8,128)(2,1)S(1)}, u32[]{:S(2)}) copy-start(bf16[256,1536]{1,0:T(8,128)(2,1)S(1)} %get-tuple-element.107) | copy-start | bytes 2359300
  45.3 5.0 %copy-start.10 = (bf16[256,1536]{1,0:T(8,128)(2,1)}, bf16[256,1536]{1,0:T(8,128)(2,1)S(1)}, u32[]{:S(2)}) copy-start(bf16[256,1536]{1,0:T(8,128)(2,1)S(1)} %get-tuple-element.108) | copy-start | bytes 2359300
  45.3 3.6 %collective-permute-start.9 = (bf16[256,1536]{1,0:T(8,128)(2,1)S(1)}, bf16[256,1536]{1,0:T(8,128)(2,1)S(1)}, u32[]{:S(2)}, u32[]{:S(2)}) collective-permute-start(bf16[256,1536]{1,0:T(8,128)(2,1)S(1)} %get-tuple-element.107), channel_id=1, source_target_pairs={{0,1},{1,0},{2,3},{3,2},{4,5},{5,4},{6,7},{7,6},{8,9},{9,8},{10,11... | collective-permute-start | bytes 2359304 | tf_op jit(solution)/shard_map/ppermute | solution.py:128
  45.4 4.9 %collective-permute-start.10 = (bf16[256,1536]{1,0:T(8,128)(2,1)S(1)}, bf16[256,1536]{1,0:T(8,128)(2,1)S(1)}, u32[]{:S(2)}, u32[]{:S(2)}) collective-permute-start(bf16[256,1536]{1,0:T(8,128)(2,1)S(1)} %get-tuple-element.108), channel_id=1, source_target_pairs={{0,1},{1,0},{2,3},{3,2},{4,5},{5,4},{6,7},{7,6},{8,9},{9,8},{10,11... | collective-permute-start | bytes 2359304 | tf_op jit(solution)/shard_map/ppermute | solution.py:128
  45.9 24.0 %collective-permute-start.13 = (bf16[2,64,1536]{2,1,0:T(8,128)(2,1)S(1)}, bf16[2,64,1536]{2,1,0:T(8,128)(2,1)S(1)}, u32[]{:S(2)}, u32[]{:S(2)}) collective-permute-start(bf16[2,64,1536]{2,1,0:T(8,128)(2,1)S(1)} %pad_maximum_fusion.3), channel_id=1, source_target_pairs={{0,6},{1,7},{2,0},{3,1},{4,2},{5,3},{6,4},{7,5},{8,14},{9,15},{10,... | collective-permute-start | bytes 1179656 | tf_op jit(solution)/shard_map/ppermute | solution.py:125
  46.5 22.6 %collective-permute-start.12 = (bf16[2,64,1536]{2,1,0:T(8,128)(2,1)S(1)}, bf16[2,64,1536]{2,1,0:T(8,128)(2,1)S(1)}, u32[]{:S(2)}, u32[]{:S(2)}) collective-permute-start(bf16[2,64,1536]{2,1,0:T(8,128)(2,1)S(1)} %pad_maximum_fusion.3), channel_id=1, source_target_pairs={{0,4},{1,5},{2,6},{3,7},{4,0},{5,1},{6,2},{7,3},{8,12},{9,13},{10,... | collective-permute-start | bytes 1179656 | tf_op jit(solution)/shard_map/ppermute | solution.py:125
  47.3 20.1 %collective-permute-start.11 = (bf16[2,64,1536]{2,1,0:T(8,128)(2,1)S(1)}, bf16[2,64,1536]{2,1,0:T(8,128)(2,1)}, u32[]{:S(2)}, u32[]{:S(2)}) collective-permute-start(bf16[2,64,1536]{2,1,0:T(8,128)(2,1)S(1)} %pad_maximum_fusion.3), channel_id=1, source_target_pairs={{0,2},{1,3},{2,4},{3,5},{4,6},{5,7},{6,0},{7,1},{8,10},{9,11},{10,... | collective-permute-start | bytes 1179656 | tf_op jit(solution)/shard_map/ppermute | solution.py:125
  48.9 1.4 copy-start.23
  50.4 1.4 copy-start.19
  53.1 25.8 %all-to-all-start = ((bf16[8,2,64,768]{3,2,1,0:T(8,128)(2,1)}), bf16[8,2,64,768]{3,2,1,0:T(8,128)(2,1)}, u32[]{:S(2)}, u32[]{:S(2)}) async-start(bf16[8,2,64,768]{3,2,1,0:T(8,128)(2,1)} %pad_maximum_fusion), calls=%async_computation | async-start | bytes 3145728 | tf_op jit(solution)/shard_map/all_to_all | solution.py:147
  70.7 4.0 %copy-start.2 = (bf16[1536,768]{1,0:T(8,128)(2,1)S(1)}, bf16[1536,768]{1,0:T(8,128)(2,1)}, u32[]{:S(2)}) copy-start(bf16[1536,768]{1,0:T(8,128)(2,1)} %weight_ref.7) | copy-start | bytes 7077892
  72.4 3.8 %copy-start.16 = (bf16[256,1536]{1,0:T(8,128)(2,1)}, bf16[256,1536]{1,0:T(8,128)(2,1)S(1)}, u32[]{:S(2)}) copy-start(bf16[256,1536]{1,0:T(8,128)(2,1)S(1)} %get-tuple-element.105) | copy-start | bytes 2359300
  72.4 3.8 %copy-start.12 = (bf16[256,1536]{1,0:T(8,128)(2,1)}, bf16[256,1536]{1,0:T(8,128)(2,1)S(1)}, u32[]{:S(2)}) copy-start(bf16[256,1536]{1,0:T(8,128)(2,1)S(1)} %get-tuple-element.106) | copy-start | bytes 2359300
  72.4 2.4 %collective-permute-start.14 = (bf16[256,1536]{1,0:T(8,128)(2,1)S(1)}, bf16[256,1536]{1,0:T(8,128)(2,1)S(1)}, u32[]{:S(2)}, u32[]{:S(2)}) collective-permute-start(bf16[256,1536]{1,0:T(8,128)(2,1)S(1)} %get-tuple-element.105), channel_id=1, source_target_pairs={{0,1},{1,0},{2,3},{3,2},{4,5},{5,4},{6,7},{7,6},{8,9},{9,8},{10,11... | collective-permute-start | bytes 2359304 | tf_op jit(solution)/shard_map/ppermute | solution.py:128
  72.5 3.7 %collective-permute-start.15 = (bf16[256,1536]{1,0:T(8,128)(2,1)S(1)}, bf16[256,1536]{1,0:T(8,128)(2,1)S(1)}, u32[]{:S(2)}, u32[]{:S(2)}) collective-permute-start(bf16[256,1536]{1,0:T(8,128)(2,1)S(1)} %get-tuple-element.106), channel_id=1, source_target_pairs={{0,1},{1,0},{2,3},{3,2},{4,5},{5,4},{6,7},{7,6},{8,9},{9,8},{10,11... | collective-permute-start | bytes 2359304 | tf_op jit(solution)/shard_map/ppermute | solution.py:128
  74.8 1.4 copy-start.25
  76.2 1.4 copy-start.21
  78.9 6.1 %copy-start.18 = (f32[768]{0:T(1024)S(1)}, f32[768]{0:T(1024)}, u32[]{:S(2)}) copy-start(f32[768]{0:T(1024)} %param.7) | copy-start | bytes 9220
  78.9 26.3 %all-to-all-start.1 = ((bf16[8,2,64,768]{3,2,1,0:T(8,128)(2,1)}), bf16[8,2,64,768]{3,2,1,0:T(8,128)(2,1)}, u32[]{:S(2)}, u32[]{:S(2)}) async-start(bf16[8,2,64,768]{3,2,1,0:T(8,128)(2,1)} %pad_maximum_fusion.1), calls=%async_computation.1 | async-start | bytes 3145728 | tf_op jit(solution)/shard_map/all_to_all | solution.py:147
  87.4 0.9 copy-start.8
  105.3 15.8 %all-to-all-start.2 = ((bf16[8,64,768]{2,1,0:T(8,128)(2,1)}), bf16[8,64,768]{2,1,0:T(8,128)(2,1)S(1)}, u32[]{:S(2)}, u32[]{:S(2)}) async-start(bf16[8,64,768]{2,1,0:T(8,128)(2,1)} %copy-done.8), calls=%async_computation.2 | async-start | bytes 1572864 | tf_op jit(solution)/shard_map/all_to_all | solution.py:147
  112.0 1.1 copy-start.6
  113.1 0.9 copy-start.7
  121.1 15.9 %all-to-all-start.3 = ((bf16[8,64,768]{2,1,0:T(8,128)(2,1)}), bf16[8,64,768]{2,1,0:T(8,128)(2,1)}, u32[]{:S(2)}, u32[]{:S(2)}) async-start(bf16[8,64,768]{2,1,0:T(8,128)(2,1)} %copy-done.7), calls=%async_computation.3 | async-start | bytes 1572864 | tf_op jit(solution)/shard_map/all_to_all | solution.py:147
  125.8 1.7 copy-start.3
  128.7 2.4 %collective-permute-start.16 = (bf16[256,1536]{1,0:T(8,128)(2,1)S(1)}, bf16[256,1536]{1,0:T(8,128)(2,1)S(1)}, u32[]{:S(2)}, u32[]{:S(2)}) collective-permute-start(bf16[256,1536]{1,0:T(8,128)(2,1)S(1)} %shard_map.78), channel_id=1, source_target_pairs={{0,1},{1,0},{2,3},{3,2},{4,5},{5,4},{6,7},{7,6},{8,9},{9,8},{10,11... | collective-permute-start | bytes 2359304 | tf_op jit(solution)/shard_map/ppermute | solution.py:128
  133.2 0.7 copy-start.9
  133.9 8.1 %collective-permute-start.17 = (bf16[64,1536]{1,0:T(8,128)(2,1)}, bf16[64,1536]{1,0:T(8,128)(2,1)}, u32[]{:S(2)}, u32[]{:S(2)}) collective-permute-start(bf16[64,1536]{1,0:T(8,128)(2,1)} %get-tuple-element.67), channel_id=1, source_target_pairs={{0,6},{1,7},{2,0},{3,1},{4,2},{5,3},{6,4},{7,5},{8,14},{9,15},{10,... | collective-permute-start | bytes 589832 | tf_op jit(solution)/shard_map/ppermute | solution.py:125
  134.7 8.5 %collective-permute-start.18 = (bf16[64,1536]{1,0:T(8,128)(2,1)}, bf16[64,1536]{1,0:T(8,128)(2,1)}, u32[]{:S(2)}, u32[]{:S(2)}) collective-permute-start(bf16[64,1536]{1,0:T(8,128)(2,1)} %get-tuple-element.68), channel_id=1, source_target_pairs={{0,4},{1,5},{2,6},{3,7},{4,0},{5,1},{6,2},{7,3},{8,12},{9,13},{10,... | collective-permute-start | bytes 589832 | tf_op jit(solution)/shard_map/ppermute | solution.py:125
  137.0 1.7 copy-start.4
  143.1 9.3 %collective-permute-start.20 = (bf16[256,1536]{1,0:T(8,128)(2,1)}, bf16[256,1536]{1,0:T(8,128)(2,1)}, u32[]{:S(2)}, u32[]{:S(2)}) collective-permute-start(bf16[256,1536]{1,0:T(8,128)(2,1)} %shard_map.80), channel_id=1, source_target_pairs={{0,1},{1,0},{2,3},{3,2},{4,5},{5,4},{6,7},{7,6},{8,9},{9,8},{10,11... | collective-permute-start | bytes 2359304 | tf_op jit(solution)/shard_map/ppermute | solution.py:128
  143.1 35.3 %all-to-all-start.4 = ((bf16[8,2,64,768]{3,2,1,0:T(8,128)(2,1)}), bf16[8,2,64,768]{3,2,1,0:T(8,128)(2,1)}, u32[]{:S(2)}, u32[]{:S(2)}) async-start(bf16[8,2,64,768]{3,2,1,0:T(8,128)(2,1)} %copy-done.6), calls=%async_computation.4 | async-start | bytes 3145728 | tf_op jit(solution)/shard_map/all_to_all | solution.py:147
  148.9 10.2 %collective-permute-start.19 = (bf16[64,1536]{1,0:T(8,128)(2,1)}, bf16[64,1536]{1,0:T(8,128)(2,1)S(1)}, u32[]{:S(2)}, u32[]{:S(2)}) collective-permute-start(bf16[64,1536]{1,0:T(8,128)(2,1)} %copy-done.9), channel_id=1, source_target_pairs={{0,2},{1,3},{2,4},{3,5},{4,6},{5,7},{6,0},{7,1},{8,10},{9,11},{10,... | collective-permute-start | bytes 589832 | tf_op jit(solution)/shard_map/ppermute | solution.py:125
  152.4 1.7 copy-start.5
  154.1 7.5 %copy-start.15 = (bf16[256,1536]{1,0:T(8,128)(2,1)S(1)}, bf16[256,1536]{1,0:T(8,128)(2,1)}, u32[]{:S(2)}) copy-start(bf16[256,1536]{1,0:T(8,128)(2,1)} %copy-done.14) | copy-start | bytes 2359300
  154.1 7.5 %copy-start.17 = (bf16[256,1536]{1,0:T(8,128)(2,1)S(1)}, bf16[256,1536]{1,0:T(8,128)(2,1)}, u32[]{:S(2)}) copy-start(bf16[256,1536]{1,0:T(8,128)(2,1)} %copy-done.16) | copy-start | bytes 2359300
  154.1 7.5 %copy-start.24 = (bf16[256,1536]{1,0:T(8,128)(2,1)S(1)}, bf16[256,1536]{1,0:T(8,128)(2,1)}, u32[]{:S(2)}) copy-start(bf16[256,1536]{1,0:T(8,128)(2,1)} %copy-done.23) | copy-start | bytes 2359300
  154.1 7.5 %copy-start.26 = (bf16[256,1536]{1,0:T(8,128)(2,1)S(1)}, bf16[256,1536]{1,0:T(8,128)(2,1)}, u32[]{:S(2)}) copy-start(bf16[256,1536]{1,0:T(8,128)(2,1)} %copy-done.25) | copy-start | bytes 2359300
  159.0 7.8 %collective-permute-start.21 = (bf16[64,1536]{1,0:T(8,128)(2,1)S(1)}, bf16[64,1536]{1,0:T(8,128)(2,1)S(1)}, u32[]{:S(2)}, u32[]{:S(2)}) collective-permute-start(bf16[64,1536]{1,0:T(8,128)(2,1)S(1)} %get-tuple-element.85), channel_id=1, source_target_pairs={{0,6},{1,7},{2,0},{3,1},{4,2},{5,3},{6,4},{7,5},{8,14},{9,15},{10,... | collective-permute-start | bytes 589832 | tf_op jit(solution)/shard_map/ppermute | solution.py:125
  160.8 9.3 %collective-permute-start.22 = (bf16[64,1536]{1,0:T(8,128)(2,1)S(1)}, bf16[64,1536]{1,0:T(8,128)(2,1)S(1)}, u32[]{:S(2)}, u32[]{:S(2)}) collective-permute-start(bf16[64,1536]{1,0:T(8,128)(2,1)S(1)} %get-tuple-element.86), channel_id=1, source_target_pairs={{0,4},{1,5},{2,6},{3,7},{4,0},{5,1},{6,2},{7,3},{8,12},{9,13},{10,... | collective-permute-start | bytes 589832 | tf_op jit(solution)/shard_map/ppermute | solution.py:125
  161.5 10.7 %collective-permute-start.23 = (bf16[64,1536]{1,0:T(8,128)(2,1)S(1)}, bf16[64,1536]{1,0:T(8,128)(2,1)S(1)}, u32[]{:S(2)}, u32[]{:S(2)}) collective-permute-start(bf16[64,1536]{1,0:T(8,128)(2,1)S(1)} %get-tuple-element.87), channel_id=1, source_target_pairs={{0,2},{1,3},{2,4},{3,5},{4,6},{5,7},{6,0},{7,1},{8,10},{9,11},{10,... | collective-permute-start | bytes 589832 | tf_op jit(solution)/shard_map/ppermute | solution.py:125
  173.4 11.4 %collective-permute-start.24 = (bf16[32,1536]{1,0:T(8,128)(2,1)S(1)}, bf16[32,1536]{1,0:T(8,128)(2,1)S(1)}, u32[]{:S(2)}, u32[]{:S(2)}) collective-permute-start(bf16[32,1536]{1,0:T(8,128)(2,1)S(1)} %pad_maximum_fusion.7), channel_id=1, source_target_pairs={{0,24},{8,0},{16,8},{24,16},{1,25},{9,1},{17,9},{25,17},{2,26},{10... | collective-permute-start | bytes 294920 | tf_op jit(solution)/shard_map/ppermute | solution.py:122
  175.5 10.5 %collective-permute-start.25 = (bf16[32,1536]{1,0:T(8,128)(2,1)S(1)}, bf16[32,1536]{1,0:T(8,128)(2,1)S(1)}, u32[]{:S(2)}, u32[]{:S(2)}) collective-permute-start(bf16[32,1536]{1,0:T(8,128)(2,1)S(1)} %pad_maximum_fusion.8), channel_id=1, source_target_pairs={{0,16},{8,24},{16,0},{24,8},{1,17},{9,25},{17,1},{25,9},{2,18},{10... | collective-permute-start | bytes 294920 | tf_op jit(solution)/shard_map/ppermute | solution.py:122
  175.8 12.9 %collective-permute-start.26 = (bf16[32,1536]{1,0:T(8,128)(2,1)S(1)}, bf16[32,1536]{1,0:T(8,128)(2,1)S(1)}, u32[]{:S(2)}, u32[]{:S(2)}) collective-permute-start(bf16[32,1536]{1,0:T(8,128)(2,1)S(1)} %pad_maximum_fusion.9), channel_id=1, source_target_pairs={{0,8},{8,16},{16,24},{24,0},{1,9},{9,17},{17,25},{25,1},{2,10},{10... | collective-permute-start | bytes 294920 | tf_op jit(solution)/shard_map/ppermute | solution.py:122
  178.5 1.7 copy-start.11
  178.5 1.8 copy-start.13
  178.5 2.1 %copy-start.20 = (bf16[256,1536]{1,0:T(8,128)(2,1)S(1)}, bf16[256,1536]{1,0:T(8,128)(2,1)}, u32[]{:S(2)}) copy-start(bf16[256,1536]{1,0:T(8,128)(2,1)} %copy-done.19) | copy-start | bytes 2359300
  178.5 2.3 %copy-start.22 = (bf16[256,1536]{1,0:T(8,128)(2,1)S(1)}, bf16[256,1536]{1,0:T(8,128)(2,1)}, u32[]{:S(2)}) copy-start(bf16[256,1536]{1,0:T(8,128)(2,1)} %copy-done.21) | copy-start | bytes 2359300

commit v8 on v6

--- a/solution.py
+++ b/solution.py
@@ -1,8 +1,11 @@
+import functools
 import math
 
 import jax
 import jax.numpy as jnp
 from jax import lax
+from jax.experimental import pallas as pl
+from jax.experimental.pallas import tpu as pltpu
 from jax.sharding import PartitionSpec as P
 
 root_coef = math.sqrt(2.0 / math.pi)
@@ -28,6 +31,53 @@
     return lax.dot_general(left, right, (((0,), (0,)), ((), ())), preferred_element_type=f32)
 
 
+def vmem(mib):
+    return pltpu.CompilerParams(vmem_limit_bytes=mib << 20)
+
+
+def hidden_kernel(n_parts, n_copies, bias, *refs):
+    parts, before, (grad_copies, act_out) = refs[:n_parts], refs[n_parts:-2], refs[-2:]
+    blocks = [ref[j] for ref in parts for j in range(ref.shape[0])]
+    sums = blocks[0].astype(f32)
+    for block in blocks[1:]:
+        sums = sums + block.astype(f32)
+    act, grad = gelu_pair(sums[0] + bias[...], sums[1])
+    for j in range(n_copies):
+        grad_copies[j] = grad
+        if before:
+            act_out[j, 0] = before[0][...]
+            act_out[j, 1] = act
+    if not before:
+        act_out[...] = act
+
+
+def hidden(parts, n_copies, bias, *before):
+    pair, rows, columns = parts[0].shape[1:]
+    tile = columns // 3
+    act_shape = (n_copies, 2, rows) if before else (rows,)
+    return pl.pallas_call(
+        functools.partial(hidden_kernel, len(parts), n_copies),
+        grid=(columns // tile,),
+        in_specs=[pl.BlockSpec((1, tile), lambda i: (0, i))]
+        + [pl.BlockSpec((a.shape[0], pair, rows, tile), lambda i: (0, 0, 0, i)) for a in parts]
+        + [pl.BlockSpec((rows, tile), lambda i: (0, i))] * len(before),
+        out_specs=[
+            pl.BlockSpec((n_copies, rows, tile), lambda i: (0, 0, i)),
+            pl.BlockSpec((*act_shape, tile), lambda i: (*([0] * len(act_shape)), i)),
+        ],
+        out_shape=[
+            jax.ShapeDtypeStruct((n_copies, rows, columns), bf16),
+            jax.ShapeDtypeStruct((*act_shape, columns), bf16),
+        ],
+        compiler_params=pltpu.CompilerParams(vmem_limit_bytes=32 << 20),
+        cost_estimate=pl.CostEstimate(
+            flops=40 * rows * columns,
+            bytes_accessed=6 * n_copies * rows * columns,
+            transcendentals=rows * columns,
+        ),
+    )(bias, *parts, *before)
+
+
 def solution(mesh):
     n_x, n_y, n_z = (mesh.shape[a] for a in ("gx", "gy", "gz"))
 
@@ -54,13 +104,20 @@
         return sums[:1] + [a.astype(bf16) for a in sums[1:]]
 
     def exchange(parts, shift):
-        return parts[:1] + [shift(part, -k) for k, part in enumerate(parts) if k]
-
-    def copies(share):
-        return jnp.broadcast_to(share[None], (n_x, *share.shape))
+        return [shift(part, -k) if k else part for k, part in enumerate(parts)]
 
     def trade_width(parts):
         return lax.all_to_all(parts, "gx", 0, 0, tiled=True)
+
+    def permute_width(parts):
+        place = lax.axis_index("gx").astype(jnp.uint32)
+        received = []
+        for flip in sorted(range(n_x), key=lambda flip: -(flip // (n_x // 2) + (flip % (n_x // 2)) % 3)):
+            block = lax.dynamic_slice_in_dim(parts, place ^ flip, 1, axis=0)
+            if flip:
+                block = lax.ppermute(block, "gx", [(i, i ^ flip) for i in range(n_x)])
+            received.append(block)
+        return received
 
     def after(a, *others):
         return lax.optimization_barrier((a, *others))[0]
@@ -77,45 +134,38 @@
         chunks = [
             jnp.stack([a[c * rows : (c + 1) * rows] for a in (tokens, grad_output)]) for c in range(2)
         ]
-
-        def partial_sums(near):
-            both = [jnp.concatenate([a, swap_core(a)], axis=0) for a in near]
+        bias = bias_hidden.reshape(1, -1)
+
+        def partial_sums(pieces):
+            both = [jnp.concatenate([a, swap_core(a)], axis=0) for a in join(pieces)]
             pre_part = jnp.dot(both[0], weight_in, preferred_element_type=f32).astype(bf16)
             up_part = contract_last(both[1], weight_out).astype(bf16)
             parts = [a.reshape(n_x, 1, -1, a.shape[1]) for a in (pre_part, up_part)]
             return both, jnp.concatenate(parts, axis=1)
 
-        def hidden(parts):
-            sums = jnp.sum(parts.astype(f32), axis=0)
-            return gelu_pair(sums[0] + bias_hidden, sums[1])
-
-        far0 = join(groups(chunks[0]))
-        groups1 = groups(after(chunks[1], far0))
-        chips0, groups1 = barrier([far0] + [shift_chip(far0, k) for k in range(1, n_chip)], groups1)
-        far1 = join(groups1)
-        both0, part0 = partial_sums(join(chips0))
-        chips1 = [far1] + [
-            shift_chip(far1, k) for k in range(1, n_chip)
-        ]
-        both1, part1 = partial_sums(join(chips1))
-        sums0 = trade_width(part0)
-        sums1 = trade_width(part1)
-        act0, grad0 = hidden(sums0)
-        copies0, sums1 = barrier(copies(grad0), sums1)
-        act1, grad1 = hidden(sums1)
-        act_copies = copies(jnp.stack([act0, act1]))
-
         def two_halves(grad_hidden):
             half = grad_hidden.shape[0] // 2
             other = contract_last(grad_hidden[half:], weight_in).astype(bf16)
             return other, contract_last(grad_hidden[:half], weight_in)
 
-        hidden0 = trade_width(copies0).reshape(-1, act0.shape[1])
-        hidden1 = trade_width(after(copies(grad1), hidden0)).reshape(-1, act0.shape[1])
+        far0 = join(groups(chunks[0]))
+        far1 = join(groups(after(chunks[1], far0)))
+        chips0, far1 = barrier([far0] + [shift_chip(far0, k) for k in range(1, n_chip)], far1)
+        both0, part0 = partial_sums(chips0)
+        both1, part1 = partial_sums([far1] + [shift_chip(far1, k) for k in range(1, n_chip)])
+        sums0 = trade_width(part0)
+        sums0, part1 = barrier(sums0, part1)
+        sums1 = permute_width(part1)
+        grad_copies0, act0 = hidden([sums0], n_x, bias)
+        columns = act0.shape[1]
+        hidden0 = trade_width(grad_copies0)
+        hidden0, sums1 = barrier(hidden0, sums1)
+        grad_copies1, act_copies = hidden(sums1, n_x, bias, act0)
+        hidden1 = trade_width(grad_copies1).reshape(-1, columns)
+        hidden0 = hidden0.reshape(-1, columns)
         other0, own0 = two_halves(hidden0)
         own0, other0 = barrier(own0, swap_core(other0))
-        parts0, act_copies = barrier(sum_blocks([own0, other0], n_chip), act_copies)
-        parts0 = exchange(parts0, shift_chip)
+        parts0 = exchange(sum_blocks([own0, other0], n_chip), shift_chip)
         other1, own1 = two_halves(hidden1)
         parts0, other1, act_copies = barrier(parts0, other1, act_copies)
         activation = trade_width(act_copies)
@@ -131,7 +181,7 @@
             for pair in zip(sum_blocks(parts0, n_y), sum_blocks(parts1, n_y))
         ]
         parts = exchange(parts, shift_y)
-        activation = activation.transpose(1, 0, 2, 3).reshape(-1, act0.shape[1])
+        activation = activation.transpose(1, 0, 2, 3).reshape(-1, columns)
         grad_all = jnp.concatenate([both0[1], both1[1]], axis=0)
         grad_weight_out = (contract_first(activation, grad_all) * norm_scale).astype(bf16)
         parts, grad_weight_out = barrier(parts, grad_weight_out)

time: 188 us -> 196 us (1.043)
  Pallas kernels: 0 us -> 5.08 us
    all_to_all x5 -> x4, waiting for transfers between devices: 31.5 us -> 8.11 us  [trade_width(): return lax.all_to_all(parts, 'gx', 0, 0, tiled=True)]
    ppermute x0 -> x7, waiting for transfers between devices: none -> 20.6 us  [permute_width(): block = lax.ppermute(block, 'gx', [(i, i ^ flip) for i in range(n_x)])]
    ppermute x0 -> x7, starting transfers between devices: none -> 10.1 us  [permute_width(): block = lax.ppermute(block, 'gx', [(i, i ^ flip) for i in range(n_x)])]
    all_to_all x5 -> x4, starting transfers between devices: 26.6 us -> 21.1 us  [trade_width(): return lax.all_to_all(parts, 'gx', 0, 0, tiled=True)]
    pallas_call x0 -> x2, Pallas kernels: none -> 5.08 us  [hidden(): pl.pallas_call(functools.partial(hidden_kernel, len(parts), n_copies), gr...]
    ppermute x9, starting transfers between devices: 26.7 us -> 22 us  [shift_y(): return lax.ppermute(a, 'gy', [(i, (i + k) % n_y) for i in range(n_y)])]
    unnamed x48 -> x62, local copies, waits for them, and re-layouts: 6.33 us -> 9.71 us
    reduce_sum x2 -> x0, other arithmetic: 3.32 us -> none  [hidden(): sums = jnp.sum(parts.astype(f32), axis=0)]
  transfers between devices with their start and end apart: 32 -> 38, of which waited for: 18 -> 21; matrix products, arithmetic and copies ran while one was open for 23% -> 20% of each run, Pallas kernels for 0% -> 0%
where the time goes in v8:
time: 196 us; the launch traced here: 195 us
  starting transfers between devices  71.2 us (36%)
  waiting for transfers between devices  67.4 us (34%)
  matrix products  20.7 us (11%)
  local copies, waits for them, and re-layouts  19.3 us (10%)
  other arithmetic  9.87 us (5%)
  Pallas kernels  5.08 us (3%)
    ppermute x9, starting transfers between devices, shift_y(): return lax.ppermute(a, 'gy', [(i, (i + k) % n_y) for i in range(n_y)])  22 us
    all_to_all x4, starting transfers between devices, trade_width(): return lax.all_to_all(parts, 'gx', 0, 0, tiled=True)  21.1 us
    ppermute x7, waiting for transfers between devices, permute_width(): block = lax.ppermute(block, 'gx', [(i, i ^ flip) for i in range(n_x)])  20.6 us
    ppermute x12, waiting for transfers between devices, shift_chip(): return lax.ppermute(a, 'gz', [(i, (i + 2 * k) % n_z) for i in range(n_z)])  17.8 us
    ppermute x9, waiting for transfers between devices, shift_y(): return lax.ppermute(a, 'gy', [(i, (i + k) % n_y) for i in range(n_y)])  17.7 us
    ppermute x12, starting transfers between devices, shift_chip(): return lax.ppermute(a, 'gz', [(i, (i + 2 * k) % n_z) for i in range(n_z)])  16.7 us
    ppermute x7, starting transfers between devices, permute_width(): block = lax.ppermute(block, 'gx', [(i, i ^ flip) for i in range(n_x)])  10.1 us
    unnamed x62, local copies, waits for them, and re-layouts  9.71 us
  transfers between devices with their start and end apart: 38, of which 21 were waited for; matrix products, arithmetic and copies ran while one was open for 20% of the time, Pallas kernels for 0%

profile of v8, /device:TPU:32, one launch (start us, length us, event | category | flops | bytes accessed | tf_op | source)
XLA Modules:
  0.0 194.7 jit_solution(10355377842934250195)
XLA Ops:
  1.7 5.5 %collective-permute-start.2 = (bf16[2,16,1536]{2,1,0:T(8,128)(2,1)S(1)}, bf16[2,16,1536]{2,1,0:T(8,128)(2,1)S(1)}, u32[]{:S(2)}, u32[]{:S(2)}) collective-permute-start(bf16[2,16,1536]{2,1,0:T(8,128)(2,1)S(1)} %pad_maximum_fusion.5), channel_id=1, source_target_pairs={{0,24},{8,0},{16,8},{24,16},{1,25},{9,1},{17,9},{25,17},{2,26},{10... | collective-permute-start | bytes 294920 | tf_op jit(solution)/shard_map/ppermute | solution.py:85
  7.2 1.4 collective-permute-start.1
  8.6 2.4 %collective-permute-start = (bf16[2,16,1536]{2,1,0:T(8,128)(2,1)S(1)}, bf16[2,16,1536]{2,1,0:T(8,128)(2,1)S(1)}, u32[]{:S(2)}, u32[]{:S(2)}) collective-permute-start(bf16[2,16,1536]{2,1,0:T(8,128)(2,1)S(1)} %pad_maximum_fusion.5), channel_id=1, source_target_pairs={{0,8},{8,16},{16,24},{24,0},{1,9},{9,17},{17,25},{25,1},{2,10},{10... | collective-permute-start | bytes 294920 | tf_op jit(solution)/shard_map/ppermute | solution.py:85
  11.0 7.0 %collective-permute-done.1 = bf16[2,16,1536]{2,1,0:T(8,128)(2,1)S(1)} collective-permute-done((bf16[2,16,1536]{2,1,0:T(8,128)(2,1)S(1)}, bf16[2,16,1536]{2,1,0:T(8,128)(2,1)S(1)}, u32[]{:S(2)}, u32[]{:S(2)}) %collective-permute-start.1) | collective-permute-done | bytes 98336 | tf_op jit(solution)/shard_map/ppermute | solution.py:85
  18.7 3.7 %collective-permute-start.8 = (bf16[2,16,1536]{2,1,0:T(8,128)(2,1)S(1)}, bf16[2,16,1536]{2,1,0:T(8,128)(2,1)S(1)}, u32[]{:S(2)}, u32[]{:S(2)}) collective-permute-start(bf16[2,16,1536]{2,1,0:T(8,128)(2,1)S(1)} %pad_maximum_fusion.6), channel_id=1, source_target_pairs={{0,24},{8,0},{16,8},{24,16},{1,25},{9,1},{17,9},{25,17},{2,26},{10... | collective-permute-start | bytes 294920 | tf_op jit(solution)/shard_map/ppermute | solution.py:85
  22.4 1.5 collective-permute-start.3
  23.9 2.7 %collective-permute-start.4 = (bf16[2,64,1536]{2,1,0:T(8,128)(2,1)S(1)}, bf16[2,64,1536]{2,1,0:T(8,128)(2,1)S(1)}, u32[]{:S(2)}, u32[]{:S(2)}) collective-permute-start(bf16[2,64,1536]{2,1,0:T(8,128)(2,1)S(1)} %pad_maximum_fusion.2), channel_id=1, source_target_pairs={{0,4},{1,5},{2,6},{3,7},{4,0},{5,1},{6,2},{7,3},{8,12},{9,13},{10,... | collective-permute-start | bytes 1179656 | tf_op jit(solution)/shard_map/ppermute | solution.py:88
  26.6 1.4 collective-permute-start.5
  28.0 1.7 collective-permute-start.7
  29.8 2.4 %collective-permute-start.6 = (bf16[2,16,1536]{2,1,0:T(8,128)(2,1)S(1)}, bf16[2,16,1536]{2,1,0:T(8,128)(2,1)S(1)}, u32[]{:S(2)}, u32[]{:S(2)}) collective-permute-start(bf16[2,16,1536]{2,1,0:T(8,128)(2,1)S(1)} %pad_maximum_fusion.6), channel_id=1, source_target_pairs={{0,8},{8,16},{16,24},{24,0},{1,9},{9,17},{17,25},{25,1},{2,10},{10... | collective-permute-start | bytes 294920 | tf_op jit(solution)/shard_map/ppermute | solution.py:85
  32.2 5.3 %collective-permute-done.7 = bf16[2,16,1536]{2,1,0:T(8,128)(2,1)S(1)} collective-permute-done((bf16[2,16,1536]{2,1,0:T(8,128)(2,1)S(1)}, bf16[2,16,1536]{2,1,0:T(8,128)(2,1)S(1)}, u32[]{:S(2)}, u32[]{:S(2)}) %collective-permute-start.7) | collective-permute-done | bytes 98336 | tf_op jit(solution)/shard_map/ppermute | solution.py:85
  38.5 4.8 %collective-permute-done.4 = bf16[2,64,1536]{2,1,0:T(8,128)(2,1)S(1)} collective-permute-done((bf16[2,64,1536]{2,1,0:T(8,128)(2,1)S(1)}, bf16[2,64,1536]{2,1,0:T(8,128)(2,1)S(1)}, u32[]{:S(2)}, u32[]{:S(2)}) %collective-permute-start.4) | collective-permute-done | bytes 393248 | tf_op jit(solution)/shard_map/ppermute | solution.py:88
  44.1 1.3 collective-permute-start.11
  45.5 2.4 %collective-permute-start.12 = (bf16[2,64,1536]{2,1,0:T(8,128)(2,1)S(1)}, bf16[2,64,1536]{2,1,0:T(8,128)(2,1)S(1)}, u32[]{:S(2)}, u32[]{:S(2)}) collective-permute-start(bf16[2,64,1536]{2,1,0:T(8,128)(2,1)S(1)} %pad_maximum_fusion.3), channel_id=1, source_target_pairs={{0,4},{1,5},{2,6},{3,7},{4,0},{5,1},{6,2},{7,3},{8,12},{9,13},{10,... | collective-permute-start | bytes 1179656 | tf_op jit(solution)/shard_map/ppermute | solution.py:88
  47.9 1.6 collective-permute-start.13
  50.2 1.4 fusion.39
  51.7 1.4 fusion.42
  53.1 1.3 pad_maximum_fusion
  54.4 5.9 %all-to-all-start = ((bf16[8,2,64,768]{3,2,1,0:T(8,128)(2,1)}), bf16[8,2,64,768]{3,2,1,0:T(8,128)(2,1)}, u32[]{:S(2)}, u32[]{:S(2)}) async-start(bf16[8,2,64,768]{3,2,1,0:T(8,128)(2,1)} %pad_maximum_fusion), calls=%async_computation | async-start | bytes 3145728 | tf_op jit(solution)/shard_map/all_to_all | solution.py:110
  60.3 1.8 constant_dynamic-update-slice_fusion.6
  62.1 3.3 %collective-permute-done.12 = bf16[2,64,1536]{2,1,0:T(8,128)(2,1)S(1)} collective-permute-done((bf16[2,64,1536]{2,1,0:T(8,128)(2,1)S(1)}, bf16[2,64,1536]{2,1,0:T(8,128)(2,1)S(1)}, u32[]{:S(2)}, u32[]{:S(2)}) %collective-permute-start.12) | collective-permute-done | bytes 393248 | tf_op jit(solution)/shard_map/ppermute | solution.py:88
  66.9 1.5 slice_bitcast_fusion.1
  69.0 1.8 collective-permute-done.15
  70.8 1.4 fusion.33
  72.3 1.4 fusion.36
  73.7 1.3 pad_maximum_fusion.1
  75.0 4.8 %all-to-all-done.refs_0_ = bf16[8,2,64,768]{3,2,1,0:T(8,128)(2,1)} async-done(((bf16[8,2,64,768]{3,2,1,0:T(8,128)(2,1)}), bf16[8,2,64,768]{3,2,1,0:T(8,128)(2,1)}, u32[]{:S(2)}, u32[]{:S(2)}) %all-to-all-start) | async-done | bytes 1572896 | tf_op jit(solution)/shard_map/all_to_all | solution.py:110
  79.7 3.2 %shard_map.76 = (bf16[8,64,768]{2,1,0:T(8,128)(2,1)}, bf16[64,768]{1,0:T(8,128)(2,1)S(1)}) custom-call(f32[1,768]{1,0:T(1,128)S(1)} %reshape.34.bias, bf16[8,2,64,768]{3,2,1,0:T(8,128)(2,1)} %all-to-all-done.refs_0_), custom_call_target="tpu_custom_call" | custom-call | flops 1966080 | bytes 2359296 | tf_op jit(solution)/shard_map/pallas_call | solution.py:58
  83.6 4.7 %all-to-all-start.1 = ((bf16[8,64,768]{2,1,0:T(8,128)(2,1)}), bf16[8,64,768]{2,1,0:T(8,128)(2,1)}, u32[]{:S(2)}, u32[]{:S(2)}) async-start(bf16[8,64,768]{2,1,0:T(8,128)(2,1)} %get-tuple-element.61), calls=%async_computation.1 | async-start | bytes 1572864 | tf_op jit(solution)/shard_map/all_to_all | solution.py:110
  88.3 1.6 constant_dynamic-slice_fusion
  89.8 3.0 %collective-permute-start.16 = (bf16[1,2,64,768]{3,2,1,0:T(8,128)(2,1)S(1)}, bf16[1,2,64,768]{3,2,1,0:T(8,128)(2,1)S(1)}, u32[]{:S(2)}, u32[]{:S(2)}) collective-permute-start(bf16[1,2,64,768]{3,2,1,0:T(8,128)(2,1)S(1)} %get-tuple-element.120), channel_id=1, source_target_pairs={{0,192},{32,224},{64,128},{96,160},{128,64},{160,96},{192,0},{224,... | collective-permute-start | bytes 589832 | tf_op jit(solution)/shard_map/ppermute | solution.py:118
  93.0 2.8 %collective-permute-start.18 = (bf16[1,2,64,768]{3,2,1,0:T(8,128)(2,1)S(1)}, bf16[1,2,64,768]{3,2,1,0:T(8,128)(2,1)S(1)}, u32[]{:S(2)}, u32[]{:S(2)}) collective-permute-start(bf16[1,2,64,768]{3,2,1,0:T(8,128)(2,1)S(1)} %get-tuple-element.118), channel_id=1, source_target_pairs={{0,160},{32,128},{64,224},{96,192},{128,32},{160,0},{192,96},{224,... | collective-permute-start | bytes 589832 | tf_op jit(solution)/shard_map/ppermute | solution.py:118
  96.5 9.1 %collective-permute-done.16.refs_0_ = bf16[1,2,64,768]{3,2,1,0:T(8,128)(2,1)S(1)} collective-permute-done((bf16[1,2,64,768]{3,2,1,0:T(8,128)(2,1)S(1)}, bf16[1,2,64,768]{3,2,1,0:T(8,128)(2,1)S(1)}, u32[]{:S(2)}, u32[]{:S(2)}) %collective-permute-start.16) | collective-permute-done | bytes 196640 | tf_op jit(solution)/shard_map/ppermute | solution.py:118
  105.7 2.2 %collective-permute-start.21 = (bf16[1,2,64,768]{3,2,1,0:T(8,128)(2,1)S(1)}, bf16[1,2,64,768]{3,2,1,0:T(8,128)(2,1)S(1)}, u32[]{:S(2)}, u32[]{:S(2)}) collective-permute-start(bf16[1,2,64,768]{3,2,1,0:T(8,128)(2,1)S(1)} %get-tuple-element.115), channel_id=1, source_target_pairs={{0,224},{32,192},{64,160},{96,128},{128,96},{160,64},{192,32},{224... | collective-permute-start | bytes 589832 | tf_op jit(solution)/shard_map/ppermute | solution.py:118
  107.8 6.4 %collective-permute-done.17.refs_1_ = bf16[1,2,64,768]{3,2,1,0:T(8,128)(2,1)S(1)} collective-permute-done((bf16[1,2,64,768]{3,2,1,0:T(8,128)(2,1)S(1)}, bf16[1,2,64,768]{3,2,1,0:T(8,128)(2,1)S(1)}, u32[]{:S(2)}, u32[]{:S(2)}) %collective-permute-start.17) | collective-permute-done | bytes 196640 | tf_op jit(solution)/shard_map/ppermute | solution.py:118
  114.2 1.3 collective-permute-start.22
  115.9 1.2 collective-permute-done.21.refs_5_
  117.8 3.4 %collective-permute-done.22.refs_7_ = bf16[1,2,64,768]{3,2,1,0:T(8,128)(2,1)S(1)} collective-permute-done((bf16[1,2,64,768]{3,2,1,0:T(8,128)(2,1)S(1)}, bf16[1,2,64,768]{3,2,1,0:T(8,128)(2,1)S(1)}, u32[]{:S(2)}, u32[]{:S(2)}) %collective-permute-start.22) | collective-permute-done | bytes 196640 | tf_op jit(solution)/shard_map/ppermute | solution.py:118
  121.9 2.1 %fusion.52 = (bf16[4,64,768]{2,1,0:T(8,128)(2,1)}, bf16[4,64,768]{2,1,0:T(8,128)(2,1)}) fusion(bf16[8,64,768]{2,1,0:T(8,128)(2,1)} %all-to-all-done.1), kind=kLoop, calls=%fused_computation.99 | loop fusion | bytes 1572864 | tf_op jit(solution)/shard_map/slice | solution.py:148
  126.8 1.8 shard_map.77
  129.8 4.8 %all-to-all-start.2 = ((bf16[8,64,768]{2,1,0:T(8,128)(2,1)}), bf16[8,64,768]{2,1,0:T(8,128)(2,1)S(1)}, u32[]{:S(2)}, u32[]{:S(2)}) async-start(bf16[8,64,768]{2,1,0:T(8,128)(2,1)} %get-tuple-element.75), calls=%async_computation.2 | async-start | bytes 1572864 | tf_op jit(solution)/shard_map/all_to_all | solution.py:110
  134.6 1.8 convolution_convert_fusion.1
  137.3 1.4 collective-permute-done.23
  139.9 2.2 %collective-permute-start.25 = (bf16[64,1536]{1,0:T(8,128)(2,1)}, bf16[64,1536]{1,0:T(8,128)(2,1)}, u32[]{:S(2)}, u32[]{:S(2)}) collective-permute-start(bf16[64,1536]{1,0:T(8,128)(2,1)} %get-tuple-element.110), channel_id=1, source_target_pairs={{0,4},{1,5},{2,6},{3,7},{4,0},{5,1},{6,2},{7,3},{8,12},{9,13},{10,... | collective-permute-start | bytes 589832 | tf_op jit(solution)/shard_map/ppermute | solution.py:88
  142.1 3.4 %all-to-all-done.2 = bf16[8,64,768]{2,1,0:T(8,128)(2,1)S(1)} async-done(((bf16[8,64,768]{2,1,0:T(8,128)(2,1)}), bf16[8,64,768]{2,1,0:T(8,128)(2,1)S(1)}, u32[]{:S(2)}, u32[]{:S(2)}) %all-to-all-start.2) | async-done | bytes 786464 | tf_op jit(solution)/shard_map/all_to_all | solution.py:110
  146.3 1.7 convolution_convert_fusion
  148.0 1.5 collective-permute-done.25
  149.5 3.1 %collective-permute-done.26 = bf16[64,1536]{1,0:T(8,128)(2,1)} collective-permute-done((bf16[64,1536]{1,0:T(8,128)(2,1)}, bf16[64,1536]{1,0:T(8,128)(2,1)}, u32[]{:S(2)}, u32[]{:S(2)}) %collective-permute-start.26) | collective-permute-done | bytes 196640 | tf_op jit(solution)/shard_map/ppermute | solution.py:88
  152.6 5.7 %all-to-all-start.3 = ((bf16[8,2,64,768]{3,2,1,0:T(8,128)(2,1)}), bf16[8,2,64,768]{3,2,1,0:T(8,128)(2,1)}, u32[]{:S(2)}, u32[]{:S(2)}) async-start(bf16[8,2,64,768]{3,2,1,0:T(8,128)(2,1)} %copy-done.1), calls=%async_computation.3 | async-start | bytes 3145728 | tf_op jit(solution)/shard_map/all_to_all | solution.py:110
  158.3 1.8 fusion.54
  160.2 1.6 add_convert_fusion
  161.8 1.2 collective-permute-start.28
  163.0 1.7 collective-permute-start.29
  165.0 5.1 %multiply_convert_fusion.1 = bf16[1536,768]{1,0:T(8,128)(2,1)} fusion(bf16[256,1536]{1,0:T(8,128)(2,1)S(1)} %copy-done.27, bf16[256,1536]{1,0:T(8,128)(2,1)S(1)} %copy-done.16, bf16[256,1536]{1,0:T(8,128)(2,1)S(1)} %copy-done.25, bf16[256,1536]{1,0:T(8,128)(2,1)S(1)} %copy-done.14, bf16[512,768]{1,0:T(8,128)(2,1)S(1)} %bitcast.41, bf16[512,768]{1,0:T(8,128)(2,1)} %bitcast.16), kind=kOutput, calls=%fused_computation.1 | convolution fusion | flops 2434007040 | bytes 7077888 | tf_op jit(solution)/shard_map/dot_general | solution.py:31
  170.1 2.3 %collective-permute-done.29 = bf16[64,1536]{1,0:T(8,128)(2,1)S(1)} collective-permute-done((bf16[64,1536]{1,0:T(8,128)(2,1)S(1)}, bf16[64,1536]{1,0:T(8,128)(2,1)S(1)}, u32[]{:S(2)}, u32[]{:S(2)}) %collective-permute-start.29) | collective-permute-done | bytes 196640 | tf_op jit(solution)/shard_map/ppermute | solution.py:88
  172.4 2.8 %collective-permute-done.30 = bf16[64,1536]{1,0:T(8,128)(2,1)S(1)} collective-permute-done((bf16[64,1536]{1,0:T(8,128)(2,1)S(1)}, bf16[64,1536]{1,0:T(8,128)(2,1)S(1)}, u32[]{:S(2)}, u32[]{:S(2)}) %collective-permute-start.30) | collective-permute-done | bytes 196640 | tf_op jit(solution)/shard_map/ppermute | solution.py:88
  175.3 1.2 add_convert_fusion.8
  177.1 2.0 %collective-permute-start.31 = (bf16[32,1536]{1,0:T(8,128)(2,1)}, bf16[32,1536]{1,0:T(8,128)(2,1)S(1)}, u32[]{:S(2)}, u32[]{:S(2)}) collective-permute-start(bf16[32,1536]{1,0:T(8,128)(2,1)} %pad_maximum_fusion.7), channel_id=1, source_target_pairs={{0,24},{8,0},{16,8},{24,16},{1,25},{9,1},{17,9},{25,17},{2,26},{10... | collective-permute-start | bytes 294920 | tf_op jit(solution)/shard_map/ppermute | solution.py:85
  180.7 2.6 %collective-permute-start.33 = (bf16[32,1536]{1,0:T(8,128)(2,1)}, bf16[32,1536]{1,0:T(8,128)(2,1)}, u32[]{:S(2)}, u32[]{:S(2)}) collective-permute-start(bf16[32,1536]{1,0:T(8,128)(2,1)} %pad_maximum_fusion.9), channel_id=1, source_target_pairs={{0,8},{8,16},{16,24},{24,0},{1,9},{9,17},{17,25},{25,1},{2,10},{10... | collective-permute-start | bytes 294920 | tf_op jit(solution)/shard_map/ppermute | solution.py:85
  183.3 1.7 copy.8
  185.3 3.9 %multiply_convert_fusion = bf16[768,1536]{1,0:T(8,128)(2,1)} fusion(bf16[1024,768]{1,0:T(8,128)(2,1)S(1)} %bitcast.42, bf16[256,1536]{1,0:T(8,128)(2,1)S(1)} %copy-done.23, bf16[256,1536]{1,0:T(8,128)(2,1)S(1)} %copy-done.12, bf16[256,1536]{1,0:T(8,128)(2,1)S(1)} %copy-done.21, bf16[256,1536]{1,0:T(8,128)(2,1)S(1)} %copy-done.10), kind=kOutput, calls=%fused_computation | convolution fusion | flops 2430861312 | bytes 7077888 | tf_op jit(solution)/shard_map/dot_general | solution.py:31
  189.3 1.3 collective-permute-done.32
  190.5 2.6 %collective-permute-done.33 = bf16[32,1536]{1,0:T(8,128)(2,1)} collective-permute-done((bf16[32,1536]{1,0:T(8,128)(2,1)}, bf16[32,1536]{1,0:T(8,128)(2,1)}, u32[]{:S(2)}, u32[]{:S(2)}) %collective-permute-start.33) | collective-permute-done | bytes 98336 | tf_op jit(solution)/shard_map/ppermute | solution.py:85
  193.1 1.6 add_convert_fusion.6
  (111 shorter events, 19.5 us)
Async XLA Ops:
  0.6 51.1 %copy-start = (bf16[1536,768]{1,0:T(8,128)(2,1)S(1)}, bf16[1536,768]{1,0:T(8,128)(2,1)}, u32[]{:S(2)}) copy-start(bf16[1536,768]{1,0:T(8,128)(2,1)} %param.6) | copy-start | bytes 7077892
  1.7 9.3 %collective-permute-start.2 = (bf16[2,16,1536]{2,1,0:T(8,128)(2,1)S(1)}, bf16[2,16,1536]{2,1,0:T(8,128)(2,1)S(1)}, u32[]{:S(2)}, u32[]{:S(2)}) collective-permute-start(bf16[2,16,1536]{2,1,0:T(8,128)(2,1)S(1)} %pad_maximum_fusion.5), channel_id=1, source_target_pairs={{0,24},{8,0},{16,8},{24,16},{1,25},{9,1},{17,9},{25,17},{2,26},{10... | collective-permute-start | bytes 294920 | tf_op jit(solution)/shard_map/ppermute | solution.py:85
  7.2 10.9 %collective-permute-start.1 = (bf16[2,16,1536]{2,1,0:T(8,128)(2,1)S(1)}, bf16[2,16,1536]{2,1,0:T(8,128)(2,1)S(1)}, u32[]{:S(2)}, u32[]{:S(2)}) collective-permute-start(bf16[2,16,1536]{2,1,0:T(8,128)(2,1)S(1)} %pad_maximum_fusion.5), channel_id=1, source_target_pairs={{0,16},{8,24},{16,0},{24,8},{1,17},{9,25},{17,1},{25,9},{2,18},{10... | collective-permute-start | bytes 294920 | tf_op jit(solution)/shard_map/ppermute | solution.py:85
  8.6 10.0 %collective-permute-start = (bf16[2,16,1536]{2,1,0:T(8,128)(2,1)S(1)}, bf16[2,16,1536]{2,1,0:T(8,128)(2,1)S(1)}, u32[]{:S(2)}, u32[]{:S(2)}) collective-permute-start(bf16[2,16,1536]{2,1,0:T(8,128)(2,1)S(1)} %pad_maximum_fusion.5), channel_id=1, source_target_pairs={{0,8},{8,16},{16,24},{24,0},{1,9},{9,17},{17,25},{25,1},{2,10},{10... | collective-permute-start | bytes 294920 | tf_op jit(solution)/shard_map/ppermute | solution.py:85
  18.7 11.1 %collective-permute-start.8 = (bf16[2,16,1536]{2,1,0:T(8,128)(2,1)S(1)}, bf16[2,16,1536]{2,1,0:T(8,128)(2,1)S(1)}, u32[]{:S(2)}, u32[]{:S(2)}) collective-permute-start(bf16[2,16,1536]{2,1,0:T(8,128)(2,1)S(1)} %pad_maximum_fusion.6), channel_id=1, source_target_pairs={{0,24},{8,0},{16,8},{24,16},{1,25},{9,1},{17,9},{25,17},{2,26},{10... | collective-permute-start | bytes 294920 | tf_op jit(solution)/shard_map/ppermute | solution.py:85
  22.4 16.1 %collective-permute-start.3 = (bf16[2,64,1536]{2,1,0:T(8,128)(2,1)S(1)}, bf16[2,64,1536]{2,1,0:T(8,128)(2,1)S(1)}, u32[]{:S(2)}, u32[]{:S(2)}) collective-permute-start(bf16[2,64,1536]{2,1,0:T(8,128)(2,1)S(1)} %pad_maximum_fusion.2), channel_id=1, source_target_pairs={{0,2},{1,3},{2,4},{3,5},{4,6},{5,7},{6,0},{7,1},{8,10},{9,11},{10,... | collective-permute-start | bytes 1179656 | tf_op jit(solution)/shard_map/ppermute | solution.py:88
  23.9 19.4 %collective-permute-start.4 = (bf16[2,64,1536]{2,1,0:T(8,128)(2,1)S(1)}, bf16[2,64,1536]{2,1,0:T(8,128)(2,1)S(1)}, u32[]{:S(2)}, u32[]{:S(2)}) collective-permute-start(bf16[2,64,1536]{2,1,0:T(8,128)(2,1)S(1)} %pad_maximum_fusion.2), channel_id=1, source_target_pairs={{0,4},{1,5},{2,6},{3,7},{4,0},{5,1},{6,2},{7,3},{8,12},{9,13},{10,... | collective-permute-start | bytes 1179656 | tf_op jit(solution)/shard_map/ppermute | solution.py:88
  26.6 16.7 %collective-permute-start.5 = (bf16[2,64,1536]{2,1,0:T(8,128)(2,1)S(1)}, bf16[2,64,1536]{2,1,0:T(8,128)(2,1)S(1)}, u32[]{:S(2)}, u32[]{:S(2)}) collective-permute-start(bf16[2,64,1536]{2,1,0:T(8,128)(2,1)S(1)} %pad_maximum_fusion.2), channel_id=1, source_target_pairs={{0,6},{1,7},{2,0},{3,1},{4,2},{5,3},{6,4},{7,5},{8,14},{9,15},{10,... | collective-permute-start | bytes 1179656 | tf_op jit(solution)/shard_map/ppermute | solution.py:88
  28.0 9.4 %collective-permute-start.7 = (bf16[2,16,1536]{2,1,0:T(8,128)(2,1)S(1)}, bf16[2,16,1536]{2,1,0:T(8,128)(2,1)S(1)}, u32[]{:S(2)}, u32[]{:S(2)}) collective-permute-start(bf16[2,16,1536]{2,1,0:T(8,128)(2,1)S(1)} %pad_maximum_fusion.6), channel_id=1, source_target_pairs={{0,16},{8,24},{16,0},{24,8},{1,17},{9,25},{17,1},{25,9},{2,18},{10... | collective-permute-start | bytes 294920 | tf_op jit(solution)/shard_map/ppermute | solution.py:85
  29.8 8.7 %collective-permute-start.6 = (bf16[2,16,1536]{2,1,0:T(8,128)(2,1)S(1)}, bf16[2,16,1536]{2,1,0:T(8,128)(2,1)S(1)}, u32[]{:S(2)}, u32[]{:S(2)}) collective-permute-start(bf16[2,16,1536]{2,1,0:T(8,128)(2,1)S(1)} %pad_maximum_fusion.6), channel_id=1, source_target_pairs={{0,8},{8,16},{16,24},{24,0},{1,9},{9,17},{17,25},{25,1},{2,10},{10... | collective-permute-start | bytes 294920 | tf_op jit(solution)/shard_map/ppermute | solution.py:85
  43.4 6.8 %copy-start.18 = (bf16[768,1536]{1,0:T(8,128)(2,1)S(1)}, bf16[768,1536]{1,0:T(8,128)(2,1)}, u32[]{:S(2)}) copy-start(bf16[768,1536]{1,0:T(8,128)(2,1)} %param.8) | copy-start | bytes 7077892
  43.5 8.1 %copy-start.9 = (bf16[256,1536]{1,0:T(8,128)(2,1)}, bf16[256,1536]{1,0:T(8,128)(2,1)S(1)}, u32[]{:S(2)}) copy-start(bf16[256,1536]{1,0:T(8,128)(2,1)S(1)} %get-tuple-element.124) | copy-start | bytes 2359300
  43.5 8.1 %copy-start.13 = (bf16[256,1536]{1,0:T(8,128)(2,1)}, bf16[256,1536]{1,0:T(8,128)(2,1)S(1)}, u32[]{:S(2)}) copy-start(bf16[256,1536]{1,0:T(8,128)(2,1)S(1)} %get-tuple-element.123) | copy-start | bytes 2359300
  43.5 6.7 %collective-permute-start.10 = (bf16[256,1536]{1,0:T(8,128)(2,1)S(1)}, bf16[256,1536]{1,0:T(8,128)(2,1)S(1)}, u32[]{:S(2)}, u32[]{:S(2)}) collective-permute-start(bf16[256,1536]{1,0:T(8,128)(2,1)S(1)} %get-tuple-element.124), channel_id=1, source_target_pairs={{0,1},{1,0},{2,3},{3,2},{4,5},{5,4},{6,7},{7,6},{8,9},{9,8},{10,11... | collective-permute-start | bytes 2359304 | tf_op jit(solution)/shard_map/ppermute | solution.py:91
  43.6 8.0 %collective-permute-start.9 = (bf16[256,1536]{1,0:T(8,128)(2,1)S(1)}, bf16[256,1536]{1,0:T(8,128)(2,1)S(1)}, u32[]{:S(2)}, u32[]{:S(2)}) collective-permute-start(bf16[256,1536]{1,0:T(8,128)(2,1)S(1)} %get-tuple-element.123), channel_id=1, source_target_pairs={{0,1},{1,0},{2,3},{3,2},{4,5},{5,4},{6,7},{7,6},{8,9},{9,8},{10,11... | collective-permute-start | bytes 2359304 | tf_op jit(solution)/shard_map/ppermute | solution.py:91
  44.1 16.2 %collective-permute-start.11 = (bf16[2,64,1536]{2,1,0:T(8,128)(2,1)S(1)}, bf16[2,64,1536]{2,1,0:T(8,128)(2,1)}, u32[]{:S(2)}, u32[]{:S(2)}) collective-permute-start(bf16[2,64,1536]{2,1,0:T(8,128)(2,1)S(1)} %pad_maximum_fusion.3), channel_id=1, source_target_pairs={{0,2},{1,3},{2,4},{3,5},{4,6},{5,7},{6,0},{7,1},{8,10},{9,11},{10,... | collective-permute-start | bytes 1179656 | tf_op jit(solution)/shard_map/ppermute | solution.py:88
  45.5 19.9 %collective-permute-start.12 = (bf16[2,64,1536]{2,1,0:T(8,128)(2,1)S(1)}, bf16[2,64,1536]{2,1,0:T(8,128)(2,1)S(1)}, u32[]{:S(2)}, u32[]{:S(2)}) collective-permute-start(bf16[2,64,1536]{2,1,0:T(8,128)(2,1)S(1)} %pad_maximum_fusion.3), channel_id=1, source_target_pairs={{0,4},{1,5},{2,6},{3,7},{4,0},{5,1},{6,2},{7,3},{8,12},{9,13},{10,... | collective-permute-start | bytes 1179656 | tf_op jit(solution)/shard_map/ppermute | solution.py:88
  47.9 18.3 %collective-permute-start.13 = (bf16[2,64,1536]{2,1,0:T(8,128)(2,1)S(1)}, bf16[2,64,1536]{2,1,0:T(8,128)(2,1)S(1)}, u32[]{:S(2)}, u32[]{:S(2)}) collective-permute-start(bf16[2,64,1536]{2,1,0:T(8,128)(2,1)S(1)} %pad_maximum_fusion.3), channel_id=1, source_target_pairs={{0,6},{1,7},{2,0},{3,1},{4,2},{5,3},{6,4},{7,5},{8,14},{9,15},{10,... | collective-permute-start | bytes 1179656 | tf_op jit(solution)/shard_map/ppermute | solution.py:88
  50.2 1.4 copy-start.20
  51.7 1.4 copy-start.24
  54.4 25.3 %all-to-all-start = ((bf16[8,2,64,768]{3,2,1,0:T(8,128)(2,1)}), bf16[8,2,64,768]{3,2,1,0:T(8,128)(2,1)}, u32[]{:S(2)}, u32[]{:S(2)}) async-start(bf16[8,2,64,768]{3,2,1,0:T(8,128)(2,1)} %pad_maximum_fusion), calls=%async_computation | async-start | bytes 3145728 | tf_op jit(solution)/shard_map/all_to_all | solution.py:110
  62.1 7.0 %copy-start.17 = (f32[768]{0:T(1024)S(1)}, f32[768]{0:T(1024)}, u32[]{:S(2)}) copy-start(f32[768]{0:T(1024)} %param.7) | copy-start | bytes 9220
  62.1 8.7 %copy-start.19 = (bf16[768,1536]{1,0:T(8,128)(2,1)S(1)}, bf16[768,1536]{1,0:T(8,128)(2,1)}, u32[]{:S(2)}) copy-start(bf16[768,1536]{1,0:T(8,128)(2,1)} %param.8) | copy-start | bytes 7077892
  68.4 3.8 %copy-start.11 = (bf16[256,1536]{1,0:T(8,128)(2,1)}, bf16[256,1536]{1,0:T(8,128)(2,1)S(1)}, u32[]{:S(2)}) copy-start(bf16[256,1536]{1,0:T(8,128)(2,1)S(1)} %get-tuple-element.122) | copy-start | bytes 2359300
  68.4 3.8 %copy-start.15 = (bf16[256,1536]{1,0:T(8,128)(2,1)}, bf16[256,1536]{1,0:T(8,128)(2,1)S(1)}, u32[]{:S(2)}) copy-start(bf16[256,1536]{1,0:T(8,128)(2,1)S(1)} %get-tuple-element.121) | copy-start | bytes 2359300
  68.4 2.4 %collective-permute-start.15 = (bf16[256,1536]{1,0:T(8,128)(2,1)S(1)}, bf16[256,1536]{1,0:T(8,128)(2,1)S(1)}, u32[]{:S(2)}, u32[]{:S(2)}) collective-permute-start(bf16[256,1536]{1,0:T(8,128)(2,1)S(1)} %get-tuple-element.122), channel_id=1, source_target_pairs={{0,1},{1,0},{2,3},{3,2},{4,5},{5,4},{6,7},{7,6},{8,9},{9,8},{10,11... | collective-permute-start | bytes 2359304 | tf_op jit(solution)/shard_map/ppermute | solution.py:91
  68.5 3.7 %collective-permute-start.14 = (bf16[256,1536]{1,0:T(8,128)(2,1)S(1)}, bf16[256,1536]{1,0:T(8,128)(2,1)S(1)}, u32[]{:S(2)}, u32[]{:S(2)}) collective-permute-start(bf16[256,1536]{1,0:T(8,128)(2,1)S(1)} %get-tuple-element.121), channel_id=1, source_target_pairs={{0,1},{1,0},{2,3},{3,2},{4,5},{5,4},{6,7},{7,6},{8,9},{9,8},{10,11... | collective-permute-start | bytes 2359304 | tf_op jit(solution)/shard_map/ppermute | solution.py:91
  70.8 1.4 copy-start.22
  72.3 1.4 copy-start.26
  83.6 38.3 %all-to-all-start.1 = ((bf16[8,64,768]{2,1,0:T(8,128)(2,1)}), bf16[8,64,768]{2,1,0:T(8,128)(2,1)}, u32[]{:S(2)}, u32[]{:S(2)}) async-start(bf16[8,64,768]{2,1,0:T(8,128)(2,1)} %get-tuple-element.61), calls=%async_computation.1 | async-start | bytes 1572864 | tf_op jit(solution)/shard_map/all_to_all | solution.py:110
  89.8 15.8 %collective-permute-start.16 = (bf16[1,2,64,768]{3,2,1,0:T(8,128)(2,1)S(1)}, bf16[1,2,64,768]{3,2,1,0:T(8,128)(2,1)S(1)}, u32[]{:S(2)}, u32[]{:S(2)}) collective-permute-start(bf16[1,2,64,768]{3,2,1,0:T(8,128)(2,1)S(1)} %get-tuple-element.120), channel_id=1, source_target_pairs={{0,192},{32,224},{64,128},{96,160},{128,64},{160,96},{192,0},{224,... | collective-permute-start | bytes 589832 | tf_op jit(solution)/shard_map/ppermute | solution.py:118
  92.9 21.3 %collective-permute-start.17 = (bf16[1,2,64,768]{3,2,1,0:T(8,128)(2,1)S(1)}, bf16[1,2,64,768]{3,2,1,0:T(8,128)(2,1)S(1)}, u32[]{:S(2)}, u32[]{:S(2)}) collective-permute-start(bf16[1,2,64,768]{3,2,1,0:T(8,128)(2,1)S(1)} %get-tuple-element.119), channel_id=1, source_target_pairs={{0,64},{32,96},{64,0},{96,32},{128,192},{160,224},{192,128},{224,1... | collective-permute-start | bytes 589832 | tf_op jit(solution)/shard_map/ppermute | solution.py:118
  93.0 22.4 %collective-permute-start.18 = (bf16[1,2,64,768]{3,2,1,0:T(8,128)(2,1)S(1)}, bf16[1,2,64,768]{3,2,1,0:T(8,128)(2,1)S(1)}, u32[]{:S(2)}, u32[]{:S(2)}) collective-permute-start(bf16[1,2,64,768]{3,2,1,0:T(8,128)(2,1)S(1)} %get-tuple-element.118), channel_id=1, source_target_pairs={{0,160},{32,128},{64,224},{96,192},{128,32},{160,0},{192,96},{224,... | collective-permute-start | bytes 589832 | tf_op jit(solution)/shard_map/ppermute | solution.py:118
  95.8 20.1 %collective-permute-start.19 = (bf16[1,2,64,768]{3,2,1,0:T(8,128)(2,1)S(1)}, bf16[1,2,64,768]{3,2,1,0:T(8,128)(2,1)S(1)}, u32[]{:S(2)}, u32[]{:S(2)}) collective-permute-start(bf16[1,2,64,768]{3,2,1,0:T(8,128)(2,1)S(1)} %get-tuple-element.117), channel_id=1, source_target_pairs={{0,32},{32,0},{64,96},{96,64},{128,160},{160,128},{192,224},{224,1... | collective-permute-start | bytes 589832 | tf_op jit(solution)/shard_map/ppermute | solution.py:118
  96.4 19.5 %collective-permute-start.20 = (bf16[1,2,64,768]{3,2,1,0:T(8,128)(2,1)S(1)}, bf16[1,2,64,768]{3,2,1,0:T(8,128)(2,1)S(1)}, u32[]{:S(2)}, u32[]{:S(2)}) collective-permute-start(bf16[1,2,64,768]{3,2,1,0:T(8,128)(2,1)S(1)} %get-tuple-element.116), channel_id=1, source_target_pairs={{0,128},{32,160},{64,192},{96,224},{128,0},{160,32},{192,64},{224,... | collective-permute-start | bytes 589832 | tf_op jit(solution)/shard_map/ppermute | solution.py:118
  105.7 11.5 %collective-permute-start.21 = (bf16[1,2,64,768]{3,2,1,0:T(8,128)(2,1)S(1)}, bf16[1,2,64,768]{3,2,1,0:T(8,128)(2,1)S(1)}, u32[]{:S(2)}, u32[]{:S(2)}) collective-permute-start(bf16[1,2,64,768]{3,2,1,0:T(8,128)(2,1)S(1)} %get-tuple-element.115), channel_id=1, source_target_pairs={{0,224},{32,192},{64,160},{96,128},{128,96},{160,64},{192,32},{224... | collective-permute-start | bytes 589832 | tf_op jit(solution)/shard_map/ppermute | solution.py:118
  114.2 7.0 %collective-permute-start.22 = (bf16[1,2,64,768]{3,2,1,0:T(8,128)(2,1)S(1)}, bf16[1,2,64,768]{3,2,1,0:T(8,128)(2,1)S(1)}, u32[]{:S(2)}, u32[]{:S(2)}) collective-permute-start(bf16[1,2,64,768]{3,2,1,0:T(8,128)(2,1)S(1)} %get-tuple-element.113), channel_id=1, source_target_pairs={{0,96},{32,64},{64,32},{96,0},{128,224},{160,192},{192,160},{224,1... | collective-permute-start | bytes 589832 | tf_op jit(solution)/shard_map/ppermute | solution.py:118
  121.2 0.7 copy-start.4
  124.0 0.9 copy-start.3
  124.9 0.9 copy-start.5
  125.9 0.9 copy-start.7
  128.6 1.1 copy-start.1
  129.7 6.7 %copy-start.8 = (bf16[4,64,768]{2,1,0:T(8,128)(2,1)S(1)}, bf16[4,64,768]{2,1,0:T(8,128)(2,1)}, u32[]{:S(2)}) copy-start(bf16[4,64,768]{2,1,0:T(8,128)(2,1)} %get-tuple-element.136) | copy-start | bytes 1179652
  129.8 15.8 %all-to-all-start.2 = ((bf16[8,64,768]{2,1,0:T(8,128)(2,1)}), bf16[8,64,768]{2,1,0:T(8,128)(2,1)S(1)}, u32[]{:S(2)}, u32[]{:S(2)}) async-start(bf16[8,64,768]{2,1,0:T(8,128)(2,1)} %get-tuple-element.75), calls=%async_computation.2 | async-start | bytes 1572864 | tf_op jit(solution)/shard_map/all_to_all | solution.py:110
  136.4 2.4 %collective-permute-start.23 = (bf16[256,1536]{1,0:T(8,128)(2,1)S(1)}, bf16[256,1536]{1,0:T(8,128)(2,1)S(1)}, u32[]{:S(2)}, u32[]{:S(2)}) collective-permute-start(bf16[256,1536]{1,0:T(8,128)(2,1)S(1)} %convolution_convert_fusion.1), channel_id=1, source_target_pairs={{0,1},{1,0},{2,3},{3,2},{4,5},{5,4},{6,7},{7,6},{8,9},{9,8},{10,11... | collective-permute-start | bytes 2359304 | tf_op jit(solution)/shard_map/ppermute | solution.py:91
  139.6 8.4 %collective-permute-start.24 = (bf16[64,1536]{1,0:T(8,128)(2,1)}, bf16[64,1536]{1,0:T(8,128)(2,1)}, u32[]{:S(2)}, u32[]{:S(2)}) collective-permute-start(bf16[64,1536]{1,0:T(8,128)(2,1)} %get-tuple-element.111), channel_id=1, source_target_pairs={{0,6},{1,7},{2,0},{3,1},{4,2},{5,3},{6,4},{7,5},{8,14},{9,15},{10,... | collective-permute-start | bytes 589832 | tf_op jit(solution)/shard_map/ppermute | solution.py:88
  139.9 9.6 %collective-permute-start.25 = (bf16[64,1536]{1,0:T(8,128)(2,1)}, bf16[64,1536]{1,0:T(8,128)(2,1)}, u32[]{:S(2)}, u32[]{:S(2)}) collective-permute-start(bf16[64,1536]{1,0:T(8,128)(2,1)} %get-tuple-element.110), channel_id=1, source_target_pairs={{0,4},{1,5},{2,6},{3,7},{4,0},{5,1},{6,2},{7,3},{8,12},{9,13},{10,... | collective-permute-start | bytes 589832 | tf_op jit(solution)/shard_map/ppermute | solution.py:88
  142.1 10.5 %collective-permute-start.26 = (bf16[64,1536]{1,0:T(8,128)(2,1)}, bf16[64,1536]{1,0:T(8,128)(2,1)}, u32[]{:S(2)}, u32[]{:S(2)}) collective-permute-start(bf16[64,1536]{1,0:T(8,128)(2,1)} %get-tuple-element.109), channel_id=1, source_target_pairs={{0,2},{1,3},{2,4},{3,5},{4,6},{5,7},{6,0},{7,1},{8,10},{9,11},{10,... | collective-permute-start | bytes 589832 | tf_op jit(solution)/shard_map/ppermute | solution.py:88
  152.6 7.6 %collective-permute-start.27 = (bf16[256,1536]{1,0:T(8,128)(2,1)}, bf16[256,1536]{1,0:T(8,128)(2,1)}, u32[]{:S(2)}, u32[]{:S(2)}) collective-permute-start(bf16[256,1536]{1,0:T(8,128)(2,1)} %convolution_convert_fusion), channel_id=1, source_target_pairs={{0,1},{1,0},{2,3},{3,2},{4,5},{5,4},{6,7},{7,6},{8,9},{9,8},{10,11... | collective-permute-start | bytes 2359304 | tf_op jit(solution)/shard_map/ppermute | solution.py:91
  152.6 30.6 %all-to-all-start.3 = ((bf16[8,2,64,768]{3,2,1,0:T(8,128)(2,1)}), bf16[8,2,64,768]{3,2,1,0:T(8,128)(2,1)}, u32[]{:S(2)}, u32[]{:S(2)}) async-start(bf16[8,2,64,768]{3,2,1,0:T(8,128)(2,1)} %copy-done.1), calls=%async_computation.3 | async-start | bytes 3145728 | tf_op jit(solution)/shard_map/all_to_all | solution.py:110
  160.1 4.9 %copy-start.14 = (bf16[256,1536]{1,0:T(8,128)(2,1)S(1)}, bf16[256,1536]{1,0:T(8,128)(2,1)}, u32[]{:S(2)}) copy-start(bf16[256,1536]{1,0:T(8,128)(2,1)} %copy-done.13) | copy-start | bytes 2359300
  160.1 4.9 %copy-start.16 = (bf16[256,1536]{1,0:T(8,128)(2,1)S(1)}, bf16[256,1536]{1,0:T(8,128)(2,1)}, u32[]{:S(2)}) copy-start(bf16[256,1536]{1,0:T(8,128)(2,1)} %copy-done.15) | copy-start | bytes 2359300
  160.2 4.9 %copy-start.25 = (bf16[256,1536]{1,0:T(8,128)(2,1)S(1)}, bf16[256,1536]{1,0:T(8,128)(2,1)}, u32[]{:S(2)}) copy-start(bf16[256,1536]{1,0:T(8,128)(2,1)} %copy-done.24) | copy-start | bytes 2359300
  160.2 4.8 %copy-start.27 = (bf16[256,1536]{1,0:T(8,128)(2,1)S(1)}, bf16[256,1536]{1,0:T(8,128)(2,1)}, u32[]{:S(2)}) copy-start(bf16[256,1536]{1,0:T(8,128)(2,1)} %copy-done.26) | copy-start | bytes 2359300
  161.8 8.3 %collective-permute-start.28 = (bf16[64,1536]{1,0:T(8,128)(2,1)S(1)}, bf16[64,1536]{1,0:T(8,128)(2,1)S(1)}, u32[]{:S(2)}, u32[]{:S(2)}) collective-permute-start(bf16[64,1536]{1,0:T(8,128)(2,1)S(1)} %get-tuple-element.85), channel_id=1, source_target_pairs={{0,6},{1,7},{2,0},{3,1},{4,2},{5,3},{6,4},{7,5},{8,14},{9,15},{10,... | collective-permute-start | bytes 589832 | tf_op jit(solution)/shard_map/ppermute | solution.py:88
  163.0 9.3 %collective-permute-start.29 = (bf16[64,1536]{1,0:T(8,128)(2,1)S(1)}, bf16[64,1536]{1,0:T(8,128)(2,1)S(1)}, u32[]{:S(2)}, u32[]{:S(2)}) collective-permute-start(bf16[64,1536]{1,0:T(8,128)(2,1)S(1)} %get-tuple-element.86), channel_id=1, source_target_pairs={{0,4},{1,5},{2,6},{3,7},{4,0},{5,1},{6,2},{7,3},{8,12},{9,13},{10,... | collective-permute-start | bytes 589832 | tf_op jit(solution)/shard_map/ppermute | solution.py:88
  164.7 10.5 %collective-permute-start.30 = (bf16[64,1536]{1,0:T(8,128)(2,1)S(1)}, bf16[64,1536]{1,0:T(8,128)(2,1)S(1)}, u32[]{:S(2)}, u32[]{:S(2)}) collective-permute-start(bf16[64,1536]{1,0:T(8,128)(2,1)S(1)} %get-tuple-element.87), channel_id=1, source_target_pairs={{0,2},{1,3},{2,4},{3,5},{4,6},{5,7},{6,0},{7,1},{8,10},{9,11},{10,... | collective-permute-start | bytes 589832 | tf_op jit(solution)/shard_map/ppermute | solution.py:88
  176.4 8.5 %copy-start.10 = (bf16[256,1536]{1,0:T(8,128)(2,1)S(1)}, bf16[256,1536]{1,0:T(8,128)(2,1)}, u32[]{:S(2)}) copy-start(bf16[256,1536]{1,0:T(8,128)(2,1)} %copy-done.9) | copy-start | bytes 2359300
  177.1 12.2 %collective-permute-start.31 = (bf16[32,1536]{1,0:T(8,128)(2,1)}, bf16[32,1536]{1,0:T(8,128)(2,1)S(1)}, u32[]{:S(2)}, u32[]{:S(2)}) collective-permute-start(bf16[32,1536]{1,0:T(8,128)(2,1)} %pad_maximum_fusion.7), channel_id=1, source_target_pairs={{0,24},{8,0},{16,8},{24,16},{1,25},{9,1},{17,9},{25,17},{2,26},{10... | collective-permute-start | bytes 294920 | tf_op jit(solution)/shard_map/ppermute | solution.py:85
  179.8 10.8 %collective-permute-start.32 = (bf16[32,1536]{1,0:T(8,128)(2,1)}, bf16[32,1536]{1,0:T(8,128)(2,1)S(1)}, u32[]{:S(2)}, u32[]{:S(2)}) collective-permute-start(bf16[32,1536]{1,0:T(8,128)(2,1)} %pad_maximum_fusion.8), channel_id=1, source_target_pairs={{0,16},{8,24},{16,0},{24,8},{1,17},{9,25},{17,1},{25,9},{2,18},{10... | collective-permute-start | bytes 294920 | tf_op jit(solution)/shard_map/ppermute | solution.py:85
  180.7 12.4 %collective-permute-start.33 = (bf16[32,1536]{1,0:T(8,128)(2,1)}, bf16[32,1536]{1,0:T(8,128)(2,1)}, u32[]{:S(2)}, u32[]{:S(2)}) collective-permute-start(bf16[32,1536]{1,0:T(8,128)(2,1)} %pad_maximum_fusion.9), channel_id=1, source_target_pairs={{0,8},{8,16},{16,24},{24,0},{1,9},{9,17},{17,25},{25,1},{2,10},{10... | collective-permute-start | bytes 294920 | tf_op jit(solution)/shard_map/ppermute | solution.py:85
  183.2 1.7 copy-start.12
  183.3 1.8 copy-start.21
  183.3 2.1 %copy-start.23 = (bf16[256,1536]{1,0:T(8,128)(2,1)S(1)}, bf16[256,1536]{1,0:T(8,128)(2,1)}, u32[]{:S(2)}) copy-start(bf16[256,1536]{1,0:T(8,128)(2,1)} %copy-done.22) | copy-start | bytes 2359300
  (2 other events, 1.3 us)

commit v9 on v8

--- a/solution.py
+++ b/solution.py
@@ -35,14 +35,13 @@
     return pltpu.CompilerParams(vmem_limit_bytes=mib << 20)
 
 
-def hidden_kernel(n_parts, n_copies, bias, *refs):
-    parts, before, (grad_copies, act_out) = refs[:n_parts], refs[n_parts:-2], refs[-2:]
-    blocks = [ref[j] for ref in parts for j in range(ref.shape[0])]
-    sums = blocks[0].astype(f32)
-    for block in blocks[1:]:
-        sums = sums + block.astype(f32)
+def hidden_kernel(parts, bias, *refs):
+    before, (grad_copies, act_out) = refs[:-2], refs[-2:]
+    sums = parts[0].astype(f32)
+    for j in range(1, parts.shape[0]):
+        sums = sums + parts[j].astype(f32)
     act, grad = gelu_pair(sums[0] + bias[...], sums[1])
-    for j in range(n_copies):
+    for j in range(parts.shape[0]):
         grad_copies[j] = grad
         if before:
             act_out[j, 0] = before[0][...]
@@ -51,31 +50,68 @@
         act_out[...] = act
 
 
-def hidden(parts, n_copies, bias, *before):
-    pair, rows, columns = parts[0].shape[1:]
+def hidden(parts, bias, *before):
+    n, pair, rows, columns = parts.shape
     tile = columns // 3
-    act_shape = (n_copies, 2, rows) if before else (rows,)
+    act_shape = (n, 2, rows) if before else (rows,)
     return pl.pallas_call(
-        functools.partial(hidden_kernel, len(parts), n_copies),
+        hidden_kernel,
         grid=(columns // tile,),
-        in_specs=[pl.BlockSpec((1, tile), lambda i: (0, i))]
-        + [pl.BlockSpec((a.shape[0], pair, rows, tile), lambda i: (0, 0, 0, i)) for a in parts]
+        in_specs=[
+            pl.BlockSpec((n, pair, rows, tile), lambda i: (0, 0, 0, i)),
+            pl.BlockSpec((1, tile), lambda i: (0, i)),
+        ]
         + [pl.BlockSpec((rows, tile), lambda i: (0, i))] * len(before),
         out_specs=[
-            pl.BlockSpec((n_copies, rows, tile), lambda i: (0, 0, i)),
+            pl.BlockSpec((n, rows, tile), lambda i: (0, 0, i)),
             pl.BlockSpec((*act_shape, tile), lambda i: (*([0] * len(act_shape)), i)),
         ],
         out_shape=[
-            jax.ShapeDtypeStruct((n_copies, rows, columns), bf16),
+            jax.ShapeDtypeStruct((n, rows, columns), bf16),
             jax.ShapeDtypeStruct((*act_shape, columns), bf16),
         ],
-        compiler_params=pltpu.CompilerParams(vmem_limit_bytes=32 << 20),
+        compiler_params=pltpu.CompilerParams(vmem_limit_bytes=8 << 20),
         cost_estimate=pl.CostEstimate(
             flops=40 * rows * columns,
-            bytes_accessed=6 * n_copies * rows * columns,
+            bytes_accessed=6 * n * rows * columns,
             transcendentals=rows * columns,
         ),
-    )(bias, *parts, *before)
+    )(parts, bias, *before)
+
+
+def join_kernel(n, *refs):
+    ins, outs = refs[:-n], refs[-n:]
+    chunk_rows = ins[0].shape[0] // n
+    chunks = [ins[j : j + n] for j in range(0, len(ins), n)]
+    for c, parts in enumerate(chunks):
+        total = parts[0][...]
+        for part in parts[1:]:
+            total = total + part[...].astype(f32)
+        for k, out in enumerate(outs):
+            block = total[k * chunk_rows : (k + 1) * chunk_rows]
+            out[c * chunk_rows : (c + 1) * chunk_rows] = block.astype(out.dtype)
+
+
+def join_sums(chunks, n):
+    rows, columns = chunks[0][0].shape
+    tile = columns // 3
+    out_rows = len(chunks) * rows // n
+    ins = [part for parts in chunks for part in parts]
+    return pl.pallas_call(
+        functools.partial(join_kernel, n),
+        grid=(columns // tile,),
+        in_specs=[pl.BlockSpec((rows, tile), lambda i: (0, i))] * len(ins),
+        out_specs=[pl.BlockSpec((out_rows, tile), lambda i: (0, i))] * n,
+        out_shape=[
+            jax.ShapeDtypeStruct((out_rows, columns), bf16 if k else f32) for k in range(n)
+        ],
+        compiler_params=pltpu.CompilerParams(vmem_limit_bytes=8 << 20),
+        cost_estimate=pl.CostEstimate(
+            flops=len(ins) * rows * columns,
+            bytes_accessed=2 * len(ins) * rows * columns,
+            transcendentals=0,
+        ),
+    )(*ins)
 
 
 def solution(mesh):
@@ -109,16 +145,6 @@
     def trade_width(parts):
         return lax.all_to_all(parts, "gx", 0, 0, tiled=True)
 
-    def permute_width(parts):
-        place = lax.axis_index("gx").astype(jnp.uint32)
-        received = []
-        for flip in sorted(range(n_x), key=lambda flip: -(flip // (n_x // 2) + (flip % (n_x // 2)) % 3)):
-            block = lax.dynamic_slice_in_dim(parts, place ^ flip, 1, axis=0)
-            if flip:
-                block = lax.ppermute(block, "gx", [(i, i ^ flip) for i in range(n_x)])
-            received.append(block)
-        return received
-
     def after(a, *others):
         return lax.optimization_barrier((a, *others))[0]
 
@@ -154,18 +180,18 @@
         both0, part0 = partial_sums(chips0)
         both1, part1 = partial_sums([far1] + [shift_chip(far1, k) for k in range(1, n_chip)])
         sums0 = trade_width(part0)
-        sums0, part1 = barrier(sums0, part1)
-        sums1 = permute_width(part1)
-        grad_copies0, act0 = hidden([sums0], n_x, bias)
+        sums1 = trade_width(part1)
+        grad_copies0, act0 = hidden(sums0, bias)
         columns = act0.shape[1]
+        grad_copies0, sums1 = barrier(grad_copies0, sums1)
         hidden0 = trade_width(grad_copies0)
-        hidden0, sums1 = barrier(hidden0, sums1)
-        grad_copies1, act_copies = hidden(sums1, n_x, bias, act0)
-        hidden1 = trade_width(grad_copies1).reshape(-1, columns)
+        grad_copies1, act_copies = hidden(sums1, bias, act0)
+        hidden1 = trade_width(after(grad_copies1, hidden0)).reshape(-1, columns)
         hidden0 = hidden0.reshape(-1, columns)
         other0, own0 = two_halves(hidden0)
         own0, other0 = barrier(own0, swap_core(other0))
-        parts0 = exchange(sum_blocks([own0, other0], n_chip), shift_chip)
+        parts0, act_copies = barrier(sum_blocks([own0, other0], n_chip), act_copies)
+        parts0 = exchange(parts0, shift_chip)
         other1, own1 = two_halves(hidden1)
         parts0, other1, act_copies = barrier(parts0, other1, act_copies)
         activation = trade_width(act_copies)
@@ -176,10 +202,7 @@
         tokens_all = jnp.concatenate([both0[0], both1[0]], axis=0)
         grad_weight_in = (contract_first(tokens_all, hidden_all) * norm_scale).astype(bf16)
         parts0, parts1, grad_weight_in = barrier(parts0, parts1, grad_weight_in)
-        parts = [
-            jnp.concatenate(pair, axis=0)
-            for pair in zip(sum_blocks(parts0, n_y), sum_blocks(parts1, n_y))
-        ]
+        parts = join_sums([parts0, parts1], n_y)
         parts = exchange(parts, shift_y)
         activation = activation.transpose(1, 0, 2, 3).reshape(-1, columns)
         grad_all = jnp.concatenate([both0[1], both1[1]], axis=0)

time: 196 us -> 183 us (0.934)
  local copies, waits for them, and re-layouts: 19.3 us -> 11.8 us
  starting transfers between devices: 71.2 us -> 65 us
  other arithmetic: 9.87 us -> 4.49 us
  Pallas kernels: 5.08 us -> 8.14 us
  waiting for transfers between devices: 67.4 us -> 69.6 us
    all_to_all x4 -> x5, waiting for transfers between devices: 8.11 us -> 33.2 us  [trade_width(): return lax.all_to_all(parts, 'gx', 0, 0, tiled=True)]
    ppermute x7 -> x0, waiting for transfers between devices: 20.6 us -> none  [permute_width(): block = lax.ppermute(block, 'gx', [(i, i ^ flip) for i in range(n_x)])]
    ppermute x7 -> x0, starting transfers between devices: 10.1 us -> none  [permute_width(): block = lax.ppermute(block, 'gx', [(i, i ^ flip) for i in range(n_x)])]
    unnamed x62 -> x48, local copies, waits for them, and re-layouts: 9.71 us -> 4.78 us
    all_to_all x4 -> x5, starting transfers between devices: 21.1 us -> 25.2 us  [trade_width(): return lax.all_to_all(parts, 'gx', 0, 0, tiled=True)]
    pallas_call x2 -> x3, Pallas kernels: 5.08 us -> 8.14 us  [the longest x2 6.54 us: hidden(): pl.pallas_call(hidden_kernel, grid=(columns // tile,), in_specs=[pl.Block...]
    convert_element_type x4 -> x2, other arithmetic: 3.69 us -> 1.14 us  [sum_blocks(): return sums[:1] + [a.astype(bf16) for a in sums[1:]]]
    slice x1, local copies, waits for them, and re-layouts: 2.09 us -> 0.05 us  [two_halves(): other = contract_last(grad_hidden[half:], weight_in).astype(bf16)]
  transfers between devices with their start and end apart: 38 -> 32, of which waited for: 21 -> 18; matrix products, arithmetic and copies ran while one was open for 20% -> 19% of each run, Pallas kernels for 0% -> 4%
where the time goes in v9:
time: 183 us; the launch traced here: 181 us
  waiting for transfers between devices  69.6 us (38%)
  starting transfers between devices  65 us (36%)
  matrix products  21.3 us (12%)
  local copies, waits for them, and re-layouts  11.8 us (6%)
  Pallas kernels  8.14 us (4%)
  other arithmetic  4.49 us (2%)
    all_to_all x5, waiting for transfers between devices, trade_width(): return lax.all_to_all(parts, 'gx', 0, 0, tiled=True)  33.2 us
    all_to_all x5, starting transfers between devices, trade_width(): return lax.all_to_all(parts, 'gx', 0, 0, tiled=True)  25.2 us
    ppermute x9, starting transfers between devices, shift_y(): return lax.ppermute(a, 'gy', [(i, (i + k) % n_y) for i in range(n_y)])  22 us
    ppermute x9, waiting for transfers between devices, shift_y(): return lax.ppermute(a, 'gy', [(i, (i + k) % n_y) for i in range(n_y)])  16.8 us
    ppermute x12, starting transfers between devices, shift_chip(): return lax.ppermute(a, 'gz', [(i, (i + 2 * k) % n_z) for i in range(n_z)])  16.5 us
    ppermute x12, waiting for transfers between devices, shift_chip(): return lax.ppermute(a, 'gz', [(i, (i + 2 * k) % n_z) for i in range(n_z)])  15.8 us
    dot_general x2, matrix products, contract_first(): lax.dot_general(left, right, (((0,), (0,)), ((), ())), preferred_element_...  10.5 us
    dot_general x6, matrix products, contract_last(): lax.dot_general(left, right, (((1,), (1,)), ((), ())), preferred_element_...  8 us
  transfers between devices with their start and end apart: 32, of which 18 were waited for; matrix products, arithmetic and copies ran while one was open for 19% of the time, Pallas kernels for 4%

profile of v9, /device:TPU:32, one launch (start us, length us, event | category | flops | bytes accessed | tf_op | source)
XLA Modules:
  0.0 181.4 jit_solution(16271804332804028859)
XLA Ops:
  0.6 1.0 slice_bitcast_fusion.4
  1.7 5.5 %collective-permute-start.2 = (bf16[2,16,1536]{2,1,0:T(8,128)(2,1)S(1)}, bf16[2,16,1536]{2,1,0:T(8,128)(2,1)S(1)}, u32[]{:S(2)}, u32[]{:S(2)}) collective-permute-start(bf16[2,16,1536]{2,1,0:T(8,128)(2,1)S(1)} %pad_maximum_fusion.4), channel_id=1, source_target_pairs={{0,24},{8,0},{16,8},{24,16},{1,25},{9,1},{17,9},{25,17},{2,26},{10... | collective-permute-start | bytes 294920 | tf_op jit(solution)/shard_map/ppermute | solution.py:121
  7.2 1.4 collective-permute-start.1
  8.6 2.4 %collective-permute-start = (bf16[2,16,1536]{2,1,0:T(8,128)(2,1)S(1)}, bf16[2,16,1536]{2,1,0:T(8,128)(2,1)S(1)}, u32[]{:S(2)}, u32[]{:S(2)}) collective-permute-start(bf16[2,16,1536]{2,1,0:T(8,128)(2,1)S(1)} %pad_maximum_fusion.4), channel_id=1, source_target_pairs={{0,8},{8,16},{16,24},{24,0},{1,9},{9,17},{17,25},{25,1},{2,10},{10... | collective-permute-start | bytes 294920 | tf_op jit(solution)/shard_map/ppermute | solution.py:121
  11.0 7.0 %collective-permute-done.1 = bf16[2,16,1536]{2,1,0:T(8,128)(2,1)S(1)} collective-permute-done((bf16[2,16,1536]{2,1,0:T(8,128)(2,1)S(1)}, bf16[2,16,1536]{2,1,0:T(8,128)(2,1)S(1)}, u32[]{:S(2)}, u32[]{:S(2)}) %collective-permute-start.1) | collective-permute-done | bytes 98336 | tf_op jit(solution)/shard_map/ppermute | solution.py:121
  18.7 3.7 %collective-permute-start.8 = (bf16[2,16,1536]{2,1,0:T(8,128)(2,1)S(1)}, bf16[2,16,1536]{2,1,0:T(8,128)(2,1)S(1)}, u32[]{:S(2)}, u32[]{:S(2)}) collective-permute-start(bf16[2,16,1536]{2,1,0:T(8,128)(2,1)S(1)} %pad_maximum_fusion.5), channel_id=1, source_target_pairs={{0,24},{8,0},{16,8},{24,16},{1,25},{9,1},{17,9},{25,17},{2,26},{10... | collective-permute-start | bytes 294920 | tf_op jit(solution)/shard_map/ppermute | solution.py:121
  22.4 1.5 collective-permute-start.3
  23.9 2.7 %collective-permute-start.4 = (bf16[2,64,1536]{2,1,0:T(8,128)(2,1)S(1)}, bf16[2,64,1536]{2,1,0:T(8,128)(2,1)S(1)}, u32[]{:S(2)}, u32[]{:S(2)}) collective-permute-start(bf16[2,64,1536]{2,1,0:T(8,128)(2,1)S(1)} %pad_maximum_fusion.2), channel_id=1, source_target_pairs={{0,4},{1,5},{2,6},{3,7},{4,0},{5,1},{6,2},{7,3},{8,12},{9,13},{10,... | collective-permute-start | bytes 1179656 | tf_op jit(solution)/shard_map/ppermute | solution.py:124
  26.6 1.4 collective-permute-start.5
  28.0 1.7 collective-permute-start.7
  29.8 2.4 %collective-permute-start.6 = (bf16[2,16,1536]{2,1,0:T(8,128)(2,1)S(1)}, bf16[2,16,1536]{2,1,0:T(8,128)(2,1)S(1)}, u32[]{:S(2)}, u32[]{:S(2)}) collective-permute-start(bf16[2,16,1536]{2,1,0:T(8,128)(2,1)S(1)} %pad_maximum_fusion.5), channel_id=1, source_target_pairs={{0,8},{8,16},{16,24},{24,0},{1,9},{9,17},{17,25},{25,1},{2,10},{10... | collective-permute-start | bytes 294920 | tf_op jit(solution)/shard_map/ppermute | solution.py:121
  32.2 5.3 %collective-permute-done.7 = bf16[2,16,1536]{2,1,0:T(8,128)(2,1)S(1)} collective-permute-done((bf16[2,16,1536]{2,1,0:T(8,128)(2,1)S(1)}, bf16[2,16,1536]{2,1,0:T(8,128)(2,1)S(1)}, u32[]{:S(2)}, u32[]{:S(2)}) %collective-permute-start.7) | collective-permute-done | bytes 98336 | tf_op jit(solution)/shard_map/ppermute | solution.py:121
  37.4 1.0 collective-permute-done.6
  38.5 4.8 %collective-permute-done.4 = bf16[2,64,1536]{2,1,0:T(8,128)(2,1)S(1)} collective-permute-done((bf16[2,64,1536]{2,1,0:T(8,128)(2,1)S(1)}, bf16[2,64,1536]{2,1,0:T(8,128)(2,1)S(1)}, u32[]{:S(2)}, u32[]{:S(2)}) %collective-permute-start.4) | collective-permute-done | bytes 393248 | tf_op jit(solution)/shard_map/ppermute | solution.py:124
  44.1 1.3 collective-permute-start.11
  45.5 2.4 %collective-permute-start.12 = (bf16[2,64,1536]{2,1,0:T(8,128)(2,1)S(1)}, bf16[2,64,1536]{2,1,0:T(8,128)(2,1)S(1)}, u32[]{:S(2)}, u32[]{:S(2)}) collective-permute-start(bf16[2,64,1536]{2,1,0:T(8,128)(2,1)S(1)} %pad_maximum_fusion.3), channel_id=1, source_target_pairs={{0,4},{1,5},{2,6},{3,7},{4,0},{5,1},{6,2},{7,3},{8,12},{9,13},{10,... | collective-permute-start | bytes 1179656 | tf_op jit(solution)/shard_map/ppermute | solution.py:124
  47.9 1.6 collective-permute-start.13
  49.4 0.8 constant_dynamic-update-slice_fusion.7
  50.2 1.4 fusion.39
  51.7 1.4 fusion.42
  53.1 1.3 pad_maximum_fusion
  54.4 5.9 %all-to-all-start = ((bf16[8,2,64,768]{3,2,1,0:T(8,128)(2,1)}), bf16[8,2,64,768]{3,2,1,0:T(8,128)(2,1)}, u32[]{:S(2)}, u32[]{:S(2)}) async-start(bf16[8,2,64,768]{3,2,1,0:T(8,128)(2,1)} %pad_maximum_fusion), calls=%async_computation | async-start | bytes 3145728 | tf_op jit(solution)/shard_map/all_to_all | solution.py:146
  60.3 1.8 constant_dynamic-update-slice_fusion.6
  62.1 3.3 %collective-permute-done.12 = bf16[2,64,1536]{2,1,0:T(8,128)(2,1)S(1)} collective-permute-done((bf16[2,64,1536]{2,1,0:T(8,128)(2,1)S(1)}, bf16[2,64,1536]{2,1,0:T(8,128)(2,1)S(1)}, u32[]{:S(2)}, u32[]{:S(2)}) %collective-permute-start.12) | collective-permute-done | bytes 393248 | tf_op jit(solution)/shard_map/ppermute | solution.py:124
  65.4 0.8 constant_dynamic-update-slice_fusion.5
  66.2 0.8 constant_dynamic-update-slice_fusion.4
  66.9 1.5 slice_bitcast_fusion.1
  69.0 1.8 collective-permute-done.15
  70.8 1.4 fusion.33
  72.3 1.4 fusion.36
  73.7 1.3 pad_maximum_fusion.1
  75.0 4.7 %all-to-all-done.parts = bf16[8,2,64,768]{3,2,1,0:T(8,128)(2,1)} async-done(((bf16[8,2,64,768]{3,2,1,0:T(8,128)(2,1)}), bf16[8,2,64,768]{3,2,1,0:T(8,128)(2,1)}, u32[]{:S(2)}, u32[]{:S(2)}) %all-to-all-start) | async-done | bytes 1572896 | tf_op jit(solution)/shard_map/all_to_all | solution.py:146
  79.7 4.8 %all-to-all-start.1 = ((bf16[8,2,64,768]{3,2,1,0:T(8,128)(2,1)}), bf16[8,2,64,768]{3,2,1,0:T(8,128)(2,1)}, u32[]{:S(2)}, u32[]{:S(2)}) async-start(bf16[8,2,64,768]{3,2,1,0:T(8,128)(2,1)} %pad_maximum_fusion.1), calls=%async_computation.1 | async-start | bytes 3145728 | tf_op jit(solution)/shard_map/all_to_all | solution.py:146
  84.5 3.3 %shard_map.76 = (bf16[8,64,768]{2,1,0:T(8,128)(2,1)}, bf16[64,768]{1,0:T(8,128)(2,1)S(1)}) custom-call(bf16[8,2,64,768]{3,2,1,0:T(8,128)(2,1)} %all-to-all-done.parts, f32[1,768]{1,0:T(1,128)S(1)} %reshape.36.bias), custom_call_target="tpu_custom_call" | custom-call | flops 1966080 | bytes 2359296 | tf_op jit(solution)/shard_map/pallas_call | solution.py:57
  87.8 16.8 %all-to-all-done.1.parts = bf16[8,2,64,768]{3,2,1,0:T(8,128)(2,1)} async-done(((bf16[8,2,64,768]{3,2,1,0:T(8,128)(2,1)}), bf16[8,2,64,768]{3,2,1,0:T(8,128)(2,1)}, u32[]{:S(2)}, u32[]{:S(2)}) %all-to-all-start.1) | async-done | bytes 1572896 | tf_op jit(solution)/shard_map/all_to_all | solution.py:146
  104.6 4.2 %all-to-all-start.2 = ((bf16[8,64,768]{2,1,0:T(8,128)(2,1)}), bf16[8,64,768]{2,1,0:T(8,128)(2,1)S(1)}, u32[]{:S(2)}, u32[]{:S(2)}) async-start(bf16[8,64,768]{2,1,0:T(8,128)(2,1)} %get-tuple-element.62), calls=%async_computation.2 | async-start | bytes 1572864 | tf_op jit(solution)/shard_map/all_to_all | solution.py:146
  108.7 3.3 %shard_map.77 = (bf16[8,64,768]{2,1,0:T(8,128)(2,1)}, bf16[8,2,64,768]{3,2,1,0:T(8,128)(2,1)S(1)}) custom-call(bf16[8,2,64,768]{3,2,1,0:T(8,128)(2,1)} %all-to-all-done.1.parts, f32[1,768]{1,0:T(1,128)S(1)} %reshape.36.bias, bf16[64,768]{1,0:T(8,128)(2,1)S(1)} %get-tuple-element.66.refs_0_), custom_call_target="tpu_custom_call" | custom-call | flops 1966080 | bytes 2359296 | tf_op jit(solution)/shard_map/pallas_call | solution.py:57
  112.0 1.1 copy-done.1
  113.1 7.2 %all-to-all-done.2 = bf16[8,64,768]{2,1,0:T(8,128)(2,1)S(1)} async-done(((bf16[8,64,768]{2,1,0:T(8,128)(2,1)}), bf16[8,64,768]{2,1,0:T(8,128)(2,1)S(1)}, u32[]{:S(2)}, u32[]{:S(2)}) %all-to-all-start.2) | async-done | bytes 786464 | tf_op jit(solution)/shard_map/all_to_all | solution.py:146
  120.3 4.7 %all-to-all-start.3 = ((bf16[8,64,768]{2,1,0:T(8,128)(2,1)}), bf16[8,64,768]{2,1,0:T(8,128)(2,1)}, u32[]{:S(2)}, u32[]{:S(2)}) async-start(bf16[8,64,768]{2,1,0:T(8,128)(2,1)} %get-tuple-element.73), calls=%async_computation.3 | async-start | bytes 1572864 | tf_op jit(solution)/shard_map/all_to_all | solution.py:146
  125.1 0.8 convolution_convert_fusion.1
  126.0 0.8 fusion.53
  126.8 1.5 collective-permute-done.16
  128.3 1.0 add_convert_fusion.3
  129.5 2.2 %collective-permute-start.18 = (bf16[64,1536]{1,0:T(8,128)(2,1)}, bf16[64,1536]{1,0:T(8,128)(2,1)S(1)}, u32[]{:S(2)}, u32[]{:S(2)}) collective-permute-start(bf16[64,1536]{1,0:T(8,128)(2,1)} %get-tuple-element.70), channel_id=1, source_target_pairs={{0,4},{1,5},{2,6},{3,7},{4,0},{5,1},{6,2},{7,3},{8,12},{9,13},{10,... | collective-permute-start | bytes 589832 | tf_op jit(solution)/shard_map/ppermute | solution.py:124
  131.7 4.5 %all-to-all-done.3 = bf16[8,64,768]{2,1,0:T(8,128)(2,1)} async-done(((bf16[8,64,768]{2,1,0:T(8,128)(2,1)}), bf16[8,64,768]{2,1,0:T(8,128)(2,1)}, u32[]{:S(2)}, u32[]{:S(2)}) %all-to-all-start.3) | async-done | bytes 786464 | tf_op jit(solution)/shard_map/all_to_all | solution.py:146
  136.2 1.9 %fusion.51 = (bf16[4,64,768]{2,1,0:T(8,128)(2,1)}, bf16[4,64,768]{2,1,0:T(8,128)(2,1)S(1)}) fusion(bf16[8,64,768]{2,1,0:T(8,128)(2,1)} %all-to-all-done.3), kind=kLoop, calls=%fused_computation.78 | loop fusion | bytes 1572864 | tf_op jit(solution)/shard_map/slice | solution.py:175
  138.2 1.7 convolution_convert_fusion
  139.9 2.2 %collective-permute-done.19.refs_3_ = bf16[64,1536]{1,0:T(8,128)(2,1)S(1)} collective-permute-done((bf16[64,1536]{1,0:T(8,128)(2,1)S(1)}, bf16[64,1536]{1,0:T(8,128)(2,1)S(1)}, u32[]{:S(2)}, u32[]{:S(2)}) %collective-permute-start.19) | collective-permute-done | bytes 196640 | tf_op jit(solution)/shard_map/ppermute | solution.py:124
  142.1 5.7 %all-to-all-start.4 = ((bf16[8,2,64,768]{3,2,1,0:T(8,128)(2,1)}), bf16[8,2,64,768]{3,2,1,0:T(8,128)(2,1)}, u32[]{:S(2)}, u32[]{:S(2)}) async-start(bf16[8,2,64,768]{3,2,1,0:T(8,128)(2,1)} %copy-done.1), calls=%async_computation.4 | async-start | bytes 3145728 | tf_op jit(solution)/shard_map/all_to_all | solution.py:146
  147.8 1.9 %fusion.54 = f32[256,1536]{1,0:T(8,128)S(1)} fusion(bf16[256,768]{1,0:T(8,128)(2,1)} %bitcast.43, bf16[1536,768]{1,0:T(8,128)(2,1)S(1)} %copy-done), kind=kOutput, calls=%fused_computation.81 | convolution fusion | flops 603979776 | bytes 4325376 | tf_op jit(solution)/shard_map/dot_general | solution.py:27
  150.5 1.2 collective-permute-start.21
  151.7 1.7 collective-permute-start.22
  153.6 5.1 %multiply_convert_fusion.1 = bf16[1536,768]{1,0:T(8,128)(2,1)} fusion(bf16[256,1536]{1,0:T(8,128)(2,1)S(1)} %copy-done.20, bf16[256,1536]{1,0:T(8,128)(2,1)S(1)} %copy-done.9, bf16[256,1536]{1,0:T(8,128)(2,1)S(1)} %copy-done.16, bf16[256,1536]{1,0:T(8,128)(2,1)S(1)} %copy-done.6, bf16[512,768]{1,0:T(8,128)(2,1)} %bitcast.17, bf16[512,768]{1,0:T(8,128)(2,1)S(1)} %bitcast.41), kind=kOutput, calls=%fused_computation.1 | convolution fusion | flops 2434007040 | bytes 7077888 | tf_op jit(solution)/shard_map/dot_general | solution.py:31
  158.7 2.4 %collective-permute-done.22.refs_6_ = bf16[64,1536]{1,0:T(8,128)(2,1)S(1)} collective-permute-done((bf16[64,1536]{1,0:T(8,128)(2,1)S(1)}, bf16[64,1536]{1,0:T(8,128)(2,1)S(1)}, u32[]{:S(2)}, u32[]{:S(2)}) %collective-permute-start.22) | collective-permute-done | bytes 196640 | tf_op jit(solution)/shard_map/ppermute | solution.py:124
  161.1 3.0 %collective-permute-done.23.refs_7_ = bf16[64,1536]{1,0:T(8,128)(2,1)S(1)} collective-permute-done((bf16[64,1536]{1,0:T(8,128)(2,1)S(1)}, bf16[64,1536]{1,0:T(8,128)(2,1)S(1)}, u32[]{:S(2)}, u32[]{:S(2)}) %collective-permute-start.23) | collective-permute-done | bytes 196640 | tf_op jit(solution)/shard_map/ppermute | solution.py:124
  164.1 1.6 shard_map.78
  165.7 2.0 %collective-permute-start.24 = (bf16[32,1536]{1,0:T(8,128)(2,1)}, bf16[32,1536]{1,0:T(8,128)(2,1)S(1)}, u32[]{:S(2)}, u32[]{:S(2)}) collective-permute-start(bf16[32,1536]{1,0:T(8,128)(2,1)} %get-tuple-element.97), channel_id=1, source_target_pairs={{0,24},{8,0},{16,8},{24,16},{1,25},{9,1},{17,9},{25,17},{2,26},{10... | collective-permute-start | bytes 294920 | tf_op jit(solution)/shard_map/ppermute | solution.py:121
  168.0 2.6 %collective-permute-start.26 = (bf16[32,1536]{1,0:T(8,128)(2,1)}, bf16[32,1536]{1,0:T(8,128)(2,1)S(1)}, u32[]{:S(2)}, u32[]{:S(2)}) collective-permute-start(bf16[32,1536]{1,0:T(8,128)(2,1)} %get-tuple-element.99), channel_id=1, source_target_pairs={{0,8},{8,16},{16,24},{24,0},{1,9},{9,17},{17,25},{25,1},{2,10},{10... | collective-permute-start | bytes 294920 | tf_op jit(solution)/shard_map/ppermute | solution.py:121
  170.6 1.7 copy.8
  172.4 5.4 %multiply_convert_fusion = bf16[768,1536]{1,0:T(8,128)(2,1)} fusion(bf16[1024,768]{1,0:T(8,128)(2,1)S(1)} %bitcast.42, bf16[256,1536]{1,0:T(8,128)(2,1)S(1)} %copy-done.18, bf16[256,1536]{1,0:T(8,128)(2,1)} %copy-done.7, bf16[256,1536]{1,0:T(8,128)(2,1)S(1)} %copy-done.14, bf16[256,1536]{1,0:T(8,128)(2,1)} %copy-done.4), kind=kOutput, calls=%fused_computation | convolution fusion | flops 2430861312 | bytes 7077888 | tf_op jit(solution)/shard_map/dot_general | solution.py:31
  177.9 0.7 collective-permute-done.25
  178.5 2.2 %collective-permute-done.26 = bf16[32,1536]{1,0:T(8,128)(2,1)S(1)} collective-permute-done((bf16[32,1536]{1,0:T(8,128)(2,1)}, bf16[32,1536]{1,0:T(8,128)(2,1)S(1)}, u32[]{:S(2)}, u32[]{:S(2)}) %collective-permute-start.26) | collective-permute-done | bytes 98336 | tf_op jit(solution)/shard_map/ppermute | solution.py:121
  180.7 0.7 add_convert_fusion.6
  (79 shorter events, 3.9 us)
Async XLA Ops:
  0.6 51.1 %copy-start = (bf16[1536,768]{1,0:T(8,128)(2,1)S(1)}, bf16[1536,768]{1,0:T(8,128)(2,1)}, u32[]{:S(2)}) copy-start(bf16[1536,768]{1,0:T(8,128)(2,1)} %param.6) | copy-start | bytes 7077892
  1.7 9.3 %collective-permute-start.2 = (bf16[2,16,1536]{2,1,0:T(8,128)(2,1)S(1)}, bf16[2,16,1536]{2,1,0:T(8,128)(2,1)S(1)}, u32[]{:S(2)}, u32[]{:S(2)}) collective-permute-start(bf16[2,16,1536]{2,1,0:T(8,128)(2,1)S(1)} %pad_maximum_fusion.4), channel_id=1, source_target_pairs={{0,24},{8,0},{16,8},{24,16},{1,25},{9,1},{17,9},{25,17},{2,26},{10... | collective-permute-start | bytes 294920 | tf_op jit(solution)/shard_map/ppermute | solution.py:121
  7.2 10.9 %collective-permute-start.1 = (bf16[2,16,1536]{2,1,0:T(8,128)(2,1)S(1)}, bf16[2,16,1536]{2,1,0:T(8,128)(2,1)S(1)}, u32[]{:S(2)}, u32[]{:S(2)}) collective-permute-start(bf16[2,16,1536]{2,1,0:T(8,128)(2,1)S(1)} %pad_maximum_fusion.4), channel_id=1, source_target_pairs={{0,16},{8,24},{16,0},{24,8},{1,17},{9,25},{17,1},{25,9},{2,18},{10... | collective-permute-start | bytes 294920 | tf_op jit(solution)/shard_map/ppermute | solution.py:121
  8.6 10.0 %collective-permute-start = (bf16[2,16,1536]{2,1,0:T(8,128)(2,1)S(1)}, bf16[2,16,1536]{2,1,0:T(8,128)(2,1)S(1)}, u32[]{:S(2)}, u32[]{:S(2)}) collective-permute-start(bf16[2,16,1536]{2,1,0:T(8,128)(2,1)S(1)} %pad_maximum_fusion.4), channel_id=1, source_target_pairs={{0,8},{8,16},{16,24},{24,0},{1,9},{9,17},{17,25},{25,1},{2,10},{10... | collective-permute-start | bytes 294920 | tf_op jit(solution)/shard_map/ppermute | solution.py:121
  18.7 11.1 %collective-permute-start.8 = (bf16[2,16,1536]{2,1,0:T(8,128)(2,1)S(1)}, bf16[2,16,1536]{2,1,0:T(8,128)(2,1)S(1)}, u32[]{:S(2)}, u32[]{:S(2)}) collective-permute-start(bf16[2,16,1536]{2,1,0:T(8,128)(2,1)S(1)} %pad_maximum_fusion.5), channel_id=1, source_target_pairs={{0,24},{8,0},{16,8},{24,16},{1,25},{9,1},{17,9},{25,17},{2,26},{10... | collective-permute-start | bytes 294920 | tf_op jit(solution)/shard_map/ppermute | solution.py:121
  22.4 16.1 %collective-permute-start.3 = (bf16[2,64,1536]{2,1,0:T(8,128)(2,1)S(1)}, bf16[2,64,1536]{2,1,0:T(8,128)(2,1)S(1)}, u32[]{:S(2)}, u32[]{:S(2)}) collective-permute-start(bf16[2,64,1536]{2,1,0:T(8,128)(2,1)S(1)} %pad_maximum_fusion.2), channel_id=1, source_target_pairs={{0,2},{1,3},{2,4},{3,5},{4,6},{5,7},{6,0},{7,1},{8,10},{9,11},{10,... | collective-permute-start | bytes 1179656 | tf_op jit(solution)/shard_map/ppermute | solution.py:124
  23.9 19.4 %collective-permute-start.4 = (bf16[2,64,1536]{2,1,0:T(8,128)(2,1)S(1)}, bf16[2,64,1536]{2,1,0:T(8,128)(2,1)S(1)}, u32[]{:S(2)}, u32[]{:S(2)}) collective-permute-start(bf16[2,64,1536]{2,1,0:T(8,128)(2,1)S(1)} %pad_maximum_fusion.2), channel_id=1, source_target_pairs={{0,4},{1,5},{2,6},{3,7},{4,0},{5,1},{6,2},{7,3},{8,12},{9,13},{10,... | collective-permute-start | bytes 1179656 | tf_op jit(solution)/shard_map/ppermute | solution.py:124
  26.6 16.7 %collective-permute-start.5 = (bf16[2,64,1536]{2,1,0:T(8,128)(2,1)S(1)}, bf16[2,64,1536]{2,1,0:T(8,128)(2,1)S(1)}, u32[]{:S(2)}, u32[]{:S(2)}) collective-permute-start(bf16[2,64,1536]{2,1,0:T(8,128)(2,1)S(1)} %pad_maximum_fusion.2), channel_id=1, source_target_pairs={{0,6},{1,7},{2,0},{3,1},{4,2},{5,3},{6,4},{7,5},{8,14},{9,15},{10,... | collective-permute-start | bytes 1179656 | tf_op jit(solution)/shard_map/ppermute | solution.py:124
  28.0 9.4 %collective-permute-start.7 = (bf16[2,16,1536]{2,1,0:T(8,128)(2,1)S(1)}, bf16[2,16,1536]{2,1,0:T(8,128)(2,1)S(1)}, u32[]{:S(2)}, u32[]{:S(2)}) collective-permute-start(bf16[2,16,1536]{2,1,0:T(8,128)(2,1)S(1)} %pad_maximum_fusion.5), channel_id=1, source_target_pairs={{0,16},{8,24},{16,0},{24,8},{1,17},{9,25},{17,1},{25,9},{2,18},{10... | collective-permute-start | bytes 294920 | tf_op jit(solution)/shard_map/ppermute | solution.py:121
  29.8 8.7 %collective-permute-start.6 = (bf16[2,16,1536]{2,1,0:T(8,128)(2,1)S(1)}, bf16[2,16,1536]{2,1,0:T(8,128)(2,1)S(1)}, u32[]{:S(2)}, u32[]{:S(2)}) collective-permute-start(bf16[2,16,1536]{2,1,0:T(8,128)(2,1)S(1)} %pad_maximum_fusion.5), channel_id=1, source_target_pairs={{0,8},{8,16},{16,24},{24,0},{1,9},{9,17},{17,25},{25,1},{2,10},{10... | collective-permute-start | bytes 294920 | tf_op jit(solution)/shard_map/ppermute | solution.py:121
  43.4 6.8 %copy-start.11 = (bf16[768,1536]{1,0:T(8,128)(2,1)S(1)}, bf16[768,1536]{1,0:T(8,128)(2,1)}, u32[]{:S(2)}) copy-start(bf16[768,1536]{1,0:T(8,128)(2,1)} %param.8) | copy-start | bytes 7077892
  43.5 8.1 %copy-start.4 = (bf16[256,1536]{1,0:T(8,128)(2,1)}, bf16[256,1536]{1,0:T(8,128)(2,1)S(1)}, u32[]{:S(2)}) copy-start(bf16[256,1536]{1,0:T(8,128)(2,1)S(1)} %get-tuple-element.118) | copy-start | bytes 2359300
  43.5 8.1 %copy-start.5 = (bf16[256,1536]{1,0:T(8,128)(2,1)}, bf16[256,1536]{1,0:T(8,128)(2,1)S(1)}, u32[]{:S(2)}) copy-start(bf16[256,1536]{1,0:T(8,128)(2,1)S(1)} %get-tuple-element.117) | copy-start | bytes 2359300
  43.5 6.7 %collective-permute-start.10 = (bf16[256,1536]{1,0:T(8,128)(2,1)S(1)}, bf16[256,1536]{1,0:T(8,128)(2,1)S(1)}, u32[]{:S(2)}, u32[]{:S(2)}) collective-permute-start(bf16[256,1536]{1,0:T(8,128)(2,1)S(1)} %get-tuple-element.118), channel_id=1, source_target_pairs={{0,1},{1,0},{2,3},{3,2},{4,5},{5,4},{6,7},{7,6},{8,9},{9,8},{10,11... | collective-permute-start | bytes 2359304 | tf_op jit(solution)/shard_map/ppermute | solution.py:127
  43.6 8.0 %collective-permute-start.9 = (bf16[256,1536]{1,0:T(8,128)(2,1)S(1)}, bf16[256,1536]{1,0:T(8,128)(2,1)S(1)}, u32[]{:S(2)}, u32[]{:S(2)}) collective-permute-start(bf16[256,1536]{1,0:T(8,128)(2,1)S(1)} %get-tuple-element.117), channel_id=1, source_target_pairs={{0,1},{1,0},{2,3},{3,2},{4,5},{5,4},{6,7},{7,6},{8,9},{9,8},{10,11... | collective-permute-start | bytes 2359304 | tf_op jit(solution)/shard_map/ppermute | solution.py:127
  44.1 16.2 %collective-permute-start.11 = (bf16[2,64,1536]{2,1,0:T(8,128)(2,1)S(1)}, bf16[2,64,1536]{2,1,0:T(8,128)(2,1)}, u32[]{:S(2)}, u32[]{:S(2)}) collective-permute-start(bf16[2,64,1536]{2,1,0:T(8,128)(2,1)S(1)} %pad_maximum_fusion.3), channel_id=1, source_target_pairs={{0,2},{1,3},{2,4},{3,5},{4,6},{5,7},{6,0},{7,1},{8,10},{9,11},{10,... | collective-permute-start | bytes 1179656 | tf_op jit(solution)/shard_map/ppermute | solution.py:124
  45.5 19.9 %collective-permute-start.12 = (bf16[2,64,1536]{2,1,0:T(8,128)(2,1)S(1)}, bf16[2,64,1536]{2,1,0:T(8,128)(2,1)S(1)}, u32[]{:S(2)}, u32[]{:S(2)}) collective-permute-start(bf16[2,64,1536]{2,1,0:T(8,128)(2,1)S(1)} %pad_maximum_fusion.3), channel_id=1, source_target_pairs={{0,4},{1,5},{2,6},{3,7},{4,0},{5,1},{6,2},{7,3},{8,12},{9,13},{10,... | collective-permute-start | bytes 1179656 | tf_op jit(solution)/shard_map/ppermute | solution.py:124
  47.9 18.3 %collective-permute-start.13 = (bf16[2,64,1536]{2,1,0:T(8,128)(2,1)S(1)}, bf16[2,64,1536]{2,1,0:T(8,128)(2,1)S(1)}, u32[]{:S(2)}, u32[]{:S(2)}) collective-permute-start(bf16[2,64,1536]{2,1,0:T(8,128)(2,1)S(1)} %pad_maximum_fusion.3), channel_id=1, source_target_pairs={{0,6},{1,7},{2,0},{3,1},{4,2},{5,3},{6,4},{7,5},{8,14},{9,15},{10,... | collective-permute-start | bytes 1179656 | tf_op jit(solution)/shard_map/ppermute | solution.py:124
  50.2 1.4 copy-start.13
  51.7 1.4 copy-start.15
  54.4 25.3 %all-to-all-start = ((bf16[8,2,64,768]{3,2,1,0:T(8,128)(2,1)}), bf16[8,2,64,768]{3,2,1,0:T(8,128)(2,1)}, u32[]{:S(2)}, u32[]{:S(2)}) async-start(bf16[8,2,64,768]{3,2,1,0:T(8,128)(2,1)} %pad_maximum_fusion), calls=%async_computation | async-start | bytes 3145728 | tf_op jit(solution)/shard_map/all_to_all | solution.py:146
  62.1 8.7 %copy-start.12 = (bf16[768,1536]{1,0:T(8,128)(2,1)S(1)}, bf16[768,1536]{1,0:T(8,128)(2,1)}, u32[]{:S(2)}) copy-start(bf16[768,1536]{1,0:T(8,128)(2,1)} %param.8) | copy-start | bytes 7077892
  68.4 3.8 %copy-start.7 = (bf16[256,1536]{1,0:T(8,128)(2,1)}, bf16[256,1536]{1,0:T(8,128)(2,1)S(1)}, u32[]{:S(2)}) copy-start(bf16[256,1536]{1,0:T(8,128)(2,1)S(1)} %get-tuple-element.116) | copy-start | bytes 2359300
  68.4 3.8 %copy-start.8 = (bf16[256,1536]{1,0:T(8,128)(2,1)}, bf16[256,1536]{1,0:T(8,128)(2,1)S(1)}, u32[]{:S(2)}) copy-start(bf16[256,1536]{1,0:T(8,128)(2,1)S(1)} %get-tuple-element.115) | copy-start | bytes 2359300
  68.4 2.4 %collective-permute-start.15 = (bf16[256,1536]{1,0:T(8,128)(2,1)S(1)}, bf16[256,1536]{1,0:T(8,128)(2,1)S(1)}, u32[]{:S(2)}, u32[]{:S(2)}) collective-permute-start(bf16[256,1536]{1,0:T(8,128)(2,1)S(1)} %get-tuple-element.116), channel_id=1, source_target_pairs={{0,1},{1,0},{2,3},{3,2},{4,5},{5,4},{6,7},{7,6},{8,9},{9,8},{10,11... | collective-permute-start | bytes 2359304 | tf_op jit(solution)/shard_map/ppermute | solution.py:127
  68.5 3.7 %collective-permute-start.14 = (bf16[256,1536]{1,0:T(8,128)(2,1)S(1)}, bf16[256,1536]{1,0:T(8,128)(2,1)S(1)}, u32[]{:S(2)}, u32[]{:S(2)}) collective-permute-start(bf16[256,1536]{1,0:T(8,128)(2,1)S(1)} %get-tuple-element.115), channel_id=1, source_target_pairs={{0,1},{1,0},{2,3},{3,2},{4,5},{5,4},{6,7},{7,6},{8,9},{9,8},{10,11... | collective-permute-start | bytes 2359304 | tf_op jit(solution)/shard_map/ppermute | solution.py:127
  70.8 1.4 copy-start.17
  72.3 1.4 copy-start.19
  75.0 9.5 %copy-start.10 = (f32[768]{0:T(1024)S(1)}, f32[768]{0:T(1024)}, u32[]{:S(2)}) copy-start(f32[768]{0:T(1024)} %param.7) | copy-start | bytes 9220
  79.7 24.8 %all-to-all-start.1 = ((bf16[8,2,64,768]{3,2,1,0:T(8,128)(2,1)}), bf16[8,2,64,768]{3,2,1,0:T(8,128)(2,1)}, u32[]{:S(2)}, u32[]{:S(2)}) async-start(bf16[8,2,64,768]{3,2,1,0:T(8,128)(2,1)} %pad_maximum_fusion.1), calls=%async_computation.1 | async-start | bytes 3145728 | tf_op jit(solution)/shard_map/all_to_all | solution.py:146
  104.6 15.8 %all-to-all-start.2 = ((bf16[8,64,768]{2,1,0:T(8,128)(2,1)}), bf16[8,64,768]{2,1,0:T(8,128)(2,1)S(1)}, u32[]{:S(2)}, u32[]{:S(2)}) async-start(bf16[8,64,768]{2,1,0:T(8,128)(2,1)} %get-tuple-element.62), calls=%async_computation.2 | async-start | bytes 1572864 | tf_op jit(solution)/shard_map/all_to_all | solution.py:146
  112.0 1.1 copy-start.1
  120.3 5.5 %copy-start.2 = (bf16[8,64,768]{2,1,0:T(8,128)(2,1)}, bf16[8,64,768]{2,1,0:T(8,128)(2,1)S(1)}, u32[]{:S(2)}) copy-start(bf16[8,64,768]{2,1,0:T(8,128)(2,1)S(1)} %all-to-all-done.2) | copy-start | bytes 2359300
  120.3 15.9 %all-to-all-start.3 = ((bf16[8,64,768]{2,1,0:T(8,128)(2,1)}), bf16[8,64,768]{2,1,0:T(8,128)(2,1)}, u32[]{:S(2)}, u32[]{:S(2)}) async-start(bf16[8,64,768]{2,1,0:T(8,128)(2,1)} %get-tuple-element.73), calls=%async_computation.3 | async-start | bytes 1572864 | tf_op jit(solution)/shard_map/all_to_all | solution.py:146
  125.9 2.4 %collective-permute-start.16 = (bf16[256,1536]{1,0:T(8,128)(2,1)S(1)}, bf16[256,1536]{1,0:T(8,128)(2,1)S(1)}, u32[]{:S(2)}, u32[]{:S(2)}) collective-permute-start(bf16[256,1536]{1,0:T(8,128)(2,1)S(1)} %convolution_convert_fusion.1), channel_id=1, source_target_pairs={{0,1},{1,0},{2,3},{3,2},{4,5},{5,4},{6,7},{7,6},{8,9},{9,8},{10,11... | collective-permute-start | bytes 2359304 | tf_op jit(solution)/shard_map/ppermute | solution.py:127
  129.2 10.6 %collective-permute-start.17 = (bf16[64,1536]{1,0:T(8,128)(2,1)}, bf16[64,1536]{1,0:T(8,128)(2,1)S(1)}, u32[]{:S(2)}, u32[]{:S(2)}) collective-permute-start(bf16[64,1536]{1,0:T(8,128)(2,1)} %get-tuple-element.69), channel_id=1, source_target_pairs={{0,6},{1,7},{2,0},{3,1},{4,2},{5,3},{6,4},{7,5},{8,14},{9,15},{10,... | collective-permute-start | bytes 589832 | tf_op jit(solution)/shard_map/ppermute | solution.py:124
  129.5 10.4 %collective-permute-start.18 = (bf16[64,1536]{1,0:T(8,128)(2,1)}, bf16[64,1536]{1,0:T(8,128)(2,1)S(1)}, u32[]{:S(2)}, u32[]{:S(2)}) collective-permute-start(bf16[64,1536]{1,0:T(8,128)(2,1)} %get-tuple-element.70), channel_id=1, source_target_pairs={{0,4},{1,5},{2,6},{3,7},{4,0},{5,1},{6,2},{7,3},{8,12},{9,13},{10,... | collective-permute-start | bytes 589832 | tf_op jit(solution)/shard_map/ppermute | solution.py:124
  131.7 10.3 %collective-permute-start.19 = (bf16[64,1536]{1,0:T(8,128)(2,1)S(1)}, bf16[64,1536]{1,0:T(8,128)(2,1)S(1)}, u32[]{:S(2)}, u32[]{:S(2)}) collective-permute-start(bf16[64,1536]{1,0:T(8,128)(2,1)S(1)} %get-tuple-element.71), channel_id=1, source_target_pairs={{0,2},{1,3},{2,4},{3,5},{4,6},{5,7},{6,0},{7,1},{8,10},{9,11},{10,... | collective-permute-start | bytes 589832 | tf_op jit(solution)/shard_map/ppermute | solution.py:124
  142.1 28.5 %all-to-all-start.4 = ((bf16[8,2,64,768]{3,2,1,0:T(8,128)(2,1)}), bf16[8,2,64,768]{3,2,1,0:T(8,128)(2,1)}, u32[]{:S(2)}, u32[]{:S(2)}) async-start(bf16[8,2,64,768]{3,2,1,0:T(8,128)(2,1)} %copy-done.1), calls=%async_computation.4 | async-start | bytes 3145728 | tf_op jit(solution)/shard_map/all_to_all | solution.py:146
  147.8 2.5 %collective-permute-start.20 = (bf16[256,1536]{1,0:T(8,128)(2,1)}, bf16[256,1536]{1,0:T(8,128)(2,1)S(1)}, u32[]{:S(2)}, u32[]{:S(2)}) collective-permute-start(bf16[256,1536]{1,0:T(8,128)(2,1)} %convolution_convert_fusion), channel_id=1, source_target_pairs={{0,1},{1,0},{2,3},{3,2},{4,5},{5,4},{6,7},{7,6},{8,9},{9,8},{10,11... | collective-permute-start | bytes 2359304 | tf_op jit(solution)/shard_map/ppermute | solution.py:127
  147.8 5.7 %copy-start.20 = (bf16[256,1536]{1,0:T(8,128)(2,1)S(1)}, bf16[256,1536]{1,0:T(8,128)(2,1)}, u32[]{:S(2)}) copy-start(bf16[256,1536]{1,0:T(8,128)(2,1)} %copy-done.19) | copy-start | bytes 2359300
  149.7 3.8 %copy-start.3 = (bf16[8,64,768]{2,1,0:T(8,128)(2,1)S(1)}, bf16[8,64,768]{2,1,0:T(8,128)(2,1)}, u32[]{:S(2)}) copy-start(bf16[8,64,768]{2,1,0:T(8,128)(2,1)} %copy-done.2) | copy-start | bytes 2359300
  149.7 3.8 %copy-start.6 = (bf16[256,1536]{1,0:T(8,128)(2,1)S(1)}, bf16[256,1536]{1,0:T(8,128)(2,1)}, u32[]{:S(2)}) copy-start(bf16[256,1536]{1,0:T(8,128)(2,1)} %copy-done.5) | copy-start | bytes 2359300
  149.7 3.8 %copy-start.9 = (bf16[256,1536]{1,0:T(8,128)(2,1)S(1)}, bf16[256,1536]{1,0:T(8,128)(2,1)}, u32[]{:S(2)}) copy-start(bf16[256,1536]{1,0:T(8,128)(2,1)} %copy-done.8) | copy-start | bytes 2359300
  149.7 3.8 %copy-start.16 = (bf16[256,1536]{1,0:T(8,128)(2,1)S(1)}, bf16[256,1536]{1,0:T(8,128)(2,1)}, u32[]{:S(2)}) copy-start(bf16[256,1536]{1,0:T(8,128)(2,1)} %copy-done.15) | copy-start | bytes 2359300
  150.5 8.2 %collective-permute-start.21 = (bf16[64,1536]{1,0:T(8,128)(2,1)S(1)}, bf16[64,1536]{1,0:T(8,128)(2,1)S(1)}, u32[]{:S(2)}, u32[]{:S(2)}) collective-permute-start(bf16[64,1536]{1,0:T(8,128)(2,1)S(1)} %get-tuple-element.83), channel_id=1, source_target_pairs={{0,6},{1,7},{2,0},{3,1},{4,2},{5,3},{6,4},{7,5},{8,14},{9,15},{10,... | collective-permute-start | bytes 589832 | tf_op jit(solution)/shard_map/ppermute | solution.py:124
  151.7 9.3 %collective-permute-start.22 = (bf16[64,1536]{1,0:T(8,128)(2,1)S(1)}, bf16[64,1536]{1,0:T(8,128)(2,1)S(1)}, u32[]{:S(2)}, u32[]{:S(2)}) collective-permute-start(bf16[64,1536]{1,0:T(8,128)(2,1)S(1)} %get-tuple-element.84), channel_id=1, source_target_pairs={{0,4},{1,5},{2,6},{3,7},{4,0},{5,1},{6,2},{7,3},{8,12},{9,13},{10,... | collective-permute-start | bytes 589832 | tf_op jit(solution)/shard_map/ppermute | solution.py:124
  153.4 10.7 %collective-permute-start.23 = (bf16[64,1536]{1,0:T(8,128)(2,1)S(1)}, bf16[64,1536]{1,0:T(8,128)(2,1)S(1)}, u32[]{:S(2)}, u32[]{:S(2)}) collective-permute-start(bf16[64,1536]{1,0:T(8,128)(2,1)S(1)} %get-tuple-element.85), channel_id=1, source_target_pairs={{0,2},{1,3},{2,4},{3,5},{4,6},{5,7},{6,0},{7,1},{8,10},{9,11},{10,... | collective-permute-start | bytes 589832 | tf_op jit(solution)/shard_map/ppermute | solution.py:124
  165.7 12.1 %collective-permute-start.24 = (bf16[32,1536]{1,0:T(8,128)(2,1)}, bf16[32,1536]{1,0:T(8,128)(2,1)S(1)}, u32[]{:S(2)}, u32[]{:S(2)}) collective-permute-start(bf16[32,1536]{1,0:T(8,128)(2,1)} %get-tuple-element.97), channel_id=1, source_target_pairs={{0,24},{8,0},{16,8},{24,16},{1,25},{9,1},{17,9},{25,17},{2,26},{10... | collective-permute-start | bytes 294920 | tf_op jit(solution)/shard_map/ppermute | solution.py:121
  167.8 10.8 %collective-permute-start.25 = (bf16[32,1536]{1,0:T(8,128)(2,1)}, bf16[32,1536]{1,0:T(8,128)(2,1)S(1)}, u32[]{:S(2)}, u32[]{:S(2)}) collective-permute-start(bf16[32,1536]{1,0:T(8,128)(2,1)} %get-tuple-element.98), channel_id=1, source_target_pairs={{0,16},{8,24},{16,0},{24,8},{1,17},{9,25},{17,1},{25,9},{2,18},{10... | collective-permute-start | bytes 294920 | tf_op jit(solution)/shard_map/ppermute | solution.py:121
  168.0 12.7 %collective-permute-start.26 = (bf16[32,1536]{1,0:T(8,128)(2,1)}, bf16[32,1536]{1,0:T(8,128)(2,1)S(1)}, u32[]{:S(2)}, u32[]{:S(2)}) collective-permute-start(bf16[32,1536]{1,0:T(8,128)(2,1)} %get-tuple-element.99), channel_id=1, source_target_pairs={{0,8},{8,16},{16,24},{24,0},{1,9},{9,17},{17,25},{25,1},{2,10},{10... | collective-permute-start | bytes 294920 | tf_op jit(solution)/shard_map/ppermute | solution.py:121
  170.6 1.7 copy-start.14
  170.6 1.8 %copy-start.18 = (bf16[256,1536]{1,0:T(8,128)(2,1)S(1)}, bf16[256,1536]{1,0:T(8,128)(2,1)}, u32[]{:S(2)}) copy-start(bf16[256,1536]{1,0:T(8,128)(2,1)} %copy-done.17) | copy-start | bytes 2359300

commit v10 on v9

--- a/solution.py
+++ b/solution.py
@@ -186,6 +186,9 @@
         grad_copies0, sums1 = barrier(grad_copies0, sums1)
         hidden0 = trade_width(grad_copies0)
         grad_copies1, act_copies = hidden(sums1, bias, act0)
+        blocks = [a.reshape(n_x, -1, a.shape[1]) for a in (both0[1], both1[1])]
+        grad_all = jnp.stack(blocks, axis=1).reshape(-1, grad_output.shape[1])
+        grad_copies1, act_copies, grad_all = barrier(grad_copies1, act_copies, grad_all)
         hidden1 = trade_width(after(grad_copies1, hidden0)).reshape(-1, columns)
         hidden0 = hidden0.reshape(-1, columns)
         other0, own0 = two_halves(hidden0)
@@ -204,8 +207,7 @@
         parts0, parts1, grad_weight_in = barrier(parts0, parts1, grad_weight_in)
         parts = join_sums([parts0, parts1], n_y)
         parts = exchange(parts, shift_y)
-        activation = activation.transpose(1, 0, 2, 3).reshape(-1, columns)
-        grad_all = jnp.concatenate([both0[1], both1[1]], axis=0)
+        activation = activation.reshape(-1, columns)
         grad_weight_out = (contract_first(activation, grad_all) * norm_scale).astype(bf16)
         parts, grad_weight_out = barrier(parts, grad_weight_out)
         (grad_tokens,) = sum_blocks(parts, 1)

time: 183 us -> 183 us (level)
  other arithmetic: 4.49 us -> 8.08 us
  waiting for transfers between devices: 69.6 us -> 66.4 us
    all_to_all x5, waiting for transfers between devices: 33.2 us -> 29.2 us  [trade_width(): return lax.all_to_all(parts, 'gx', 0, 0, tiled=True)]
    another operation x0 -> x1, other arithmetic: none -> 1.92 us  [shards(): grad_all = jnp.stack(blocks, axis=1).reshape(-1, grad_output.shape[1])]
  transfers between devices with their start and end apart: 32 -> 32, of which waited for: 18 -> 18; matrix products, arithmetic and copies ran while one was open for 19% -> 21% of each run, Pallas kernels for 4% -> 4%
where the time goes in v10:
time: 183 us; the launch traced here: 181 us
  waiting for transfers between devices  66.4 us (36%)
  starting transfers between devices  64.9 us (35%)
  matrix products  22.3 us (12%)
  local copies, waits for them, and re-layouts  10.4 us (6%)
  Pallas kernels  8.15 us (4%)
  other arithmetic  8.08 us (4%)
    all_to_all x5, waiting for transfers between devices, trade_width(): return lax.all_to_all(parts, 'gx', 0, 0, tiled=True)  29.2 us
    all_to_all x5, starting transfers between devices, trade_width(): return lax.all_to_all(parts, 'gx', 0, 0, tiled=True)  25.2 us
    ppermute x9, starting transfers between devices, shift_y(): return lax.ppermute(a, 'gy', [(i, (i + k) % n_y) for i in range(n_y)])  22 us
    ppermute x9, waiting for transfers between devices, shift_y(): return lax.ppermute(a, 'gy', [(i, (i + k) % n_y) for i in range(n_y)])  17.6 us
    ppermute x12, starting transfers between devices, shift_chip(): return lax.ppermute(a, 'gz', [(i, (i + 2 * k) % n_z) for i in range(n_z)])  16.5 us
    ppermute x12, waiting for transfers between devices, shift_chip(): return lax.ppermute(a, 'gz', [(i, (i + 2 * k) % n_z) for i in range(n_z)])  15.8 us
    dot_general x2, matrix products, contract_first(): lax.dot_general(left, right, (((0,), (0,)), ((), ())), preferred_element_...  11.5 us
    dot_general x6, matrix products, contract_last(): lax.dot_general(left, right, (((1,), (1,)), ((), ())), preferred_element_...  8.01 us
  transfers between devices with their start and end apart: 32, of which 18 were waited for; matrix products, arithmetic and copies ran while one was open for 21% of the time, Pallas kernels for 4%

profile of v10, /device:TPU:32, one launch (start us, length us, event | category | flops | bytes accessed | tf_op | source)
XLA Modules:
  0.0 181.4 jit_solution(5157561983859743601)
XLA Ops:
  0.6 1.0 slice_bitcast_fusion.4
  1.7 5.5 %collective-permute-start.2 = (bf16[2,16,1536]{2,1,0:T(8,128)(2,1)S(1)}, bf16[2,16,1536]{2,1,0:T(8,128)(2,1)S(1)}, u32[]{:S(2)}, u32[]{:S(2)}) collective-permute-start(bf16[2,16,1536]{2,1,0:T(8,128)(2,1)S(1)} %pad_maximum_fusion.7), channel_id=1, source_target_pairs={{0,24},{8,0},{16,8},{24,16},{1,25},{9,1},{17,9},{25,17},{2,26},{10... | collective-permute-start | bytes 294920 | tf_op jit(solution)/shard_map/ppermute | solution.py:121
  7.2 1.4 collective-permute-start.1
  8.6 2.4 %collective-permute-start = (bf16[2,16,1536]{2,1,0:T(8,128)(2,1)S(1)}, bf16[2,16,1536]{2,1,0:T(8,128)(2,1)S(1)}, u32[]{:S(2)}, u32[]{:S(2)}) collective-permute-start(bf16[2,16,1536]{2,1,0:T(8,128)(2,1)S(1)} %pad_maximum_fusion.7), channel_id=1, source_target_pairs={{0,8},{8,16},{16,24},{24,0},{1,9},{9,17},{17,25},{25,1},{2,10},{10... | collective-permute-start | bytes 294920 | tf_op jit(solution)/shard_map/ppermute | solution.py:121
  11.0 7.0 %collective-permute-done.1 = bf16[2,16,1536]{2,1,0:T(8,128)(2,1)S(1)} collective-permute-done((bf16[2,16,1536]{2,1,0:T(8,128)(2,1)S(1)}, bf16[2,16,1536]{2,1,0:T(8,128)(2,1)S(1)}, u32[]{:S(2)}, u32[]{:S(2)}) %collective-permute-start.1) | collective-permute-done | bytes 98336 | tf_op jit(solution)/shard_map/ppermute | solution.py:121
  18.7 3.7 %collective-permute-start.8 = (bf16[2,16,1536]{2,1,0:T(8,128)(2,1)S(1)}, bf16[2,16,1536]{2,1,0:T(8,128)(2,1)S(1)}, u32[]{:S(2)}, u32[]{:S(2)}) collective-permute-start(bf16[2,16,1536]{2,1,0:T(8,128)(2,1)S(1)} %pad_maximum_fusion.8), channel_id=1, source_target_pairs={{0,24},{8,0},{16,8},{24,16},{1,25},{9,1},{17,9},{25,17},{2,26},{10... | collective-permute-start | bytes 294920 | tf_op jit(solution)/shard_map/ppermute | solution.py:121
  22.4 1.5 collective-permute-start.3
  23.9 2.7 %collective-permute-start.4 = (bf16[2,64,1536]{2,1,0:T(8,128)(2,1)S(1)}, bf16[2,64,1536]{2,1,0:T(8,128)(2,1)S(1)}, u32[]{:S(2)}, u32[]{:S(2)}) collective-permute-start(bf16[2,64,1536]{2,1,0:T(8,128)(2,1)S(1)} %pad_maximum_fusion.5), channel_id=1, source_target_pairs={{0,4},{1,5},{2,6},{3,7},{4,0},{5,1},{6,2},{7,3},{8,12},{9,13},{10,... | collective-permute-start | bytes 1179656 | tf_op jit(solution)/shard_map/ppermute | solution.py:124
  26.6 1.4 collective-permute-start.5
  28.0 1.7 collective-permute-start.7
  29.8 2.4 %collective-permute-start.6 = (bf16[2,16,1536]{2,1,0:T(8,128)(2,1)S(1)}, bf16[2,16,1536]{2,1,0:T(8,128)(2,1)S(1)}, u32[]{:S(2)}, u32[]{:S(2)}) collective-permute-start(bf16[2,16,1536]{2,1,0:T(8,128)(2,1)S(1)} %pad_maximum_fusion.8), channel_id=1, source_target_pairs={{0,8},{8,16},{16,24},{24,0},{1,9},{9,17},{17,25},{25,1},{2,10},{10... | collective-permute-start | bytes 294920 | tf_op jit(solution)/shard_map/ppermute | solution.py:121
  32.2 5.3 %collective-permute-done.7 = bf16[2,16,1536]{2,1,0:T(8,128)(2,1)S(1)} collective-permute-done((bf16[2,16,1536]{2,1,0:T(8,128)(2,1)S(1)}, bf16[2,16,1536]{2,1,0:T(8,128)(2,1)S(1)}, u32[]{:S(2)}, u32[]{:S(2)}) %collective-permute-start.7) | collective-permute-done | bytes 98336 | tf_op jit(solution)/shard_map/ppermute | solution.py:121
  37.4 1.0 collective-permute-done.6
  38.5 4.8 %collective-permute-done.4 = bf16[2,64,1536]{2,1,0:T(8,128)(2,1)S(1)} collective-permute-done((bf16[2,64,1536]{2,1,0:T(8,128)(2,1)S(1)}, bf16[2,64,1536]{2,1,0:T(8,128)(2,1)S(1)}, u32[]{:S(2)}, u32[]{:S(2)}) %collective-permute-start.4) | collective-permute-done | bytes 393248 | tf_op jit(solution)/shard_map/ppermute | solution.py:124
  44.1 1.3 collective-permute-start.11
  45.5 2.4 %collective-permute-start.12 = (bf16[2,64,1536]{2,1,0:T(8,128)(2,1)S(1)}, bf16[2,64,1536]{2,1,0:T(8,128)(2,1)S(1)}, u32[]{:S(2)}, u32[]{:S(2)}) collective-permute-start(bf16[2,64,1536]{2,1,0:T(8,128)(2,1)S(1)} %pad_maximum_fusion.6), channel_id=1, source_target_pairs={{0,4},{1,5},{2,6},{3,7},{4,0},{5,1},{6,2},{7,3},{8,12},{9,13},{10,... | collective-permute-start | bytes 1179656 | tf_op jit(solution)/shard_map/ppermute | solution.py:124
  47.9 1.6 collective-permute-start.13
  49.4 0.8 constant_dynamic-update-slice_fusion.7
  50.2 1.4 convolution_convert_fusion.3
  51.7 1.4 fusion.21
  53.1 1.3 pad_maximum_fusion.2
  54.4 5.9 %all-to-all-start = ((bf16[8,2,64,768]{3,2,1,0:T(8,128)(2,1)}), bf16[8,2,64,768]{3,2,1,0:T(8,128)(2,1)}, u32[]{:S(2)}, u32[]{:S(2)}) async-start(bf16[8,2,64,768]{3,2,1,0:T(8,128)(2,1)} %pad_maximum_fusion.2), calls=%async_computation | async-start | bytes 3145728 | tf_op jit(solution)/shard_map/all_to_all | solution.py:146
  60.3 1.8 constant_dynamic-update-slice_fusion.6
  62.1 3.3 %collective-permute-done.12 = bf16[2,64,1536]{2,1,0:T(8,128)(2,1)S(1)} collective-permute-done((bf16[2,64,1536]{2,1,0:T(8,128)(2,1)S(1)}, bf16[2,64,1536]{2,1,0:T(8,128)(2,1)S(1)}, u32[]{:S(2)}, u32[]{:S(2)}) %collective-permute-start.12) | collective-permute-done | bytes 393248 | tf_op jit(solution)/shard_map/ppermute | solution.py:124
  65.4 0.8 constant_dynamic-update-slice_fusion.5
  66.2 0.8 constant_dynamic-update-slice_fusion.4
  66.9 1.6 slice_bitcast_fusion.1
  69.2 1.8 collective-permute-done.15
  71.0 1.4 convolution_convert_fusion.2
  72.4 1.4 fusion.18
  73.8 1.3 pad_maximum_fusion.4
  75.1 4.6 %all-to-all-done.parts = bf16[8,2,64,768]{3,2,1,0:T(8,128)(2,1)} async-done(((bf16[8,2,64,768]{3,2,1,0:T(8,128)(2,1)}), bf16[8,2,64,768]{3,2,1,0:T(8,128)(2,1)}, u32[]{:S(2)}, u32[]{:S(2)}) %all-to-all-start) | async-done | bytes 1572896 | tf_op jit(solution)/shard_map/all_to_all | solution.py:146
  79.7 4.7 %all-to-all-start.1 = ((bf16[8,2,64,768]{3,2,1,0:T(8,128)(2,1)}), bf16[8,2,64,768]{3,2,1,0:T(8,128)(2,1)}, u32[]{:S(2)}, u32[]{:S(2)}) async-start(bf16[8,2,64,768]{3,2,1,0:T(8,128)(2,1)} %pad_maximum_fusion.4), calls=%async_computation.1 | async-start | bytes 3145728 | tf_op jit(solution)/shard_map/all_to_all | solution.py:146
  84.5 3.3 %shard_map.76 = (bf16[8,64,768]{2,1,0:T(8,128)(2,1)}, bf16[64,768]{1,0:T(8,128)(2,1)S(1)}) custom-call(bf16[8,2,64,768]{3,2,1,0:T(8,128)(2,1)} %all-to-all-done.parts, f32[1,768]{1,0:T(1,128)S(1)} %reshape.39.bias), custom_call_target="tpu_custom_call" | custom-call | flops 1966080 | bytes 2359296 | tf_op jit(solution)/shard_map/pallas_call | solution.py:57
  87.8 16.8 %all-to-all-done.1.parts = bf16[8,2,64,768]{3,2,1,0:T(8,128)(2,1)} async-done(((bf16[8,2,64,768]{3,2,1,0:T(8,128)(2,1)}), bf16[8,2,64,768]{3,2,1,0:T(8,128)(2,1)}, u32[]{:S(2)}, u32[]{:S(2)}) %all-to-all-start.1) | async-done | bytes 1572896 | tf_op jit(solution)/shard_map/all_to_all | solution.py:146
  104.5 4.2 %all-to-all-start.2 = ((bf16[8,64,768]{2,1,0:T(8,128)(2,1)}), bf16[8,64,768]{2,1,0:T(8,128)(2,1)S(1)}, u32[]{:S(2)}, u32[]{:S(2)}) async-start(bf16[8,64,768]{2,1,0:T(8,128)(2,1)} %get-tuple-element.65), calls=%async_computation.2 | async-start | bytes 1572864 | tf_op jit(solution)/shard_map/all_to_all | solution.py:146
  108.7 1.6 pad_maximum_fusion.1
  110.6 1.9 %pad_maximum_fusion = bf16[8,2,64,1536]{3,2,1,0:T(8,128)(2,1)} fusion(bf16[8,1,64,1536]{3,2,1,0:T(8,128)(2,1)S(1)} %bitcast.45, bf16[8,1,64,1536]{3,2,1,0:T(8,128)(2,1)S(1)} %bitcast.44), kind=kLoop, calls=%fused_computation.2 | loop fusion | flops 1572864 | bytes 6291456 | tf_op jit(solution)/shard_map/stack | solution.py:190
  112.6 3.3 %shard_map.77 = (bf16[8,64,768]{2,1,0:T(8,128)(2,1)}, bf16[8,2,64,768]{3,2,1,0:T(8,128)(2,1)S(1)}) custom-call(bf16[8,2,64,768]{3,2,1,0:T(8,128)(2,1)} %all-to-all-done.1.parts, f32[1,768]{1,0:T(1,128)S(1)} %reshape.39.bias, bf16[64,768]{1,0:T(8,128)(2,1)S(1)} %get-tuple-element.69.refs_0_), custom_call_target="tpu_custom_call" | custom-call | flops 1966080 | bytes 2359296 | tf_op jit(solution)/shard_map/pallas_call | solution.py:57
  115.8 1.1 copy-done.1
  117.0 3.3 %all-to-all-done.2 = bf16[8,64,768]{2,1,0:T(8,128)(2,1)S(1)} async-done(((bf16[8,64,768]{2,1,0:T(8,128)(2,1)}), bf16[8,64,768]{2,1,0:T(8,128)(2,1)S(1)}, u32[]{:S(2)}, u32[]{:S(2)}) %all-to-all-start.2) | async-done | bytes 786464 | tf_op jit(solution)/shard_map/all_to_all | solution.py:146
  120.3 4.7 %all-to-all-start.3 = ((bf16[8,64,768]{2,1,0:T(8,128)(2,1)}), bf16[8,64,768]{2,1,0:T(8,128)(2,1)}, u32[]{:S(2)}, u32[]{:S(2)}) async-start(bf16[8,64,768]{2,1,0:T(8,128)(2,1)} %get-tuple-element.78), calls=%async_computation.3 | async-start | bytes 1572864 | tf_op jit(solution)/shard_map/all_to_all | solution.py:146
  125.1 0.8 convolution_convert_fusion.1
  126.0 0.8 fusion.29
  126.8 1.5 collective-permute-done.16
  128.2 1.0 add_convert_fusion.3
  129.5 2.2 %collective-permute-start.18 = (bf16[64,1536]{1,0:T(8,128)(2,1)}, bf16[64,1536]{1,0:T(8,128)(2,1)S(1)}, u32[]{:S(2)}, u32[]{:S(2)}) collective-permute-start(bf16[64,1536]{1,0:T(8,128)(2,1)} %get-tuple-element.75), channel_id=1, source_target_pairs={{0,4},{1,5},{2,6},{3,7},{4,0},{5,1},{6,2},{7,3},{8,12},{9,13},{10,... | collective-permute-start | bytes 589832 | tf_op jit(solution)/shard_map/ppermute | solution.py:124
  131.7 4.5 %all-to-all-done.3 = bf16[8,64,768]{2,1,0:T(8,128)(2,1)} async-done(((bf16[8,64,768]{2,1,0:T(8,128)(2,1)}), bf16[8,64,768]{2,1,0:T(8,128)(2,1)}, u32[]{:S(2)}, u32[]{:S(2)}) %all-to-all-start.3) | async-done | bytes 786464 | tf_op jit(solution)/shard_map/all_to_all | solution.py:146
  136.2 1.9 %fusion.27 = (bf16[4,64,768]{2,1,0:T(8,128)(2,1)}, bf16[4,64,768]{2,1,0:T(8,128)(2,1)S(1)}) fusion(bf16[8,64,768]{2,1,0:T(8,128)(2,1)} %all-to-all-done.3), kind=kLoop, calls=%fused_computation.63 | loop fusion | bytes 1572864 | tf_op jit(solution)/shard_map/slice | solution.py:175
  138.2 1.7 convolution_convert_fusion
  139.9 2.2 %collective-permute-done.19.refs_3_ = bf16[64,1536]{1,0:T(8,128)(2,1)S(1)} collective-permute-done((bf16[64,1536]{1,0:T(8,128)(2,1)S(1)}, bf16[64,1536]{1,0:T(8,128)(2,1)S(1)}, u32[]{:S(2)}, u32[]{:S(2)}) %collective-permute-start.19) | collective-permute-done | bytes 196640 | tf_op jit(solution)/shard_map/ppermute | solution.py:124
  142.1 5.7 %all-to-all-start.4 = ((bf16[8,2,64,768]{3,2,1,0:T(8,128)(2,1)}), bf16[8,2,64,768]{3,2,1,0:T(8,128)(2,1)}, u32[]{:S(2)}, u32[]{:S(2)}) async-start(bf16[8,2,64,768]{3,2,1,0:T(8,128)(2,1)} %copy-done.1), calls=%async_computation.4 | async-start | bytes 3145728 | tf_op jit(solution)/shard_map/all_to_all | solution.py:146
  147.8 1.9 %fusion.30 = f32[256,1536]{1,0:T(8,128)S(1)} fusion(bf16[256,768]{1,0:T(8,128)(2,1)} %bitcast.48, bf16[1536,768]{1,0:T(8,128)(2,1)S(1)} %copy-done), kind=kOutput, calls=%fused_computation.66 | convolution fusion | flops 603979776 | bytes 4325376 | tf_op jit(solution)/shard_map/dot_general | solution.py:27
  150.5 1.2 collective-permute-start.21
  151.7 1.7 collective-permute-start.22
  153.5 5.1 %multiply_convert_fusion.1 = bf16[1536,768]{1,0:T(8,128)(2,1)} fusion(bf16[256,1536]{1,0:T(8,128)(2,1)S(1)} %copy-done.20, bf16[256,1536]{1,0:T(8,128)(2,1)S(1)} %copy-done.10, bf16[256,1536]{1,0:T(8,128)(2,1)S(1)} %copy-done.18, bf16[256,1536]{1,0:T(8,128)(2,1)S(1)} %copy-done.8, bf16[512,768]{1,0:T(8,128)(2,1)} %bitcast.20, bf16[512,768]{1,0:T(8,128)(2,1)S(1)} %bitcast.47), kind=kOutput, calls=%fused_computation.1 | convolution fusion | flops 2434007040 | bytes 7077888 | tf_op jit(solution)/shard_map/dot_general | solution.py:31
  158.6 2.4 %collective-permute-done.22.refs_6_ = bf16[64,1536]{1,0:T(8,128)(2,1)S(1)} collective-permute-done((bf16[64,1536]{1,0:T(8,128)(2,1)S(1)}, bf16[64,1536]{1,0:T(8,128)(2,1)S(1)}, u32[]{:S(2)}, u32[]{:S(2)}) %collective-permute-start.22) | collective-permute-done | bytes 196640 | tf_op jit(solution)/shard_map/ppermute | solution.py:124
  161.1 3.0 %collective-permute-done.23.refs_7_ = bf16[64,1536]{1,0:T(8,128)(2,1)S(1)} collective-permute-done((bf16[64,1536]{1,0:T(8,128)(2,1)S(1)}, bf16[64,1536]{1,0:T(8,128)(2,1)S(1)}, u32[]{:S(2)}, u32[]{:S(2)}) %collective-permute-start.23) | collective-permute-done | bytes 196640 | tf_op jit(solution)/shard_map/ppermute | solution.py:124
  164.1 1.6 shard_map.78
  165.7 2.0 %collective-permute-start.24 = (bf16[32,1536]{1,0:T(8,128)(2,1)}, bf16[32,1536]{1,0:T(8,128)(2,1)S(1)}, u32[]{:S(2)}, u32[]{:S(2)}) collective-permute-start(bf16[32,1536]{1,0:T(8,128)(2,1)} %get-tuple-element.102), channel_id=1, source_target_pairs={{0,24},{8,0},{16,8},{24,16},{1,25},{9,1},{17,9},{25,17},{2,26},{10... | collective-permute-start | bytes 294920 | tf_op jit(solution)/shard_map/ppermute | solution.py:121
  168.0 2.6 %collective-permute-start.26 = (bf16[32,1536]{1,0:T(8,128)(2,1)}, bf16[32,1536]{1,0:T(8,128)(2,1)S(1)}, u32[]{:S(2)}, u32[]{:S(2)}) collective-permute-start(bf16[32,1536]{1,0:T(8,128)(2,1)} %get-tuple-element.104), channel_id=1, source_target_pairs={{0,8},{8,16},{16,24},{24,0},{1,9},{9,17},{17,25},{25,1},{2,10},{10... | collective-permute-start | bytes 294920 | tf_op jit(solution)/shard_map/ppermute | solution.py:121
  170.5 6.4 %multiply_convert_fusion = bf16[768,1536]{1,0:T(8,128)(2,1)} fusion(bf16[1024,768]{1,0:T(8,128)(2,1)} %bitcast.21, bf16[1024,1536]{1,0:T(8,128)(2,1)} %bitcast.46), kind=kOutput, calls=%fused_computation | convolution fusion | flops 2418278400 | bytes 7077888 | tf_op jit(solution)/shard_map/dot_general | solution.py:31
  176.9 1.5 collective-permute-done.25
  178.5 2.2 %collective-permute-done.26 = bf16[32,1536]{1,0:T(8,128)(2,1)S(1)} collective-permute-done((bf16[32,1536]{1,0:T(8,128)(2,1)}, bf16[32,1536]{1,0:T(8,128)(2,1)S(1)}, u32[]{:S(2)}, u32[]{:S(2)}) %collective-permute-start.26) | collective-permute-done | bytes 98336 | tf_op jit(solution)/shard_map/ppermute | solution.py:121
  (81 shorter events, 4.7 us)
Async XLA Ops:
  0.6 51.1 %copy-start = (bf16[1536,768]{1,0:T(8,128)(2,1)S(1)}, bf16[1536,768]{1,0:T(8,128)(2,1)}, u32[]{:S(2)}) copy-start(bf16[1536,768]{1,0:T(8,128)(2,1)} %param.6) | copy-start | bytes 7077892
  1.7 9.3 %collective-permute-start.2 = (bf16[2,16,1536]{2,1,0:T(8,128)(2,1)S(1)}, bf16[2,16,1536]{2,1,0:T(8,128)(2,1)S(1)}, u32[]{:S(2)}, u32[]{:S(2)}) collective-permute-start(bf16[2,16,1536]{2,1,0:T(8,128)(2,1)S(1)} %pad_maximum_fusion.7), channel_id=1, source_target_pairs={{0,24},{8,0},{16,8},{24,16},{1,25},{9,1},{17,9},{25,17},{2,26},{10... | collective-permute-start | bytes 294920 | tf_op jit(solution)/shard_map/ppermute | solution.py:121
  7.2 10.9 %collective-permute-start.1 = (bf16[2,16,1536]{2,1,0:T(8,128)(2,1)S(1)}, bf16[2,16,1536]{2,1,0:T(8,128)(2,1)S(1)}, u32[]{:S(2)}, u32[]{:S(2)}) collective-permute-start(bf16[2,16,1536]{2,1,0:T(8,128)(2,1)S(1)} %pad_maximum_fusion.7), channel_id=1, source_target_pairs={{0,16},{8,24},{16,0},{24,8},{1,17},{9,25},{17,1},{25,9},{2,18},{10... | collective-permute-start | bytes 294920 | tf_op jit(solution)/shard_map/ppermute | solution.py:121
  8.6 10.0 %collective-permute-start = (bf16[2,16,1536]{2,1,0:T(8,128)(2,1)S(1)}, bf16[2,16,1536]{2,1,0:T(8,128)(2,1)S(1)}, u32[]{:S(2)}, u32[]{:S(2)}) collective-permute-start(bf16[2,16,1536]{2,1,0:T(8,128)(2,1)S(1)} %pad_maximum_fusion.7), channel_id=1, source_target_pairs={{0,8},{8,16},{16,24},{24,0},{1,9},{9,17},{17,25},{25,1},{2,10},{10... | collective-permute-start | bytes 294920 | tf_op jit(solution)/shard_map/ppermute | solution.py:121
  18.7 11.1 %collective-permute-start.8 = (bf16[2,16,1536]{2,1,0:T(8,128)(2,1)S(1)}, bf16[2,16,1536]{2,1,0:T(8,128)(2,1)S(1)}, u32[]{:S(2)}, u32[]{:S(2)}) collective-permute-start(bf16[2,16,1536]{2,1,0:T(8,128)(2,1)S(1)} %pad_maximum_fusion.8), channel_id=1, source_target_pairs={{0,24},{8,0},{16,8},{24,16},{1,25},{9,1},{17,9},{25,17},{2,26},{10... | collective-permute-start | bytes 294920 | tf_op jit(solution)/shard_map/ppermute | solution.py:121
  22.4 16.1 %collective-permute-start.3 = (bf16[2,64,1536]{2,1,0:T(8,128)(2,1)S(1)}, bf16[2,64,1536]{2,1,0:T(8,128)(2,1)S(1)}, u32[]{:S(2)}, u32[]{:S(2)}) collective-permute-start(bf16[2,64,1536]{2,1,0:T(8,128)(2,1)S(1)} %pad_maximum_fusion.5), channel_id=1, source_target_pairs={{0,2},{1,3},{2,4},{3,5},{4,6},{5,7},{6,0},{7,1},{8,10},{9,11},{10,... | collective-permute-start | bytes 1179656 | tf_op jit(solution)/shard_map/ppermute | solution.py:124
  23.9 19.4 %collective-permute-start.4 = (bf16[2,64,1536]{2,1,0:T(8,128)(2,1)S(1)}, bf16[2,64,1536]{2,1,0:T(8,128)(2,1)S(1)}, u32[]{:S(2)}, u32[]{:S(2)}) collective-permute-start(bf16[2,64,1536]{2,1,0:T(8,128)(2,1)S(1)} %pad_maximum_fusion.5), channel_id=1, source_target_pairs={{0,4},{1,5},{2,6},{3,7},{4,0},{5,1},{6,2},{7,3},{8,12},{9,13},{10,... | collective-permute-start | bytes 1179656 | tf_op jit(solution)/shard_map/ppermute | solution.py:124
  26.6 16.7 %collective-permute-start.5 = (bf16[2,64,1536]{2,1,0:T(8,128)(2,1)S(1)}, bf16[2,64,1536]{2,1,0:T(8,128)(2,1)S(1)}, u32[]{:S(2)}, u32[]{:S(2)}) collective-permute-start(bf16[2,64,1536]{2,1,0:T(8,128)(2,1)S(1)} %pad_maximum_fusion.5), channel_id=1, source_target_pairs={{0,6},{1,7},{2,0},{3,1},{4,2},{5,3},{6,4},{7,5},{8,14},{9,15},{10,... | collective-permute-start | bytes 1179656 | tf_op jit(solution)/shard_map/ppermute | solution.py:124
  28.0 9.4 %collective-permute-start.7 = (bf16[2,16,1536]{2,1,0:T(8,128)(2,1)S(1)}, bf16[2,16,1536]{2,1,0:T(8,128)(2,1)S(1)}, u32[]{:S(2)}, u32[]{:S(2)}) collective-permute-start(bf16[2,16,1536]{2,1,0:T(8,128)(2,1)S(1)} %pad_maximum_fusion.8), channel_id=1, source_target_pairs={{0,16},{8,24},{16,0},{24,8},{1,17},{9,25},{17,1},{25,9},{2,18},{10... | collective-permute-start | bytes 294920 | tf_op jit(solution)/shard_map/ppermute | solution.py:121
  29.8 8.7 %collective-permute-start.6 = (bf16[2,16,1536]{2,1,0:T(8,128)(2,1)S(1)}, bf16[2,16,1536]{2,1,0:T(8,128)(2,1)S(1)}, u32[]{:S(2)}, u32[]{:S(2)}) collective-permute-start(bf16[2,16,1536]{2,1,0:T(8,128)(2,1)S(1)} %pad_maximum_fusion.8), channel_id=1, source_target_pairs={{0,8},{8,16},{16,24},{24,0},{1,9},{9,17},{17,25},{25,1},{2,10},{10... | collective-permute-start | bytes 294920 | tf_op jit(solution)/shard_map/ppermute | solution.py:121
  43.4 6.8 %copy-start.15 = (bf16[768,1536]{1,0:T(8,128)(2,1)S(1)}, bf16[768,1536]{1,0:T(8,128)(2,1)}, u32[]{:S(2)}) copy-start(bf16[768,1536]{1,0:T(8,128)(2,1)} %param.8) | copy-start | bytes 7077892
  43.5 8.1 %copy-start.4 = (bf16[256,1536]{1,0:T(8,128)(2,1)}, bf16[256,1536]{1,0:T(8,128)(2,1)S(1)}, u32[]{:S(2)}) copy-start(bf16[256,1536]{1,0:T(8,128)(2,1)S(1)} %get-tuple-element.124) | copy-start | bytes 2359300
  43.5 8.1 %copy-start.7 = (bf16[256,1536]{1,0:T(8,128)(2,1)}, bf16[256,1536]{1,0:T(8,128)(2,1)S(1)}, u32[]{:S(2)}) copy-start(bf16[256,1536]{1,0:T(8,128)(2,1)S(1)} %get-tuple-element.123) | copy-start | bytes 2359300
  43.5 6.7 %collective-permute-start.10 = (bf16[256,1536]{1,0:T(8,128)(2,1)S(1)}, bf16[256,1536]{1,0:T(8,128)(2,1)S(1)}, u32[]{:S(2)}, u32[]{:S(2)}) collective-permute-start(bf16[256,1536]{1,0:T(8,128)(2,1)S(1)} %get-tuple-element.124), channel_id=1, source_target_pairs={{0,1},{1,0},{2,3},{3,2},{4,5},{5,4},{6,7},{7,6},{8,9},{9,8},{10,11... | collective-permute-start | bytes 2359304 | tf_op jit(solution)/shard_map/ppermute | solution.py:127
  43.6 8.0 %collective-permute-start.9 = (bf16[256,1536]{1,0:T(8,128)(2,1)S(1)}, bf16[256,1536]{1,0:T(8,128)(2,1)S(1)}, u32[]{:S(2)}, u32[]{:S(2)}) collective-permute-start(bf16[256,1536]{1,0:T(8,128)(2,1)S(1)} %get-tuple-element.123), channel_id=1, source_target_pairs={{0,1},{1,0},{2,3},{3,2},{4,5},{5,4},{6,7},{7,6},{8,9},{9,8},{10,11... | collective-permute-start | bytes 2359304 | tf_op jit(solution)/shard_map/ppermute | solution.py:127
  44.1 16.2 %collective-permute-start.11 = (bf16[2,64,1536]{2,1,0:T(8,128)(2,1)S(1)}, bf16[2,64,1536]{2,1,0:T(8,128)(2,1)}, u32[]{:S(2)}, u32[]{:S(2)}) collective-permute-start(bf16[2,64,1536]{2,1,0:T(8,128)(2,1)S(1)} %pad_maximum_fusion.6), channel_id=1, source_target_pairs={{0,2},{1,3},{2,4},{3,5},{4,6},{5,7},{6,0},{7,1},{8,10},{9,11},{10,... | collective-permute-start | bytes 1179656 | tf_op jit(solution)/shard_map/ppermute | solution.py:124
  45.5 19.9 %collective-permute-start.12 = (bf16[2,64,1536]{2,1,0:T(8,128)(2,1)S(1)}, bf16[2,64,1536]{2,1,0:T(8,128)(2,1)S(1)}, u32[]{:S(2)}, u32[]{:S(2)}) collective-permute-start(bf16[2,64,1536]{2,1,0:T(8,128)(2,1)S(1)} %pad_maximum_fusion.6), channel_id=1, source_target_pairs={{0,4},{1,5},{2,6},{3,7},{4,0},{5,1},{6,2},{7,3},{8,12},{9,13},{10,... | collective-permute-start | bytes 1179656 | tf_op jit(solution)/shard_map/ppermute | solution.py:124
  47.9 18.3 %collective-permute-start.13 = (bf16[2,64,1536]{2,1,0:T(8,128)(2,1)S(1)}, bf16[2,64,1536]{2,1,0:T(8,128)(2,1)S(1)}, u32[]{:S(2)}, u32[]{:S(2)}) collective-permute-start(bf16[2,64,1536]{2,1,0:T(8,128)(2,1)S(1)} %pad_maximum_fusion.6), channel_id=1, source_target_pairs={{0,6},{1,7},{2,0},{3,1},{4,2},{5,3},{6,4},{7,5},{8,14},{9,15},{10,... | collective-permute-start | bytes 1179656 | tf_op jit(solution)/shard_map/ppermute | solution.py:124
  50.2 1.4 copy-start.11
  51.7 1.4 copy-start.17
  54.4 25.3 %all-to-all-start = ((bf16[8,2,64,768]{3,2,1,0:T(8,128)(2,1)}), bf16[8,2,64,768]{3,2,1,0:T(8,128)(2,1)}, u32[]{:S(2)}, u32[]{:S(2)}) async-start(bf16[8,2,64,768]{3,2,1,0:T(8,128)(2,1)} %pad_maximum_fusion.2), calls=%async_computation | async-start | bytes 3145728 | tf_op jit(solution)/shard_map/all_to_all | solution.py:146
  66.9 4.0 %copy-start.16 = (bf16[768,1536]{1,0:T(8,128)(2,1)S(1)}, bf16[768,1536]{1,0:T(8,128)(2,1)}, u32[]{:S(2)}) copy-start(bf16[768,1536]{1,0:T(8,128)(2,1)} %param.8) | copy-start | bytes 7077892
  68.6 3.8 %copy-start.5 = (bf16[256,1536]{1,0:T(8,128)(2,1)}, bf16[256,1536]{1,0:T(8,128)(2,1)S(1)}, u32[]{:S(2)}) copy-start(bf16[256,1536]{1,0:T(8,128)(2,1)S(1)} %get-tuple-element.122) | copy-start | bytes 2359300
  68.6 3.8 %copy-start.9 = (bf16[256,1536]{1,0:T(8,128)(2,1)}, bf16[256,1536]{1,0:T(8,128)(2,1)S(1)}, u32[]{:S(2)}) copy-start(bf16[256,1536]{1,0:T(8,128)(2,1)S(1)} %get-tuple-element.121) | copy-start | bytes 2359300
  68.6 2.4 %collective-permute-start.15 = (bf16[256,1536]{1,0:T(8,128)(2,1)S(1)}, bf16[256,1536]{1,0:T(8,128)(2,1)S(1)}, u32[]{:S(2)}, u32[]{:S(2)}) collective-permute-start(bf16[256,1536]{1,0:T(8,128)(2,1)S(1)} %get-tuple-element.122), channel_id=1, source_target_pairs={{0,1},{1,0},{2,3},{3,2},{4,5},{5,4},{6,7},{7,6},{8,9},{9,8},{10,11... | collective-permute-start | bytes 2359304 | tf_op jit(solution)/shard_map/ppermute | solution.py:127
  68.7 3.7 %collective-permute-start.14 = (bf16[256,1536]{1,0:T(8,128)(2,1)S(1)}, bf16[256,1536]{1,0:T(8,128)(2,1)S(1)}, u32[]{:S(2)}, u32[]{:S(2)}) collective-permute-start(bf16[256,1536]{1,0:T(8,128)(2,1)S(1)} %get-tuple-element.121), channel_id=1, source_target_pairs={{0,1},{1,0},{2,3},{3,2},{4,5},{5,4},{6,7},{7,6},{8,9},{9,8},{10,11... | collective-permute-start | bytes 2359304 | tf_op jit(solution)/shard_map/ppermute | solution.py:127
  71.0 1.4 copy-start.12
  72.4 1.4 copy-start.19
  75.1 9.3 %copy-start.14 = (f32[768]{0:T(1024)S(1)}, f32[768]{0:T(1024)}, u32[]{:S(2)}) copy-start(f32[768]{0:T(1024)} %param.7) | copy-start | bytes 9220
  79.7 24.8 %all-to-all-start.1 = ((bf16[8,2,64,768]{3,2,1,0:T(8,128)(2,1)}), bf16[8,2,64,768]{3,2,1,0:T(8,128)(2,1)}, u32[]{:S(2)}, u32[]{:S(2)}) async-start(bf16[8,2,64,768]{3,2,1,0:T(8,128)(2,1)} %pad_maximum_fusion.4), calls=%async_computation.1 | async-start | bytes 3145728 | tf_op jit(solution)/shard_map/all_to_all | solution.py:146
  104.5 15.8 %all-to-all-start.2 = ((bf16[8,64,768]{2,1,0:T(8,128)(2,1)}), bf16[8,64,768]{2,1,0:T(8,128)(2,1)S(1)}, u32[]{:S(2)}, u32[]{:S(2)}) async-start(bf16[8,64,768]{2,1,0:T(8,128)(2,1)} %get-tuple-element.65), calls=%async_computation.2 | async-start | bytes 1572864 | tf_op jit(solution)/shard_map/all_to_all | solution.py:146
  108.7 1.6 copy-start.6
  108.7 1.8 %copy-start.13 = (bf16[256,1536]{1,0:T(8,128)(2,1)S(1)}, bf16[256,1536]{1,0:T(8,128)(2,1)}, u32[]{:S(2)}) copy-start(bf16[256,1536]{1,0:T(8,128)(2,1)} %copy-done.12) | copy-start | bytes 2359300
  115.8 1.1 copy-start.1
  120.3 4.7 %copy-start.2 = (bf16[8,64,768]{2,1,0:T(8,128)(2,1)}, bf16[8,64,768]{2,1,0:T(8,128)(2,1)S(1)}, u32[]{:S(2)}) copy-start(bf16[8,64,768]{2,1,0:T(8,128)(2,1)S(1)} %all-to-all-done.2) | copy-start | bytes 2359300
  120.3 15.9 %all-to-all-start.3 = ((bf16[8,64,768]{2,1,0:T(8,128)(2,1)}), bf16[8,64,768]{2,1,0:T(8,128)(2,1)}, u32[]{:S(2)}, u32[]{:S(2)}) async-start(bf16[8,64,768]{2,1,0:T(8,128)(2,1)} %get-tuple-element.78), calls=%async_computation.3 | async-start | bytes 1572864 | tf_op jit(solution)/shard_map/all_to_all | solution.py:146
  125.9 2.4 %collective-permute-start.16 = (bf16[256,1536]{1,0:T(8,128)(2,1)S(1)}, bf16[256,1536]{1,0:T(8,128)(2,1)S(1)}, u32[]{:S(2)}, u32[]{:S(2)}) collective-permute-start(bf16[256,1536]{1,0:T(8,128)(2,1)S(1)} %convolution_convert_fusion.1), channel_id=1, source_target_pairs={{0,1},{1,0},{2,3},{3,2},{4,5},{5,4},{6,7},{7,6},{8,9},{9,8},{10,11... | collective-permute-start | bytes 2359304 | tf_op jit(solution)/shard_map/ppermute | solution.py:127
  129.2 10.6 %collective-permute-start.17 = (bf16[64,1536]{1,0:T(8,128)(2,1)}, bf16[64,1536]{1,0:T(8,128)(2,1)S(1)}, u32[]{:S(2)}, u32[]{:S(2)}) collective-permute-start(bf16[64,1536]{1,0:T(8,128)(2,1)} %get-tuple-element.74), channel_id=1, source_target_pairs={{0,6},{1,7},{2,0},{3,1},{4,2},{5,3},{6,4},{7,5},{8,14},{9,15},{10,... | collective-permute-start | bytes 589832 | tf_op jit(solution)/shard_map/ppermute | solution.py:124
  129.5 10.4 %collective-permute-start.18 = (bf16[64,1536]{1,0:T(8,128)(2,1)}, bf16[64,1536]{1,0:T(8,128)(2,1)S(1)}, u32[]{:S(2)}, u32[]{:S(2)}) collective-permute-start(bf16[64,1536]{1,0:T(8,128)(2,1)} %get-tuple-element.75), channel_id=1, source_target_pairs={{0,4},{1,5},{2,6},{3,7},{4,0},{5,1},{6,2},{7,3},{8,12},{9,13},{10,... | collective-permute-start | bytes 589832 | tf_op jit(solution)/shard_map/ppermute | solution.py:124
  131.7 10.4 %collective-permute-start.19 = (bf16[64,1536]{1,0:T(8,128)(2,1)S(1)}, bf16[64,1536]{1,0:T(8,128)(2,1)S(1)}, u32[]{:S(2)}, u32[]{:S(2)}) collective-permute-start(bf16[64,1536]{1,0:T(8,128)(2,1)S(1)} %get-tuple-element.76), channel_id=1, source_target_pairs={{0,2},{1,3},{2,4},{3,5},{4,6},{5,7},{6,0},{7,1},{8,10},{9,11},{10,... | collective-permute-start | bytes 589832 | tf_op jit(solution)/shard_map/ppermute | solution.py:124
  142.1 28.4 %all-to-all-start.4 = ((bf16[8,2,64,768]{3,2,1,0:T(8,128)(2,1)}), bf16[8,2,64,768]{3,2,1,0:T(8,128)(2,1)}, u32[]{:S(2)}, u32[]{:S(2)}) async-start(bf16[8,2,64,768]{3,2,1,0:T(8,128)(2,1)} %copy-done.1), calls=%async_computation.4 | async-start | bytes 3145728 | tf_op jit(solution)/shard_map/all_to_all | solution.py:146
  147.8 2.5 %collective-permute-start.20 = (bf16[256,1536]{1,0:T(8,128)(2,1)}, bf16[256,1536]{1,0:T(8,128)(2,1)S(1)}, u32[]{:S(2)}, u32[]{:S(2)}) collective-permute-start(bf16[256,1536]{1,0:T(8,128)(2,1)} %convolution_convert_fusion), channel_id=1, source_target_pairs={{0,1},{1,0},{2,3},{3,2},{4,5},{5,4},{6,7},{7,6},{8,9},{9,8},{10,11... | collective-permute-start | bytes 2359304 | tf_op jit(solution)/shard_map/ppermute | solution.py:127
  147.8 5.7 %copy-start.20 = (bf16[256,1536]{1,0:T(8,128)(2,1)S(1)}, bf16[256,1536]{1,0:T(8,128)(2,1)}, u32[]{:S(2)}) copy-start(bf16[256,1536]{1,0:T(8,128)(2,1)} %copy-done.19) | copy-start | bytes 2359300
  149.7 3.8 %copy-start.3 = (bf16[8,64,768]{2,1,0:T(8,128)(2,1)S(1)}, bf16[8,64,768]{2,1,0:T(8,128)(2,1)}, u32[]{:S(2)}) copy-start(bf16[8,64,768]{2,1,0:T(8,128)(2,1)} %copy-done.2) | copy-start | bytes 2359300
  149.7 3.8 %copy-start.8 = (bf16[256,1536]{1,0:T(8,128)(2,1)S(1)}, bf16[256,1536]{1,0:T(8,128)(2,1)}, u32[]{:S(2)}) copy-start(bf16[256,1536]{1,0:T(8,128)(2,1)} %copy-done.7) | copy-start | bytes 2359300
  149.7 3.8 %copy-start.10 = (bf16[256,1536]{1,0:T(8,128)(2,1)S(1)}, bf16[256,1536]{1,0:T(8,128)(2,1)}, u32[]{:S(2)}) copy-start(bf16[256,1536]{1,0:T(8,128)(2,1)} %copy-done.9) | copy-start | bytes 2359300
  149.7 3.8 %copy-start.18 = (bf16[256,1536]{1,0:T(8,128)(2,1)S(1)}, bf16[256,1536]{1,0:T(8,128)(2,1)}, u32[]{:S(2)}) copy-start(bf16[256,1536]{1,0:T(8,128)(2,1)} %copy-done.17) | copy-start | bytes 2359300
  150.5 8.2 %collective-permute-start.21 = (bf16[64,1536]{1,0:T(8,128)(2,1)S(1)}, bf16[64,1536]{1,0:T(8,128)(2,1)S(1)}, u32[]{:S(2)}, u32[]{:S(2)}) collective-permute-start(bf16[64,1536]{1,0:T(8,128)(2,1)S(1)} %get-tuple-element.88), channel_id=1, source_target_pairs={{0,6},{1,7},{2,0},{3,1},{4,2},{5,3},{6,4},{7,5},{8,14},{9,15},{10,... | collective-permute-start | bytes 589832 | tf_op jit(solution)/shard_map/ppermute | solution.py:124
  151.7 9.3 %collective-permute-start.22 = (bf16[64,1536]{1,0:T(8,128)(2,1)S(1)}, bf16[64,1536]{1,0:T(8,128)(2,1)S(1)}, u32[]{:S(2)}, u32[]{:S(2)}) collective-permute-start(bf16[64,1536]{1,0:T(8,128)(2,1)S(1)} %get-tuple-element.89), channel_id=1, source_target_pairs={{0,4},{1,5},{2,6},{3,7},{4,0},{5,1},{6,2},{7,3},{8,12},{9,13},{10,... | collective-permute-start | bytes 589832 | tf_op jit(solution)/shard_map/ppermute | solution.py:124
  153.4 10.7 %collective-permute-start.23 = (bf16[64,1536]{1,0:T(8,128)(2,1)S(1)}, bf16[64,1536]{1,0:T(8,128)(2,1)S(1)}, u32[]{:S(2)}, u32[]{:S(2)}) collective-permute-start(bf16[64,1536]{1,0:T(8,128)(2,1)S(1)} %get-tuple-element.90), channel_id=1, source_target_pairs={{0,2},{1,3},{2,4},{3,5},{4,6},{5,7},{6,0},{7,1},{8,10},{9,11},{10,... | collective-permute-start | bytes 589832 | tf_op jit(solution)/shard_map/ppermute | solution.py:124
  165.7 11.3 %collective-permute-start.24 = (bf16[32,1536]{1,0:T(8,128)(2,1)}, bf16[32,1536]{1,0:T(8,128)(2,1)S(1)}, u32[]{:S(2)}, u32[]{:S(2)}) collective-permute-start(bf16[32,1536]{1,0:T(8,128)(2,1)} %get-tuple-element.102), channel_id=1, source_target_pairs={{0,24},{8,0},{16,8},{24,16},{1,25},{9,1},{17,9},{25,17},{2,26},{10... | collective-permute-start | bytes 294920 | tf_op jit(solution)/shard_map/ppermute | solution.py:121
  167.7 10.8 %collective-permute-start.25 = (bf16[32,1536]{1,0:T(8,128)(2,1)}, bf16[32,1536]{1,0:T(8,128)(2,1)S(1)}, u32[]{:S(2)}, u32[]{:S(2)}) collective-permute-start(bf16[32,1536]{1,0:T(8,128)(2,1)} %get-tuple-element.103), channel_id=1, source_target_pairs={{0,16},{8,24},{16,0},{24,8},{1,17},{9,25},{17,1},{25,9},{2,18},{10... | collective-permute-start | bytes 294920 | tf_op jit(solution)/shard_map/ppermute | solution.py:121
  168.0 12.7 %collective-permute-start.26 = (bf16[32,1536]{1,0:T(8,128)(2,1)}, bf16[32,1536]{1,0:T(8,128)(2,1)S(1)}, u32[]{:S(2)}, u32[]{:S(2)}) collective-permute-start(bf16[32,1536]{1,0:T(8,128)(2,1)} %get-tuple-element.104), channel_id=1, source_target_pairs={{0,8},{8,16},{16,24},{24,0},{1,9},{9,17},{17,25},{25,1},{2,10},{10... | collective-permute-start | bytes 294920 | tf_op jit(solution)/shard_map/ppermute | solution.py:121

commit v11 on v10

--- a/solution.py
+++ b/solution.py
@@ -10,7 +10,10 @@
 
 root_coef = math.sqrt(2.0 / math.pi)
 cubic_coef = 0.044715
+pre_scale = 64.0
+up_scale = 128.0
 bf16 = jnp.bfloat16
+f16 = jnp.float16
 f32 = jnp.float32
 
 
@@ -35,13 +38,10 @@
     return pltpu.CompilerParams(vmem_limit_bytes=mib << 20)
 
 
-def hidden_kernel(parts, bias, *refs):
+def hidden_kernel(sums, bias, *refs):
     before, (grad_copies, act_out) = refs[:-2], refs[-2:]
-    sums = parts[0].astype(f32)
-    for j in range(1, parts.shape[0]):
-        sums = sums + parts[j].astype(f32)
-    act, grad = gelu_pair(sums[0] + bias[...], sums[1])
-    for j in range(parts.shape[0]):
+    act, grad = gelu_pair(sums[0] * (1.0 / pre_scale) + bias[...], sums[1] * (1.0 / up_scale))
+    for j in range(grad_copies.shape[0]):
         grad_copies[j] = grad
         if before:
             act_out[j, 0] = before[0][...]
@@ -52,13 +52,14 @@
 
 def hidden(parts, bias, *before):
     n, pair, rows, columns = parts.shape
+    sums = jnp.sum(parts.astype(f32), axis=0)
     tile = columns // 3
     act_shape = (n, 2, rows) if before else (rows,)
     return pl.pallas_call(
         hidden_kernel,
         grid=(columns // tile,),
         in_specs=[
-            pl.BlockSpec((n, pair, rows, tile), lambda i: (0, 0, 0, i)),
+            pl.BlockSpec((pair, rows, tile), lambda i: (0, 0, i)),
             pl.BlockSpec((1, tile), lambda i: (0, i)),
         ]
         + [pl.BlockSpec((rows, tile), lambda i: (0, i))] * len(before),
@@ -76,13 +77,13 @@
             bytes_accessed=6 * n * rows * columns,
             transcendentals=rows * columns,
         ),
-    )(parts, bias, *before)
-
-
-def join_kernel(n, *refs):
+    )(sums, bias, *before)
+
+
+def join_kernel(n, n_parts, *refs):
     ins, outs = refs[:-n], refs[-n:]
     chunk_rows = ins[0].shape[0] // n
-    chunks = [ins[j : j + n] for j in range(0, len(ins), n)]
+    chunks = [ins[j : j + n_parts] for j in range(0, len(ins), n_parts)]
     for c, parts in enumerate(chunks):
         total = parts[0][...]
         for part in parts[1:]:
@@ -92,18 +93,18 @@
             out[c * chunk_rows : (c + 1) * chunk_rows] = block.astype(out.dtype)
 
 
-def join_sums(chunks, n):
+def join_sums(chunks, n, own_type=f32):
     rows, columns = chunks[0][0].shape
     tile = columns // 3
     out_rows = len(chunks) * rows // n
     ins = [part for parts in chunks for part in parts]
     return pl.pallas_call(
-        functools.partial(join_kernel, n),
+        functools.partial(join_kernel, n, len(chunks[0])),
         grid=(columns // tile,),
         in_specs=[pl.BlockSpec((rows, tile), lambda i: (0, i))] * len(ins),
         out_specs=[pl.BlockSpec((out_rows, tile), lambda i: (0, i))] * n,
         out_shape=[
-            jax.ShapeDtypeStruct((out_rows, columns), bf16 if k else f32) for k in range(n)
+            jax.ShapeDtypeStruct((out_rows, columns), bf16 if k else own_type) for k in range(n)
         ],
         compiler_params=pltpu.CompilerParams(vmem_limit_bytes=8 << 20),
         cost_estimate=pl.CostEstimate(
@@ -164,8 +165,8 @@
 
         def partial_sums(pieces):
             both = [jnp.concatenate([a, swap_core(a)], axis=0) for a in join(pieces)]
-            pre_part = jnp.dot(both[0], weight_in, preferred_element_type=f32).astype(bf16)
-            up_part = contract_last(both[1], weight_out).astype(bf16)
+            pre_part = (jnp.dot(both[0], weight_in, preferred_element_type=f32) * pre_scale).astype(f16)
+            up_part = (contract_last(both[1], weight_out) * up_scale).astype(f16)
             parts = [a.reshape(n_x, 1, -1, a.shape[1]) for a in (pre_part, up_part)]
             return both, jnp.concatenate(parts, axis=1)
 
@@ -204,14 +205,14 @@
         hidden_all = jnp.concatenate([hidden0, hidden1], axis=0)
         tokens_all = jnp.concatenate([both0[0], both1[0]], axis=0)
         grad_weight_in = (contract_first(tokens_all, hidden_all) * norm_scale).astype(bf16)
-        parts0, parts1, grad_weight_in = barrier(parts0, parts1, grad_weight_in)
-        parts = join_sums([parts0, parts1], n_y)
-        parts = exchange(parts, shift_y)
+        parts0, grad_weight_in = barrier(parts0, grad_weight_in)
+        parts0 = exchange(join_sums([parts0], n_y), shift_y)
+        parts1 = exchange(join_sums([parts1], n_y), shift_y)
         activation = activation.reshape(-1, columns)
         grad_weight_out = (contract_first(activation, grad_all) * norm_scale).astype(bf16)
-        parts, grad_weight_out = barrier(parts, grad_weight_out)
-        (grad_tokens,) = sum_blocks(parts, 1)
-        return (grad_tokens.astype(bf16), grad_weight_in, grad_weight_out)
+        parts0, parts1, grad_weight_out = barrier(parts0, parts1, grad_weight_out)
+        (grad_tokens,) = join_sums([parts0, parts1], 1, bf16)
+        return (grad_tokens, grad_weight_in, grad_weight_out)
 
     return jax.shard_map(
         shards,

time: 183 us -> 181 us (0.989)
  waiting for transfers between devices: 66.4 us -> 57 us
  starting transfers between devices: 64.9 us -> 72.3 us
  other arithmetic: 8.08 us -> 11.4 us
  Pallas kernels: 8.15 us -> 5.28 us
    ppermute x9 -> x12, starting transfers between devices: 22 us -> 29.1 us  [shift_y(): return lax.ppermute(a, 'gy', [(i, (i + k) % n_y) for i in range(n_y)])]
    ppermute x12, waiting for transfers between devices: 15.8 us -> 10.3 us  [shift_chip(): return lax.ppermute(a, 'gz', [(i, (i + 2 * k) % n_z) for i in range(n_z)])]
    ppermute x9 -> x12, waiting for transfers between devices: 17.6 us -> 13.9 us  [shift_y(): return lax.ppermute(a, 'gy', [(i, (i + k) % n_y) for i in range(n_y)])]
    reduce_sum x0 -> x2, other arithmetic: none -> 3.36 us  [hidden(): sums = jnp.sum(parts.astype(f32), axis=0)]
    pallas_call x2, Pallas kernels: 6.58 us -> 3.38 us  [hidden(): pl.pallas_call(hidden_kernel, grid=(columns // tile,), in_specs=[pl.Block...]
  transfers between devices with their start and end apart: 32 -> 35, of which waited for: 18 -> 15; matrix products, arithmetic and copies ran while one was open for 21% -> 23% of each run, Pallas kernels for 4% -> 2%
where the time goes in v11:
time: 181 us; the launch traced here: 180 us
  starting transfers between devices  72.3 us (40%)
  waiting for transfers between devices  57 us (31%)
  matrix products  22.3 us (12%)
  other arithmetic  11.4 us (6%)
  local copies, waits for them, and re-layouts  10.4 us (6%)
  Pallas kernels  5.28 us (3%)
    ppermute x12, starting transfers between devices, shift_y(): return lax.ppermute(a, 'gy', [(i, (i + k) % n_y) for i in range(n_y)])  29.1 us
    all_to_all x5, waiting for transfers between devices, trade_width(): return lax.all_to_all(parts, 'gx', 0, 0, tiled=True)  29 us
    all_to_all x5, starting transfers between devices, trade_width(): return lax.all_to_all(parts, 'gx', 0, 0, tiled=True)  25.2 us
    ppermute x12, starting transfers between devices, shift_chip(): return lax.ppermute(a, 'gz', [(i, (i + 2 * k) % n_z) for i in range(n_z)])  16.7 us
    ppermute x12, waiting for transfers between devices, shift_y(): return lax.ppermute(a, 'gy', [(i, (i + k) % n_y) for i in range(n_y)])  13.9 us
    dot_general x2, matrix products, contract_first(): lax.dot_general(left, right, (((0,), (0,)), ((), ())), preferred_element_...  11.5 us
    ppermute x12, waiting for transfers between devices, shift_chip(): return lax.ppermute(a, 'gz', [(i, (i + 2 * k) % n_z) for i in range(n_z)])  10.3 us
    dot_general x6, matrix products, contract_last(): lax.dot_general(left, right, (((1,), (1,)), ((), ())), preferred_element_...  8.01 us
  transfers between devices with their start and end apart: 35, of which 15 were waited for; matrix products, arithmetic and copies ran while one was open for 23% of the time, Pallas kernels for 2%

profile of v11, /device:TPU:32, one launch (start us, length us, event | category | flops | bytes accessed | tf_op | source)
XLA Modules:
  0.0 179.8 jit_solution(10883471379173724112)
XLA Ops:
  0.6 1.0 slice_bitcast_fusion.4
  1.7 5.5 %collective-permute-start.2 = (bf16[2,16,1536]{2,1,0:T(8,128)(2,1)S(1)}, bf16[2,16,1536]{2,1,0:T(8,128)(2,1)S(1)}, u32[]{:S(2)}, u32[]{:S(2)}) collective-permute-start(bf16[2,16,1536]{2,1,0:T(8,128)(2,1)S(1)} %pad_maximum_fusion.7), channel_id=1, source_target_pairs={{0,24},{8,0},{16,8},{24,16},{1,25},{9,1},{17,9},{25,17},{2,26},{10... | collective-permute-start | bytes 294920 | tf_op jit(solution)/shard_map/ppermute | solution.py:122
  7.2 1.4 collective-permute-start.1
  8.6 2.4 %collective-permute-start = (bf16[2,16,1536]{2,1,0:T(8,128)(2,1)S(1)}, bf16[2,16,1536]{2,1,0:T(8,128)(2,1)S(1)}, u32[]{:S(2)}, u32[]{:S(2)}) collective-permute-start(bf16[2,16,1536]{2,1,0:T(8,128)(2,1)S(1)} %pad_maximum_fusion.7), channel_id=1, source_target_pairs={{0,8},{8,16},{16,24},{24,0},{1,9},{9,17},{17,25},{25,1},{2,10},{10... | collective-permute-start | bytes 294920 | tf_op jit(solution)/shard_map/ppermute | solution.py:122
  11.0 7.0 %collective-permute-done.1 = bf16[2,16,1536]{2,1,0:T(8,128)(2,1)S(1)} collective-permute-done((bf16[2,16,1536]{2,1,0:T(8,128)(2,1)S(1)}, bf16[2,16,1536]{2,1,0:T(8,128)(2,1)S(1)}, u32[]{:S(2)}, u32[]{:S(2)}) %collective-permute-start.1) | collective-permute-done | bytes 98336 | tf_op jit(solution)/shard_map/ppermute | solution.py:122
  18.7 3.7 %collective-permute-start.8 = (bf16[2,16,1536]{2,1,0:T(8,128)(2,1)S(1)}, bf16[2,16,1536]{2,1,0:T(8,128)(2,1)S(1)}, u32[]{:S(2)}, u32[]{:S(2)}) collective-permute-start(bf16[2,16,1536]{2,1,0:T(8,128)(2,1)S(1)} %pad_maximum_fusion.8), channel_id=1, source_target_pairs={{0,24},{8,0},{16,8},{24,16},{1,25},{9,1},{17,9},{25,17},{2,26},{10... | collective-permute-start | bytes 294920 | tf_op jit(solution)/shard_map/ppermute | solution.py:122
  22.4 1.5 collective-permute-start.3
  23.9 2.7 %collective-permute-start.4 = (bf16[2,64,1536]{2,1,0:T(8,128)(2,1)S(1)}, bf16[2,64,1536]{2,1,0:T(8,128)(2,1)S(1)}, u32[]{:S(2)}, u32[]{:S(2)}) collective-permute-start(bf16[2,64,1536]{2,1,0:T(8,128)(2,1)S(1)} %pad_maximum_fusion.5), channel_id=1, source_target_pairs={{0,4},{1,5},{2,6},{3,7},{4,0},{5,1},{6,2},{7,3},{8,12},{9,13},{10,... | collective-permute-start | bytes 1179656 | tf_op jit(solution)/shard_map/ppermute | solution.py:125
  26.6 1.4 collective-permute-start.5
  28.0 1.7 collective-permute-start.7
  29.8 2.4 %collective-permute-start.6 = (bf16[2,16,1536]{2,1,0:T(8,128)(2,1)S(1)}, bf16[2,16,1536]{2,1,0:T(8,128)(2,1)S(1)}, u32[]{:S(2)}, u32[]{:S(2)}) collective-permute-start(bf16[2,16,1536]{2,1,0:T(8,128)(2,1)S(1)} %pad_maximum_fusion.8), channel_id=1, source_target_pairs={{0,8},{8,16},{16,24},{24,0},{1,9},{9,17},{17,25},{25,1},{2,10},{10... | collective-permute-start | bytes 294920 | tf_op jit(solution)/shard_map/ppermute | solution.py:122
  32.2 5.3 %collective-permute-done.7 = bf16[2,16,1536]{2,1,0:T(8,128)(2,1)S(1)} collective-permute-done((bf16[2,16,1536]{2,1,0:T(8,128)(2,1)S(1)}, bf16[2,16,1536]{2,1,0:T(8,128)(2,1)S(1)}, u32[]{:S(2)}, u32[]{:S(2)}) %collective-permute-start.7) | collective-permute-done | bytes 98336 | tf_op jit(solution)/shard_map/ppermute | solution.py:122
  37.4 1.0 collective-permute-done.6
  38.5 4.8 %collective-permute-done.4 = bf16[2,64,1536]{2,1,0:T(8,128)(2,1)S(1)} collective-permute-done((bf16[2,64,1536]{2,1,0:T(8,128)(2,1)S(1)}, bf16[2,64,1536]{2,1,0:T(8,128)(2,1)S(1)}, u32[]{:S(2)}, u32[]{:S(2)}) %collective-permute-start.4) | collective-permute-done | bytes 393248 | tf_op jit(solution)/shard_map/ppermute | solution.py:125
  44.1 1.3 collective-permute-start.11
  45.5 2.4 %collective-permute-start.12 = (bf16[2,64,1536]{2,1,0:T(8,128)(2,1)S(1)}, bf16[2,64,1536]{2,1,0:T(8,128)(2,1)S(1)}, u32[]{:S(2)}, u32[]{:S(2)}) collective-permute-start(bf16[2,64,1536]{2,1,0:T(8,128)(2,1)S(1)} %pad_maximum_fusion.6), channel_id=1, source_target_pairs={{0,4},{1,5},{2,6},{3,7},{4,0},{5,1},{6,2},{7,3},{8,12},{9,13},{10,... | collective-permute-start | bytes 1179656 | tf_op jit(solution)/shard_map/ppermute | solution.py:125
  47.9 1.6 collective-permute-start.13
  49.4 0.8 constant_dynamic-update-slice_fusion.7
  50.2 1.4 multiply_convert_fusion.4
  51.7 1.4 multiply_convert_fusion.5
  53.1 1.6 pad_maximum_fusion.2
  54.7 5.9 %all-to-all-start = ((f16[8,2,64,768]{3,2,1,0:T(8,128)(2,1)}), f16[8,2,64,768]{3,2,1,0:T(8,128)(2,1)}, u32[]{:S(2)}, u32[]{:S(2)}) async-start(f16[8,2,64,768]{3,2,1,0:T(8,128)(2,1)} %pad_maximum_fusion.2), calls=%async_computation | async-start | bytes 3145728 | tf_op jit(solution)/shard_map/all_to_all | solution.py:147
  60.6 1.8 constant_dynamic-update-slice_fusion.6
  62.4 3.0 %collective-permute-done.12 = bf16[2,64,1536]{2,1,0:T(8,128)(2,1)S(1)} collective-permute-done((bf16[2,64,1536]{2,1,0:T(8,128)(2,1)S(1)}, bf16[2,64,1536]{2,1,0:T(8,128)(2,1)S(1)}, u32[]{:S(2)}, u32[]{:S(2)}) %collective-permute-start.12) | collective-permute-done | bytes 393248 | tf_op jit(solution)/shard_map/ppermute | solution.py:125
  65.4 0.8 constant_dynamic-update-slice_fusion.5
  66.2 0.8 constant_dynamic-update-slice_fusion.4
  66.9 1.6 slice_bitcast_fusion.1
  69.2 1.8 collective-permute-done.15
  71.0 1.4 multiply_convert_fusion.2
  72.4 1.4 multiply_convert_fusion.3
  73.8 1.6 pad_maximum_fusion.4
  75.4 4.6 %all-to-all-done = f16[8,2,64,768]{3,2,1,0:T(8,128)(2,1)} async-done(((f16[8,2,64,768]{3,2,1,0:T(8,128)(2,1)}), f16[8,2,64,768]{3,2,1,0:T(8,128)(2,1)}, u32[]{:S(2)}, u32[]{:S(2)}) %all-to-all-start) | async-done | bytes 1572896 | tf_op jit(solution)/shard_map/all_to_all | solution.py:147
  80.0 4.8 %all-to-all-start.1 = ((f16[8,2,64,768]{3,2,1,0:T(8,128)(2,1)}), f16[8,2,64,768]{3,2,1,0:T(8,128)(2,1)}, u32[]{:S(2)}, u32[]{:S(2)}) async-start(f16[8,2,64,768]{3,2,1,0:T(8,128)(2,1)} %pad_maximum_fusion.4), calls=%async_computation.1 | async-start | bytes 3145728 | tf_op jit(solution)/shard_map/all_to_all | solution.py:147
  84.8 1.7 convert_reduce_fusion.1.sums
  86.5 1.7 shard_map.76
  88.2 16.6 %all-to-all-done.1 = f16[8,2,64,768]{3,2,1,0:T(8,128)(2,1)} async-done(((f16[8,2,64,768]{3,2,1,0:T(8,128)(2,1)}), f16[8,2,64,768]{3,2,1,0:T(8,128)(2,1)}, u32[]{:S(2)}, u32[]{:S(2)}) %all-to-all-start.1) | async-done | bytes 1572896 | tf_op jit(solution)/shard_map/all_to_all | solution.py:147
  104.9 4.2 %all-to-all-start.2 = ((bf16[8,64,768]{2,1,0:T(8,128)(2,1)}), bf16[8,64,768]{2,1,0:T(8,128)(2,1)S(1)}, u32[]{:S(2)}, u32[]{:S(2)}) async-start(bf16[8,64,768]{2,1,0:T(8,128)(2,1)} %get-tuple-element.69), calls=%async_computation.2 | async-start | bytes 1572864 | tf_op jit(solution)/shard_map/all_to_all | solution.py:147
  109.0 1.6 pad_maximum_fusion.1
  111.0 2.0 %pad_maximum_fusion = bf16[8,2,64,1536]{3,2,1,0:T(8,128)(2,1)} fusion(bf16[8,1,64,1536]{3,2,1,0:T(8,128)(2,1)S(1)} %bitcast.53, bf16[8,1,64,1536]{3,2,1,0:T(8,128)(2,1)S(1)} %bitcast.52), kind=kLoop, calls=%fused_computation.2 | loop fusion | flops 1572864 | bytes 6291456 | tf_op jit(solution)/shard_map/stack | solution.py:191
  112.9 1.7 convert_reduce_fusion.sums
  114.6 1.6 shard_map.77
  116.2 1.1 copy-done.1
  117.4 3.2 %all-to-all-done.2 = bf16[8,64,768]{2,1,0:T(8,128)(2,1)S(1)} async-done(((bf16[8,64,768]{2,1,0:T(8,128)(2,1)}), bf16[8,64,768]{2,1,0:T(8,128)(2,1)S(1)}, u32[]{:S(2)}, u32[]{:S(2)}) %all-to-all-start.2) | async-done | bytes 786464 | tf_op jit(solution)/shard_map/all_to_all | solution.py:147
  120.6 4.7 %all-to-all-start.3 = ((bf16[8,64,768]{2,1,0:T(8,128)(2,1)}), bf16[8,64,768]{2,1,0:T(8,128)(2,1)}, u32[]{:S(2)}, u32[]{:S(2)}) async-start(bf16[8,64,768]{2,1,0:T(8,128)(2,1)} %get-tuple-element.82), calls=%async_computation.3 | async-start | bytes 1572864 | tf_op jit(solution)/shard_map/all_to_all | solution.py:147
  125.4 0.8 convolution_convert_fusion.1
  126.3 0.8 fusion.27
  127.1 1.5 collective-permute-done.16
  128.6 1.0 add_convert_fusion.3
  129.8 2.2 %collective-permute-start.18 = (bf16[64,1536]{1,0:T(8,128)(2,1)}, bf16[64,1536]{1,0:T(8,128)(2,1)S(1)}, u32[]{:S(2)}, u32[]{:S(2)}) collective-permute-start(bf16[64,1536]{1,0:T(8,128)(2,1)} %get-tuple-element.79), channel_id=1, source_target_pairs={{0,4},{1,5},{2,6},{3,7},{4,0},{5,1},{6,2},{7,3},{8,12},{9,13},{10,... | collective-permute-start | bytes 589832 | tf_op jit(solution)/shard_map/ppermute | solution.py:125
  132.1 4.5 %all-to-all-done.3 = bf16[8,64,768]{2,1,0:T(8,128)(2,1)} async-done(((bf16[8,64,768]{2,1,0:T(8,128)(2,1)}), bf16[8,64,768]{2,1,0:T(8,128)(2,1)}, u32[]{:S(2)}, u32[]{:S(2)}) %all-to-all-start.3) | async-done | bytes 786464 | tf_op jit(solution)/shard_map/all_to_all | solution.py:147
  136.5 1.9 %fusion.25 = (bf16[4,64,768]{2,1,0:T(8,128)(2,1)}, bf16[4,64,768]{2,1,0:T(8,128)(2,1)S(1)}) fusion(bf16[8,64,768]{2,1,0:T(8,128)(2,1)} %all-to-all-done.3), kind=kLoop, calls=%fused_computation.64 | loop fusion | bytes 1572864 | tf_op jit(solution)/shard_map/slice | solution.py:176
  138.5 1.7 convolution_convert_fusion
  140.2 2.2 %collective-permute-done.19.refs_3_ = bf16[64,1536]{1,0:T(8,128)(2,1)S(1)} collective-permute-done((bf16[64,1536]{1,0:T(8,128)(2,1)S(1)}, bf16[64,1536]{1,0:T(8,128)(2,1)S(1)}, u32[]{:S(2)}, u32[]{:S(2)}) %collective-permute-start.19) | collective-permute-done | bytes 196640 | tf_op jit(solution)/shard_map/ppermute | solution.py:125
  142.4 5.7 %all-to-all-start.4 = ((bf16[8,2,64,768]{3,2,1,0:T(8,128)(2,1)}), bf16[8,2,64,768]{3,2,1,0:T(8,128)(2,1)}, u32[]{:S(2)}, u32[]{:S(2)}) async-start(bf16[8,2,64,768]{3,2,1,0:T(8,128)(2,1)} %copy-done.1), calls=%async_computation.4 | async-start | bytes 3145728 | tf_op jit(solution)/shard_map/all_to_all | solution.py:147
  148.2 1.9 %fusion.28 = f32[256,1536]{1,0:T(8,128)S(1)} fusion(bf16[256,768]{1,0:T(8,128)(2,1)} %bitcast.56, bf16[1536,768]{1,0:T(8,128)(2,1)S(1)} %copy-done), kind=kOutput, calls=%fused_computation.67 | convolution fusion | flops 603979776 | bytes 4325376 | tf_op jit(solution)/shard_map/dot_general | solution.py:30
  150.8 1.5 collective-permute-start.24
  152.3 1.7 collective-permute-start.25
  154.1 5.1 %multiply_convert_fusion.1 = bf16[1536,768]{1,0:T(8,128)(2,1)} fusion(bf16[256,1536]{1,0:T(8,128)(2,1)S(1)} %copy-done.20, bf16[256,1536]{1,0:T(8,128)(2,1)S(1)} %copy-done.10, bf16[256,1536]{1,0:T(8,128)(2,1)S(1)} %copy-done.18, bf16[256,1536]{1,0:T(8,128)(2,1)S(1)} %copy-done.8, bf16[512,768]{1,0:T(8,128)(2,1)} %bitcast.24, bf16[512,768]{1,0:T(8,128)(2,1)S(1)} %bitcast.55), kind=kOutput, calls=%fused_computation.1 | convolution fusion | flops 2434007040 | bytes 7077888 | tf_op jit(solution)/shard_map/dot_general | solution.py:34
  159.5 2.1 %collective-permute-start.21 = (bf16[16,1536]{1,0:T(8,128)(2,1)S(1)}, bf16[16,1536]{1,0:T(8,128)(2,1)S(1)}, u32[]{:S(2)}, u32[]{:S(2)}) collective-permute-start(bf16[16,1536]{1,0:T(8,128)(2,1)S(1)} %get-tuple-element.98), channel_id=1, source_target_pairs={{0,24},{8,0},{16,8},{24,16},{1,25},{9,1},{17,9},{25,17},{2,26},{10... | collective-permute-start | bytes 147464 | tf_op jit(solution)/shard_map/ppermute | solution.py:122
  161.8 2.6 %collective-permute-start.23 = (bf16[16,1536]{1,0:T(8,128)(2,1)S(1)}, bf16[16,1536]{1,0:T(8,128)(2,1)S(1)}, u32[]{:S(2)}, u32[]{:S(2)}) collective-permute-start(bf16[16,1536]{1,0:T(8,128)(2,1)S(1)} %get-tuple-element.100), channel_id=1, source_target_pairs={{0,8},{8,16},{16,24},{24,0},{1,9},{9,17},{17,25},{25,1},{2,10},{10... | collective-permute-start | bytes 147464 | tf_op jit(solution)/shard_map/ppermute | solution.py:122
  165.0 2.1 %collective-permute-start.27 = (bf16[16,1536]{1,0:T(8,128)(2,1)S(1)}, bf16[16,1536]{1,0:T(8,128)(2,1)S(1)}, u32[]{:S(2)}, u32[]{:S(2)}) collective-permute-start(bf16[16,1536]{1,0:T(8,128)(2,1)S(1)} %get-tuple-element.106), channel_id=1, source_target_pairs={{0,24},{8,0},{16,8},{24,16},{1,25},{9,1},{17,9},{25,17},{2,26},{10... | collective-permute-start | bytes 147464 | tf_op jit(solution)/shard_map/ppermute | solution.py:122
  167.1 5.0 %collective-permute-start.28 = (bf16[16,1536]{1,0:T(8,128)(2,1)S(1)}, bf16[16,1536]{1,0:T(8,128)(2,1)S(1)}, u32[]{:S(2)}, u32[]{:S(2)}) collective-permute-start(bf16[16,1536]{1,0:T(8,128)(2,1)S(1)} %get-tuple-element.107), channel_id=1, source_target_pairs={{0,16},{8,24},{16,0},{24,8},{1,17},{9,25},{17,1},{25,9},{2,18},{10... | collective-permute-start | bytes 147464 | tf_op jit(solution)/shard_map/ppermute | solution.py:122
  172.0 6.4 %multiply_convert_fusion = bf16[768,1536]{1,0:T(8,128)(2,1)} fusion(bf16[1024,768]{1,0:T(8,128)(2,1)} %bitcast.25, bf16[1024,1536]{1,0:T(8,128)(2,1)} %bitcast.54), kind=kOutput, calls=%fused_computation | convolution fusion | flops 2418278400 | bytes 7077888 | tf_op jit(solution)/shard_map/dot_general | solution.py:34
  178.5 1.4 shard_map.80
  (90 shorter events, 4.9 us)
Async XLA Ops:
  0.6 51.1 %copy-start = (bf16[1536,768]{1,0:T(8,128)(2,1)S(1)}, bf16[1536,768]{1,0:T(8,128)(2,1)}, u32[]{:S(2)}) copy-start(bf16[1536,768]{1,0:T(8,128)(2,1)} %param.6) | copy-start | bytes 7077892
  1.7 9.3 %collective-permute-start.2 = (bf16[2,16,1536]{2,1,0:T(8,128)(2,1)S(1)}, bf16[2,16,1536]{2,1,0:T(8,128)(2,1)S(1)}, u32[]{:S(2)}, u32[]{:S(2)}) collective-permute-start(bf16[2,16,1536]{2,1,0:T(8,128)(2,1)S(1)} %pad_maximum_fusion.7), channel_id=1, source_target_pairs={{0,24},{8,0},{16,8},{24,16},{1,25},{9,1},{17,9},{25,17},{2,26},{10... | collective-permute-start | bytes 294920 | tf_op jit(solution)/shard_map/ppermute | solution.py:122
  7.2 10.9 %collective-permute-start.1 = (bf16[2,16,1536]{2,1,0:T(8,128)(2,1)S(1)}, bf16[2,16,1536]{2,1,0:T(8,128)(2,1)S(1)}, u32[]{:S(2)}, u32[]{:S(2)}) collective-permute-start(bf16[2,16,1536]{2,1,0:T(8,128)(2,1)S(1)} %pad_maximum_fusion.7), channel_id=1, source_target_pairs={{0,16},{8,24},{16,0},{24,8},{1,17},{9,25},{17,1},{25,9},{2,18},{10... | collective-permute-start | bytes 294920 | tf_op jit(solution)/shard_map/ppermute | solution.py:122
  8.6 10.0 %collective-permute-start = (bf16[2,16,1536]{2,1,0:T(8,128)(2,1)S(1)}, bf16[2,16,1536]{2,1,0:T(8,128)(2,1)S(1)}, u32[]{:S(2)}, u32[]{:S(2)}) collective-permute-start(bf16[2,16,1536]{2,1,0:T(8,128)(2,1)S(1)} %pad_maximum_fusion.7), channel_id=1, source_target_pairs={{0,8},{8,16},{16,24},{24,0},{1,9},{9,17},{17,25},{25,1},{2,10},{10... | collective-permute-start | bytes 294920 | tf_op jit(solution)/shard_map/ppermute | solution.py:122
  18.7 11.1 %collective-permute-start.8 = (bf16[2,16,1536]{2,1,0:T(8,128)(2,1)S(1)}, bf16[2,16,1536]{2,1,0:T(8,128)(2,1)S(1)}, u32[]{:S(2)}, u32[]{:S(2)}) collective-permute-start(bf16[2,16,1536]{2,1,0:T(8,128)(2,1)S(1)} %pad_maximum_fusion.8), channel_id=1, source_target_pairs={{0,24},{8,0},{16,8},{24,16},{1,25},{9,1},{17,9},{25,17},{2,26},{10... | collective-permute-start | bytes 294920 | tf_op jit(solution)/shard_map/ppermute | solution.py:122
  22.4 16.1 %collective-permute-start.3 = (bf16[2,64,1536]{2,1,0:T(8,128)(2,1)S(1)}, bf16[2,64,1536]{2,1,0:T(8,128)(2,1)S(1)}, u32[]{:S(2)}, u32[]{:S(2)}) collective-permute-start(bf16[2,64,1536]{2,1,0:T(8,128)(2,1)S(1)} %pad_maximum_fusion.5), channel_id=1, source_target_pairs={{0,2},{1,3},{2,4},{3,5},{4,6},{5,7},{6,0},{7,1},{8,10},{9,11},{10,... | collective-permute-start | bytes 1179656 | tf_op jit(solution)/shard_map/ppermute | solution.py:125
  23.9 19.4 %collective-permute-start.4 = (bf16[2,64,1536]{2,1,0:T(8,128)(2,1)S(1)}, bf16[2,64,1536]{2,1,0:T(8,128)(2,1)S(1)}, u32[]{:S(2)}, u32[]{:S(2)}) collective-permute-start(bf16[2,64,1536]{2,1,0:T(8,128)(2,1)S(1)} %pad_maximum_fusion.5), channel_id=1, source_target_pairs={{0,4},{1,5},{2,6},{3,7},{4,0},{5,1},{6,2},{7,3},{8,12},{9,13},{10,... | collective-permute-start | bytes 1179656 | tf_op jit(solution)/shard_map/ppermute | solution.py:125
  26.6 16.7 %collective-permute-start.5 = (bf16[2,64,1536]{2,1,0:T(8,128)(2,1)S(1)}, bf16[2,64,1536]{2,1,0:T(8,128)(2,1)S(1)}, u32[]{:S(2)}, u32[]{:S(2)}) collective-permute-start(bf16[2,64,1536]{2,1,0:T(8,128)(2,1)S(1)} %pad_maximum_fusion.5), channel_id=1, source_target_pairs={{0,6},{1,7},{2,0},{3,1},{4,2},{5,3},{6,4},{7,5},{8,14},{9,15},{10,... | collective-permute-start | bytes 1179656 | tf_op jit(solution)/shard_map/ppermute | solution.py:125
  28.0 9.4 %collective-permute-start.7 = (bf16[2,16,1536]{2,1,0:T(8,128)(2,1)S(1)}, bf16[2,16,1536]{2,1,0:T(8,128)(2,1)S(1)}, u32[]{:S(2)}, u32[]{:S(2)}) collective-permute-start(bf16[2,16,1536]{2,1,0:T(8,128)(2,1)S(1)} %pad_maximum_fusion.8), channel_id=1, source_target_pairs={{0,16},{8,24},{16,0},{24,8},{1,17},{9,25},{17,1},{25,9},{2,18},{10... | collective-permute-start | bytes 294920 | tf_op jit(solution)/shard_map/ppermute | solution.py:122
  29.8 8.7 %collective-permute-start.6 = (bf16[2,16,1536]{2,1,0:T(8,128)(2,1)S(1)}, bf16[2,16,1536]{2,1,0:T(8,128)(2,1)S(1)}, u32[]{:S(2)}, u32[]{:S(2)}) collective-permute-start(bf16[2,16,1536]{2,1,0:T(8,128)(2,1)S(1)} %pad_maximum_fusion.8), channel_id=1, source_target_pairs={{0,8},{8,16},{16,24},{24,0},{1,9},{9,17},{17,25},{25,1},{2,10},{10... | collective-permute-start | bytes 294920 | tf_op jit(solution)/shard_map/ppermute | solution.py:122
  43.4 6.8 %copy-start.15 = (bf16[768,1536]{1,0:T(8,128)(2,1)S(1)}, bf16[768,1536]{1,0:T(8,128)(2,1)}, u32[]{:S(2)}) copy-start(bf16[768,1536]{1,0:T(8,128)(2,1)} %param.8) | copy-start | bytes 7077892
  43.5 8.1 %copy-start.4 = (bf16[256,1536]{1,0:T(8,128)(2,1)}, bf16[256,1536]{1,0:T(8,128)(2,1)S(1)}, u32[]{:S(2)}) copy-start(bf16[256,1536]{1,0:T(8,128)(2,1)S(1)} %get-tuple-element.132) | copy-start | bytes 2359300
  43.5 8.1 %copy-start.7 = (bf16[256,1536]{1,0:T(8,128)(2,1)}, bf16[256,1536]{1,0:T(8,128)(2,1)S(1)}, u32[]{:S(2)}) copy-start(bf16[256,1536]{1,0:T(8,128)(2,1)S(1)} %get-tuple-element.131) | copy-start | bytes 2359300
  43.5 6.7 %collective-permute-start.10 = (bf16[256,1536]{1,0:T(8,128)(2,1)S(1)}, bf16[256,1536]{1,0:T(8,128)(2,1)S(1)}, u32[]{:S(2)}, u32[]{:S(2)}) collective-permute-start(bf16[256,1536]{1,0:T(8,128)(2,1)S(1)} %get-tuple-element.132), channel_id=1, source_target_pairs={{0,1},{1,0},{2,3},{3,2},{4,5},{5,4},{6,7},{7,6},{8,9},{9,8},{10,11... | collective-permute-start | bytes 2359304 | tf_op jit(solution)/shard_map/ppermute | solution.py:128
  43.6 8.0 %collective-permute-start.9 = (bf16[256,1536]{1,0:T(8,128)(2,1)S(1)}, bf16[256,1536]{1,0:T(8,128)(2,1)S(1)}, u32[]{:S(2)}, u32[]{:S(2)}) collective-permute-start(bf16[256,1536]{1,0:T(8,128)(2,1)S(1)} %get-tuple-element.131), channel_id=1, source_target_pairs={{0,1},{1,0},{2,3},{3,2},{4,5},{5,4},{6,7},{7,6},{8,9},{9,8},{10,11... | collective-permute-start | bytes 2359304 | tf_op jit(solution)/shard_map/ppermute | solution.py:128
  44.1 16.5 %collective-permute-start.11 = (bf16[2,64,1536]{2,1,0:T(8,128)(2,1)S(1)}, bf16[2,64,1536]{2,1,0:T(8,128)(2,1)}, u32[]{:S(2)}, u32[]{:S(2)}) collective-permute-start(bf16[2,64,1536]{2,1,0:T(8,128)(2,1)S(1)} %pad_maximum_fusion.6), channel_id=1, source_target_pairs={{0,2},{1,3},{2,4},{3,5},{4,6},{5,7},{6,0},{7,1},{8,10},{9,11},{10,... | collective-permute-start | bytes 1179656 | tf_op jit(solution)/shard_map/ppermute | solution.py:125
  45.5 19.9 %collective-permute-start.12 = (bf16[2,64,1536]{2,1,0:T(8,128)(2,1)S(1)}, bf16[2,64,1536]{2,1,0:T(8,128)(2,1)S(1)}, u32[]{:S(2)}, u32[]{:S(2)}) collective-permute-start(bf16[2,64,1536]{2,1,0:T(8,128)(2,1)S(1)} %pad_maximum_fusion.6), channel_id=1, source_target_pairs={{0,4},{1,5},{2,6},{3,7},{4,0},{5,1},{6,2},{7,3},{8,12},{9,13},{10,... | collective-permute-start | bytes 1179656 | tf_op jit(solution)/shard_map/ppermute | solution.py:125
  47.9 18.3 %collective-permute-start.13 = (bf16[2,64,1536]{2,1,0:T(8,128)(2,1)S(1)}, bf16[2,64,1536]{2,1,0:T(8,128)(2,1)S(1)}, u32[]{:S(2)}, u32[]{:S(2)}) collective-permute-start(bf16[2,64,1536]{2,1,0:T(8,128)(2,1)S(1)} %pad_maximum_fusion.6), channel_id=1, source_target_pairs={{0,6},{1,7},{2,0},{3,1},{4,2},{5,3},{6,4},{7,5},{8,14},{9,15},{10,... | collective-permute-start | bytes 1179656 | tf_op jit(solution)/shard_map/ppermute | solution.py:125
  50.2 1.4 copy-start.11
  51.7 1.4 copy-start.17
  54.7 25.3 %all-to-all-start = ((f16[8,2,64,768]{3,2,1,0:T(8,128)(2,1)}), f16[8,2,64,768]{3,2,1,0:T(8,128)(2,1)}, u32[]{:S(2)}, u32[]{:S(2)}) async-start(f16[8,2,64,768]{3,2,1,0:T(8,128)(2,1)} %pad_maximum_fusion.2), calls=%async_computation | async-start | bytes 3145728 | tf_op jit(solution)/shard_map/all_to_all | solution.py:147
  66.9 4.0 %copy-start.16 = (bf16[768,1536]{1,0:T(8,128)(2,1)S(1)}, bf16[768,1536]{1,0:T(8,128)(2,1)}, u32[]{:S(2)}) copy-start(bf16[768,1536]{1,0:T(8,128)(2,1)} %param.8) | copy-start | bytes 7077892
  68.6 3.8 %copy-start.5 = (bf16[256,1536]{1,0:T(8,128)(2,1)}, bf16[256,1536]{1,0:T(8,128)(2,1)S(1)}, u32[]{:S(2)}) copy-start(bf16[256,1536]{1,0:T(8,128)(2,1)S(1)} %get-tuple-element.130) | copy-start | bytes 2359300
  68.6 3.8 %copy-start.9 = (bf16[256,1536]{1,0:T(8,128)(2,1)}, bf16[256,1536]{1,0:T(8,128)(2,1)S(1)}, u32[]{:S(2)}) copy-start(bf16[256,1536]{1,0:T(8,128)(2,1)S(1)} %get-tuple-element.129) | copy-start | bytes 2359300
  68.6 2.4 %collective-permute-start.15 = (bf16[256,1536]{1,0:T(8,128)(2,1)S(1)}, bf16[256,1536]{1,0:T(8,128)(2,1)S(1)}, u32[]{:S(2)}, u32[]{:S(2)}) collective-permute-start(bf16[256,1536]{1,0:T(8,128)(2,1)S(1)} %get-tuple-element.130), channel_id=1, source_target_pairs={{0,1},{1,0},{2,3},{3,2},{4,5},{5,4},{6,7},{7,6},{8,9},{9,8},{10,11... | collective-permute-start | bytes 2359304 | tf_op jit(solution)/shard_map/ppermute | solution.py:128
  68.7 3.7 %collective-permute-start.14 = (bf16[256,1536]{1,0:T(8,128)(2,1)S(1)}, bf16[256,1536]{1,0:T(8,128)(2,1)S(1)}, u32[]{:S(2)}, u32[]{:S(2)}) collective-permute-start(bf16[256,1536]{1,0:T(8,128)(2,1)S(1)} %get-tuple-element.129), channel_id=1, source_target_pairs={{0,1},{1,0},{2,3},{3,2},{4,5},{5,4},{6,7},{7,6},{8,9},{9,8},{10,11... | collective-permute-start | bytes 2359304 | tf_op jit(solution)/shard_map/ppermute | solution.py:128
  71.0 1.4 copy-start.12
  72.4 1.4 copy-start.19
  75.4 9.4 %copy-start.14 = (f32[768]{0:T(1024)S(1)}, f32[768]{0:T(1024)}, u32[]{:S(2)}) copy-start(f32[768]{0:T(1024)} %param.7) | copy-start | bytes 9220
  80.0 24.9 %all-to-all-start.1 = ((f16[8,2,64,768]{3,2,1,0:T(8,128)(2,1)}), f16[8,2,64,768]{3,2,1,0:T(8,128)(2,1)}, u32[]{:S(2)}, u32[]{:S(2)}) async-start(f16[8,2,64,768]{3,2,1,0:T(8,128)(2,1)} %pad_maximum_fusion.4), calls=%async_computation.1 | async-start | bytes 3145728 | tf_op jit(solution)/shard_map/all_to_all | solution.py:147
  104.9 15.8 %all-to-all-start.2 = ((bf16[8,64,768]{2,1,0:T(8,128)(2,1)}), bf16[8,64,768]{2,1,0:T(8,128)(2,1)S(1)}, u32[]{:S(2)}, u32[]{:S(2)}) async-start(bf16[8,64,768]{2,1,0:T(8,128)(2,1)} %get-tuple-element.69), calls=%async_computation.2 | async-start | bytes 1572864 | tf_op jit(solution)/shard_map/all_to_all | solution.py:147
  109.0 1.6 copy-start.6
  109.0 1.8 %copy-start.13 = (bf16[256,1536]{1,0:T(8,128)(2,1)S(1)}, bf16[256,1536]{1,0:T(8,128)(2,1)}, u32[]{:S(2)}) copy-start(bf16[256,1536]{1,0:T(8,128)(2,1)} %copy-done.12) | copy-start | bytes 2359300
  116.2 1.1 copy-start.1
  120.6 4.7 %copy-start.2 = (bf16[8,64,768]{2,1,0:T(8,128)(2,1)}, bf16[8,64,768]{2,1,0:T(8,128)(2,1)S(1)}, u32[]{:S(2)}) copy-start(bf16[8,64,768]{2,1,0:T(8,128)(2,1)S(1)} %all-to-all-done.2) | copy-start | bytes 2359300
  120.6 15.9 %all-to-all-start.3 = ((bf16[8,64,768]{2,1,0:T(8,128)(2,1)}), bf16[8,64,768]{2,1,0:T(8,128)(2,1)}, u32[]{:S(2)}, u32[]{:S(2)}) async-start(bf16[8,64,768]{2,1,0:T(8,128)(2,1)} %get-tuple-element.82), calls=%async_computation.3 | async-start | bytes 1572864 | tf_op jit(solution)/shard_map/all_to_all | solution.py:147
  126.2 2.4 %collective-permute-start.16 = (bf16[256,1536]{1,0:T(8,128)(2,1)S(1)}, bf16[256,1536]{1,0:T(8,128)(2,1)S(1)}, u32[]{:S(2)}, u32[]{:S(2)}) collective-permute-start(bf16[256,1536]{1,0:T(8,128)(2,1)S(1)} %convolution_convert_fusion.1), channel_id=1, source_target_pairs={{0,1},{1,0},{2,3},{3,2},{4,5},{5,4},{6,7},{7,6},{8,9},{9,8},{10,11... | collective-permute-start | bytes 2359304 | tf_op jit(solution)/shard_map/ppermute | solution.py:128
  129.6 10.6 %collective-permute-start.17 = (bf16[64,1536]{1,0:T(8,128)(2,1)}, bf16[64,1536]{1,0:T(8,128)(2,1)S(1)}, u32[]{:S(2)}, u32[]{:S(2)}) collective-permute-start(bf16[64,1536]{1,0:T(8,128)(2,1)} %get-tuple-element.78), channel_id=1, source_target_pairs={{0,6},{1,7},{2,0},{3,1},{4,2},{5,3},{6,4},{7,5},{8,14},{9,15},{10,... | collective-permute-start | bytes 589832 | tf_op jit(solution)/shard_map/ppermute | solution.py:125
  129.8 10.4 %collective-permute-start.18 = (bf16[64,1536]{1,0:T(8,128)(2,1)}, bf16[64,1536]{1,0:T(8,128)(2,1)S(1)}, u32[]{:S(2)}, u32[]{:S(2)}) collective-permute-start(bf16[64,1536]{1,0:T(8,128)(2,1)} %get-tuple-element.79), channel_id=1, source_target_pairs={{0,4},{1,5},{2,6},{3,7},{4,0},{5,1},{6,2},{7,3},{8,12},{9,13},{10,... | collective-permute-start | bytes 589832 | tf_op jit(solution)/shard_map/ppermute | solution.py:125
  132.1 10.4 %collective-permute-start.19 = (bf16[64,1536]{1,0:T(8,128)(2,1)S(1)}, bf16[64,1536]{1,0:T(8,128)(2,1)S(1)}, u32[]{:S(2)}, u32[]{:S(2)}) collective-permute-start(bf16[64,1536]{1,0:T(8,128)(2,1)S(1)} %get-tuple-element.80), channel_id=1, source_target_pairs={{0,2},{1,3},{2,4},{3,5},{4,6},{5,7},{6,0},{7,1},{8,10},{9,11},{10,... | collective-permute-start | bytes 589832 | tf_op jit(solution)/shard_map/ppermute | solution.py:125
  142.4 29.6 %all-to-all-start.4 = ((bf16[8,2,64,768]{3,2,1,0:T(8,128)(2,1)}), bf16[8,2,64,768]{3,2,1,0:T(8,128)(2,1)}, u32[]{:S(2)}, u32[]{:S(2)}) async-start(bf16[8,2,64,768]{3,2,1,0:T(8,128)(2,1)} %copy-done.1), calls=%async_computation.4 | async-start | bytes 3145728 | tf_op jit(solution)/shard_map/all_to_all | solution.py:147
  148.1 2.5 %collective-permute-start.20 = (bf16[256,1536]{1,0:T(8,128)(2,1)}, bf16[256,1536]{1,0:T(8,128)(2,1)S(1)}, u32[]{:S(2)}, u32[]{:S(2)}) collective-permute-start(bf16[256,1536]{1,0:T(8,128)(2,1)} %convolution_convert_fusion), channel_id=1, source_target_pairs={{0,1},{1,0},{2,3},{3,2},{4,5},{5,4},{6,7},{7,6},{8,9},{9,8},{10,11... | collective-permute-start | bytes 2359304 | tf_op jit(solution)/shard_map/ppermute | solution.py:128
  148.2 5.9 %copy-start.20 = (bf16[256,1536]{1,0:T(8,128)(2,1)S(1)}, bf16[256,1536]{1,0:T(8,128)(2,1)}, u32[]{:S(2)}) copy-start(bf16[256,1536]{1,0:T(8,128)(2,1)} %copy-done.19) | copy-start | bytes 2359300
  150.0 4.1 %copy-start.3 = (bf16[8,64,768]{2,1,0:T(8,128)(2,1)S(1)}, bf16[8,64,768]{2,1,0:T(8,128)(2,1)}, u32[]{:S(2)}) copy-start(bf16[8,64,768]{2,1,0:T(8,128)(2,1)} %copy-done.2) | copy-start | bytes 2359300
  150.0 4.0 %copy-start.8 = (bf16[256,1536]{1,0:T(8,128)(2,1)S(1)}, bf16[256,1536]{1,0:T(8,128)(2,1)}, u32[]{:S(2)}) copy-start(bf16[256,1536]{1,0:T(8,128)(2,1)} %copy-done.7) | copy-start | bytes 2359300
  150.1 4.0 %copy-start.10 = (bf16[256,1536]{1,0:T(8,128)(2,1)S(1)}, bf16[256,1536]{1,0:T(8,128)(2,1)}, u32[]{:S(2)}) copy-start(bf16[256,1536]{1,0:T(8,128)(2,1)} %copy-done.9) | copy-start | bytes 2359300
  150.1 4.0 %copy-start.18 = (bf16[256,1536]{1,0:T(8,128)(2,1)S(1)}, bf16[256,1536]{1,0:T(8,128)(2,1)}, u32[]{:S(2)}) copy-start(bf16[256,1536]{1,0:T(8,128)(2,1)} %copy-done.17) | copy-start | bytes 2359300
  150.8 11.0 %collective-permute-start.24 = (bf16[64,1536]{1,0:T(8,128)(2,1)S(1)}, bf16[64,1536]{1,0:T(8,128)(2,1)S(1)}, u32[]{:S(2)}, u32[]{:S(2)}) collective-permute-start(bf16[64,1536]{1,0:T(8,128)(2,1)S(1)} %get-tuple-element.102), channel_id=1, source_target_pairs={{0,6},{1,7},{2,0},{3,1},{4,2},{5,3},{6,4},{7,5},{8,14},{9,15},{10,... | collective-permute-start | bytes 589832 | tf_op jit(solution)/shard_map/ppermute | solution.py:125
  152.3 12.1 %collective-permute-start.25 = (bf16[64,1536]{1,0:T(8,128)(2,1)S(1)}, bf16[64,1536]{1,0:T(8,128)(2,1)S(1)}, u32[]{:S(2)}, u32[]{:S(2)}) collective-permute-start(bf16[64,1536]{1,0:T(8,128)(2,1)S(1)} %get-tuple-element.103), channel_id=1, source_target_pairs={{0,4},{1,5},{2,6},{3,7},{4,0},{5,1},{6,2},{7,3},{8,12},{9,13},{10,... | collective-permute-start | bytes 589832 | tf_op jit(solution)/shard_map/ppermute | solution.py:125
  154.0 10.7 %collective-permute-start.26 = (bf16[64,1536]{1,0:T(8,128)(2,1)S(1)}, bf16[64,1536]{1,0:T(8,128)(2,1)S(1)}, u32[]{:S(2)}, u32[]{:S(2)}) collective-permute-start(bf16[64,1536]{1,0:T(8,128)(2,1)S(1)} %get-tuple-element.104), channel_id=1, source_target_pairs={{0,2},{1,3},{2,4},{3,5},{4,6},{5,7},{6,0},{7,1},{8,10},{9,11},{10,... | collective-permute-start | bytes 589832 | tf_op jit(solution)/shard_map/ppermute | solution.py:125
  159.5 12.5 %collective-permute-start.21 = (bf16[16,1536]{1,0:T(8,128)(2,1)S(1)}, bf16[16,1536]{1,0:T(8,128)(2,1)S(1)}, u32[]{:S(2)}, u32[]{:S(2)}) collective-permute-start(bf16[16,1536]{1,0:T(8,128)(2,1)S(1)} %get-tuple-element.98), channel_id=1, source_target_pairs={{0,24},{8,0},{16,8},{24,16},{1,25},{9,1},{17,9},{25,17},{2,26},{10... | collective-permute-start | bytes 147464 | tf_op jit(solution)/shard_map/ppermute | solution.py:122
  161.6 16.9 %collective-permute-start.22 = (bf16[16,1536]{1,0:T(8,128)(2,1)S(1)}, bf16[16,1536]{1,0:T(8,128)(2,1)S(1)}, u32[]{:S(2)}, u32[]{:S(2)}) collective-permute-start(bf16[16,1536]{1,0:T(8,128)(2,1)S(1)} %get-tuple-element.99), channel_id=1, source_target_pairs={{0,16},{8,24},{16,0},{24,8},{1,17},{9,25},{17,1},{25,9},{2,18},{10... | collective-permute-start | bytes 147464 | tf_op jit(solution)/shard_map/ppermute | solution.py:122
  161.8 16.6 %collective-permute-start.23 = (bf16[16,1536]{1,0:T(8,128)(2,1)S(1)}, bf16[16,1536]{1,0:T(8,128)(2,1)S(1)}, u32[]{:S(2)}, u32[]{:S(2)}) collective-permute-start(bf16[16,1536]{1,0:T(8,128)(2,1)S(1)} %get-tuple-element.100), channel_id=1, source_target_pairs={{0,8},{8,16},{16,24},{24,0},{1,9},{9,17},{17,25},{25,1},{2,10},{10... | collective-permute-start | bytes 147464 | tf_op jit(solution)/shard_map/ppermute | solution.py:122
  165.0 13.5 %collective-permute-start.27 = (bf16[16,1536]{1,0:T(8,128)(2,1)S(1)}, bf16[16,1536]{1,0:T(8,128)(2,1)S(1)}, u32[]{:S(2)}, u32[]{:S(2)}) collective-permute-start(bf16[16,1536]{1,0:T(8,128)(2,1)S(1)} %get-tuple-element.106), channel_id=1, source_target_pairs={{0,24},{8,0},{16,8},{24,16},{1,25},{9,1},{17,9},{25,17},{2,26},{10... | collective-permute-start | bytes 147464 | tf_op jit(solution)/shard_map/ppermute | solution.py:122
  167.1 11.4 %collective-permute-start.28 = (bf16[16,1536]{1,0:T(8,128)(2,1)S(1)}, bf16[16,1536]{1,0:T(8,128)(2,1)S(1)}, u32[]{:S(2)}, u32[]{:S(2)}) collective-permute-start(bf16[16,1536]{1,0:T(8,128)(2,1)S(1)} %get-tuple-element.107), channel_id=1, source_target_pairs={{0,16},{8,24},{16,0},{24,8},{1,17},{9,25},{17,1},{25,9},{2,18},{10... | collective-permute-start | bytes 147464 | tf_op jit(solution)/shard_map/ppermute | solution.py:122
  172.0 6.4 %collective-permute-start.29 = (bf16[16,1536]{1,0:T(8,128)(2,1)S(1)}, bf16[16,1536]{1,0:T(8,128)(2,1)S(1)}, u32[]{:S(2)}, u32[]{:S(2)}) collective-permute-start(bf16[16,1536]{1,0:T(8,128)(2,1)S(1)} %get-tuple-element.108), channel_id=1, source_target_pairs={{0,8},{8,16},{16,24},{24,0},{1,9},{9,17},{17,25},{25,1},{2,10},{10... | collective-permute-start | bytes 147464 | tf_op jit(solution)/shard_map/ppermute | solution.py:122

commit v12 on v11

--- a/solution.py
+++ b/solution.py
@@ -196,8 +196,9 @@
         own0, other0 = barrier(own0, swap_core(other0))
         parts0, act_copies = barrier(sum_blocks([own0, other0], n_chip), act_copies)
         parts0 = exchange(parts0, shift_chip)
-        other1, own1 = two_halves(hidden1)
-        parts0, other1, act_copies = barrier(parts0, other1, act_copies)
+        other1, _ = two_halves(hidden1)
+        parts0, other1, act_copies, hidden1 = barrier(parts0, other1, act_copies, hidden1)
+        _, own1 = two_halves(hidden1)
         activation = trade_width(act_copies)
         own1, other1 = barrier(own1, swap_core(other1))
         parts1, hidden0, hidden1 = barrier(sum_blocks([own1, other1], n_chip), hidden0, hidden1)
@@ -205,14 +206,14 @@
         hidden_all = jnp.concatenate([hidden0, hidden1], axis=0)
         tokens_all = jnp.concatenate([both0[0], both1[0]], axis=0)
         grad_weight_in = (contract_first(tokens_all, hidden_all) * norm_scale).astype(bf16)
-        parts0, grad_weight_in = barrier(parts0, grad_weight_in)
+        parts0, parts1[1] = barrier(parts0, parts1[1])
         parts0 = exchange(join_sums([parts0], n_y), shift_y)
         parts1 = exchange(join_sums([parts1], n_y), shift_y)
         activation = activation.reshape(-1, columns)
         grad_weight_out = (contract_first(activation, grad_all) * norm_scale).astype(bf16)
-        parts0, parts1, grad_weight_out = barrier(parts0, parts1, grad_weight_out)
+        parts0, parts1, *grads = barrier(parts0, parts1, grad_weight_in, grad_weight_out)
         (grad_tokens,) = join_sums([parts0, parts1], 1, bf16)
-        return (grad_tokens, grad_weight_in, grad_weight_out)
+        return (grad_tokens, *grads)
 
     return jax.shard_map(
         shards,

time: 181 us -> 187 us (1.033)
  waiting for transfers between devices: 57 us -> 65.6 us
    ppermute x12, waiting for transfers between devices: 10.3 us -> 24.4 us  [shift_chip(): return lax.ppermute(a, 'gz', [(i, (i + 2 * k) % n_z) for i in range(n_z)])]
    all_to_all x5, waiting for transfers between devices: 29 us -> 23.4 us  [trade_width(): return lax.all_to_all(parts, 'gx', 0, 0, tiled=True)]
    ppermute x12, starting transfers between devices: 16.7 us -> 13.8 us  [shift_chip(): return lax.ppermute(a, 'gz', [(i, (i + 2 * k) % n_z) for i in range(n_z)])]
    slice x1 -> x0, local copies, waits for them, and re-layouts: 1.94 us -> none  [two_halves(): return (other, contract_last(grad_hidden[:half], weight_in))]
  transfers between devices with their start and end apart: 35 -> 35, of which waited for: 15 -> 17; matrix products, arithmetic and copies ran while one was open for 23% -> 22% of each run, Pallas kernels for 2% -> 2%
where the time goes in v12:
time: 187 us; the launch traced here: 186 us
  starting transfers between devices  70.9 us (38%)
  waiting for transfers between devices  65.6 us (35%)
  matrix products  22.2 us (12%)
  other arithmetic  11.4 us (6%)
  local copies, waits for them, and re-layouts  9.84 us (5%)
  Pallas kernels  5.24 us (3%)
    ppermute x12, starting transfers between devices, shift_y(): return lax.ppermute(a, 'gy', [(i, (i + k) % n_y) for i in range(n_y)])  29.4 us
    all_to_all x5, starting transfers between devices, trade_width(): return lax.all_to_all(parts, 'gx', 0, 0, tiled=True)  26.4 us
    ppermute x12, waiting for transfers between devices, shift_chip(): return lax.ppermute(a, 'gz', [(i, (i + 2 * k) % n_z) for i in range(n_z)])  24.4 us
    all_to_all x5, waiting for transfers between devices, trade_width(): return lax.all_to_all(parts, 'gx', 0, 0, tiled=True)  23.4 us
    ppermute x12, waiting for transfers between devices, shift_y(): return lax.ppermute(a, 'gy', [(i, (i + k) % n_y) for i in range(n_y)])  13.9 us
    ppermute x12, starting transfers between devices, shift_chip(): return lax.ppermute(a, 'gz', [(i, (i + 2 * k) % n_z) for i in range(n_z)])  13.8 us
    dot_general x2, matrix products, contract_first(): lax.dot_general(left, right, (((0,), (0,)), ((), ())), preferred_element_...  11.5 us
    dot_general x6, matrix products, contract_last(): lax.dot_general(left, right, (((1,), (1,)), ((), ())), preferred_element_...  7.94 us
  transfers between devices with their start and end apart: 35, of which 17 were waited for; matrix products, arithmetic and copies ran while one was open for 22% of the time, Pallas kernels for 2%

profile of v12, /device:TPU:32, one launch (start us, length us, event | category | flops | bytes accessed | tf_op | source)
XLA Modules:
  0.0 186.2 jit_solution(6435195878672269972)
XLA Ops:
  0.6 1.0 slice_bitcast_fusion.4
  1.7 5.5 %collective-permute-start.2 = (bf16[2,16,1536]{2,1,0:T(8,128)(2,1)S(1)}, bf16[2,16,1536]{2,1,0:T(8,128)(2,1)S(1)}, u32[]{:S(2)}, u32[]{:S(2)}) collective-permute-start(bf16[2,16,1536]{2,1,0:T(8,128)(2,1)S(1)} %pad_maximum_fusion.7), channel_id=1, source_target_pairs={{0,24},{8,0},{16,8},{24,16},{1,25},{9,1},{17,9},{25,17},{2,26},{10... | collective-permute-start | bytes 294920 | tf_op jit(solution)/shard_map/ppermute | solution.py:122
  7.2 1.4 collective-permute-start.1
  8.6 2.4 %collective-permute-start = (bf16[2,16,1536]{2,1,0:T(8,128)(2,1)S(1)}, bf16[2,16,1536]{2,1,0:T(8,128)(2,1)S(1)}, u32[]{:S(2)}, u32[]{:S(2)}) collective-permute-start(bf16[2,16,1536]{2,1,0:T(8,128)(2,1)S(1)} %pad_maximum_fusion.7), channel_id=1, source_target_pairs={{0,8},{8,16},{16,24},{24,0},{1,9},{9,17},{17,25},{25,1},{2,10},{10... | collective-permute-start | bytes 294920 | tf_op jit(solution)/shard_map/ppermute | solution.py:122
  11.0 7.0 %collective-permute-done.1 = bf16[2,16,1536]{2,1,0:T(8,128)(2,1)S(1)} collective-permute-done((bf16[2,16,1536]{2,1,0:T(8,128)(2,1)S(1)}, bf16[2,16,1536]{2,1,0:T(8,128)(2,1)S(1)}, u32[]{:S(2)}, u32[]{:S(2)}) %collective-permute-start.1) | collective-permute-done | bytes 98336 | tf_op jit(solution)/shard_map/ppermute | solution.py:122
  18.7 3.7 %collective-permute-start.8 = (bf16[2,16,1536]{2,1,0:T(8,128)(2,1)S(1)}, bf16[2,16,1536]{2,1,0:T(8,128)(2,1)S(1)}, u32[]{:S(2)}, u32[]{:S(2)}) collective-permute-start(bf16[2,16,1536]{2,1,0:T(8,128)(2,1)S(1)} %pad_maximum_fusion.8), channel_id=1, source_target_pairs={{0,24},{8,0},{16,8},{24,16},{1,25},{9,1},{17,9},{25,17},{2,26},{10... | collective-permute-start | bytes 294920 | tf_op jit(solution)/shard_map/ppermute | solution.py:122
  22.4 2.8 %collective-permute-start.5 = (bf16[2,64,1536]{2,1,0:T(8,128)(2,1)S(1)}, bf16[2,64,1536]{2,1,0:T(8,128)(2,1)S(1)}, u32[]{:S(2)}, u32[]{:S(2)}) collective-permute-start(bf16[2,64,1536]{2,1,0:T(8,128)(2,1)S(1)} %pad_maximum_fusion.5), channel_id=1, source_target_pairs={{0,6},{1,7},{2,0},{3,1},{4,2},{5,3},{6,4},{7,5},{8,14},{9,15},{10,... | collective-permute-start | bytes 1179656 | tf_op jit(solution)/shard_map/ppermute | solution.py:125
  25.1 0.8 collective-permute-start.4
  25.9 0.9 collective-permute-start.3
  26.8 1.7 collective-permute-start.7
  28.5 2.4 %collective-permute-start.6 = (bf16[2,16,1536]{2,1,0:T(8,128)(2,1)S(1)}, bf16[2,16,1536]{2,1,0:T(8,128)(2,1)S(1)}, u32[]{:S(2)}, u32[]{:S(2)}) collective-permute-start(bf16[2,16,1536]{2,1,0:T(8,128)(2,1)S(1)} %pad_maximum_fusion.8), channel_id=1, source_target_pairs={{0,8},{8,16},{16,24},{24,0},{1,9},{9,17},{17,25},{25,1},{2,10},{10... | collective-permute-start | bytes 294920 | tf_op jit(solution)/shard_map/ppermute | solution.py:122
  30.9 5.3 %collective-permute-done.7 = bf16[2,16,1536]{2,1,0:T(8,128)(2,1)S(1)} collective-permute-done((bf16[2,16,1536]{2,1,0:T(8,128)(2,1)S(1)}, bf16[2,16,1536]{2,1,0:T(8,128)(2,1)S(1)}, u32[]{:S(2)}, u32[]{:S(2)}) %collective-permute-start.7) | collective-permute-done | bytes 98336 | tf_op jit(solution)/shard_map/ppermute | solution.py:122
  36.2 1.0 collective-permute-done.6
  37.3 4.1 %collective-permute-done.5 = bf16[2,64,1536]{2,1,0:T(8,128)(2,1)S(1)} collective-permute-done((bf16[2,64,1536]{2,1,0:T(8,128)(2,1)S(1)}, bf16[2,64,1536]{2,1,0:T(8,128)(2,1)S(1)}, u32[]{:S(2)}, u32[]{:S(2)}) %collective-permute-start.5) | collective-permute-done | bytes 393248 | tf_op jit(solution)/shard_map/ppermute | solution.py:125
  41.4 3.7 %collective-permute-done.3 = bf16[2,64,1536]{2,1,0:T(8,128)(2,1)S(1)} collective-permute-done((bf16[2,64,1536]{2,1,0:T(8,128)(2,1)S(1)}, bf16[2,64,1536]{2,1,0:T(8,128)(2,1)S(1)}, u32[]{:S(2)}, u32[]{:S(2)}) %collective-permute-start.3) | collective-permute-done | bytes 393248 | tf_op jit(solution)/shard_map/ppermute | solution.py:125
  47.3 0.8 collective-permute-start.11
  48.9 1.4 multiply_convert_fusion.5
  50.9 1.4 multiply_convert_fusion.4
  52.3 1.6 pad_maximum_fusion.2
  53.9 5.9 %all-to-all-start = ((f16[8,2,64,768]{3,2,1,0:T(8,128)(2,1)}), f16[8,2,64,768]{3,2,1,0:T(8,128)(2,1)}, u32[]{:S(2)}, u32[]{:S(2)}) async-start(f16[8,2,64,768]{3,2,1,0:T(8,128)(2,1)} %pad_maximum_fusion.2), calls=%async_computation | async-start | bytes 3145728 | tf_op jit(solution)/shard_map/all_to_all | solution.py:147
  59.8 7.6 %collective-permute-done.11 = bf16[2,64,1536]{2,1,0:T(8,128)(2,1)} collective-permute-done((bf16[2,64,1536]{2,1,0:T(8,128)(2,1)S(1)}, bf16[2,64,1536]{2,1,0:T(8,128)(2,1)}, u32[]{:S(2)}, u32[]{:S(2)}) %collective-permute-start.11) | collective-permute-done | bytes 393248 | tf_op jit(solution)/shard_map/ppermute | solution.py:125
  67.4 1.8 constant_dynamic-update-slice_fusion.6
  70.7 1.5 slice_bitcast_fusion.1
  72.8 1.8 collective-permute-done.14
  74.6 1.4 multiply_convert_fusion.3
  76.0 1.4 multiply_convert_fusion.2
  77.5 1.6 pad_maximum_fusion.4
  79.3 5.8 %all-to-all-start.1 = ((f16[8,2,64,768]{3,2,1,0:T(8,128)(2,1)}), f16[8,2,64,768]{3,2,1,0:T(8,128)(2,1)}, u32[]{:S(2)}, u32[]{:S(2)}) async-start(f16[8,2,64,768]{3,2,1,0:T(8,128)(2,1)} %pad_maximum_fusion.4), calls=%async_computation.1 | async-start | bytes 3145728 | tf_op jit(solution)/shard_map/all_to_all | solution.py:147
  85.1 1.7 convert_reduce_fusion.1.sums
  86.8 1.7 shard_map.76
  88.5 16.9 %all-to-all-done.1 = f16[8,2,64,768]{3,2,1,0:T(8,128)(2,1)} async-done(((f16[8,2,64,768]{3,2,1,0:T(8,128)(2,1)}), f16[8,2,64,768]{3,2,1,0:T(8,128)(2,1)}, u32[]{:S(2)}, u32[]{:S(2)}) %all-to-all-start.1) | async-done | bytes 1572896 | tf_op jit(solution)/shard_map/all_to_all | solution.py:147
  105.4 4.2 %all-to-all-start.2 = ((bf16[8,64,768]{2,1,0:T(8,128)(2,1)}), bf16[8,64,768]{2,1,0:T(8,128)(2,1)S(1)}, u32[]{:S(2)}, u32[]{:S(2)}) async-start(bf16[8,64,768]{2,1,0:T(8,128)(2,1)} %get-tuple-element.71), calls=%async_computation.2 | async-start | bytes 1572864 | tf_op jit(solution)/shard_map/all_to_all | solution.py:147
  109.6 1.6 pad_maximum_fusion.1
  111.5 2.0 %pad_maximum_fusion = bf16[8,2,64,1536]{3,2,1,0:T(8,128)(2,1)} fusion(bf16[8,1,64,1536]{3,2,1,0:T(8,128)(2,1)S(1)} %bitcast.51, bf16[8,1,64,1536]{3,2,1,0:T(8,128)(2,1)S(1)} %bitcast.50), kind=kLoop, calls=%fused_computation.2 | loop fusion | flops 1572864 | bytes 6291456 | tf_op jit(solution)/shard_map/stack | solution.py:191
  113.5 1.7 convert_reduce_fusion.sums
  115.2 1.6 shard_map.77
  116.8 1.1 copy-done.1
  117.9 3.2 %all-to-all-done.2 = bf16[8,64,768]{2,1,0:T(8,128)(2,1)S(1)} async-done(((bf16[8,64,768]{2,1,0:T(8,128)(2,1)}), bf16[8,64,768]{2,1,0:T(8,128)(2,1)S(1)}, u32[]{:S(2)}, u32[]{:S(2)}) %all-to-all-start.2) | async-done | bytes 786464 | tf_op jit(solution)/shard_map/all_to_all | solution.py:147
  121.2 4.7 %all-to-all-start.3 = ((bf16[8,64,768]{2,1,0:T(8,128)(2,1)}), bf16[8,64,768]{2,1,0:T(8,128)(2,1)}, u32[]{:S(2)}, u32[]{:S(2)}) async-start(bf16[8,64,768]{2,1,0:T(8,128)(2,1)} %get-tuple-element.84), calls=%async_computation.3 | async-start | bytes 1572864 | tf_op jit(solution)/shard_map/all_to_all | solution.py:147
  125.9 0.8 convolution_convert_fusion.1
  126.9 0.8 fusion.28
  127.7 1.5 collective-permute-done.16
  129.1 0.9 add_convert_fusion.3
  130.0 1.4 collective-permute-start.17
  131.4 1.2 collective-permute-start.18
  132.6 1.4 collective-permute-start.19
  134.0 3.1 %all-to-all-done.3 = bf16[8,64,768]{2,1,0:T(8,128)(2,1)} async-done(((bf16[8,64,768]{2,1,0:T(8,128)(2,1)}), bf16[8,64,768]{2,1,0:T(8,128)(2,1)}, u32[]{:S(2)}, u32[]{:S(2)}) %all-to-all-start.3) | async-done | bytes 786464 | tf_op jit(solution)/shard_map/all_to_all | solution.py:147
  137.1 1.0 slice.110
  138.1 1.7 convolution_convert_fusion
  139.8 1.1 collective-permute-done.18.refs_2_
  141.0 3.0 %collective-permute-done.19.refs_3_ = bf16[64,1536]{1,0:T(8,128)(2,1)S(1)} collective-permute-done((bf16[64,1536]{1,0:T(8,128)(2,1)}, bf16[64,1536]{1,0:T(8,128)(2,1)S(1)}, u32[]{:S(2)}, u32[]{:S(2)}) %collective-permute-start.19) | collective-permute-done | bytes 196640 | tf_op jit(solution)/shard_map/ppermute | solution.py:125
  144.0 5.7 %all-to-all-start.4 = ((bf16[8,2,64,768]{3,2,1,0:T(8,128)(2,1)}), bf16[8,2,64,768]{3,2,1,0:T(8,128)(2,1)}, u32[]{:S(2)}, u32[]{:S(2)}) async-start(bf16[8,2,64,768]{3,2,1,0:T(8,128)(2,1)} %copy-done.1), calls=%async_computation.4 | async-start | bytes 3145728 | tf_op jit(solution)/shard_map/all_to_all | solution.py:147
  149.7 1.8 fusion.22
  152.4 0.9 collective-permute-start.21
  153.3 1.5 collective-permute-start.25
  154.8 0.8 collective-permute-start.26
  155.6 4.9 %collective-permute-done.21.refs_1_ = bf16[64,1536]{1,0:T(8,128)(2,1)S(1)} collective-permute-done((bf16[64,1536]{1,0:T(8,128)(2,1)S(1)}, bf16[64,1536]{1,0:T(8,128)(2,1)S(1)}, u32[]{:S(2)}, u32[]{:S(2)}) %collective-permute-start.21) | collective-permute-done | bytes 196640 | tf_op jit(solution)/shard_map/ppermute | solution.py:125
  160.7 2.1 %collective-permute-start.22 = (bf16[16,1536]{1,0:T(8,128)(2,1)S(1)}, bf16[16,1536]{1,0:T(8,128)(2,1)S(1)}, u32[]{:S(2)}, u32[]{:S(2)}) collective-permute-start(bf16[16,1536]{1,0:T(8,128)(2,1)S(1)} %get-tuple-element.100), channel_id=1, source_target_pairs={{0,24},{8,0},{16,8},{24,16},{1,25},{9,1},{17,9},{25,17},{2,26},{10... | collective-permute-start | bytes 147464 | tf_op jit(solution)/shard_map/ppermute | solution.py:122
  162.9 5.1 %multiply_convert_fusion.1 = bf16[1536,768]{1,0:T(8,128)(2,1)} fusion(bf16[256,1536]{1,0:T(8,128)(2,1)S(1)} %copy-done.20, bf16[256,1536]{1,0:T(8,128)(2,1)S(1)} %copy-done.10, bf16[256,1536]{1,0:T(8,128)(2,1)S(1)} %copy-done.18, bf16[256,1536]{1,0:T(8,128)(2,1)S(1)} %copy-done.8, bf16[512,768]{1,0:T(8,128)(2,1)} %bitcast.22, bf16[512,768]{1,0:T(8,128)(2,1)S(1)} %bitcast.53), kind=kOutput, calls=%fused_computation.1 | convolution fusion | flops 2434007040 | bytes 7077888 | tf_op jit(solution)/shard_map/dot_general | solution.py:34
  168.2 2.6 %collective-permute-start.24 = (bf16[16,1536]{1,0:T(8,128)(2,1)S(1)}, bf16[16,1536]{1,0:T(8,128)(2,1)S(1)}, u32[]{:S(2)}, u32[]{:S(2)}) collective-permute-start(bf16[16,1536]{1,0:T(8,128)(2,1)S(1)} %get-tuple-element.102), channel_id=1, source_target_pairs={{0,8},{8,16},{16,24},{24,0},{1,9},{9,17},{17,25},{25,1},{2,10},{10... | collective-permute-start | bytes 147464 | tf_op jit(solution)/shard_map/ppermute | solution.py:122
  171.1 1.7 collective-permute-start.27
  172.8 5.6 %collective-permute-start.28 = (bf16[16,1536]{1,0:T(8,128)(2,1)S(1)}, bf16[16,1536]{1,0:T(8,128)(2,1)S(1)}, u32[]{:S(2)}, u32[]{:S(2)}) collective-permute-start(bf16[16,1536]{1,0:T(8,128)(2,1)S(1)} %get-tuple-element.109), channel_id=1, source_target_pairs={{0,16},{8,24},{16,0},{24,8},{1,17},{9,25},{17,1},{25,9},{2,18},{10... | collective-permute-start | bytes 147464 | tf_op jit(solution)/shard_map/ppermute | solution.py:122
  178.4 6.4 %multiply_convert_fusion = bf16[768,1536]{1,0:T(8,128)(2,1)} fusion(bf16[1024,768]{1,0:T(8,128)(2,1)} %bitcast.24, bf16[1024,1536]{1,0:T(8,128)(2,1)} %bitcast.52), kind=kOutput, calls=%fused_computation | convolution fusion | flops 2418278400 | bytes 7077888 | tf_op jit(solution)/shard_map/dot_general | solution.py:34
  184.9 1.4 shard_map.80
  (90 shorter events, 8.7 us)
Async XLA Ops:
  0.6 48.3 %copy-start = (bf16[1536,768]{1,0:T(8,128)(2,1)S(1)}, bf16[1536,768]{1,0:T(8,128)(2,1)}, u32[]{:S(2)}) copy-start(bf16[1536,768]{1,0:T(8,128)(2,1)} %param.6) | copy-start | bytes 7077892
  1.7 9.3 %collective-permute-start.2 = (bf16[2,16,1536]{2,1,0:T(8,128)(2,1)S(1)}, bf16[2,16,1536]{2,1,0:T(8,128)(2,1)S(1)}, u32[]{:S(2)}, u32[]{:S(2)}) collective-permute-start(bf16[2,16,1536]{2,1,0:T(8,128)(2,1)S(1)} %pad_maximum_fusion.7), channel_id=1, source_target_pairs={{0,24},{8,0},{16,8},{24,16},{1,25},{9,1},{17,9},{25,17},{2,26},{10... | collective-permute-start | bytes 294920 | tf_op jit(solution)/shard_map/ppermute | solution.py:122
  7.2 10.9 %collective-permute-start.1 = (bf16[2,16,1536]{2,1,0:T(8,128)(2,1)S(1)}, bf16[2,16,1536]{2,1,0:T(8,128)(2,1)S(1)}, u32[]{:S(2)}, u32[]{:S(2)}) collective-permute-start(bf16[2,16,1536]{2,1,0:T(8,128)(2,1)S(1)} %pad_maximum_fusion.7), channel_id=1, source_target_pairs={{0,16},{8,24},{16,0},{24,8},{1,17},{9,25},{17,1},{25,9},{2,18},{10... | collective-permute-start | bytes 294920 | tf_op jit(solution)/shard_map/ppermute | solution.py:122
  8.6 10.0 %collective-permute-start = (bf16[2,16,1536]{2,1,0:T(8,128)(2,1)S(1)}, bf16[2,16,1536]{2,1,0:T(8,128)(2,1)S(1)}, u32[]{:S(2)}, u32[]{:S(2)}) collective-permute-start(bf16[2,16,1536]{2,1,0:T(8,128)(2,1)S(1)} %pad_maximum_fusion.7), channel_id=1, source_target_pairs={{0,8},{8,16},{16,24},{24,0},{1,9},{9,17},{17,25},{25,1},{2,10},{10... | collective-permute-start | bytes 294920 | tf_op jit(solution)/shard_map/ppermute | solution.py:122
  18.7 9.9 %collective-permute-start.8 = (bf16[2,16,1536]{2,1,0:T(8,128)(2,1)S(1)}, bf16[2,16,1536]{2,1,0:T(8,128)(2,1)S(1)}, u32[]{:S(2)}, u32[]{:S(2)}) collective-permute-start(bf16[2,16,1536]{2,1,0:T(8,128)(2,1)S(1)} %pad_maximum_fusion.8), channel_id=1, source_target_pairs={{0,24},{8,0},{16,8},{24,16},{1,25},{9,1},{17,9},{25,17},{2,26},{10... | collective-permute-start | bytes 294920 | tf_op jit(solution)/shard_map/ppermute | solution.py:122
  22.4 19.0 %collective-permute-start.5 = (bf16[2,64,1536]{2,1,0:T(8,128)(2,1)S(1)}, bf16[2,64,1536]{2,1,0:T(8,128)(2,1)S(1)}, u32[]{:S(2)}, u32[]{:S(2)}) collective-permute-start(bf16[2,64,1536]{2,1,0:T(8,128)(2,1)S(1)} %pad_maximum_fusion.5), channel_id=1, source_target_pairs={{0,6},{1,7},{2,0},{3,1},{4,2},{5,3},{6,4},{7,5},{8,14},{9,15},{10,... | collective-permute-start | bytes 1179656 | tf_op jit(solution)/shard_map/ppermute | solution.py:125
  25.1 16.2 %collective-permute-start.4 = (bf16[2,64,1536]{2,1,0:T(8,128)(2,1)S(1)}, bf16[2,64,1536]{2,1,0:T(8,128)(2,1)S(1)}, u32[]{:S(2)}, u32[]{:S(2)}) collective-permute-start(bf16[2,64,1536]{2,1,0:T(8,128)(2,1)S(1)} %pad_maximum_fusion.5), channel_id=1, source_target_pairs={{0,4},{1,5},{2,6},{3,7},{4,0},{5,1},{6,2},{7,3},{8,12},{9,13},{10,... | collective-permute-start | bytes 1179656 | tf_op jit(solution)/shard_map/ppermute | solution.py:125
  25.9 19.1 %collective-permute-start.3 = (bf16[2,64,1536]{2,1,0:T(8,128)(2,1)S(1)}, bf16[2,64,1536]{2,1,0:T(8,128)(2,1)S(1)}, u32[]{:S(2)}, u32[]{:S(2)}) collective-permute-start(bf16[2,64,1536]{2,1,0:T(8,128)(2,1)S(1)} %pad_maximum_fusion.5), channel_id=1, source_target_pairs={{0,2},{1,3},{2,4},{3,5},{4,6},{5,7},{6,0},{7,1},{8,10},{9,11},{10,... | collective-permute-start | bytes 1179656 | tf_op jit(solution)/shard_map/ppermute | solution.py:125
  26.8 9.4 %collective-permute-start.7 = (bf16[2,16,1536]{2,1,0:T(8,128)(2,1)S(1)}, bf16[2,16,1536]{2,1,0:T(8,128)(2,1)S(1)}, u32[]{:S(2)}, u32[]{:S(2)}) collective-permute-start(bf16[2,16,1536]{2,1,0:T(8,128)(2,1)S(1)} %pad_maximum_fusion.8), channel_id=1, source_target_pairs={{0,16},{8,24},{16,0},{24,8},{1,17},{9,25},{17,1},{25,9},{2,18},{10... | collective-permute-start | bytes 294920 | tf_op jit(solution)/shard_map/ppermute | solution.py:122
  28.5 8.7 %collective-permute-start.6 = (bf16[2,16,1536]{2,1,0:T(8,128)(2,1)S(1)}, bf16[2,16,1536]{2,1,0:T(8,128)(2,1)S(1)}, u32[]{:S(2)}, u32[]{:S(2)}) collective-permute-start(bf16[2,16,1536]{2,1,0:T(8,128)(2,1)S(1)} %pad_maximum_fusion.8), channel_id=1, source_target_pairs={{0,8},{8,16},{16,24},{24,0},{1,9},{9,17},{17,25},{25,1},{2,10},{10... | collective-permute-start | bytes 294920 | tf_op jit(solution)/shard_map/ppermute | solution.py:122
  45.3 5.0 %copy-start.7 = (bf16[256,1536]{1,0:T(8,128)(2,1)}, bf16[256,1536]{1,0:T(8,128)(2,1)S(1)}, u32[]{:S(2)}) copy-start(bf16[256,1536]{1,0:T(8,128)(2,1)S(1)} %get-tuple-element.135) | copy-start | bytes 2359300
  45.3 5.0 %copy-start.4 = (bf16[256,1536]{1,0:T(8,128)(2,1)}, bf16[256,1536]{1,0:T(8,128)(2,1)S(1)}, u32[]{:S(2)}) copy-start(bf16[256,1536]{1,0:T(8,128)(2,1)S(1)} %get-tuple-element.136) | copy-start | bytes 2359300
  45.3 3.6 %collective-permute-start.9 = (bf16[256,1536]{1,0:T(8,128)(2,1)S(1)}, bf16[256,1536]{1,0:T(8,128)(2,1)S(1)}, u32[]{:S(2)}, u32[]{:S(2)}) collective-permute-start(bf16[256,1536]{1,0:T(8,128)(2,1)S(1)} %get-tuple-element.135), channel_id=1, source_target_pairs={{0,1},{1,0},{2,3},{3,2},{4,5},{5,4},{6,7},{7,6},{8,9},{9,8},{10,11... | collective-permute-start | bytes 2359304 | tf_op jit(solution)/shard_map/ppermute | solution.py:128
  45.4 4.9 %collective-permute-start.10 = (bf16[256,1536]{1,0:T(8,128)(2,1)S(1)}, bf16[256,1536]{1,0:T(8,128)(2,1)S(1)}, u32[]{:S(2)}, u32[]{:S(2)}) collective-permute-start(bf16[256,1536]{1,0:T(8,128)(2,1)S(1)} %get-tuple-element.136), channel_id=1, source_target_pairs={{0,1},{1,0},{2,3},{3,2},{4,5},{5,4},{6,7},{7,6},{8,9},{9,8},{10,11... | collective-permute-start | bytes 2359304 | tf_op jit(solution)/shard_map/ppermute | solution.py:128
  45.9 24.0 %collective-permute-start.13 = (bf16[2,64,1536]{2,1,0:T(8,128)(2,1)S(1)}, bf16[2,64,1536]{2,1,0:T(8,128)(2,1)S(1)}, u32[]{:S(2)}, u32[]{:S(2)}) collective-permute-start(bf16[2,64,1536]{2,1,0:T(8,128)(2,1)S(1)} %pad_maximum_fusion.6), channel_id=1, source_target_pairs={{0,6},{1,7},{2,0},{3,1},{4,2},{5,3},{6,4},{7,5},{8,14},{9,15},{10,... | collective-permute-start | bytes 1179656 | tf_op jit(solution)/shard_map/ppermute | solution.py:125
  46.5 22.6 %collective-permute-start.12 = (bf16[2,64,1536]{2,1,0:T(8,128)(2,1)S(1)}, bf16[2,64,1536]{2,1,0:T(8,128)(2,1)S(1)}, u32[]{:S(2)}, u32[]{:S(2)}) collective-permute-start(bf16[2,64,1536]{2,1,0:T(8,128)(2,1)S(1)} %pad_maximum_fusion.6), channel_id=1, source_target_pairs={{0,4},{1,5},{2,6},{3,7},{4,0},{5,1},{6,2},{7,3},{8,12},{9,13},{10,... | collective-permute-start | bytes 1179656 | tf_op jit(solution)/shard_map/ppermute | solution.py:125
  47.3 20.1 %collective-permute-start.11 = (bf16[2,64,1536]{2,1,0:T(8,128)(2,1)S(1)}, bf16[2,64,1536]{2,1,0:T(8,128)(2,1)}, u32[]{:S(2)}, u32[]{:S(2)}) collective-permute-start(bf16[2,64,1536]{2,1,0:T(8,128)(2,1)S(1)} %pad_maximum_fusion.6), channel_id=1, source_target_pairs={{0,2},{1,3},{2,4},{3,5},{4,6},{5,7},{6,0},{7,1},{8,10},{9,11},{10,... | collective-permute-start | bytes 1179656 | tf_op jit(solution)/shard_map/ppermute | solution.py:125
  48.9 1.9 %copy-start.15 = (bf16[768,1536]{1,0:T(8,128)(2,1)S(1)}, bf16[768,1536]{1,0:T(8,128)(2,1)}, u32[]{:S(2)}) copy-start(bf16[768,1536]{1,0:T(8,128)(2,1)} %param.8) | copy-start | bytes 7077892
  48.9 1.4 copy-start.17
  50.9 1.4 copy-start.11
  53.9 25.4 %all-to-all-start = ((f16[8,2,64,768]{3,2,1,0:T(8,128)(2,1)}), f16[8,2,64,768]{3,2,1,0:T(8,128)(2,1)}, u32[]{:S(2)}, u32[]{:S(2)}) async-start(f16[8,2,64,768]{3,2,1,0:T(8,128)(2,1)} %pad_maximum_fusion.2), calls=%async_computation | async-start | bytes 3145728 | tf_op jit(solution)/shard_map/all_to_all | solution.py:147
  72.2 3.8 %copy-start.9 = (bf16[256,1536]{1,0:T(8,128)(2,1)}, bf16[256,1536]{1,0:T(8,128)(2,1)S(1)}, u32[]{:S(2)}) copy-start(bf16[256,1536]{1,0:T(8,128)(2,1)S(1)} %get-tuple-element.133) | copy-start | bytes 2359300
  72.2 3.8 %copy-start.5 = (bf16[256,1536]{1,0:T(8,128)(2,1)}, bf16[256,1536]{1,0:T(8,128)(2,1)S(1)}, u32[]{:S(2)}) copy-start(bf16[256,1536]{1,0:T(8,128)(2,1)S(1)} %get-tuple-element.134) | copy-start | bytes 2359300
  72.2 2.4 %collective-permute-start.14 = (bf16[256,1536]{1,0:T(8,128)(2,1)S(1)}, bf16[256,1536]{1,0:T(8,128)(2,1)S(1)}, u32[]{:S(2)}, u32[]{:S(2)}) collective-permute-start(bf16[256,1536]{1,0:T(8,128)(2,1)S(1)} %get-tuple-element.133), channel_id=1, source_target_pairs={{0,1},{1,0},{2,3},{3,2},{4,5},{5,4},{6,7},{7,6},{8,9},{9,8},{10,11... | collective-permute-start | bytes 2359304 | tf_op jit(solution)/shard_map/ppermute | solution.py:128
  72.3 3.7 %copy-start.16 = (bf16[768,1536]{1,0:T(8,128)(2,1)S(1)}, bf16[768,1536]{1,0:T(8,128)(2,1)}, u32[]{:S(2)}) copy-start(bf16[768,1536]{1,0:T(8,128)(2,1)} %param.8) | copy-start | bytes 7077892
  72.3 3.7 %collective-permute-start.15 = (bf16[256,1536]{1,0:T(8,128)(2,1)S(1)}, bf16[256,1536]{1,0:T(8,128)(2,1)S(1)}, u32[]{:S(2)}, u32[]{:S(2)}) collective-permute-start(bf16[256,1536]{1,0:T(8,128)(2,1)S(1)} %get-tuple-element.134), channel_id=1, source_target_pairs={{0,1},{1,0},{2,3},{3,2},{4,5},{5,4},{6,7},{7,6},{8,9},{9,8},{10,11... | collective-permute-start | bytes 2359304 | tf_op jit(solution)/shard_map/ppermute | solution.py:128
  74.6 1.4 copy-start.19
  76.0 1.4 copy-start.12
  79.1 6.1 %copy-start.14 = (f32[768]{0:T(1024)S(1)}, f32[768]{0:T(1024)}, u32[]{:S(2)}) copy-start(f32[768]{0:T(1024)} %param.7) | copy-start | bytes 9220
  79.3 26.1 %all-to-all-start.1 = ((f16[8,2,64,768]{3,2,1,0:T(8,128)(2,1)}), f16[8,2,64,768]{3,2,1,0:T(8,128)(2,1)}, u32[]{:S(2)}, u32[]{:S(2)}) async-start(f16[8,2,64,768]{3,2,1,0:T(8,128)(2,1)} %pad_maximum_fusion.4), calls=%async_computation.1 | async-start | bytes 3145728 | tf_op jit(solution)/shard_map/all_to_all | solution.py:147
  105.4 15.8 %all-to-all-start.2 = ((bf16[8,64,768]{2,1,0:T(8,128)(2,1)}), bf16[8,64,768]{2,1,0:T(8,128)(2,1)S(1)}, u32[]{:S(2)}, u32[]{:S(2)}) async-start(bf16[8,64,768]{2,1,0:T(8,128)(2,1)} %get-tuple-element.71), calls=%async_computation.2 | async-start | bytes 1572864 | tf_op jit(solution)/shard_map/all_to_all | solution.py:147
  109.6 1.6 copy-start.6
  109.6 1.8 copy-start.13
  116.8 1.1 copy-start.1
  121.2 4.7 %copy-start.2 = (bf16[8,64,768]{2,1,0:T(8,128)(2,1)}, bf16[8,64,768]{2,1,0:T(8,128)(2,1)S(1)}, u32[]{:S(2)}) copy-start(bf16[8,64,768]{2,1,0:T(8,128)(2,1)S(1)} %all-to-all-done.2) | copy-start | bytes 2359300
  121.2 15.9 %all-to-all-start.3 = ((bf16[8,64,768]{2,1,0:T(8,128)(2,1)}), bf16[8,64,768]{2,1,0:T(8,128)(2,1)}, u32[]{:S(2)}, u32[]{:S(2)}) async-start(bf16[8,64,768]{2,1,0:T(8,128)(2,1)} %get-tuple-element.84), calls=%async_computation.3 | async-start | bytes 1572864 | tf_op jit(solution)/shard_map/all_to_all | solution.py:147
  126.8 2.4 %collective-permute-start.16 = (bf16[256,1536]{1,0:T(8,128)(2,1)S(1)}, bf16[256,1536]{1,0:T(8,128)(2,1)S(1)}, u32[]{:S(2)}, u32[]{:S(2)}) collective-permute-start(bf16[256,1536]{1,0:T(8,128)(2,1)S(1)} %convolution_convert_fusion.1), channel_id=1, source_target_pairs={{0,1},{1,0},{2,3},{3,2},{4,5},{5,4},{6,7},{7,6},{8,9},{9,8},{10,11... | collective-permute-start | bytes 2359304 | tf_op jit(solution)/shard_map/ppermute | solution.py:128
  130.0 9.8 %collective-permute-start.17 = (bf16[64,1536]{1,0:T(8,128)(2,1)}, bf16[64,1536]{1,0:T(8,128)(2,1)S(1)}, u32[]{:S(2)}, u32[]{:S(2)}) collective-permute-start(bf16[64,1536]{1,0:T(8,128)(2,1)} %get-tuple-element.80), channel_id=1, source_target_pairs={{0,6},{1,7},{2,0},{3,1},{4,2},{5,3},{6,4},{7,5},{8,14},{9,15},{10,... | collective-permute-start | bytes 589832 | tf_op jit(solution)/shard_map/ppermute | solution.py:125
  131.4 9.5 %collective-permute-start.18 = (bf16[64,1536]{1,0:T(8,128)(2,1)}, bf16[64,1536]{1,0:T(8,128)(2,1)S(1)}, u32[]{:S(2)}, u32[]{:S(2)}) collective-permute-start(bf16[64,1536]{1,0:T(8,128)(2,1)} %get-tuple-element.81), channel_id=1, source_target_pairs={{0,4},{1,5},{2,6},{3,7},{4,0},{5,1},{6,2},{7,3},{8,12},{9,13},{10,... | collective-permute-start | bytes 589832 | tf_op jit(solution)/shard_map/ppermute | solution.py:125
  132.6 11.4 %collective-permute-start.19 = (bf16[64,1536]{1,0:T(8,128)(2,1)}, bf16[64,1536]{1,0:T(8,128)(2,1)S(1)}, u32[]{:S(2)}, u32[]{:S(2)}) collective-permute-start(bf16[64,1536]{1,0:T(8,128)(2,1)} %get-tuple-element.82), channel_id=1, source_target_pairs={{0,2},{1,3},{2,4},{3,5},{4,6},{5,7},{6,0},{7,1},{8,10},{9,11},{10,... | collective-permute-start | bytes 589832 | tf_op jit(solution)/shard_map/ppermute | solution.py:125
  144.0 34.4 %all-to-all-start.4 = ((bf16[8,2,64,768]{3,2,1,0:T(8,128)(2,1)}), bf16[8,2,64,768]{3,2,1,0:T(8,128)(2,1)}, u32[]{:S(2)}, u32[]{:S(2)}) async-start(bf16[8,2,64,768]{3,2,1,0:T(8,128)(2,1)} %copy-done.1), calls=%async_computation.4 | async-start | bytes 3145728 | tf_op jit(solution)/shard_map/all_to_all | solution.py:147
  149.7 2.5 %collective-permute-start.20 = (bf16[256,1536]{1,0:T(8,128)(2,1)}, bf16[256,1536]{1,0:T(8,128)(2,1)S(1)}, u32[]{:S(2)}, u32[]{:S(2)}) collective-permute-start(bf16[256,1536]{1,0:T(8,128)(2,1)} %convolution_convert_fusion), channel_id=1, source_target_pairs={{0,1},{1,0},{2,3},{3,2},{4,5},{5,4},{6,7},{7,6},{8,9},{9,8},{10,11... | collective-permute-start | bytes 2359304 | tf_op jit(solution)/shard_map/ppermute | solution.py:128
  151.5 11.3 %copy-start.3 = (bf16[8,64,768]{2,1,0:T(8,128)(2,1)S(1)}, bf16[8,64,768]{2,1,0:T(8,128)(2,1)}, u32[]{:S(2)}) copy-start(bf16[8,64,768]{2,1,0:T(8,128)(2,1)} %copy-done.2) | copy-start | bytes 2359300
  151.6 11.3 %copy-start.8 = (bf16[256,1536]{1,0:T(8,128)(2,1)S(1)}, bf16[256,1536]{1,0:T(8,128)(2,1)}, u32[]{:S(2)}) copy-start(bf16[256,1536]{1,0:T(8,128)(2,1)} %copy-done.7) | copy-start | bytes 2359300
  151.6 11.3 %copy-start.10 = (bf16[256,1536]{1,0:T(8,128)(2,1)S(1)}, bf16[256,1536]{1,0:T(8,128)(2,1)}, u32[]{:S(2)}) copy-start(bf16[256,1536]{1,0:T(8,128)(2,1)} %copy-done.9) | copy-start | bytes 2359300
  151.6 11.3 %copy-start.18 = (bf16[256,1536]{1,0:T(8,128)(2,1)S(1)}, bf16[256,1536]{1,0:T(8,128)(2,1)}, u32[]{:S(2)}) copy-start(bf16[256,1536]{1,0:T(8,128)(2,1)} %copy-done.17) | copy-start | bytes 2359300
  151.6 11.3 %copy-start.20 = (bf16[256,1536]{1,0:T(8,128)(2,1)S(1)}, bf16[256,1536]{1,0:T(8,128)(2,1)}, u32[]{:S(2)}) copy-start(bf16[256,1536]{1,0:T(8,128)(2,1)} %copy-done.19) | copy-start | bytes 2359300
  152.4 8.0 %collective-permute-start.21 = (bf16[64,1536]{1,0:T(8,128)(2,1)S(1)}, bf16[64,1536]{1,0:T(8,128)(2,1)S(1)}, u32[]{:S(2)}, u32[]{:S(2)}) collective-permute-start(bf16[64,1536]{1,0:T(8,128)(2,1)S(1)} %get-tuple-element.94), channel_id=1, source_target_pairs={{0,6},{1,7},{2,0},{3,1},{4,2},{5,3},{6,4},{7,5},{8,14},{9,15},{10,... | collective-permute-start | bytes 589832 | tf_op jit(solution)/shard_map/ppermute | solution.py:125
  153.3 17.5 %collective-permute-start.25 = (bf16[64,1536]{1,0:T(8,128)(2,1)S(1)}, bf16[64,1536]{1,0:T(8,128)(2,1)S(1)}, u32[]{:S(2)}, u32[]{:S(2)}) collective-permute-start(bf16[64,1536]{1,0:T(8,128)(2,1)S(1)} %get-tuple-element.105), channel_id=1, source_target_pairs={{0,4},{1,5},{2,6},{3,7},{4,0},{5,1},{6,2},{7,3},{8,12},{9,13},{10,... | collective-permute-start | bytes 589832 | tf_op jit(solution)/shard_map/ppermute | solution.py:125
  154.8 16.0 %collective-permute-start.26 = (bf16[64,1536]{1,0:T(8,128)(2,1)S(1)}, bf16[64,1536]{1,0:T(8,128)(2,1)S(1)}, u32[]{:S(2)}, u32[]{:S(2)}) collective-permute-start(bf16[64,1536]{1,0:T(8,128)(2,1)S(1)} %get-tuple-element.106), channel_id=1, source_target_pairs={{0,2},{1,3},{2,4},{3,5},{4,6},{5,7},{6,0},{7,1},{8,10},{9,11},{10,... | collective-permute-start | bytes 589832 | tf_op jit(solution)/shard_map/ppermute | solution.py:125
  160.7 17.7 %collective-permute-start.22 = (bf16[16,1536]{1,0:T(8,128)(2,1)S(1)}, bf16[16,1536]{1,0:T(8,128)(2,1)S(1)}, u32[]{:S(2)}, u32[]{:S(2)}) collective-permute-start(bf16[16,1536]{1,0:T(8,128)(2,1)S(1)} %get-tuple-element.100), channel_id=1, source_target_pairs={{0,24},{8,0},{16,8},{24,16},{1,25},{9,1},{17,9},{25,17},{2,26},{10... | collective-permute-start | bytes 147464 | tf_op jit(solution)/shard_map/ppermute | solution.py:122
  168.0 16.9 %collective-permute-start.23 = (bf16[16,1536]{1,0:T(8,128)(2,1)S(1)}, bf16[16,1536]{1,0:T(8,128)(2,1)S(1)}, u32[]{:S(2)}, u32[]{:S(2)}) collective-permute-start(bf16[16,1536]{1,0:T(8,128)(2,1)S(1)} %get-tuple-element.101), channel_id=1, source_target_pairs={{0,16},{8,24},{16,0},{24,8},{1,17},{9,25},{17,1},{25,9},{2,18},{10... | collective-permute-start | bytes 147464 | tf_op jit(solution)/shard_map/ppermute | solution.py:122
  168.2 16.6 %collective-permute-start.24 = (bf16[16,1536]{1,0:T(8,128)(2,1)S(1)}, bf16[16,1536]{1,0:T(8,128)(2,1)S(1)}, u32[]{:S(2)}, u32[]{:S(2)}) collective-permute-start(bf16[16,1536]{1,0:T(8,128)(2,1)S(1)} %get-tuple-element.102), channel_id=1, source_target_pairs={{0,8},{8,16},{16,24},{24,0},{1,9},{9,17},{17,25},{25,1},{2,10},{10... | collective-permute-start | bytes 147464 | tf_op jit(solution)/shard_map/ppermute | solution.py:122
  171.1 13.8 %collective-permute-start.27 = (bf16[16,1536]{1,0:T(8,128)(2,1)S(1)}, bf16[16,1536]{1,0:T(8,128)(2,1)S(1)}, u32[]{:S(2)}, u32[]{:S(2)}) collective-permute-start(bf16[16,1536]{1,0:T(8,128)(2,1)S(1)} %get-tuple-element.108), channel_id=1, source_target_pairs={{0,24},{8,0},{16,8},{24,16},{1,25},{9,1},{17,9},{25,17},{2,26},{10... | collective-permute-start | bytes 147464 | tf_op jit(solution)/shard_map/ppermute | solution.py:122
  172.8 12.0 %collective-permute-start.28 = (bf16[16,1536]{1,0:T(8,128)(2,1)S(1)}, bf16[16,1536]{1,0:T(8,128)(2,1)S(1)}, u32[]{:S(2)}, u32[]{:S(2)}) collective-permute-start(bf16[16,1536]{1,0:T(8,128)(2,1)S(1)} %get-tuple-element.109), channel_id=1, source_target_pairs={{0,16},{8,24},{16,0},{24,8},{1,17},{9,25},{17,1},{25,9},{2,18},{10... | collective-permute-start | bytes 147464 | tf_op jit(solution)/shard_map/ppermute | solution.py:122
  178.4 6.4 %collective-permute-start.29 = (bf16[16,1536]{1,0:T(8,128)(2,1)S(1)}, bf16[16,1536]{1,0:T(8,128)(2,1)S(1)}, u32[]{:S(2)}, u32[]{:S(2)}) collective-permute-start(bf16[16,1536]{1,0:T(8,128)(2,1)S(1)} %get-tuple-element.110), channel_id=1, source_target_pairs={{0,8},{8,16},{16,24},{24,0},{1,9},{9,17},{17,25},{25,1},{2,10},{10... | collective-permute-start | bytes 147464 | tf_op jit(solution)/shard_map/ppermute | solution.py:122

commit v13 on v11

--- a/solution.py
+++ b/solution.py
@@ -196,8 +196,11 @@
         own0, other0 = barrier(own0, swap_core(other0))
         parts0, act_copies = barrier(sum_blocks([own0, other0], n_chip), act_copies)
         parts0 = exchange(parts0, shift_chip)
-        other1, own1 = two_halves(hidden1)
-        parts0, other1, act_copies = barrier(parts0, other1, act_copies)
+        other1, _ = two_halves(hidden1)
+        parts0[:-1], other1, act_copies, hidden1 = barrier(
+            parts0[:-1], other1, act_copies, hidden1
+        )
+        _, own1 = two_halves(hidden1)
         activation = trade_width(act_copies)
         own1, other1 = barrier(own1, swap_core(other1))
         parts1, hidden0, hidden1 = barrier(sum_blocks([own1, other1], n_chip), hidden0, hidden1)

time: 181 us -> 182 us (level)
    ppermute x12, waiting for transfers between devices: 10.3 us -> 15.4 us  [shift_chip(): return lax.ppermute(a, 'gz', [(i, (i + 2 * k) % n_z) for i in range(n_z)])]
    all_to_all x5, waiting for transfers between devices: 29 us -> 24.7 us  [trade_width(): return lax.all_to_all(parts, 'gx', 0, 0, tiled=True)]
    slice x1 -> x0, local copies, waits for them, and re-layouts: 1.94 us -> none  [two_halves(): return (other, contract_last(grad_hidden[:half], weight_in))]
  transfers between devices with their start and end apart: 35 -> 35, of which waited for: 15 -> 14; matrix products, arithmetic and copies ran while one was open for 23% -> 22% of each run, Pallas kernels for 2% -> 2%
where the time goes in v13:
time: 182 us; the launch traced here: 181 us
  starting transfers between devices  73.7 us (40%)
  waiting for transfers between devices  57.3 us (31%)
  matrix products  22.3 us (12%)
  other arithmetic  11.4 us (6%)
  local copies, waits for them, and re-layouts  9.84 us (5%)
  Pallas kernels  5.24 us (3%)
    ppermute x12, starting transfers between devices, shift_y(): return lax.ppermute(a, 'gy', [(i, (i + k) % n_y) for i in range(n_y)])  29.4 us
    all_to_all x5, starting transfers between devices, trade_width(): return lax.all_to_all(parts, 'gx', 0, 0, tiled=True)  26.4 us
    all_to_all x5, waiting for transfers between devices, trade_width(): return lax.all_to_all(parts, 'gx', 0, 0, tiled=True)  24.7 us
    ppermute x12, starting transfers between devices, shift_chip(): return lax.ppermute(a, 'gz', [(i, (i + 2 * k) % n_z) for i in range(n_z)])  16.7 us
    ppermute x12, waiting for transfers between devices, shift_chip(): return lax.ppermute(a, 'gz', [(i, (i + 2 * k) % n_z) for i in range(n_z)])  15.4 us
    ppermute x12, waiting for transfers between devices, shift_y(): return lax.ppermute(a, 'gy', [(i, (i + k) % n_y) for i in range(n_y)])  13.9 us
    dot_general x2, matrix products, contract_first(): lax.dot_general(left, right, (((0,), (0,)), ((), ())), preferred_element_...  11.5 us
    dot_general x6, matrix products, contract_last(): lax.dot_general(left, right, (((1,), (1,)), ((), ())), preferred_element_...  8.01 us
  transfers between devices with their start and end apart: 35, of which 14 were waited for; matrix products, arithmetic and copies ran while one was open for 22% of the time, Pallas kernels for 2%

profile of v13, /device:TPU:32, one launch (start us, length us, event | category | flops | bytes accessed | tf_op | source)
XLA Modules:
  0.0 180.9 jit_solution(3969022191023688879)
XLA Ops:
  0.6 1.0 slice_bitcast_fusion.4
  1.7 5.5 %collective-permute-start.2 = (bf16[2,16,1536]{2,1,0:T(8,128)(2,1)S(1)}, bf16[2,16,1536]{2,1,0:T(8,128)(2,1)S(1)}, u32[]{:S(2)}, u32[]{:S(2)}) collective-permute-start(bf16[2,16,1536]{2,1,0:T(8,128)(2,1)S(1)} %pad_maximum_fusion.7), channel_id=1, source_target_pairs={{0,24},{8,0},{16,8},{24,16},{1,25},{9,1},{17,9},{25,17},{2,26},{10... | collective-permute-start | bytes 294920 | tf_op jit(solution)/shard_map/ppermute | solution.py:122
  7.2 1.4 collective-permute-start.1
  8.6 2.4 %collective-permute-start = (bf16[2,16,1536]{2,1,0:T(8,128)(2,1)S(1)}, bf16[2,16,1536]{2,1,0:T(8,128)(2,1)S(1)}, u32[]{:S(2)}, u32[]{:S(2)}) collective-permute-start(bf16[2,16,1536]{2,1,0:T(8,128)(2,1)S(1)} %pad_maximum_fusion.7), channel_id=1, source_target_pairs={{0,8},{8,16},{16,24},{24,0},{1,9},{9,17},{17,25},{25,1},{2,10},{10... | collective-permute-start | bytes 294920 | tf_op jit(solution)/shard_map/ppermute | solution.py:122
  11.0 7.0 %collective-permute-done.1 = bf16[2,16,1536]{2,1,0:T(8,128)(2,1)S(1)} collective-permute-done((bf16[2,16,1536]{2,1,0:T(8,128)(2,1)S(1)}, bf16[2,16,1536]{2,1,0:T(8,128)(2,1)S(1)}, u32[]{:S(2)}, u32[]{:S(2)}) %collective-permute-start.1) | collective-permute-done | bytes 98336 | tf_op jit(solution)/shard_map/ppermute | solution.py:122
  18.7 3.7 %collective-permute-start.8 = (bf16[2,16,1536]{2,1,0:T(8,128)(2,1)S(1)}, bf16[2,16,1536]{2,1,0:T(8,128)(2,1)S(1)}, u32[]{:S(2)}, u32[]{:S(2)}) collective-permute-start(bf16[2,16,1536]{2,1,0:T(8,128)(2,1)S(1)} %pad_maximum_fusion.8), channel_id=1, source_target_pairs={{0,24},{8,0},{16,8},{24,16},{1,25},{9,1},{17,9},{25,17},{2,26},{10... | collective-permute-start | bytes 294920 | tf_op jit(solution)/shard_map/ppermute | solution.py:122
  22.4 2.8 %collective-permute-start.5 = (bf16[2,64,1536]{2,1,0:T(8,128)(2,1)S(1)}, bf16[2,64,1536]{2,1,0:T(8,128)(2,1)S(1)}, u32[]{:S(2)}, u32[]{:S(2)}) collective-permute-start(bf16[2,64,1536]{2,1,0:T(8,128)(2,1)S(1)} %pad_maximum_fusion.5), channel_id=1, source_target_pairs={{0,6},{1,7},{2,0},{3,1},{4,2},{5,3},{6,4},{7,5},{8,14},{9,15},{10,... | collective-permute-start | bytes 1179656 | tf_op jit(solution)/shard_map/ppermute | solution.py:125
  25.1 0.8 collective-permute-start.4
  25.9 0.9 collective-permute-start.3
  26.8 1.7 collective-permute-start.7
  28.5 2.4 %collective-permute-start.6 = (bf16[2,16,1536]{2,1,0:T(8,128)(2,1)S(1)}, bf16[2,16,1536]{2,1,0:T(8,128)(2,1)S(1)}, u32[]{:S(2)}, u32[]{:S(2)}) collective-permute-start(bf16[2,16,1536]{2,1,0:T(8,128)(2,1)S(1)} %pad_maximum_fusion.8), channel_id=1, source_target_pairs={{0,8},{8,16},{16,24},{24,0},{1,9},{9,17},{17,25},{25,1},{2,10},{10... | collective-permute-start | bytes 294920 | tf_op jit(solution)/shard_map/ppermute | solution.py:122
  30.9 5.3 %collective-permute-done.7 = bf16[2,16,1536]{2,1,0:T(8,128)(2,1)S(1)} collective-permute-done((bf16[2,16,1536]{2,1,0:T(8,128)(2,1)S(1)}, bf16[2,16,1536]{2,1,0:T(8,128)(2,1)S(1)}, u32[]{:S(2)}, u32[]{:S(2)}) %collective-permute-start.7) | collective-permute-done | bytes 98336 | tf_op jit(solution)/shard_map/ppermute | solution.py:122
  36.2 1.0 collective-permute-done.6
  37.3 4.1 %collective-permute-done.5 = bf16[2,64,1536]{2,1,0:T(8,128)(2,1)S(1)} collective-permute-done((bf16[2,64,1536]{2,1,0:T(8,128)(2,1)S(1)}, bf16[2,64,1536]{2,1,0:T(8,128)(2,1)S(1)}, u32[]{:S(2)}, u32[]{:S(2)}) %collective-permute-start.5) | collective-permute-done | bytes 393248 | tf_op jit(solution)/shard_map/ppermute | solution.py:125
  41.4 3.7 %collective-permute-done.3 = bf16[2,64,1536]{2,1,0:T(8,128)(2,1)S(1)} collective-permute-done((bf16[2,64,1536]{2,1,0:T(8,128)(2,1)S(1)}, bf16[2,64,1536]{2,1,0:T(8,128)(2,1)S(1)}, u32[]{:S(2)}, u32[]{:S(2)}) %collective-permute-start.3) | collective-permute-done | bytes 393248 | tf_op jit(solution)/shard_map/ppermute | solution.py:125
  46.5 0.8 collective-permute-start.12
  47.3 0.8 collective-permute-start.11
  48.9 1.4 multiply_convert_fusion.5
  50.9 1.4 multiply_convert_fusion.4
  52.3 1.6 pad_maximum_fusion.2
  53.9 5.9 %all-to-all-start = ((f16[8,2,64,768]{3,2,1,0:T(8,128)(2,1)}), f16[8,2,64,768]{3,2,1,0:T(8,128)(2,1)}, u32[]{:S(2)}, u32[]{:S(2)}) async-start(f16[8,2,64,768]{3,2,1,0:T(8,128)(2,1)} %pad_maximum_fusion.2), calls=%async_computation | async-start | bytes 3145728 | tf_op jit(solution)/shard_map/all_to_all | solution.py:147
  59.8 7.6 %collective-permute-done.11 = bf16[2,64,1536]{2,1,0:T(8,128)(2,1)} collective-permute-done((bf16[2,64,1536]{2,1,0:T(8,128)(2,1)S(1)}, bf16[2,64,1536]{2,1,0:T(8,128)(2,1)}, u32[]{:S(2)}, u32[]{:S(2)}) %collective-permute-start.11) | collective-permute-done | bytes 393248 | tf_op jit(solution)/shard_map/ppermute | solution.py:125
  67.4 1.8 constant_dynamic-update-slice_fusion.6
  69.2 0.8 constant_dynamic-update-slice_fusion.5
  69.9 0.8 constant_dynamic-update-slice_fusion.4
  70.7 1.5 slice_bitcast_fusion.1
  72.8 1.8 collective-permute-done.14
  74.6 1.4 multiply_convert_fusion.3
  76.0 1.4 multiply_convert_fusion.2
  77.5 1.6 pad_maximum_fusion.4
  79.3 5.8 %all-to-all-start.1 = ((f16[8,2,64,768]{3,2,1,0:T(8,128)(2,1)}), f16[8,2,64,768]{3,2,1,0:T(8,128)(2,1)}, u32[]{:S(2)}, u32[]{:S(2)}) async-start(f16[8,2,64,768]{3,2,1,0:T(8,128)(2,1)} %pad_maximum_fusion.4), calls=%async_computation.1 | async-start | bytes 3145728 | tf_op jit(solution)/shard_map/all_to_all | solution.py:147
  85.1 1.7 convert_reduce_fusion.1.sums
  86.8 1.7 shard_map.76
  88.5 16.9 %all-to-all-done.1 = f16[8,2,64,768]{3,2,1,0:T(8,128)(2,1)} async-done(((f16[8,2,64,768]{3,2,1,0:T(8,128)(2,1)}), f16[8,2,64,768]{3,2,1,0:T(8,128)(2,1)}, u32[]{:S(2)}, u32[]{:S(2)}) %all-to-all-start.1) | async-done | bytes 1572896 | tf_op jit(solution)/shard_map/all_to_all | solution.py:147
  105.4 4.2 %all-to-all-start.2 = ((bf16[8,64,768]{2,1,0:T(8,128)(2,1)}), bf16[8,64,768]{2,1,0:T(8,128)(2,1)S(1)}, u32[]{:S(2)}, u32[]{:S(2)}) async-start(bf16[8,64,768]{2,1,0:T(8,128)(2,1)} %get-tuple-element.69), calls=%async_computation.2 | async-start | bytes 1572864 | tf_op jit(solution)/shard_map/all_to_all | solution.py:147
  109.6 1.6 pad_maximum_fusion.1
  111.5 2.0 %pad_maximum_fusion = bf16[8,2,64,1536]{3,2,1,0:T(8,128)(2,1)} fusion(bf16[8,1,64,1536]{3,2,1,0:T(8,128)(2,1)S(1)} %bitcast.51, bf16[8,1,64,1536]{3,2,1,0:T(8,128)(2,1)S(1)} %bitcast.50), kind=kLoop, calls=%fused_computation.2 | loop fusion | flops 1572864 | bytes 6291456 | tf_op jit(solution)/shard_map/stack | solution.py:191
  113.5 1.7 convert_reduce_fusion.sums
  115.2 1.6 shard_map.77
  116.8 1.1 copy-done.1
  117.9 3.2 %all-to-all-done.2 = bf16[8,64,768]{2,1,0:T(8,128)(2,1)S(1)} async-done(((bf16[8,64,768]{2,1,0:T(8,128)(2,1)}), bf16[8,64,768]{2,1,0:T(8,128)(2,1)S(1)}, u32[]{:S(2)}, u32[]{:S(2)}) %all-to-all-start.2) | async-done | bytes 786464 | tf_op jit(solution)/shard_map/all_to_all | solution.py:147
  121.2 4.7 %all-to-all-start.3 = ((bf16[8,64,768]{2,1,0:T(8,128)(2,1)}), bf16[8,64,768]{2,1,0:T(8,128)(2,1)}, u32[]{:S(2)}, u32[]{:S(2)}) async-start(bf16[8,64,768]{2,1,0:T(8,128)(2,1)} %get-tuple-element.81), calls=%async_computation.3 | async-start | bytes 1572864 | tf_op jit(solution)/shard_map/all_to_all | solution.py:147
  125.9 0.8 convolution_convert_fusion.1
  126.9 0.8 fusion.28
  127.7 1.5 collective-permute-done.16
  129.1 1.0 add_convert_fusion.3
  130.1 1.4 collective-permute-start.17
  131.5 1.2 collective-permute-start.18
  132.7 4.4 %all-to-all-done.3 = bf16[8,64,768]{2,1,0:T(8,128)(2,1)} async-done(((bf16[8,64,768]{2,1,0:T(8,128)(2,1)}), bf16[8,64,768]{2,1,0:T(8,128)(2,1)}, u32[]{:S(2)}, u32[]{:S(2)}) %all-to-all-start.3) | async-done | bytes 786464 | tf_op jit(solution)/shard_map/all_to_all | solution.py:147
  137.1 1.0 slice.110
  138.1 1.7 convolution_convert_fusion
  139.9 5.7 %all-to-all-start.4 = ((bf16[8,2,64,768]{3,2,1,0:T(8,128)(2,1)}), bf16[8,2,64,768]{3,2,1,0:T(8,128)(2,1)}, u32[]{:S(2)}, u32[]{:S(2)}) async-start(bf16[8,2,64,768]{3,2,1,0:T(8,128)(2,1)} %copy-done.1), calls=%async_computation.4 | async-start | bytes 3145728 | tf_op jit(solution)/shard_map/all_to_all | solution.py:147
  145.6 3.6 %collective-permute-start.19 = (bf16[64,1536]{1,0:T(8,128)(2,1)S(1)}, bf16[64,1536]{1,0:T(8,128)(2,1)S(1)}, u32[]{:S(2)}, u32[]{:S(2)}) collective-permute-start(bf16[64,1536]{1,0:T(8,128)(2,1)S(1)} %get-tuple-element.86), channel_id=1, source_target_pairs={{0,2},{1,3},{2,4},{3,5},{4,6},{5,7},{6,0},{7,1},{8,10},{9,11},{10,... | collective-permute-start | bytes 589832 | tf_op jit(solution)/shard_map/ppermute | solution.py:125
  149.2 1.9 %fusion.22 = f32[256,1536]{1,0:T(8,128)S(1)} fusion(bf16[1536,768]{1,0:T(8,128)(2,1)S(1)} %copy-done, bf16[512,768]{1,0:T(8,128)(2,1)} %bitcast.22), kind=kOutput, calls=%fused_computation.43 | convolution fusion | flops 603979776 | bytes 4325376 | tf_op jit(solution)/shard_map/dot_general | solution.py:30
  151.3 1.6 collective-permute-start.24
  152.9 1.3 collective-permute-start.25
  154.2 1.0 collective-permute-start.26
  155.2 5.1 %multiply_convert_fusion.1 = bf16[1536,768]{1,0:T(8,128)(2,1)} fusion(bf16[256,1536]{1,0:T(8,128)(2,1)S(1)} %copy-done.20, bf16[256,1536]{1,0:T(8,128)(2,1)S(1)} %copy-done.10, bf16[256,1536]{1,0:T(8,128)(2,1)S(1)} %copy-done.18, bf16[256,1536]{1,0:T(8,128)(2,1)S(1)} %copy-done.8, bf16[512,768]{1,0:T(8,128)(2,1)} %bitcast.22, bf16[512,768]{1,0:T(8,128)(2,1)S(1)} %bitcast.53), kind=kOutput, calls=%fused_computation.1 | convolution fusion | flops 2434007040 | bytes 7077888 | tf_op jit(solution)/shard_map/dot_general | solution.py:34
  160.6 2.1 %collective-permute-start.21 = (bf16[16,1536]{1,0:T(8,128)(2,1)S(1)}, bf16[16,1536]{1,0:T(8,128)(2,1)S(1)}, u32[]{:S(2)}, u32[]{:S(2)}) collective-permute-start(bf16[16,1536]{1,0:T(8,128)(2,1)S(1)} %get-tuple-element.98), channel_id=1, source_target_pairs={{0,24},{8,0},{16,8},{24,16},{1,25},{9,1},{17,9},{25,17},{2,26},{10... | collective-permute-start | bytes 147464 | tf_op jit(solution)/shard_map/ppermute | solution.py:122
  163.0 2.6 %collective-permute-start.23 = (bf16[16,1536]{1,0:T(8,128)(2,1)S(1)}, bf16[16,1536]{1,0:T(8,128)(2,1)S(1)}, u32[]{:S(2)}, u32[]{:S(2)}) collective-permute-start(bf16[16,1536]{1,0:T(8,128)(2,1)S(1)} %get-tuple-element.100), channel_id=1, source_target_pairs={{0,8},{8,16},{16,24},{24,0},{1,9},{9,17},{17,25},{25,1},{2,10},{10... | collective-permute-start | bytes 147464 | tf_op jit(solution)/shard_map/ppermute | solution.py:122
  165.8 1.8 %collective-permute-start.27 = (bf16[16,1536]{1,0:T(8,128)(2,1)S(1)}, bf16[16,1536]{1,0:T(8,128)(2,1)S(1)}, u32[]{:S(2)}, u32[]{:S(2)}) collective-permute-start(bf16[16,1536]{1,0:T(8,128)(2,1)S(1)} %get-tuple-element.106), channel_id=1, source_target_pairs={{0,24},{8,0},{16,8},{24,16},{1,25},{9,1},{17,9},{25,17},{2,26},{10... | collective-permute-start | bytes 147464 | tf_op jit(solution)/shard_map/ppermute | solution.py:122
  167.6 5.5 %collective-permute-start.28 = (bf16[16,1536]{1,0:T(8,128)(2,1)S(1)}, bf16[16,1536]{1,0:T(8,128)(2,1)S(1)}, u32[]{:S(2)}, u32[]{:S(2)}) collective-permute-start(bf16[16,1536]{1,0:T(8,128)(2,1)S(1)} %get-tuple-element.107), channel_id=1, source_target_pairs={{0,16},{8,24},{16,0},{24,8},{1,17},{9,25},{17,1},{25,9},{2,18},{10... | collective-permute-start | bytes 147464 | tf_op jit(solution)/shard_map/ppermute | solution.py:122
  173.1 6.4 %multiply_convert_fusion = bf16[768,1536]{1,0:T(8,128)(2,1)} fusion(bf16[1024,768]{1,0:T(8,128)(2,1)} %bitcast.24, bf16[1024,1536]{1,0:T(8,128)(2,1)} %bitcast.52), kind=kOutput, calls=%fused_computation | convolution fusion | flops 2418278400 | bytes 7077888 | tf_op jit(solution)/shard_map/dot_general | solution.py:34
  179.6 1.4 shard_map.80
  (90 shorter events, 5.8 us)
Async XLA Ops:
  0.6 48.3 %copy-start = (bf16[1536,768]{1,0:T(8,128)(2,1)S(1)}, bf16[1536,768]{1,0:T(8,128)(2,1)}, u32[]{:S(2)}) copy-start(bf16[1536,768]{1,0:T(8,128)(2,1)} %param.6) | copy-start | bytes 7077892
  1.7 9.3 %collective-permute-start.2 = (bf16[2,16,1536]{2,1,0:T(8,128)(2,1)S(1)}, bf16[2,16,1536]{2,1,0:T(8,128)(2,1)S(1)}, u32[]{:S(2)}, u32[]{:S(2)}) collective-permute-start(bf16[2,16,1536]{2,1,0:T(8,128)(2,1)S(1)} %pad_maximum_fusion.7), channel_id=1, source_target_pairs={{0,24},{8,0},{16,8},{24,16},{1,25},{9,1},{17,9},{25,17},{2,26},{10... | collective-permute-start | bytes 294920 | tf_op jit(solution)/shard_map/ppermute | solution.py:122
  7.2 10.9 %collective-permute-start.1 = (bf16[2,16,1536]{2,1,0:T(8,128)(2,1)S(1)}, bf16[2,16,1536]{2,1,0:T(8,128)(2,1)S(1)}, u32[]{:S(2)}, u32[]{:S(2)}) collective-permute-start(bf16[2,16,1536]{2,1,0:T(8,128)(2,1)S(1)} %pad_maximum_fusion.7), channel_id=1, source_target_pairs={{0,16},{8,24},{16,0},{24,8},{1,17},{9,25},{17,1},{25,9},{2,18},{10... | collective-permute-start | bytes 294920 | tf_op jit(solution)/shard_map/ppermute | solution.py:122
  8.6 10.0 %collective-permute-start = (bf16[2,16,1536]{2,1,0:T(8,128)(2,1)S(1)}, bf16[2,16,1536]{2,1,0:T(8,128)(2,1)S(1)}, u32[]{:S(2)}, u32[]{:S(2)}) collective-permute-start(bf16[2,16,1536]{2,1,0:T(8,128)(2,1)S(1)} %pad_maximum_fusion.7), channel_id=1, source_target_pairs={{0,8},{8,16},{16,24},{24,0},{1,9},{9,17},{17,25},{25,1},{2,10},{10... | collective-permute-start | bytes 294920 | tf_op jit(solution)/shard_map/ppermute | solution.py:122
  18.7 9.9 %collective-permute-start.8 = (bf16[2,16,1536]{2,1,0:T(8,128)(2,1)S(1)}, bf16[2,16,1536]{2,1,0:T(8,128)(2,1)S(1)}, u32[]{:S(2)}, u32[]{:S(2)}) collective-permute-start(bf16[2,16,1536]{2,1,0:T(8,128)(2,1)S(1)} %pad_maximum_fusion.8), channel_id=1, source_target_pairs={{0,24},{8,0},{16,8},{24,16},{1,25},{9,1},{17,9},{25,17},{2,26},{10... | collective-permute-start | bytes 294920 | tf_op jit(solution)/shard_map/ppermute | solution.py:122
  22.4 19.0 %collective-permute-start.5 = (bf16[2,64,1536]{2,1,0:T(8,128)(2,1)S(1)}, bf16[2,64,1536]{2,1,0:T(8,128)(2,1)S(1)}, u32[]{:S(2)}, u32[]{:S(2)}) collective-permute-start(bf16[2,64,1536]{2,1,0:T(8,128)(2,1)S(1)} %pad_maximum_fusion.5), channel_id=1, source_target_pairs={{0,6},{1,7},{2,0},{3,1},{4,2},{5,3},{6,4},{7,5},{8,14},{9,15},{10,... | collective-permute-start | bytes 1179656 | tf_op jit(solution)/shard_map/ppermute | solution.py:125
  25.1 16.2 %collective-permute-start.4 = (bf16[2,64,1536]{2,1,0:T(8,128)(2,1)S(1)}, bf16[2,64,1536]{2,1,0:T(8,128)(2,1)S(1)}, u32[]{:S(2)}, u32[]{:S(2)}) collective-permute-start(bf16[2,64,1536]{2,1,0:T(8,128)(2,1)S(1)} %pad_maximum_fusion.5), channel_id=1, source_target_pairs={{0,4},{1,5},{2,6},{3,7},{4,0},{5,1},{6,2},{7,3},{8,12},{9,13},{10,... | collective-permute-start | bytes 1179656 | tf_op jit(solution)/shard_map/ppermute | solution.py:125
  25.9 19.1 %collective-permute-start.3 = (bf16[2,64,1536]{2,1,0:T(8,128)(2,1)S(1)}, bf16[2,64,1536]{2,1,0:T(8,128)(2,1)S(1)}, u32[]{:S(2)}, u32[]{:S(2)}) collective-permute-start(bf16[2,64,1536]{2,1,0:T(8,128)(2,1)S(1)} %pad_maximum_fusion.5), channel_id=1, source_target_pairs={{0,2},{1,3},{2,4},{3,5},{4,6},{5,7},{6,0},{7,1},{8,10},{9,11},{10,... | collective-permute-start | bytes 1179656 | tf_op jit(solution)/shard_map/ppermute | solution.py:125
  26.8 9.4 %collective-permute-start.7 = (bf16[2,16,1536]{2,1,0:T(8,128)(2,1)S(1)}, bf16[2,16,1536]{2,1,0:T(8,128)(2,1)S(1)}, u32[]{:S(2)}, u32[]{:S(2)}) collective-permute-start(bf16[2,16,1536]{2,1,0:T(8,128)(2,1)S(1)} %pad_maximum_fusion.8), channel_id=1, source_target_pairs={{0,16},{8,24},{16,0},{24,8},{1,17},{9,25},{17,1},{25,9},{2,18},{10... | collective-permute-start | bytes 294920 | tf_op jit(solution)/shard_map/ppermute | solution.py:122
  28.5 8.7 %collective-permute-start.6 = (bf16[2,16,1536]{2,1,0:T(8,128)(2,1)S(1)}, bf16[2,16,1536]{2,1,0:T(8,128)(2,1)S(1)}, u32[]{:S(2)}, u32[]{:S(2)}) collective-permute-start(bf16[2,16,1536]{2,1,0:T(8,128)(2,1)S(1)} %pad_maximum_fusion.8), channel_id=1, source_target_pairs={{0,8},{8,16},{16,24},{24,0},{1,9},{9,17},{17,25},{25,1},{2,10},{10... | collective-permute-start | bytes 294920 | tf_op jit(solution)/shard_map/ppermute | solution.py:122
  45.3 5.0 %copy-start.7 = (bf16[256,1536]{1,0:T(8,128)(2,1)}, bf16[256,1536]{1,0:T(8,128)(2,1)S(1)}, u32[]{:S(2)}) copy-start(bf16[256,1536]{1,0:T(8,128)(2,1)S(1)} %get-tuple-element.131) | copy-start | bytes 2359300
  45.3 5.0 %copy-start.4 = (bf16[256,1536]{1,0:T(8,128)(2,1)}, bf16[256,1536]{1,0:T(8,128)(2,1)S(1)}, u32[]{:S(2)}) copy-start(bf16[256,1536]{1,0:T(8,128)(2,1)S(1)} %get-tuple-element.132) | copy-start | bytes 2359300
  45.3 3.6 %collective-permute-start.9 = (bf16[256,1536]{1,0:T(8,128)(2,1)S(1)}, bf16[256,1536]{1,0:T(8,128)(2,1)S(1)}, u32[]{:S(2)}, u32[]{:S(2)}) collective-permute-start(bf16[256,1536]{1,0:T(8,128)(2,1)S(1)} %get-tuple-element.131), channel_id=1, source_target_pairs={{0,1},{1,0},{2,3},{3,2},{4,5},{5,4},{6,7},{7,6},{8,9},{9,8},{10,11... | collective-permute-start | bytes 2359304 | tf_op jit(solution)/shard_map/ppermute | solution.py:128
  45.4 4.9 %collective-permute-start.10 = (bf16[256,1536]{1,0:T(8,128)(2,1)S(1)}, bf16[256,1536]{1,0:T(8,128)(2,1)S(1)}, u32[]{:S(2)}, u32[]{:S(2)}) collective-permute-start(bf16[256,1536]{1,0:T(8,128)(2,1)S(1)} %get-tuple-element.132), channel_id=1, source_target_pairs={{0,1},{1,0},{2,3},{3,2},{4,5},{5,4},{6,7},{7,6},{8,9},{9,8},{10,11... | collective-permute-start | bytes 2359304 | tf_op jit(solution)/shard_map/ppermute | solution.py:128
  45.9 24.0 %collective-permute-start.13 = (bf16[2,64,1536]{2,1,0:T(8,128)(2,1)S(1)}, bf16[2,64,1536]{2,1,0:T(8,128)(2,1)S(1)}, u32[]{:S(2)}, u32[]{:S(2)}) collective-permute-start(bf16[2,64,1536]{2,1,0:T(8,128)(2,1)S(1)} %pad_maximum_fusion.6), channel_id=1, source_target_pairs={{0,6},{1,7},{2,0},{3,1},{4,2},{5,3},{6,4},{7,5},{8,14},{9,15},{10,... | collective-permute-start | bytes 1179656 | tf_op jit(solution)/shard_map/ppermute | solution.py:125
  46.5 22.6 %collective-permute-start.12 = (bf16[2,64,1536]{2,1,0:T(8,128)(2,1)S(1)}, bf16[2,64,1536]{2,1,0:T(8,128)(2,1)S(1)}, u32[]{:S(2)}, u32[]{:S(2)}) collective-permute-start(bf16[2,64,1536]{2,1,0:T(8,128)(2,1)S(1)} %pad_maximum_fusion.6), channel_id=1, source_target_pairs={{0,4},{1,5},{2,6},{3,7},{4,0},{5,1},{6,2},{7,3},{8,12},{9,13},{10,... | collective-permute-start | bytes 1179656 | tf_op jit(solution)/shard_map/ppermute | solution.py:125
  47.3 20.1 %collective-permute-start.11 = (bf16[2,64,1536]{2,1,0:T(8,128)(2,1)S(1)}, bf16[2,64,1536]{2,1,0:T(8,128)(2,1)}, u32[]{:S(2)}, u32[]{:S(2)}) collective-permute-start(bf16[2,64,1536]{2,1,0:T(8,128)(2,1)S(1)} %pad_maximum_fusion.6), channel_id=1, source_target_pairs={{0,2},{1,3},{2,4},{3,5},{4,6},{5,7},{6,0},{7,1},{8,10},{9,11},{10,... | collective-permute-start | bytes 1179656 | tf_op jit(solution)/shard_map/ppermute | solution.py:125
  48.9 1.9 %copy-start.15 = (bf16[768,1536]{1,0:T(8,128)(2,1)S(1)}, bf16[768,1536]{1,0:T(8,128)(2,1)}, u32[]{:S(2)}) copy-start(bf16[768,1536]{1,0:T(8,128)(2,1)} %param.8) | copy-start | bytes 7077892
  48.9 1.4 copy-start.17
  50.9 1.4 copy-start.11
  53.9 25.4 %all-to-all-start = ((f16[8,2,64,768]{3,2,1,0:T(8,128)(2,1)}), f16[8,2,64,768]{3,2,1,0:T(8,128)(2,1)}, u32[]{:S(2)}, u32[]{:S(2)}) async-start(f16[8,2,64,768]{3,2,1,0:T(8,128)(2,1)} %pad_maximum_fusion.2), calls=%async_computation | async-start | bytes 3145728 | tf_op jit(solution)/shard_map/all_to_all | solution.py:147
  72.2 3.8 %copy-start.9 = (bf16[256,1536]{1,0:T(8,128)(2,1)}, bf16[256,1536]{1,0:T(8,128)(2,1)S(1)}, u32[]{:S(2)}) copy-start(bf16[256,1536]{1,0:T(8,128)(2,1)S(1)} %get-tuple-element.129) | copy-start | bytes 2359300
  72.2 3.8 %copy-start.5 = (bf16[256,1536]{1,0:T(8,128)(2,1)}, bf16[256,1536]{1,0:T(8,128)(2,1)S(1)}, u32[]{:S(2)}) copy-start(bf16[256,1536]{1,0:T(8,128)(2,1)S(1)} %get-tuple-element.130) | copy-start | bytes 2359300
  72.2 2.4 %collective-permute-start.14 = (bf16[256,1536]{1,0:T(8,128)(2,1)S(1)}, bf16[256,1536]{1,0:T(8,128)(2,1)S(1)}, u32[]{:S(2)}, u32[]{:S(2)}) collective-permute-start(bf16[256,1536]{1,0:T(8,128)(2,1)S(1)} %get-tuple-element.129), channel_id=1, source_target_pairs={{0,1},{1,0},{2,3},{3,2},{4,5},{5,4},{6,7},{7,6},{8,9},{9,8},{10,11... | collective-permute-start | bytes 2359304 | tf_op jit(solution)/shard_map/ppermute | solution.py:128
  72.3 3.7 %copy-start.16 = (bf16[768,1536]{1,0:T(8,128)(2,1)S(1)}, bf16[768,1536]{1,0:T(8,128)(2,1)}, u32[]{:S(2)}) copy-start(bf16[768,1536]{1,0:T(8,128)(2,1)} %param.8) | copy-start | bytes 7077892
  72.3 3.7 %collective-permute-start.15 = (bf16[256,1536]{1,0:T(8,128)(2,1)S(1)}, bf16[256,1536]{1,0:T(8,128)(2,1)S(1)}, u32[]{:S(2)}, u32[]{:S(2)}) collective-permute-start(bf16[256,1536]{1,0:T(8,128)(2,1)S(1)} %get-tuple-element.130), channel_id=1, source_target_pairs={{0,1},{1,0},{2,3},{3,2},{4,5},{5,4},{6,7},{7,6},{8,9},{9,8},{10,11... | collective-permute-start | bytes 2359304 | tf_op jit(solution)/shard_map/ppermute | solution.py:128
  74.6 1.4 copy-start.19
  76.0 1.4 copy-start.12
  79.1 6.1 %copy-start.14 = (f32[768]{0:T(1024)S(1)}, f32[768]{0:T(1024)}, u32[]{:S(2)}) copy-start(f32[768]{0:T(1024)} %param.7) | copy-start | bytes 9220
  79.3 26.1 %all-to-all-start.1 = ((f16[8,2,64,768]{3,2,1,0:T(8,128)(2,1)}), f16[8,2,64,768]{3,2,1,0:T(8,128)(2,1)}, u32[]{:S(2)}, u32[]{:S(2)}) async-start(f16[8,2,64,768]{3,2,1,0:T(8,128)(2,1)} %pad_maximum_fusion.4), calls=%async_computation.1 | async-start | bytes 3145728 | tf_op jit(solution)/shard_map/all_to_all | solution.py:147
  105.4 15.8 %all-to-all-start.2 = ((bf16[8,64,768]{2,1,0:T(8,128)(2,1)}), bf16[8,64,768]{2,1,0:T(8,128)(2,1)S(1)}, u32[]{:S(2)}, u32[]{:S(2)}) async-start(bf16[8,64,768]{2,1,0:T(8,128)(2,1)} %get-tuple-element.69), calls=%async_computation.2 | async-start | bytes 1572864 | tf_op jit(solution)/shard_map/all_to_all | solution.py:147
  109.6 1.6 copy-start.6
  109.6 1.8 %copy-start.13 = (bf16[256,1536]{1,0:T(8,128)(2,1)S(1)}, bf16[256,1536]{1,0:T(8,128)(2,1)}, u32[]{:S(2)}) copy-start(bf16[256,1536]{1,0:T(8,128)(2,1)} %copy-done.12) | copy-start | bytes 2359300
  116.8 1.1 copy-start.1
  121.2 4.7 %copy-start.2 = (bf16[8,64,768]{2,1,0:T(8,128)(2,1)}, bf16[8,64,768]{2,1,0:T(8,128)(2,1)S(1)}, u32[]{:S(2)}) copy-start(bf16[8,64,768]{2,1,0:T(8,128)(2,1)S(1)} %all-to-all-done.2) | copy-start | bytes 2359300
  121.2 15.9 %all-to-all-start.3 = ((bf16[8,64,768]{2,1,0:T(8,128)(2,1)}), bf16[8,64,768]{2,1,0:T(8,128)(2,1)}, u32[]{:S(2)}, u32[]{:S(2)}) async-start(bf16[8,64,768]{2,1,0:T(8,128)(2,1)} %get-tuple-element.81), calls=%async_computation.3 | async-start | bytes 1572864 | tf_op jit(solution)/shard_map/all_to_all | solution.py:147
  126.8 2.4 %collective-permute-start.16 = (bf16[256,1536]{1,0:T(8,128)(2,1)S(1)}, bf16[256,1536]{1,0:T(8,128)(2,1)S(1)}, u32[]{:S(2)}, u32[]{:S(2)}) collective-permute-start(bf16[256,1536]{1,0:T(8,128)(2,1)S(1)} %convolution_convert_fusion.1), channel_id=1, source_target_pairs={{0,1},{1,0},{2,3},{3,2},{4,5},{5,4},{6,7},{7,6},{8,9},{9,8},{10,11... | collective-permute-start | bytes 2359304 | tf_op jit(solution)/shard_map/ppermute | solution.py:128
  130.1 9.7 %collective-permute-start.17 = (bf16[64,1536]{1,0:T(8,128)(2,1)}, bf16[64,1536]{1,0:T(8,128)(2,1)S(1)}, u32[]{:S(2)}, u32[]{:S(2)}) collective-permute-start(bf16[64,1536]{1,0:T(8,128)(2,1)} %get-tuple-element.78), channel_id=1, source_target_pairs={{0,6},{1,7},{2,0},{3,1},{4,2},{5,3},{6,4},{7,5},{8,14},{9,15},{10,... | collective-permute-start | bytes 589832 | tf_op jit(solution)/shard_map/ppermute | solution.py:125
  131.5 8.4 %collective-permute-start.18 = (bf16[64,1536]{1,0:T(8,128)(2,1)}, bf16[64,1536]{1,0:T(8,128)(2,1)S(1)}, u32[]{:S(2)}, u32[]{:S(2)}) collective-permute-start(bf16[64,1536]{1,0:T(8,128)(2,1)} %get-tuple-element.79), channel_id=1, source_target_pairs={{0,4},{1,5},{2,6},{3,7},{4,0},{5,1},{6,2},{7,3},{8,12},{9,13},{10,... | collective-permute-start | bytes 589832 | tf_op jit(solution)/shard_map/ppermute | solution.py:125
  139.9 33.3 %all-to-all-start.4 = ((bf16[8,2,64,768]{3,2,1,0:T(8,128)(2,1)}), bf16[8,2,64,768]{3,2,1,0:T(8,128)(2,1)}, u32[]{:S(2)}, u32[]{:S(2)}) async-start(bf16[8,2,64,768]{3,2,1,0:T(8,128)(2,1)} %copy-done.1), calls=%async_computation.4 | async-start | bytes 3145728 | tf_op jit(solution)/shard_map/all_to_all | solution.py:147
  145.6 5.5 %collective-permute-start.20 = (bf16[256,1536]{1,0:T(8,128)(2,1)}, bf16[256,1536]{1,0:T(8,128)(2,1)S(1)}, u32[]{:S(2)}, u32[]{:S(2)}) collective-permute-start(bf16[256,1536]{1,0:T(8,128)(2,1)} %convolution_convert_fusion), channel_id=1, source_target_pairs={{0,1},{1,0},{2,3},{3,2},{4,5},{5,4},{6,7},{7,6},{8,9},{9,8},{10,11... | collective-permute-start | bytes 2359304 | tf_op jit(solution)/shard_map/ppermute | solution.py:128
  145.6 14.7 %collective-permute-start.19 = (bf16[64,1536]{1,0:T(8,128)(2,1)S(1)}, bf16[64,1536]{1,0:T(8,128)(2,1)S(1)}, u32[]{:S(2)}, u32[]{:S(2)}) collective-permute-start(bf16[64,1536]{1,0:T(8,128)(2,1)S(1)} %get-tuple-element.86), channel_id=1, source_target_pairs={{0,2},{1,3},{2,4},{3,5},{4,6},{5,7},{6,0},{7,1},{8,10},{9,11},{10,... | collective-permute-start | bytes 589832 | tf_op jit(solution)/shard_map/ppermute | solution.py:125
  149.2 6.0 %copy-start.20 = (bf16[256,1536]{1,0:T(8,128)(2,1)S(1)}, bf16[256,1536]{1,0:T(8,128)(2,1)}, u32[]{:S(2)}) copy-start(bf16[256,1536]{1,0:T(8,128)(2,1)} %copy-done.19) | copy-start | bytes 2359300
  151.0 4.1 %copy-start.3 = (bf16[8,64,768]{2,1,0:T(8,128)(2,1)S(1)}, bf16[8,64,768]{2,1,0:T(8,128)(2,1)}, u32[]{:S(2)}) copy-start(bf16[8,64,768]{2,1,0:T(8,128)(2,1)} %copy-done.2) | copy-start | bytes 2359300
  151.1 4.1 %copy-start.8 = (bf16[256,1536]{1,0:T(8,128)(2,1)S(1)}, bf16[256,1536]{1,0:T(8,128)(2,1)}, u32[]{:S(2)}) copy-start(bf16[256,1536]{1,0:T(8,128)(2,1)} %copy-done.7) | copy-start | bytes 2359300
  151.1 4.1 %copy-start.10 = (bf16[256,1536]{1,0:T(8,128)(2,1)S(1)}, bf16[256,1536]{1,0:T(8,128)(2,1)}, u32[]{:S(2)}) copy-start(bf16[256,1536]{1,0:T(8,128)(2,1)} %copy-done.9) | copy-start | bytes 2359300
  151.1 4.1 %copy-start.18 = (bf16[256,1536]{1,0:T(8,128)(2,1)S(1)}, bf16[256,1536]{1,0:T(8,128)(2,1)}, u32[]{:S(2)}) copy-start(bf16[256,1536]{1,0:T(8,128)(2,1)} %copy-done.17) | copy-start | bytes 2359300
  151.3 11.7 %collective-permute-start.24 = (bf16[64,1536]{1,0:T(8,128)(2,1)S(1)}, bf16[64,1536]{1,0:T(8,128)(2,1)S(1)}, u32[]{:S(2)}, u32[]{:S(2)}) collective-permute-start(bf16[64,1536]{1,0:T(8,128)(2,1)S(1)} %get-tuple-element.102), channel_id=1, source_target_pairs={{0,6},{1,7},{2,0},{3,1},{4,2},{5,3},{6,4},{7,5},{8,14},{9,15},{10,... | collective-permute-start | bytes 589832 | tf_op jit(solution)/shard_map/ppermute | solution.py:125
  152.9 12.7 %collective-permute-start.25 = (bf16[64,1536]{1,0:T(8,128)(2,1)S(1)}, bf16[64,1536]{1,0:T(8,128)(2,1)S(1)}, u32[]{:S(2)}, u32[]{:S(2)}) collective-permute-start(bf16[64,1536]{1,0:T(8,128)(2,1)S(1)} %get-tuple-element.103), channel_id=1, source_target_pairs={{0,4},{1,5},{2,6},{3,7},{4,0},{5,1},{6,2},{7,3},{8,12},{9,13},{10,... | collective-permute-start | bytes 589832 | tf_op jit(solution)/shard_map/ppermute | solution.py:125
  154.2 11.3 %collective-permute-start.26 = (bf16[64,1536]{1,0:T(8,128)(2,1)S(1)}, bf16[64,1536]{1,0:T(8,128)(2,1)S(1)}, u32[]{:S(2)}, u32[]{:S(2)}) collective-permute-start(bf16[64,1536]{1,0:T(8,128)(2,1)S(1)} %get-tuple-element.104), channel_id=1, source_target_pairs={{0,2},{1,3},{2,4},{3,5},{4,6},{5,7},{6,0},{7,1},{8,10},{9,11},{10,... | collective-permute-start | bytes 589832 | tf_op jit(solution)/shard_map/ppermute | solution.py:125
  160.6 12.6 %collective-permute-start.21 = (bf16[16,1536]{1,0:T(8,128)(2,1)S(1)}, bf16[16,1536]{1,0:T(8,128)(2,1)S(1)}, u32[]{:S(2)}, u32[]{:S(2)}) collective-permute-start(bf16[16,1536]{1,0:T(8,128)(2,1)S(1)} %get-tuple-element.98), channel_id=1, source_target_pairs={{0,24},{8,0},{16,8},{24,16},{1,25},{9,1},{17,9},{25,17},{2,26},{10... | collective-permute-start | bytes 147464 | tf_op jit(solution)/shard_map/ppermute | solution.py:122
  162.7 16.9 %collective-permute-start.22 = (bf16[16,1536]{1,0:T(8,128)(2,1)S(1)}, bf16[16,1536]{1,0:T(8,128)(2,1)S(1)}, u32[]{:S(2)}, u32[]{:S(2)}) collective-permute-start(bf16[16,1536]{1,0:T(8,128)(2,1)S(1)} %get-tuple-element.99), channel_id=1, source_target_pairs={{0,16},{8,24},{16,0},{24,8},{1,17},{9,25},{17,1},{25,9},{2,18},{10... | collective-permute-start | bytes 147464 | tf_op jit(solution)/shard_map/ppermute | solution.py:122
  163.0 16.6 %collective-permute-start.23 = (bf16[16,1536]{1,0:T(8,128)(2,1)S(1)}, bf16[16,1536]{1,0:T(8,128)(2,1)S(1)}, u32[]{:S(2)}, u32[]{:S(2)}) collective-permute-start(bf16[16,1536]{1,0:T(8,128)(2,1)S(1)} %get-tuple-element.100), channel_id=1, source_target_pairs={{0,8},{8,16},{16,24},{24,0},{1,9},{9,17},{17,25},{25,1},{2,10},{10... | collective-permute-start | bytes 147464 | tf_op jit(solution)/shard_map/ppermute | solution.py:122
  165.8 13.7 %collective-permute-start.27 = (bf16[16,1536]{1,0:T(8,128)(2,1)S(1)}, bf16[16,1536]{1,0:T(8,128)(2,1)S(1)}, u32[]{:S(2)}, u32[]{:S(2)}) collective-permute-start(bf16[16,1536]{1,0:T(8,128)(2,1)S(1)} %get-tuple-element.106), channel_id=1, source_target_pairs={{0,24},{8,0},{16,8},{24,16},{1,25},{9,1},{17,9},{25,17},{2,26},{10... | collective-permute-start | bytes 147464 | tf_op jit(solution)/shard_map/ppermute | solution.py:122
  167.6 11.9 %collective-permute-start.28 = (bf16[16,1536]{1,0:T(8,128)(2,1)S(1)}, bf16[16,1536]{1,0:T(8,128)(2,1)S(1)}, u32[]{:S(2)}, u32[]{:S(2)}) collective-permute-start(bf16[16,1536]{1,0:T(8,128)(2,1)S(1)} %get-tuple-element.107), channel_id=1, source_target_pairs={{0,16},{8,24},{16,0},{24,8},{1,17},{9,25},{17,1},{25,9},{2,18},{10... | collective-permute-start | bytes 147464 | tf_op jit(solution)/shard_map/ppermute | solution.py:122
  173.1 6.4 %collective-permute-start.29 = (bf16[16,1536]{1,0:T(8,128)(2,1)S(1)}, bf16[16,1536]{1,0:T(8,128)(2,1)S(1)}, u32[]{:S(2)}, u32[]{:S(2)}) collective-permute-start(bf16[16,1536]{1,0:T(8,128)(2,1)S(1)} %get-tuple-element.108), channel_id=1, source_target_pairs={{0,8},{8,16},{16,24},{24,0},{1,9},{9,17},{17,25},{25,1},{2,10},{10... | collective-permute-start | bytes 147464 | tf_op jit(solution)/shard_map/ppermute | solution.py:122
